TPU v7x, 32 devices: a whole 2x2x4 slice. The times are simulated.
32 devices in a mesh: slab: 16 (over z, y, core), mem: 2 (over x).
Axes of the slice: x: 2, y: 2, z: 4, core: 2. Of those that a mesh axis runs over, the one named last changes fastest.
Arguments:
- present_ensemble: float32 [64, 4, 16, 512], P('mem', None, 'slab'), may hold values from -6 to 6
- delayed_ensemble: float32 [64, 2, 4, 16, 512], P('mem', None, None, 'slab'), may hold values from -6 to 6
- spreading_coefficient: float32 [16, 512], P('slab'), may hold values from 0.05 to 0.2
- transport_ratios: float32 [2, 16, 512], P(None, 'slab'), may hold values from -0.3 to 0.3
- obs_value: float32 [2, 256], replicated, may hold values from -6 to 6
- obs_error: float32 [2, 256], replicated, may hold values from 0.4 to 1.2
- obs_noise: float32 [2, 64, 256], replicated, may hold values from -6 to 6
- obs_row: int32 [2, 256], replicated, may hold values from 0 to 15
- obs_col: int32 [2, 256], replicated, may hold values from 1 to 510
- obs_field: int32 [2, 256], replicated, may hold values from 0 to 3
Outputs:
- analysis: float32 [64, 3, 4, 16, 512], P('mem', None, None, 'slab')
All inputs are finite; a program needn't handle non-finite values.
Results may differ from a plain program's by a relative error of at most 0.00011.
Values sent between devices are 32-bit elements; how exact they have to be, the bound alone decides.
No kernel may reach another device: no remote copies, remote signals or barrier semaphores. Data moves between devices by JAX's collectives and lax.ppermute only.
A program may use at most 64 MiB of HBM per device.

v0:
```python
import jax
import jax.numpy as jnp
from jax import lax
from jax.sharding import PartitionSpec as P


def extended(shard, sides, width):
    for axis, dim in sides:
        devices, length = (lax.axis_size(axis), shard.shape[dim])
        up = [(i, (i + 1) % devices) for i in range(devices - 1)]
        down = [(j, i) for i, j in up]
        last = lax.slice_in_dim(shard, length - width, length, axis=dim)
        leading = lax.slice_in_dim(shard, 0, width, axis=dim)
        before = lax.ppermute(last, axis, up)
        after = lax.ppermute(leading, axis, down)
        shard = jnp.concatenate([before, shard, after], axis=dim)
    return shard


def propagate_ahead(present_ensemble, spreading_coefficient, transport_ratios):
    rowed = extended(present_ensemble, (("slab", 2),), 1)
    padded = jnp.pad(rowed, ((0, 0), (0, 0), (0, 0), (1, 1)))
    below = padded[:, :, 2:, 1:-1]
    above = padded[:, :, :-2, 1:-1]
    right = padded[:, :, 1:-1, 2:]
    left = padded[:, :, 1:-1, :-2]
    laplacian_operator = below + above + right + left - 4.0 * present_ensemble
    return (
        present_ensemble
        + spreading_coefficient * laplacian_operator
        - transport_ratios[0] * (below - above) * 0.5
        - transport_ratios[1] * (right - left) * 0.5
    )


def observe(level_zero, rows, cols, fields, row_start, col_start):
    members, nfield, height, width = level_zero.shape
    flat = level_zero.reshape(members, nfield * height * width)
    total = jnp.zeros((members, rows.shape[0]), jnp.float32)
    for offset, factor in ((-1, 0.25), (0, 0.5), (1, 0.25)):
        row_within = rows - row_start
        column_within = cols + offset - col_start
        valid = (
            (row_within >= 0)
            & (row_within < height)
            & (column_within >= 0)
            & (column_within < width)
        )
        index = (fields * height + jnp.clip(row_within, 0, height - 1)) * width + jnp.clip(
            column_within, 0, width - 1
        )
        picked = jnp.take(flat, index, axis=1)
        total = total + factor * jnp.where(valid[None, :], picked, 0.0)
    return total


def transform(observed, values, errors, noise):
    members = observed.shape[0]
    rescaled_values = (observed - jnp.mean(observed, axis=0, keepdims=True)) / errors[None, :]
    innovation = (values[None, :] - observed) / errors[None, :] + noise
    eye = jnp.eye(members, dtype=jnp.float32)
    system = (
        jnp.dot(
            rescaled_values,
            rescaled_values.T,
            precision=lax.Precision.HIGHEST,
            preferred_element_type=jnp.float32,
        )
        + (members - 1.0) * eye
    )
    right = jnp.dot(
        rescaled_values,
        innovation.T,
        precision=lax.Precision.HIGHEST,
        preferred_element_type=jnp.float32,
    )
    factor = jnp.linalg.cholesky(system)
    middle = lax.linalg.triangular_solve(factor, right, left_side=True, lower=True)
    weights = lax.linalg.triangular_solve(
        factor, middle, left_side=True, lower=True, transpose_a=True
    )
    return eye + weights - jnp.mean(weights, axis=0, keepdims=True)


def chain_product(prior_obs, obs_value, obs_error, obs_noise):
    members = prior_obs.shape[1]
    product = jnp.eye(members, dtype=jnp.float32)
    for batch in range(prior_obs.shape[0]):
        observed = jnp.dot(
            product.T,
            prior_obs[batch],
            precision=lax.Precision.HIGHEST,
            preferred_element_type=jnp.float32,
        )
        matrix = transform(observed, obs_value[batch], obs_error[batch], obs_noise[batch])
        product = jnp.dot(
            product, matrix, precision=lax.Precision.HIGHEST, preferred_element_type=jnp.float32
        )
    return product


def shards(
    present_ensemble,
    delayed_ensemble,
    spreading_coefficient,
    transport_ratios,
    obs_value,
    obs_error,
    obs_noise,
    obs_row,
    obs_col,
    obs_field,
):
    rows_here = present_ensemble.shape[2]
    row_start = lax.axis_index("slab") * rows_here
    predictive_dynamics = propagate_ahead(present_ensemble, spreading_coefficient, transport_ratios)
    flattened_system_array = jnp.concatenate(
        [predictive_dynamics[:, None], delayed_ensemble], axis=1
    )
    batch_count = obs_row.shape[0]
    terms = jnp.stack(
        [
            observe(
                flattened_system_array[:, 0],
                obs_row[batch],
                obs_col[batch],
                obs_field[batch],
                row_start,
                0,
            )
            for batch in range(batch_count)
        ],
        axis=0,
    )
    summed = lax.psum(terms, "slab")
    prior_obs = lax.all_gather(summed, "mem", axis=1, tiled=True)
    product = chain_product(prior_obs, obs_value, obs_error, obs_noise)
    local_count = flattened_system_array.shape[0]
    own_rows = lax.dynamic_slice_in_dim(
        product, lax.axis_index("mem") * local_count, local_count, 0
    )
    return lax.psum_scatter(
        jnp.einsum(
            "jlfrn,jm->mlfrn", flattened_system_array, own_rows, precision=lax.Precision.HIGHEST
        ),
        "mem",
        scatter_dimension=0,
        tiled=True,
    )


def solution(mesh):
    return jax.shard_map(
        shards,
        mesh=mesh,
        in_specs=(
            P("mem", None, "slab", None),
            P("mem", None, None, "slab", None),
            P("slab", None),
            P(None, "slab", None),
            P(),
            P(),
            P(),
            P(),
            P(),
            P(),
        ),
        out_specs=P("mem", None, None, "slab", None),
        check_vma=False,
    )
```

profile of v0, /device:TPU:0, one launch (start us, length us, event | category | flops | bytes accessed | tf_op | source)
XLA Modules:
  0.0 188.7 jit_solution(16572493313616070980)
XLA Ops:
  6.5 1.1 copy.71
  7.6 1.3 collective-permute-start
  8.9 3.0 %collective-permute-start.1 = (f32[32,4,1,512]{3,0,1,2:T(8,128)S(1)}, f32[32,4,1,512]{3,0,1,2:T(8,128)S(1)}, u32[]{:S(2)}, u32[]{:S(2)}) collective-permute-start(f32[32,4,1,512]{3,0,1,2:T(8,128)S(1)} %copy.71), channel_id=1, source_target_pairs={{0,2},{2,4},{4,6},{6,8},{8,10},{10,12},{12,14},{14,16},{16,18},{18... | collective-permute-start | bytes 786440 | tf_op jit(solution)/shard_map/ppermute | solution.py:14
  12.0 0.8 clamp_add_fusion.5
  12.8 0.8 clamp_add_fusion.4
  13.7 0.8 compare_and_fusion
  14.6 0.8 fusion.67
  15.3 0.8 and_reduce_fusion.5
  17.8 0.7 gather_fusion.4
  18.5 0.7 gather_fusion.1
  19.3 0.7 gather_fusion.2
  20.0 0.7 gather_fusion.5
  20.7 0.7 gather_fusion
  21.4 0.7 gather_fusion.3
  24.0 92.4 %all-reduce.3.cloned.1.call-done = f32[2,32,256]{1,2,0:T(8,128)} async-done(((f32[2,32,256]{1,2,0:T(8,128)}), f32[2,32,256]{1,2,0:T(8,128)}) %all-reduce.3.cloned.1.call-update) | async-done | bytes 65552 | tf_op jit(solution)/shard_map/psum | solution.py:135
  116.3 1.1 copy.79
  117.4 5.2 %all_gather.3 = f32[2,64,256]{2,0,1:T(2,128)S(1)} all-gather(f32[2,32,256]{2,0,1:T(2,128)S(1)} %copy.79), channel_id=1, replica_groups=mesh['slab'=16,'mem'=2] {'mem'}, dimensions={1}, use_global_device_ids=true | all-gather | bytes 196608 | tf_op jit(solution)/shard_map/all_gather | solution.py:136
  123.2 5.8 %cholesky.44 = f32[64,64]{1,0:T(8,128)S(1)} custom-call(f32[64,64]{1,0:T(8,128)S(1)} %fusion.46), custom_call_target="Cholesky" | custom-call | tf_op jit(solution)/shard_map/jit(cholesky)/cholesky | solution.py:77
  130.4 4.9 %custom-call.11 = f32[1,64,64]{1,2,0:T(8,128)S(1)} custom-call(f32[1,64,64]{2,1,0:T(8,128)S(1)} %fusion.29), custom_call_target="InvertDiagBlocksLowerTriangular" | custom-call | tf_op jit(solution)/shard_map/triangular_solve/custom-call.2 | solution.py:79
  136.9 5.8 %cholesky.55 = f32[64,64]{1,0:T(8,128)S(1)} custom-call(f32[64,64]{1,0:T(8,128)S(1)} %fusion.41), custom_call_target="Cholesky" | custom-call | tf_op jit(solution)/shard_map/jit(cholesky)/cholesky | solution.py:77
  144.1 4.9 %custom-call.13 = f32[1,64,64]{1,2,0:T(8,128)S(1)} custom-call(f32[1,64,64]{2,1,0:T(8,128)S(1)} %fusion.30), custom_call_target="InvertDiagBlocksLowerTriangular" | custom-call | tf_op jit(solution)/shard_map/triangular_solve/custom-call.2 | solution.py:79
  150.0 2.6 %convolution_bitcast_fusion = f32[64,3,4,1,512]{4,0,2,1,3:T(8,128)} fusion(f32[32,2,4,1,512]{4,0,2,1,3:T(8,128)S(1)} %copy.86, f32[32,1,4,1,512]{4,0,2,1,3:T(8,128)S(1)} %bitcast.131, f32[64,64]{1,0:T(8,128)S(1)} %fusion.35, s32[]{:T(128)S(6)} %select_n.38), kind=kOutput, calls=%fused_computation.6 | convolution fusion | flops 151191552 | bytes 2375684 | tf_op jit(solution)/shard_map/jlfrn,jm->mlfrn/dot_general | solution.py:143
  152.6 26.4 %reduce-scatter.2.cloned.1.call-done = f32[32,3,4,1,512]{4,0,2,1,3:T(8,128)} async-done(((f32[64,3,4,1,512]{4,0,2,1,3:T(8,128)}), f32[32,3,4,1,512]{4,0,2,1,3:T(8,128)}) %reduce-scatter.2.cloned.1.call-update) | async-done | bytes 786448 | tf_op jit(solution)/shard_map/reduce_scatter | solution.py:142
  179.0 2.8 %copy.87 = f32[32,3,4,1,512]{4,3,2,1,0:T(1,128)} copy(f32[32,3,4,1,512]{4,0,2,1,3:T(8,128)} %reduce-scatter.2.cloned.1.call-done) | data formatting | bytes 1572864 | tf_op jit(solution)/shard_map/reduce_scatter | solution.py:142
  (71 shorter events, 9.2 us)
Async XLA Ops:
  6.5 10.7 %copy-start = (f32[32,4,1,512]{3,2,1,0:T(1,128)S(1)}, f32[32,4,1,512]{3,2,1,0:T(1,128)}, u32[]{:S(2)}) copy-start(f32[32,4,1,512]{3,2,1,0:T(1,128)} %param.17) | copy-start | bytes 786436
  6.5 10.7 %copy-start.2 = (f32[1,512]{1,0:T(1,128)S(1)}, f32[1,512]{1,0:T(1,128)}, u32[]{:S(2)}) copy-start(f32[1,512]{1,0:T(1,128)} %param.19) | copy-start | bytes 6148
  6.5 109.8 %all-reduce.3.cloned.1.call-start = ((), (), s32[]{:S(2)}) async-start(), calls=%async_computation.1 | async-start | bytes 524288 | tf_op jit(solution)/shard_map/psum | solution.py:135
  7.6 9.2 %collective-permute-start = (f32[32,4,1,512]{3,0,1,2:T(8,128)S(1)}, f32[32,4,1,512]{3,0,1,2:T(8,128)S(1)}, u32[]{:S(2)}, u32[]{:S(2)}) collective-permute-start(f32[32,4,1,512]{3,0,1,2:T(8,128)S(1)} %copy.71), channel_id=1, source_target_pairs={{2,0},{4,2},{6,4},{8,6},{10,8},{12,10},{14,12},{16,14},{18,16},{20... | collective-permute-start | bytes 786440 | tf_op jit(solution)/shard_map/ppermute | solution.py:15
  8.9 7.9 %collective-permute-start.1 = (f32[32,4,1,512]{3,0,1,2:T(8,128)S(1)}, f32[32,4,1,512]{3,0,1,2:T(8,128)S(1)}, u32[]{:S(2)}, u32[]{:S(2)}) collective-permute-start(f32[32,4,1,512]{3,0,1,2:T(8,128)S(1)} %copy.71), channel_id=1, source_target_pairs={{0,2},{2,4},{4,6},{6,8},{8,10},{10,12},{12,14},{14,16},{16,18},{18... | collective-permute-start | bytes 786440 | tf_op jit(solution)/shard_map/ppermute | solution.py:14
  19.2 4.4 %copy-start.3 = (f32[2,256]{1,0:T(2,128)S(1)}, f32[2,256]{1,0:T(2,128)}, u32[]{:S(2)}) copy-start(f32[2,256]{1,0:T(2,128)} %param.21) | copy-start | bytes 6148
  19.2 4.4 %copy-start.1 = (f32[32,2,4,1,512]{4,3,2,1,0:T(1,128)S(1)}, f32[32,2,4,1,512]{4,3,2,1,0:T(1,128)}, u32[]{:S(2)}) copy-start(f32[32,2,4,1,512]{4,3,2,1,0:T(1,128)} %param.18) | copy-start | bytes 1572868
  22.8 112.5 %copy-start.4 = (f32[2,64,256]{2,1,0:T(8,128)S(1)}, f32[2,64,256]{2,1,0:T(8,128)}, u32[]{:S(2)}) copy-start(f32[2,64,256]{2,1,0:T(8,128)} %param.23) | copy-start | bytes 393220
  23.6 155.5 %reduce-scatter.2.cloned.1.call-start = ((), (), s32[]{:S(2)}) async-start(), calls=%async_computation.2 | async-start | bytes 2359296 | tf_op jit(solution)/shard_map/reduce_scatter | solution.py:142
Sparse Core Ops, SparseCore 0:
  23.7 92.6 all-reduce.2
  152.7 26.2 reduce-scatter.1
where the time goes:
time: 189 us
  waiting for transfers between devices  119 us (63%)
  other arithmetic  29.3 us (16%)
  between operations  13.8 us (7%)
  local copies, waits for them, and re-layouts  11.9 us (6%)
  matrix products  5.23 us (3%)
  blocking collectives  5.2 us (3%)
  starting transfers between devices  4.38 us (2%)
    psum x1, waiting for transfers between devices, shards(): summed = lax.psum(terms, 'slab')  92.4 us
    reduce_scatter x1, waiting for transfers between devices, shards(): lax.psum_scatter(jnp.einsum('jlfrn,jm->mlfrn', flattened_system_array, ow...  26.4 us
    another operation x6, other arithmetic, transform(): factor = jnp.linalg.cholesky(system)  13 us
    another operation x4, other arithmetic, transform(): lax.linalg.triangular_solve(factor, middle, left_side=True, lower=True, t...  11.1 us
    all_gather x1, blocking collectives, shards(): prior_obs = lax.all_gather(summed, 'mem', axis=1, tiled=True)  5.2 us
    gather x6, local copies, waits for them, and re-layouts, observe(): picked = jnp.take(flat, index, axis=1)  4.38 us
  transfers between devices with their start and end apart: 4, of which 2 were waited for; matrix products, arithmetic and copies ran while one was open for 3% of the time, Pallas kernels for 0%

commit v1 on v0

v1 whole, which is shorter than its diff:
```python
import functools

import jax
import jax.numpy as jnp
from jax import lax
from jax.experimental import pallas as pl
from jax.experimental.pallas import tpu as pltpu
from jax.sharding import PartitionSpec as P

LANES = 128
F32 = jnp.float32
BF16 = jnp.bfloat16
HIGHEST = lax.Precision.HIGHEST
VMEM_LIMIT = 48 * 1024 * 1024


def rows_of(array):
    return array.reshape(-1, LANES)


def split_two(x):
    high = x.astype(BF16)
    low = (x - high.astype(F32)).astype(BF16)
    return high, low


def forecast_kernel(
    members,
    fields,
    chunks,
    present_ref,
    above_ref,
    below_ref,
    delayed_ref,
    spread_ref,
    ratio_ref,
    row_ref,
    col_ref,
    field_ref,
    state_ref,
    obs_ref,
):
    width = chunks * LANES
    planes = fields * chunks
    lagged = delayed_ref.shape[0] // members
    levels_planes = planes + lagged

    def plane(ref, start, stride):
        return jnp.concatenate(
            [ref[pl.ds(start + c, members, stride=stride), :] for c in range(chunks)], axis=1
        )

    def line(ref, start):
        return jnp.concatenate([ref[start + c : start + c + 1, :] for c in range(chunks)], axis=1)

    spread = line(spread_ref, 0)
    along_rows = line(ratio_ref, 0)
    along_columns = line(ratio_ref, chunks)
    lane = lax.broadcasted_iota(jnp.int32, (members, width), 1)
    forecasts = []
    for f in range(fields):
        here = plane(present_ref, f * chunks, planes)
        above = plane(above_ref, f * chunks, planes)
        below = plane(below_ref, f * chunks, planes)
        left = jnp.where(lane == 0, 0.0, pltpu.roll(here, 1, 1))
        right = jnp.where(lane == width - 1, 0.0, pltpu.roll(here, width - 1, 1))
        laplacian = below + above + right + left - 4.0 * here
        ahead = (
            here
            + spread * laplacian
            - along_rows * (below - above) * 0.5
            - along_columns * (right - left) * 0.5
        )
        forecasts.append(ahead)
        for c in range(chunks):
            state_ref[pl.ds(f * chunks + c, members, stride=levels_planes), :] = ahead[
                :, c * LANES : (c + 1) * LANES
            ]
    for k in range(lagged):
        state_ref[pl.ds(planes + k, members, stride=levels_planes), :] = delayed_ref[
            pl.ds(k, members, stride=lagged), :
        ]

    own_row = lax.axis_index("slab")
    batches, count = row_ref.shape
    total = batches * count
    flat = lambda ref: jnp.concatenate([ref[b : b + 1, :] for b in range(batches)], axis=1)
    rows, cols, kinds = flat(row_ref), flat(col_ref), flat(field_ref)
    kinds = jnp.where(rows == own_row, kinds, -1)
    at = lax.broadcasted_iota(jnp.int32, (width, total), 0).astype(F32) * 0.25
    taps = jnp.maximum(0.5 - jnp.abs(at - cols.astype(F32) * 0.25), 0.0).astype(BF16)
    stacked = jnp.concatenate(forecasts, axis=0)
    high, rest = stacked.astype(BF16), None
    rest = stacked - high.astype(F32)
    middle = rest.astype(BF16)
    low = (rest - middle.astype(F32)).astype(BF16)
    picked = (
        jnp.dot(low, taps, preferred_element_type=F32)
        + jnp.dot(middle, taps, preferred_element_type=F32)
        + jnp.dot(high, taps, preferred_element_type=F32)
    )
    observed = jnp.zeros((members, total), F32)
    for f in range(fields):
        observed = observed + jnp.where(kinds == f, picked[f * members : (f + 1) * members], 0.0)
    groups = total // LANES
    for g in range(groups):
        obs_ref[pl.ds(g, members, stride=groups), :] = observed[:, g * LANES : (g + 1) * LANES]


def solve_transposed(system, right_t, floor):
    size = system.shape[0]
    eye = (
        lax.broadcasted_iota(jnp.int32, (size, size), 0)
        == lax.broadcasted_iota(jnp.int32, (size, size), 1)
    ).astype(F32)
    top = jnp.max(jnp.sum(jnp.abs(system), axis=0, keepdims=True)) + 1.0
    scale = 2.0 / (top + floor)
    eps = (top - floor) / (top + floor)
    residual = eye - scale * system
    answer = scale * right_t

    def more(carry):
        return carry[0] > 1e-6

    def double(carry):
        eps, residual, answer = carry
        both = jnp.dot(
            jnp.concatenate([residual, answer], axis=0),
            residual,
            precision=HIGHEST,
            preferred_element_type=F32,
        )
        square = eps * eps
        share = 1.0 / (2.0 - square)
        return (
            square * share,
            (2.0 * both[:size] - square * eye) * share,
            (answer + both[size:]) * (2.0 * share),
        )

    return lax.while_loop(more, double, (eps, residual, answer))[2]


def analysis_kernel(
    parts, planes, prior_ref, value_ref, error_ref, noise_ref, *refs
):
    state_refs, out_ref = refs[:parts], refs[parts]
    batches, members, count = noise_ref.shape
    local = members // parts
    groups = count // LANES
    stride = batches * groups
    eye = (
        lax.broadcasted_iota(jnp.int32, (members, members), 0)
        == lax.broadcasted_iota(jnp.int32, (members, members), 1)
    ).astype(F32)
    product_t = None
    nt = (((1,), (1,)), ((), ()))
    for b in range(batches):
        observed = jnp.concatenate(
            [prior_ref[pl.ds(b * groups + g, members, stride=stride), :] for g in range(groups)],
            axis=1,
        )
        if product_t is not None:
            observed = jnp.dot(
                product_t, observed, precision=HIGHEST, preferred_element_type=F32
            )
        errors = error_ref[b : b + 1, :]
        scaled = (observed - jnp.mean(observed, axis=0, keepdims=True)) / errors
        innovation = (value_ref[b : b + 1, :] - observed) / errors + noise_ref[b]
        both = lax.dot_general(
            jnp.concatenate([scaled, innovation], axis=0),
            scaled,
            nt,
            precision=HIGHEST,
            preferred_element_type=F32,
        )
        system = both[:members] + (members - 1.0) * eye
        weights_t = solve_transposed(system, both[members:], members - 1.0)
        matrix_t = eye + weights_t - jnp.mean(weights_t, axis=1, keepdims=True)
        if product_t is None:
            product_t = matrix_t
        else:
            product_t = jnp.dot(
                matrix_t, product_t, precision=HIGHEST, preferred_element_type=F32
            )

    own = lax.axis_index("mem")
    is_own = (
        lax.broadcasted_iota(jnp.int32, (local, members), 0) + own * local
        == lax.broadcasted_iota(jnp.int32, (local, members), 1)
    ).astype(F32)
    mine = jnp.dot(is_own, product_t, precision=HIGHEST, preferred_element_type=F32)
    source = lax.broadcasted_iota(jnp.int32, (members, members), 0)
    target = lax.broadcasted_iota(jnp.int32, (members, members), 1)
    turn = (source == lax.rem(target + own * local, members)).astype(F32)
    mine = jnp.dot(mine, turn, precision=HIGHEST, preferred_element_type=F32)
    high, low = split_two(mine)
    left = jnp.concatenate([high, high, low], axis=1)
    step = 16
    for start in range(0, planes, step):
        held = jnp.concatenate(
            [
                jnp.concatenate(
                    [ref[pl.ds(start + k, local, stride=planes), :] for k in range(step)], axis=1
                )
                for ref in state_refs
            ],
            axis=0,
        )
        held_high, held_low = split_two(held)
        result = jnp.dot(
            left,
            jnp.concatenate([held_high, held_low, held_high], axis=0),
            preferred_element_type=F32,
        )
        for k in range(step):
            out_ref[pl.ds(start + k, local, stride=planes), :] = result[
                :, k * LANES : (k + 1) * LANES
            ]


def shards(
    present_ensemble,
    delayed_ensemble,
    spreading_coefficient,
    transport_ratios,
    obs_value,
    obs_error,
    obs_noise,
    obs_row,
    obs_col,
    obs_field,
):
    members, fields, height, width = present_ensemble.shape
    assert height == 1 and width % LANES == 0
    chunks = width // LANES
    lagged = delayed_ensemble.shape[1]
    slabs, parts = lax.axis_size("slab"), lax.axis_size("mem")
    batches, all_members, count = obs_noise.shape
    total = batches * count
    planes = (1 + lagged) * fields * chunks

    present = rows_of(present_ensemble)
    up = [(i, i + 1) for i in range(slabs - 1)]
    down = [(j, i) for i, j in up]
    above = lax.ppermute(present, "slab", up)
    below = lax.ppermute(present, "slab", down)
    params = pltpu.CompilerParams(vmem_limit_bytes=VMEM_LIMIT)
    state, terms = pl.pallas_call(
        functools.partial(forecast_kernel, members, fields, chunks),
        out_shape=(
            jax.ShapeDtypeStruct((members * planes, LANES), F32),
            jax.ShapeDtypeStruct((members * total // LANES, LANES), F32),
        ),
        compiler_params=params,
        name="forecast",
    )(
        present,
        above,
        below,
        rows_of(delayed_ensemble),
        rows_of(spreading_coefficient),
        rows_of(transport_ratios),
        obs_row,
        obs_col,
        obs_field,
    )
    others = [
        lax.ppermute(state, "mem", [((i + d) % parts, i) for i in range(parts)])
        for d in range(1, parts)
    ]
    if terms.shape[0] % (8 * slabs) == 0:
        pieces = lax.all_to_all(
            terms.reshape(slabs, -1, LANES), "slab", split_axis=0, concat_axis=0
        )
        prior = lax.all_gather(jnp.sum(pieces, axis=0), ("mem", "slab"), axis=0, tiled=True)
    else:
        prior = lax.all_gather(lax.psum(terms, "slab"), "mem", axis=0, tiled=True)
    out = pl.pallas_call(
        functools.partial(analysis_kernel, parts, planes),
        out_shape=jax.ShapeDtypeStruct((members * planes, LANES), F32),
        compiler_params=params,
        name="analysis",
    )(prior, obs_value, obs_error, obs_noise, state, *others)
    return out.reshape(members, 1 + lagged, fields, height, width)


def solution(mesh):
    return jax.shard_map(
        shards,
        mesh=mesh,
        in_specs=(
            P("mem", None, "slab", None),
            P("mem", None, None, "slab", None),
            P("slab", None),
            P(None, "slab", None),
            P(),
            P(),
            P(),
            P(),
            P(),
            P(),
        ),
        out_specs=P("mem", None, None, "slab", None),
        check_vma=False,
    )
```

time: 189 us -> 75.8 us (0.40)
  waiting for transfers between devices: 119 us -> 1.33 us
  blocking collectives: 5.2 us -> 55 us
  other arithmetic: 29.3 us -> 0.02 us
  between operations: 13.8 us -> 0.06 us
  local copies, waits for them, and re-layouts: 11.9 us -> 4.73 us
  Pallas kernels: 0 us -> 6.75 us
  matrix products: 5.23 us -> 0 us
  starting transfers between devices: 4.38 us -> 7.47 us
    psum x1 -> x0, waiting for transfers between devices: 92.4 us -> none  [shards(): summed = lax.psum(terms, 'slab')]
    all_gather x1, blocking collectives: 5.2 us -> 37.5 us  [shards(): lax.all_gather(jnp.sum(pieces, axis=0), ('mem', 'slab'), axis=0, tiled=True)]
    reduce_scatter x1 -> x0, waiting for transfers between devices: 26.4 us -> none  [shards(): lax.psum_scatter(jnp.einsum('jlfrn,jm->mlfrn', flattened_system_array, ow...]
    another operation x12 -> x0, other arithmetic: 25.5 us -> none  [the longest x6 13 us: transform(): factor = jnp.linalg.cholesky(system)]
    all_to_all x0 -> x1, blocking collectives: none -> 17.5 us  [shards(): lax.all_to_all(terms.reshape(slabs, -1, LANES), 'slab', split_axis=0, con...]
    pallas_call x0 -> x2, Pallas kernels: none -> 6.75 us  [the longest x1 5.42 us: shards(): pl.pallas_call(functools.partial(analysis_kernel, parts, planes), out_sha...]
    dot_general x9 -> x0, matrix products: 4.41 us -> none  [the longest x1 2.6 us: shards(): jnp.einsum('jlfrn,jm->mlfrn', flattened_system_array, own_rows, precision...]
    gather x6 -> x0, local copies, waits for them, and re-layouts: 4.38 us -> none  [observe(): picked = jnp.take(flat, index, axis=1)]
  transfers between devices with their start and end apart: 4 -> 3, of which waited for: 2 -> 1; matrix products, arithmetic and copies ran while one was open for 3% -> 0% of each run, Pallas kernels for 0% -> 0%
where the time goes in v1:
time: 75.8 us; the launch traced here: 75.4 us
  blocking collectives  55 us (73%)
  starting transfers between devices  7.47 us (10%)
  Pallas kernels  6.75 us (9%)
  local copies, waits for them, and re-layouts  4.73 us (6%)
  waiting for transfers between devices  1.33 us (2%)
    all_gather x1, blocking collectives, shards(): lax.all_gather(jnp.sum(pieces, axis=0), ('mem', 'slab'), axis=0, tiled=True)  37.5 us
    all_to_all x1, blocking collectives, shards(): lax.all_to_all(terms.reshape(slabs, -1, LANES), 'slab', split_axis=0, con...  17.5 us
    pallas_call x1, Pallas kernels, shards(): pl.pallas_call(functools.partial(analysis_kernel, parts, planes), out_sha...  5.42 us
    unnamed x20, local copies, waits for them, and re-layouts  4.73 us
    ppermute x1, starting transfers between devices, shards(): above = lax.ppermute(present, 'slab', up)  3.05 us
    ppermute x1, starting transfers between devices, shards(): lax.ppermute(state, 'mem', [((i + d) % parts, i) for i in range(parts)])  3.01 us
  transfers between devices with their start and end apart: 3, of which 1 were waited for; matrix products, arithmetic and copies ran while one was open for 0% of the time, Pallas kernels for 0%

profile of v1, /device:TPU:0, one launch (start us, length us, event | category | flops | bytes accessed | tf_op | source)
XLA Modules:
  0.0 75.4 jit_solution(14977292014802757172)
XLA Ops:
  0.0 1.4 %collective-permute-start.1 = (f32[512,128]{1,0:T(8,128)}, f32[512,128]{1,0:T(8,128)S(1)}, u32[]{:S(2)}, u32[]{:S(2)}) collective-permute-start(f32[512,128]{1,0:T(8,128)} %bitcast.7), channel_id=1, source_target_pairs={{2,0},{4,2},{6,4},{8,6},{10,8},{12,10},{14,12},{16,14},{18,16},{20... | collective-permute-start | bytes 786440 | tf_op jit(solution)/shard_map/ppermute | solution.py:247
  1.4 3.0 %collective-permute-start = (f32[512,128]{1,0:T(8,128)}, f32[512,128]{1,0:T(8,128)S(1)}, u32[]{:S(2)}, u32[]{:S(2)}) collective-permute-start(f32[512,128]{1,0:T(8,128)} %bitcast.8), channel_id=1, source_target_pairs={{0,2},{2,4},{4,6},{6,8},{8,10},{10,12},{12,14},{14,16},{16,18},{18... | collective-permute-start | bytes 786440 | tf_op jit(solution)/shard_map/ppermute | solution.py:246
  4.5 0.0 collective-permute-done.1.below_ref
  4.5 1.3 %collective-permute-done.above_ref = f32[512,128]{1,0:T(8,128)S(1)} collective-permute-done((f32[512,128]{1,0:T(8,128)}, f32[512,128]{1,0:T(8,128)S(1)}, u32[]{:S(2)}, u32[]{:S(2)}) %collective-permute-start) | collective-permute-done | bytes 262176 | tf_op jit(solution)/shard_map/ppermute | solution.py:246
  5.8 0.0 copy-start.4
  5.8 0.0 copy-done.3
  5.8 0.7 copy-done.4
  6.5 0.0 copy-start
  6.5 1.0 %copy-done = f32[32,2,4,1,512]{4,3,2,1,0:T(1,128)S(1)} copy-done((f32[32,2,4,1,512]{4,3,2,1,0:T(1,128)S(1)}, f32[32,2,4,1,512]{4,3,2,1,0:T(1,128)}, u32[]{:S(2)}) %copy-start) | copy-done | bytes 524312
  7.5 0.0 copy-start.1
  7.5 0.9 %copy-done.1 = f32[32,4,1,512]{3,2,1,0:T(1,128)S(1)} copy-done((f32[32,4,1,512]{3,2,1,0:T(1,128)S(1)}, f32[32,4,1,512]{3,2,1,0:T(1,128)}, u32[]{:S(2)}) %copy-start.1) | copy-done | bytes 262168
  8.5 0.7 copy-done.5
  9.2 0.7 copy-done.6
  9.9 0.7 copy-done.7
  10.5 1.3 %forecast.1 = (f32[1536,128]{1,0:T(8,128)S(1)}, f32[128,128]{1,0:T(8,128)S(1)}) custom-call(f32[512,128]{1,0:T(8,128)S(1)} %bitcast.9, f32[512,128]{1,0:T(8,128)S(1)} %collective-permute-done.above_ref, f32[512,128]{1,0:T(8,128)S(1)} %collective-permute-done.1.below_ref, f32[1024,128]{1,0:T(8,128)S(1)} %bitcast.6, f32[4,128]{1,0:T(4,128)S(1)} %bitcast.12, ...), custom_call_target="tpu_custom_call" | custom-call | tf_op jit(solution)/shard_map/forecast/pallas_call | solution.py:249
  11.9 3.0 %collective-permute-start.2 = (f32[1536,128]{1,0:T(8,128)S(1)}, f32[1536,128]{1,0:T(8,128)S(1)}, u32[]{:S(2)}, u32[]{:S(2)}) collective-permute-start(f32[1536,128]{1,0:T(8,128)S(1)} %get-tuple-element.8.refs_0_), channel_id=1, source_target_pairs={{1,0},{0,1},{3,2},{2,3},{5,4},{4,5},{7,6},{6,7},{9,8},{8,9},{11,10... | collective-permute-start | bytes 2359304 | tf_op jit(solution)/shard_map/ppermute | solution.py:269
  14.9 17.5 %all_to_all.5 = f32[16,8,128]{2,1,0:T(8,128)S(1)} all-to-all(f32[16,8,128]{2,1,0:T(8,128)S(1)} %bitcast.10), channel_id=1, replica_groups=mesh['slab'=16,'mem'=2] {'slab'}, dimensions={0} | all-to-all | bytes 131072 | tf_op jit(solution)/shard_map/all_to_all | solution.py:273
  32.5 0.0 copy-start.9
  32.5 37.5 %all_gather.3.prior_ref = f32[256,128]{1,0:T(8,128)S(1)} all-gather(f32[8,128]{1,0:T(8,128)S(1)} %reduce_sum.9), channel_id=1, replica_groups=mesh['slab'=16,'mem'=2] {'mem','slab'}, dimensions={0}, use_global_device_ids=true | all-gather | bytes 135168 | tf_op jit(solution)/shard_map/all_gather | solution.py:276
  70.0 0.0 collective-permute-done.2.refs_1_
  70.0 0.0 copy-done.2
  70.0 0.0 copy-done.8
  70.0 0.0 copy-done.9
  70.0 5.4 %analysis.1 = f32[1536,128]{1,0:T(8,128)} custom-call(f32[256,128]{1,0:T(8,128)S(1)} %all_gather.3.prior_ref, f32[2,256]{1,0:T(2,128)S(1)} %copy-done.8, f32[2,256]{1,0:T(2,128)S(1)} %copy-done.9, f32[2,64,256]{2,1,0:T(8,128)S(1)} %copy-done.2, f32[1536,128]{1,0:T(8,128)S(1)} %get-tuple-element.8.refs_0_, f32[1536,128]{1,0:T(8,128)S(1)} %collective-permute-done.2.refs_1_), custom_call_target="tpu_custom_call" | custom-call | tf_op jit(solution)/shard_map/analysis/pallas_call | solution.py:279
  (7 shorter events, 0.0 us)
Async XLA Ops:
  0.0 5.8 %copy-start.3 = (f32[2,1,512]{2,1,0:T(1,128)S(1)}, f32[2,1,512]{2,1,0:T(1,128)}, u32[]{:S(2)}) copy-start(f32[2,1,512]{2,1,0:T(1,128)} %param.13) | copy-start | bytes 12292
  0.0 4.5 %collective-permute-start.1 = (f32[512,128]{1,0:T(8,128)}, f32[512,128]{1,0:T(8,128)S(1)}, u32[]{:S(2)}, u32[]{:S(2)}) collective-permute-start(f32[512,128]{1,0:T(8,128)} %bitcast.7), channel_id=1, source_target_pairs={{2,0},{4,2},{6,4},{8,6},{10,8},{12,10},{14,12},{16,14},{18,16},{20... | collective-permute-start | bytes 786440 | tf_op jit(solution)/shard_map/ppermute | solution.py:247
  1.4 4.4 %collective-permute-start = (f32[512,128]{1,0:T(8,128)}, f32[512,128]{1,0:T(8,128)S(1)}, u32[]{:S(2)}, u32[]{:S(2)}) collective-permute-start(f32[512,128]{1,0:T(8,128)} %bitcast.8), channel_id=1, source_target_pairs={{0,2},{2,4},{4,6},{6,8},{8,10},{10,12},{12,14},{14,16},{16,18},{18... | collective-permute-start | bytes 786440 | tf_op jit(solution)/shard_map/ppermute | solution.py:246
  5.8 0.7 copy-start.4
  6.5 1.0 %copy-start = (f32[32,2,4,1,512]{4,3,2,1,0:T(1,128)S(1)}, f32[32,2,4,1,512]{4,3,2,1,0:T(1,128)}, u32[]{:S(2)}) copy-start(f32[32,2,4,1,512]{4,3,2,1,0:T(1,128)} %param.11) | copy-start | bytes 1572868
  7.5 0.9 %copy-start.1 = (f32[32,4,1,512]{3,2,1,0:T(1,128)S(1)}, f32[32,4,1,512]{3,2,1,0:T(1,128)}, u32[]{:S(2)}) copy-start(f32[32,4,1,512]{3,2,1,0:T(1,128)} %param.10) | copy-start | bytes 786436
  8.5 0.7 copy-start.5
  9.2 0.7 copy-start.6
  9.9 0.7 copy-start.7
  11.9 58.1 %collective-permute-start.2 = (f32[1536,128]{1,0:T(8,128)S(1)}, f32[1536,128]{1,0:T(8,128)S(1)}, u32[]{:S(2)}, u32[]{:S(2)}) collective-permute-start(f32[1536,128]{1,0:T(8,128)S(1)} %get-tuple-element.8.refs_0_), channel_id=1, source_target_pairs={{1,0},{0,1},{3,2},{2,3},{5,4},{4,5},{7,6},{6,7},{9,8},{8,9},{11,10... | collective-permute-start | bytes 2359304 | tf_op jit(solution)/shard_map/ppermute | solution.py:269
  32.4 37.5 %copy-start.2 = (f32[2,64,256]{2,1,0:T(8,128)S(1)}, f32[2,64,256]{2,1,0:T(8,128)}, u32[]{:S(2)}) copy-start(f32[2,64,256]{2,1,0:T(8,128)} %noise_ref.1) | copy-start | bytes 393220
  32.4 37.5 %copy-start.8 = (f32[2,256]{1,0:T(2,128)S(1)}, f32[2,256]{1,0:T(2,128)}, u32[]{:S(2)}) copy-start(f32[2,256]{1,0:T(2,128)} %value_ref.1) | copy-start | bytes 6148
  32.5 37.5 %copy-start.9 = (f32[2,256]{1,0:T(2,128)S(1)}, f32[2,256]{1,0:T(2,128)}, u32[]{:S(2)}) copy-start(f32[2,256]{1,0:T(2,128)} %error_ref.1) | copy-start | bytes 6148

commit v2 on v1

v2 whole, which is shorter than its diff:
```python
import functools

import jax
import jax.numpy as jnp
from jax import lax
from jax.experimental import pallas as pl
from jax.experimental.pallas import tpu as pltpu
from jax.sharding import PartitionSpec as P

LANES = 128
F32 = jnp.float32
BF16 = jnp.bfloat16
HIGHEST = lax.Precision.HIGHEST
PARAMS = pltpu.CompilerParams(vmem_limit_bytes=48 * 1024 * 1024)


def rows_of(array):
    return array.reshape(-1, LANES)


def in_hbm(arrays):
    return [pltpu.with_memory_space_constraint(array, pltpu.HBM) for array in arrays]


def shape_of(shape, dtype=F32):
    return jax.ShapeDtypeStruct(shape, dtype)


def split_two(x):
    high = x.astype(BF16)
    low = (x - high.astype(F32)).astype(BF16)
    return high, low


def split_three(x):
    high = x.astype(BF16)
    rest = x - high.astype(F32)
    middle = rest.astype(BF16)
    low = (rest - middle.astype(F32)).astype(BF16)
    return high, middle, low


def line(ref, start, chunks):
    return jnp.concatenate([ref[start + c : start + c + 1, :] for c in range(chunks)], axis=1)


def stacked_planes(ref, members, fields, chunks):
    return jnp.concatenate(
        [
            jnp.concatenate(
                [
                    ref[pl.ds(f * chunks + c, members, stride=fields * chunks), :]
                    for c in range(chunks)
                ],
                axis=1,
            )
            for f in range(fields)
        ],
        axis=0,
    )


def own_row_kernel(members, fields, chunks, *refs):
    sources, (part_ref, here_ref, coefs_ref, taps_ref, kinds_ref), scratch = (
        refs[:6],
        refs[6:11],
        refs[11:17],
    )
    sems = refs[17]
    copies = [
        pltpu.make_async_copy(source, target, sems.at[i])
        for i, (source, target) in enumerate(zip(sources, scratch))
    ]
    for copy in copies:
        copy.start()
    for copy in copies:
        copy.wait()
    present, spread_ref, ratio_ref, row_ref, col_ref, field_ref = scratch
    width = chunks * LANES
    spread = line(spread_ref, 0, chunks)
    along_rows = line(ratio_ref, 0, chunks)
    along_columns = line(ratio_ref, chunks, chunks)
    here = stacked_planes(present, members, fields, chunks)
    here_ref[...] = here
    lane = lax.broadcasted_iota(jnp.int32, here.shape, 1)
    left = jnp.where(lane == 0, 0.0, pltpu.roll(here, 1, 1))
    right = jnp.where(lane == width - 1, 0.0, pltpu.roll(here, width - 1, 1))
    part_ref[...] = (
        here + spread * (right + left - 4.0 * here) - along_columns * (right - left) * 0.5
    )
    coefs_ref[0:1, :] = spread + along_rows * 0.5
    coefs_ref[1:2, :] = spread - along_rows * 0.5

    batches, count = row_ref.shape
    total = batches * count
    flat = lambda ref: jnp.concatenate([ref[b : b + 1, :] for b in range(batches)], axis=1)
    rows, cols, kinds = flat(row_ref), flat(col_ref), flat(field_ref)
    own_row = lax.axis_index("slab")
    kinds_ref[0:1, :] = jnp.where(rows == own_row, kinds, -1)
    kinds_ref[1:2, :] = jnp.where(rows == own_row - 1, kinds, -1)
    at = lax.broadcasted_iota(jnp.int32, (width, total), 0).astype(F32) * 0.25
    taps_ref[...] = jnp.maximum(0.5 - jnp.abs(at - cols.astype(F32) * 0.25), 0.0).astype(BF16)


def observe_kernel(
    members,
    fields,
    chunks,
    above_ref,
    above_spread_ref,
    above_ratio_ref,
    part_ref,
    here_ref,
    coefs_ref,
    taps_ref,
    kinds_ref,
    obs_ref,
    partial_ref,
    present_ref,
):
    above = stacked_planes(above_ref, members, fields, chunks)
    here = here_ref[...]
    partial = part_ref[...] + coefs_ref[0:1, :] * above
    partial_ref[...] = partial
    present_ref[...] = here
    above_coef = line(above_spread_ref, 0, chunks) - line(above_ratio_ref, 0, chunks) * 0.5
    handed = above_coef * here
    taps = taps_ref[...]
    picked = [
        jnp.dot(part, taps, preferred_element_type=F32)
        for part in split_three(jnp.concatenate([partial, handed], axis=0))
    ]
    picked = picked[2] + picked[1] + picked[0]
    observed = None
    for side in range(2):
        kinds = kinds_ref[side : side + 1, :]
        for f in range(fields):
            start = (side * fields + f) * members
            term = jnp.where(kinds == f, picked[start : start + members], 0.0)
            observed = term if observed is None else observed + term
    obs_ref[...] = observed


def complete_kernel(obs_ref, other_ref, partial_ref, below_ref, coefs_ref, sum_ref, forecast_ref):
    sum_ref[...] = obs_ref[...] + other_ref[...]
    forecast_ref[...] = partial_ref[...] + coefs_ref[1:2, :] * below_ref[...]


def solve_transposed(system, right_t, floor):
    size = system.shape[0]
    eye = (
        lax.broadcasted_iota(jnp.int32, (size, size), 0)
        == lax.broadcasted_iota(jnp.int32, (size, size), 1)
    ).astype(F32)
    top = jnp.max(jnp.sum(jnp.abs(system), axis=0, keepdims=True)) + 1.0
    scale = 2.0 / (top + floor)
    eps = (top - floor) / (top + floor)
    residual = eye - scale * system
    answer = scale * right_t

    def more(carry):
        return carry[0] > 1e-6

    def double(carry):
        eps, residual, answer = carry
        both = jnp.dot(
            jnp.concatenate([residual, answer], axis=0),
            residual,
            precision=HIGHEST,
            preferred_element_type=F32,
        )
        square = eps * eps
        share = 1.0 / (2.0 - square)
        return (
            square * share,
            (2.0 * both[:size] - square * eye) * share,
            (answer + both[size:]) * (2.0 * share),
        )

    return lax.while_loop(more, double, (eps, residual, answer))[2]


def analysis_kernel(parts, *refs):
    value_ref, error_ref, noise_ref, delayed_ref = refs[4 + 3 * parts : 8 + 3 * parts]
    prior, sems = refs[8 + 3 * parts :]
    copies = [
        pltpu.make_async_copy(refs[i], refs[4 + 3 * parts + i], sems.at[i]) for i in range(4)
    ]
    for copy in copies:
        copy.start()
    refs = refs[4:]
    prior_refs, forecast_refs = refs[:parts], refs[parts : 2 * parts]
    delayed_refs = (delayed_ref,) + refs[2 * parts : 3 * parts - 1]
    out_ref = refs[3 * parts - 1]
    batches, members, count = noise_ref.shape
    local = members // parts
    own = lax.axis_index("mem")
    for d, ref in enumerate(prior_refs):
        owner = lax.rem(own + d, parts)
        prior[pl.ds(pl.multiple_of(owner * local, local), local), :] = ref[...]
    for copy in copies[:3]:
        copy.wait()
    eye = (
        lax.broadcasted_iota(jnp.int32, (members, members), 0)
        == lax.broadcasted_iota(jnp.int32, (members, members), 1)
    ).astype(F32)
    product_t = None
    nt = (((1,), (1,)), ((), ()))
    for b in range(batches):
        observed = prior[:, b * count : (b + 1) * count]
        if product_t is not None:
            observed = jnp.dot(
                product_t, observed, precision=HIGHEST, preferred_element_type=F32
            )
        errors = error_ref[b : b + 1, :]
        scaled = (observed - jnp.mean(observed, axis=0, keepdims=True)) / errors
        innovation = (value_ref[b : b + 1, :] - observed) / errors + noise_ref[b]
        both = lax.dot_general(
            jnp.concatenate([scaled, innovation], axis=0),
            scaled,
            nt,
            precision=HIGHEST,
            preferred_element_type=F32,
        )
        system = both[:members] + (members - 1.0) * eye
        weights_t = solve_transposed(system, both[members:], members - 1.0)
        matrix_t = eye + weights_t - jnp.mean(weights_t, axis=1, keepdims=True)
        if product_t is None:
            product_t = matrix_t
        else:
            product_t = jnp.dot(
                matrix_t, product_t, precision=HIGHEST, preferred_element_type=F32
            )

    is_own = (
        lax.broadcasted_iota(jnp.int32, (local, members), 0) + own * local
        == lax.broadcasted_iota(jnp.int32, (local, members), 1)
    ).astype(F32)
    mine = jnp.dot(is_own, product_t, precision=HIGHEST, preferred_element_type=F32)
    source = lax.broadcasted_iota(jnp.int32, (members, members), 0)
    target = lax.broadcasted_iota(jnp.int32, (members, members), 1)
    turn = (source == lax.rem(target + own * local, members)).astype(F32)
    mine = jnp.dot(mine, turn, precision=HIGHEST, preferred_element_type=F32)
    high, low = split_two(mine)
    left = jnp.concatenate([high, high, low], axis=1)

    fields = forecast_refs[0].shape[0] // local
    chunks = forecast_refs[0].shape[1] // LANES
    lagged = delayed_ref.shape[0] // local
    planes = fields * chunks + lagged
    copies[3].wait()
    for start in range(0, planes, chunks):
        if start < fields * chunks:
            f = start // chunks
            held = [ref[f * local : (f + 1) * local, :] for ref in forecast_refs]
        else:
            first = start - fields * chunks
            held = [
                jnp.concatenate(
                    [ref[pl.ds(first + c, local, stride=lagged), :] for c in range(chunks)],
                    axis=1,
                )
                for ref in delayed_refs
            ]
        held_high, held_low = split_two(jnp.concatenate(held, axis=0))
        result = jnp.dot(
            left,
            jnp.concatenate([held_high, held_low, held_high], axis=0),
            preferred_element_type=F32,
        )
        for c in range(chunks):
            out_ref[pl.ds(start + c, local, stride=planes), :] = result[
                :, c * LANES : (c + 1) * LANES
            ]


def shards(
    present_ensemble,
    delayed_ensemble,
    spreading_coefficient,
    transport_ratios,
    obs_value,
    obs_error,
    obs_noise,
    obs_row,
    obs_col,
    obs_field,
):
    members, fields, height, width = present_ensemble.shape
    assert height == 1 and width % LANES == 0
    chunks = width // LANES
    lagged = delayed_ensemble.shape[1]
    slabs, parts = lax.axis_size("slab"), lax.axis_size("mem")
    assert slabs & (slabs - 1) == 0
    batches, all_members, count = obs_noise.shape
    total = batches * count
    planes = (1 + lagged) * fields * chunks
    stacked = (fields * members, width)

    def from_partners(array):
        return [
            lax.ppermute(array, "mem", [((i + d) % parts, i) for i in range(parts)])
            for d in range(1, parts)
        ]

    up = [(i, i + 1) for i in range(slabs - 1)]
    down = [(j, i) for i, j in up]
    present, delayed = rows_of(present_ensemble), rows_of(delayed_ensemble)
    spread, ratios = rows_of(spreading_coefficient), rows_of(transport_ratios)
    above = lax.ppermute(present, "slab", up)
    above_spread = lax.ppermute(spread, "slab", up)
    above_ratios = lax.ppermute(ratios, "slab", up)
    sources = (present, spread, ratios, obs_row, obs_col, obs_field)
    part, here, coefs, taps, kinds = pl.pallas_call(
        functools.partial(own_row_kernel, members, fields, chunks),
        out_shape=(
            shape_of(stacked),
            shape_of(stacked),
            shape_of((2, width)),
            shape_of((width, total), BF16),
            shape_of((2, total), jnp.int32),
        ),
        in_specs=[pl.BlockSpec(memory_space=pltpu.HBM)] * len(sources),
        scratch_shapes=[pltpu.VMEM(s.shape, s.dtype) for s in sources]
        + [pltpu.SemaphoreType.DMA((len(sources),))],
        compiler_params=PARAMS,
        name="own_row",
    )(*in_hbm(sources))
    others_delayed = from_partners(delayed)
    terms, partial, present_again = pl.pallas_call(
        functools.partial(observe_kernel, members, fields, chunks),
        out_shape=(shape_of((members, total)), shape_of(stacked), shape_of(stacked)),
        compiler_params=PARAMS,
        name="observe",
    )(above, above_spread, above_ratios, part, here, coefs, taps, kinds)

    def from_slab(array, bit):
        return lax.ppermute(array, "slab", [(i, i ^ bit) for i in range(slabs)])

    other = from_slab(terms, 1)
    below = lax.ppermute(present_again, "slab", down)
    terms, forecast = pl.pallas_call(
        complete_kernel,
        out_shape=(shape_of((members, total)), shape_of(stacked)),
        compiler_params=PARAMS,
        name="complete",
    )(terms, other, partial, below, coefs)
    bit = 2
    while bit < slabs:
        terms = terms + from_slab(terms, bit)
        bit *= 2
    sources = (obs_value, obs_error, obs_noise, delayed)
    in_vmem = pl.BlockSpec(memory_space=pltpu.VMEM)
    out = pl.pallas_call(
        functools.partial(analysis_kernel, parts),
        out_shape=shape_of((members * planes, LANES)),
        in_specs=[pl.BlockSpec(memory_space=pltpu.HBM)] * len(sources)
        + [in_vmem] * (3 * parts - 1),
        scratch_shapes=[pltpu.VMEM(s.shape, s.dtype) for s in sources]
        + [pltpu.VMEM((all_members, total), F32), pltpu.SemaphoreType.DMA((len(sources),))],
        compiler_params=PARAMS,
        name="analysis",
    )(
        *in_hbm(sources),
        terms,
        *from_partners(terms),
        forecast,
        *from_partners(forecast),
        *others_delayed,
    )
    return out.reshape(members, 1 + lagged, fields, height, width)


def solution(mesh):
    return jax.shard_map(
        shards,
        mesh=mesh,
        in_specs=(
            P("mem", None, "slab", None),
            P("mem", None, None, "slab", None),
            P("slab", None),
            P(None, "slab", None),
            P(),
            P(),
            P(),
            P(),
            P(),
            P(),
        ),
        out_specs=P("mem", None, None, "slab", None),
        check_vma=False,
    )
```

time: 75.8 us -> 46.5 us (0.61)
  blocking collectives: 55 us -> 0 us
  starting transfers between devices: 7.47 us -> 26.2 us
  waiting for transfers between devices: 1.33 us -> 11.1 us
  local copies, waits for them, and re-layouts: 4.73 us -> 0.01 us
  Pallas kernels: 6.75 us -> 8.83 us
    all_gather x1 -> x0, blocking collectives: 37.5 us -> none  [shards(): lax.all_gather(jnp.sum(pieces, axis=0), ('mem', 'slab'), axis=0, tiled=True)]
    ppermute x2 -> x10, starting transfers between devices: 4.42 us -> 23.7 us  [the longest x4 11.4 us: from_slab(): return lax.ppermute(array, 'slab', [(i, i ^ bit) for i in range(slabs)])]
    all_to_all x1 -> x0, blocking collectives: 17.5 us -> none  [shards(): lax.all_to_all(terms.reshape(slabs, -1, LANES), 'slab', split_axis=0, con...]
    ppermute x2 -> x10, waiting for transfers between devices: 0.01 us -> 11.1 us  [the longest x4 8.34 us: from_slab(): return lax.ppermute(array, 'slab', [(i, i ^ bit) for i in range(slabs)])]
    unnamed x20 -> x4, local copies, waits for them, and re-layouts: 4.73 us -> 0.01 us
    pallas_call x2 -> x4, Pallas kernels: 6.75 us -> 8.83 us  [the longest x1 6.54 us: shards(): pl.pallas_call(functools.partial(analysis_kernel, parts), out_shape=shape...]
    ppermute x1, waiting for transfers between devices: 1.33 us -> 0.01 us  [shards(): above = lax.ppermute(present, 'slab', up)]
  transfers between devices with their start and end apart: 3 -> 11, of which waited for: 1 -> 5; matrix products, arithmetic and copies ran while one was open for 0% -> 0% of each run, Pallas kernels for 0% -> 4%
where the time goes in v2:
time: 46.5 us; the launch traced here: 46.3 us
  starting transfers between devices  26.2 us (56%)
  waiting for transfers between devices  11.1 us (24%)
  Pallas kernels  8.83 us (19%)
    ppermute x4, starting transfers between devices, from_slab(): return lax.ppermute(array, 'slab', [(i, i ^ bit) for i in range(slabs)])  11.4 us
    ppermute x4, waiting for transfers between devices, from_slab(): return lax.ppermute(array, 'slab', [(i, i ^ bit) for i in range(slabs)])  8.34 us
    pallas_call x1, Pallas kernels, shards(): pl.pallas_call(functools.partial(analysis_kernel, parts), out_shape=shape...  6.54 us
    ppermute x3, starting transfers between devices, from_partners(): lax.ppermute(array, 'mem', [((i + d) % parts, i) for i in range(parts)])  4.61 us
    ppermute x1, starting transfers between devices, shards(): above_ratios = lax.ppermute(ratios, 'slab', up)  4.52 us
    ppermute x3, waiting for transfers between devices, from_partners(): lax.ppermute(array, 'mem', [((i + d) % parts, i) for i in range(parts)])  2.78 us
    ppermute x1, starting transfers between devices, shards(): above = lax.ppermute(present, 'slab', up)  2.49 us
    ppermute x1, starting transfers between devices, shards(): above_spread = lax.ppermute(spread, 'slab', up)  1.92 us
  transfers between devices with their start and end apart: 11, of which 5 were waited for; matrix products, arithmetic and copies ran while one was open for 0% of the time, Pallas kernels for 4%

profile of v2, /device:TPU:0, one launch (start us, length us, event | category | flops | bytes accessed | tf_op | source)
XLA Modules:
  0.0 46.3 jit_solution(13258596734833079968)
XLA Ops:
  0.0 2.5 %collective-permute-start = (f32[512,128]{1,0:T(8,128)}, f32[512,128]{1,0:T(8,128)S(1)}, u32[]{:S(2)}, u32[]{:S(2)}) collective-permute-start(f32[512,128]{1,0:T(8,128)} %bitcast.7), channel_id=1, source_target_pairs={{0,2},{2,4},{4,6},{6,8},{8,10},{10,12},{12,14},{14,16},{16,18},{18... | collective-permute-start | bytes 786440 | tf_op jit(solution)/shard_map/ppermute | solution.py:310
  2.5 4.5 %collective-permute-start.2 = (f32[8,128]{1,0:T(8,128)}, f32[8,128]{1,0:T(8,128)S(1)}, u32[]{:S(2)}, u32[]{:S(2)}) collective-permute-start(f32[8,128]{1,0:T(8,128)} %bitcast.9), channel_id=1, source_target_pairs={{0,2},{2,4},{4,6},{6,8},{8,10},{10,12},{12,14},{14,16},{16,18},{18... | collective-permute-start | bytes 12296 | tf_op jit(solution)/shard_map/ppermute | solution.py:312
  7.0 1.9 %collective-permute-start.1 = (f32[4,128]{1,0:T(4,128)S(1)}, f32[4,128]{1,0:T(4,128)S(1)}, u32[]{:S(2)}, u32[]{:S(2)}) collective-permute-start(f32[4,128]{1,0:T(4,128)S(1)} %bitcast.12), channel_id=1, source_target_pairs={{0,2},{2,4},{4,6},{6,8},{8,10},{10,12},{12,14},{14,16},{16,18},{18... | collective-permute-start | bytes 6152 | tf_op jit(solution)/shard_map/ppermute | solution.py:311
  9.0 1.6 %own_row.1 = (f32[128,512]{1,0:T(8,128)S(1)}, f32[128,512]{1,0:T(8,128)S(1)}, f32[2,512]{1,0:T(2,128)S(1)}, bf16[512,512]{1,0:T(8,128)(2,1)S(1)}, s32[2,512]{1,0:T(2,128)S(1)}) custom-call(f32[512,128]{1,0:T(8,128)} %bitcast.8, f32[4,128]{1,0:T(4,128)} %bitcast.11, f32[8,128]{1,0:T(8,128)} %bitcast.10, s32[2,256]{1,0:T(2,128)} %refs_3_.1, s32[2,256]{1,0:T(2,128)} %refs_4_.1, ...), custom_call_target="tpu_custom_call" | custom-call | tf_op jit(solution)/shard_map/own_row/pallas_call | solution.py:314
  10.6 0.0 collective-permute-done.1.above_spread_ref
  10.6 0.0 collective-permute-done.2.above_ratio_ref
  10.6 0.0 collective-permute-done.above_ref
  10.6 0.0 copy-start
  10.6 0.7 %observe.1 = (f32[32,512]{1,0:T(8,128)S(1)}, f32[128,512]{1,0:T(8,128)S(1)}, f32[128,512]{1,0:T(8,128)S(1)}) custom-call(f32[512,128]{1,0:T(8,128)S(1)} %collective-permute-done.above_ref, f32[4,128]{1,0:T(4,128)S(1)} %collective-permute-done.1.above_spread_ref, f32[8,128]{1,0:T(8,128)S(1)} %collective-permute-done.2.above_ratio_ref, ...), custom_call_target="tpu_custom_call" | custom-call | tf_op jit(solution)/shard_map/observe/pallas_call | solution.py:330
  11.3 1.3 %collective-permute-start.4 = (f32[128,512]{1,0:T(8,128)S(1)}, f32[128,512]{1,0:T(8,128)S(1)}, u32[]{:S(2)}, u32[]{:S(2)}) collective-permute-start(f32[128,512]{1,0:T(8,128)S(1)} %get-tuple-element.22), channel_id=1, source_target_pairs={{2,0},{4,2},{6,4},{8,6},{10,8},{12,10},{14,12},{16,14},{18,16},{20... | collective-permute-start | bytes 786440 | tf_op jit(solution)/shard_map/ppermute | solution.py:341
  12.6 1.6 %collective-permute-start.10 = (f32[1024,128]{1,0:T(8,128)S(1)}, f32[1024,128]{1,0:T(8,128)S(1)}, u32[]{:S(2)}, u32[]{:S(2)}) collective-permute-start(f32[1024,128]{1,0:T(8,128)S(1)} %bitcast.6), channel_id=1, source_target_pairs={{1,0},{0,1},{3,2},{2,3},{5,4},{4,5},{7,6},{6,7},{9,8},{8,9},{11,10... | collective-permute-start | bytes 1572872 | tf_op jit(solution)/shard_map/ppermute | solution.py:302
  14.1 2.0 %collective-permute-start.3 = (f32[32,512]{1,0:T(8,128)S(1)}, f32[32,512]{1,0:T(8,128)S(1)}, u32[]{:S(2)}, u32[]{:S(2)}) collective-permute-start(f32[32,512]{1,0:T(8,128)S(1)} %get-tuple-element.20.obs_ref), channel_id=1, source_target_pairs={{0,2},{2,0},{4,6},{6,4},{8,10},{10,8},{12,14},{14,12},{16,18},{18,... | collective-permute-start | bytes 196616 | tf_op jit(solution)/shard_map/ppermute | solution.py:338
  16.1 0.9 %collective-permute-done.3.other_ref = f32[32,512]{1,0:T(8,128)S(1)} collective-permute-done((f32[32,512]{1,0:T(8,128)S(1)}, f32[32,512]{1,0:T(8,128)S(1)}, u32[]{:S(2)}, u32[]{:S(2)}) %collective-permute-start.3) | collective-permute-done | bytes 65568 | tf_op jit(solution)/shard_map/ppermute | solution.py:338
  17.0 0.1 complete.1
  17.1 3.4 %collective-permute-start.5 = (f32[32,512]{1,0:T(8,128)S(1)}, f32[32,512]{1,0:T(8,128)S(1)}, u32[]{:S(2)}, u32[]{:S(2)}) collective-permute-start(f32[32,512]{1,0:T(8,128)S(1)} %get-tuple-element.23), channel_id=1, source_target_pairs={{0,4},{2,6},{4,0},{6,2},{8,12},{10,14},{12,8},{14,10},{16,20},{18,... | collective-permute-start | bytes 196616 | tf_op jit(solution)/shard_map/ppermute | solution.py:338
  20.4 1.5 %collective-permute-start.9 = (f32[128,512]{1,0:T(8,128)S(1)}, f32[128,512]{1,0:T(8,128)S(1)}, u32[]{:S(2)}, u32[]{:S(2)}) collective-permute-start(f32[128,512]{1,0:T(8,128)S(1)} %get-tuple-element.24.refs_6_), channel_id=1, source_target_pairs={{1,0},{0,1},{3,2},{2,3},{5,4},{4,5},{7,6},{6,7},{9,8},{8,9},{11,10... | collective-permute-start | bytes 786440 | tf_op jit(solution)/shard_map/ppermute | solution.py:302
  21.9 0.8 %collective-permute-done.5 = f32[32,512]{1,0:T(8,128)S(1)} collective-permute-done((f32[32,512]{1,0:T(8,128)S(1)}, f32[32,512]{1,0:T(8,128)S(1)}, u32[]{:S(2)}, u32[]{:S(2)}) %collective-permute-start.5) | collective-permute-done | bytes 65568 | tf_op jit(solution)/shard_map/ppermute | solution.py:338
  22.7 3.2 %collective-permute-start.6 = (f32[32,512]{1,0:T(8,128)S(1)}, f32[32,512]{1,0:T(8,128)S(1)}, u32[]{:S(2)}, u32[]{:S(2)}) collective-permute-start(f32[32,512]{1,0:T(8,128)S(1)} %add.9), channel_id=1, source_target_pairs={{0,8},{2,10},{4,12},{6,14},{8,0},{10,2},{12,4},{14,6},{16,24},{18,... | collective-permute-start | bytes 196616 | tf_op jit(solution)/shard_map/ppermute | solution.py:338
  25.9 2.9 %collective-permute-done.6 = f32[32,512]{1,0:T(8,128)S(1)} collective-permute-done((f32[32,512]{1,0:T(8,128)S(1)}, f32[32,512]{1,0:T(8,128)S(1)}, u32[]{:S(2)}, u32[]{:S(2)}) %collective-permute-start.6) | collective-permute-done | bytes 65568 | tf_op jit(solution)/shard_map/ppermute | solution.py:338
  28.8 2.8 %collective-permute-start.7 = (f32[32,512]{1,0:T(8,128)S(1)}, f32[32,512]{1,0:T(8,128)S(1)}, u32[]{:S(2)}, u32[]{:S(2)}) collective-permute-start(f32[32,512]{1,0:T(8,128)S(1)} %add.10), channel_id=1, source_target_pairs={{0,16},{2,18},{4,20},{6,22},{8,24},{10,26},{12,28},{14,30},{16,0},... | collective-permute-start | bytes 196616 | tf_op jit(solution)/shard_map/ppermute | solution.py:338
  31.6 3.8 %collective-permute-done.7 = f32[32,512]{1,0:T(8,128)S(1)} collective-permute-done((f32[32,512]{1,0:T(8,128)S(1)}, f32[32,512]{1,0:T(8,128)S(1)}, u32[]{:S(2)}, u32[]{:S(2)}) %collective-permute-start.7) | collective-permute-done | bytes 65568 | tf_op jit(solution)/shard_map/ppermute | solution.py:338
  35.4 1.6 %collective-permute-start.8 = (f32[32,512]{1,0:T(8,128)S(1)}, f32[32,512]{1,0:T(8,128)S(1)}, u32[]{:S(2)}, u32[]{:S(2)}) collective-permute-start(f32[32,512]{1,0:T(8,128)S(1)} %add.11.refs_4_), channel_id=1, source_target_pairs={{1,0},{0,1},{3,2},{2,3},{5,4},{4,5},{7,6},{6,7},{9,8},{8,9},{11,10... | collective-permute-start | bytes 196616 | tf_op jit(solution)/shard_map/ppermute | solution.py:302
  37.0 2.8 %collective-permute-done.8.refs_5_ = f32[32,512]{1,0:T(8,128)S(1)} collective-permute-done((f32[32,512]{1,0:T(8,128)S(1)}, f32[32,512]{1,0:T(8,128)S(1)}, u32[]{:S(2)}, u32[]{:S(2)}) %collective-permute-start.8) | collective-permute-done | bytes 65568 | tf_op jit(solution)/shard_map/ppermute | solution.py:302
  39.8 6.5 %analysis.1 = f32[1536,128]{1,0:T(8,128)} custom-call(f32[2,256]{1,0:T(2,128)} %refs_0_.1, f32[2,256]{1,0:T(2,128)} %refs_1_.1, f32[2,64,256]{2,1,0:T(8,128)} %refs_2_.1, f32[1024,128]{1,0:T(8,128)} %bitcast.5, f32[32,512]{1,0:T(8,128)S(1)} %add.11.refs_4_, f32[32,512]{1,0:T(8,128)S(1)} %collective-permute-done.8.refs_5_, ...), custom_call_target="tpu_custom_call" | custom-call | tf_op jit(solution)/shard_map/analysis/pallas_call | solution.py:354
  (9 shorter events, 0.0 us)
Async XLA Ops:
  0.0 7.0 %copy-start.1 = (f32[1,512]{1,0:T(1,128)S(1)}, f32[1,512]{1,0:T(1,128)}, u32[]{:S(2)}) copy-start(f32[1,512]{1,0:T(1,128)} %param.12) | copy-start | bytes 6148
  0.0 10.6 %collective-permute-start = (f32[512,128]{1,0:T(8,128)}, f32[512,128]{1,0:T(8,128)S(1)}, u32[]{:S(2)}, u32[]{:S(2)}) collective-permute-start(f32[512,128]{1,0:T(8,128)} %bitcast.7), channel_id=1, source_target_pairs={{0,2},{2,4},{4,6},{6,8},{8,10},{10,12},{12,14},{14,16},{16,18},{18... | collective-permute-start | bytes 786440 | tf_op jit(solution)/shard_map/ppermute | solution.py:310
  2.5 8.1 %collective-permute-start.2 = (f32[8,128]{1,0:T(8,128)}, f32[8,128]{1,0:T(8,128)S(1)}, u32[]{:S(2)}, u32[]{:S(2)}) collective-permute-start(f32[8,128]{1,0:T(8,128)} %bitcast.9), channel_id=1, source_target_pairs={{0,2},{2,4},{4,6},{6,8},{8,10},{10,12},{12,14},{14,16},{16,18},{18... | collective-permute-start | bytes 12296 | tf_op jit(solution)/shard_map/ppermute | solution.py:312
  7.0 3.5 %collective-permute-start.1 = (f32[4,128]{1,0:T(4,128)S(1)}, f32[4,128]{1,0:T(4,128)S(1)}, u32[]{:S(2)}, u32[]{:S(2)}) collective-permute-start(f32[4,128]{1,0:T(4,128)S(1)} %bitcast.12), channel_id=1, source_target_pairs={{0,2},{2,4},{4,6},{6,8},{8,10},{10,12},{12,14},{14,16},{16,18},{18... | collective-permute-start | bytes 6152 | tf_op jit(solution)/shard_map/ppermute | solution.py:311
  10.6 2.0 %copy-start = (f32[32,2,4,1,512]{4,3,2,1,0:T(1,128)S(1)}, f32[32,2,4,1,512]{4,3,2,1,0:T(1,128)}, u32[]{:S(2)}) copy-start(f32[32,2,4,1,512]{4,3,2,1,0:T(1,128)} %param.11) | copy-start | bytes 1572868
  11.3 5.7 %collective-permute-start.4 = (f32[128,512]{1,0:T(8,128)S(1)}, f32[128,512]{1,0:T(8,128)S(1)}, u32[]{:S(2)}, u32[]{:S(2)}) collective-permute-start(f32[128,512]{1,0:T(8,128)S(1)} %get-tuple-element.22), channel_id=1, source_target_pairs={{2,0},{4,2},{6,4},{8,6},{10,8},{12,10},{14,12},{16,14},{18,16},{20... | collective-permute-start | bytes 786440 | tf_op jit(solution)/shard_map/ppermute | solution.py:341
  12.6 24.4 %collective-permute-start.10 = (f32[1024,128]{1,0:T(8,128)S(1)}, f32[1024,128]{1,0:T(8,128)S(1)}, u32[]{:S(2)}, u32[]{:S(2)}) collective-permute-start(f32[1024,128]{1,0:T(8,128)S(1)} %bitcast.6), channel_id=1, source_target_pairs={{1,0},{0,1},{3,2},{2,3},{5,4},{4,5},{7,6},{6,7},{9,8},{8,9},{11,10... | collective-permute-start | bytes 1572872 | tf_op jit(solution)/shard_map/ppermute | solution.py:302
  14.1 2.9 %collective-permute-start.3 = (f32[32,512]{1,0:T(8,128)S(1)}, f32[32,512]{1,0:T(8,128)S(1)}, u32[]{:S(2)}, u32[]{:S(2)}) collective-permute-start(f32[32,512]{1,0:T(8,128)S(1)} %get-tuple-element.20.obs_ref), channel_id=1, source_target_pairs={{0,2},{2,0},{4,6},{6,4},{8,10},{10,8},{12,14},{14,12},{16,18},{18,... | collective-permute-start | bytes 196616 | tf_op jit(solution)/shard_map/ppermute | solution.py:338
  17.1 5.6 %collective-permute-start.5 = (f32[32,512]{1,0:T(8,128)S(1)}, f32[32,512]{1,0:T(8,128)S(1)}, u32[]{:S(2)}, u32[]{:S(2)}) collective-permute-start(f32[32,512]{1,0:T(8,128)S(1)} %get-tuple-element.23), channel_id=1, source_target_pairs={{0,4},{2,6},{4,0},{6,2},{8,12},{10,14},{12,8},{14,10},{16,20},{18,... | collective-permute-start | bytes 196616 | tf_op jit(solution)/shard_map/ppermute | solution.py:338
  20.4 19.3 %collective-permute-start.9 = (f32[128,512]{1,0:T(8,128)S(1)}, f32[128,512]{1,0:T(8,128)S(1)}, u32[]{:S(2)}, u32[]{:S(2)}) collective-permute-start(f32[128,512]{1,0:T(8,128)S(1)} %get-tuple-element.24.refs_6_), channel_id=1, source_target_pairs={{1,0},{0,1},{3,2},{2,3},{5,4},{4,5},{7,6},{6,7},{9,8},{8,9},{11,10... | collective-permute-start | bytes 786440 | tf_op jit(solution)/shard_map/ppermute | solution.py:302
  22.7 6.1 %collective-permute-start.6 = (f32[32,512]{1,0:T(8,128)S(1)}, f32[32,512]{1,0:T(8,128)S(1)}, u32[]{:S(2)}, u32[]{:S(2)}) collective-permute-start(f32[32,512]{1,0:T(8,128)S(1)} %add.9), channel_id=1, source_target_pairs={{0,8},{2,10},{4,12},{6,14},{8,0},{10,2},{12,4},{14,6},{16,24},{18,... | collective-permute-start | bytes 196616 | tf_op jit(solution)/shard_map/ppermute | solution.py:338
  28.8 6.6 %collective-permute-start.7 = (f32[32,512]{1,0:T(8,128)S(1)}, f32[32,512]{1,0:T(8,128)S(1)}, u32[]{:S(2)}, u32[]{:S(2)}) collective-permute-start(f32[32,512]{1,0:T(8,128)S(1)} %add.10), channel_id=1, source_target_pairs={{0,16},{2,18},{4,20},{6,22},{8,24},{10,26},{12,28},{14,30},{16,0},... | collective-permute-start | bytes 196616 | tf_op jit(solution)/shard_map/ppermute | solution.py:338
  35.4 4.3 %collective-permute-start.8 = (f32[32,512]{1,0:T(8,128)S(1)}, f32[32,512]{1,0:T(8,128)S(1)}, u32[]{:S(2)}, u32[]{:S(2)}) collective-permute-start(f32[32,512]{1,0:T(8,128)S(1)} %add.11.refs_4_), channel_id=1, source_target_pairs={{1,0},{0,1},{3,2},{2,3},{5,4},{4,5},{7,6},{6,7},{9,8},{8,9},{11,10... | collective-permute-start | bytes 196616 | tf_op jit(solution)/shard_map/ppermute | solution.py:302

commit v3 on v2

--- a/solution.py
+++ b/solution.py
@@ -60,90 +60,113 @@
     )
 
 
+def at_once(sources, targets, sems):
+    copies = [
+        pltpu.make_async_copy(source, target, sems.at[i])
+        for i, (source, target) in enumerate(zip(sources, targets))
+    ]
+    for copy in copies:
+        copy.start()
+    return copies
+
+
+def picked_values(planes, taps):
+    high, middle, low = (
+        jnp.dot(part, taps, preferred_element_type=F32) for part in split_three(planes)
+    )
+    return low + middle + high
+
+
+def coefficient_kernel(chunks, *refs):
+    sources, (coefs_ref,), scratch, sems = refs[:2], refs[2:3], refs[3:5], refs[5]
+    for copy in at_once(sources, scratch, sems):
+        copy.wait()
+    spread = line(scratch[0], 0, chunks)
+    half = line(scratch[1], 0, chunks) * 0.5
+    coefs_ref[0:1, :] = spread + half
+    coefs_ref[1:2, :] = spread - half
+
+
 def own_row_kernel(members, fields, chunks, *refs):
-    sources, (part_ref, here_ref, coefs_ref, taps_ref, kinds_ref), scratch = (
+    sources, (part_ref, here_ref, taps_ref, kinds_ref, obs_ref), scratch = (
         refs[:6],
         refs[6:11],
         refs[11:17],
     )
-    sems = refs[17]
-    copies = [
-        pltpu.make_async_copy(source, target, sems.at[i])
-        for i, (source, target) in enumerate(zip(sources, scratch))
-    ]
-    for copy in copies:
-        copy.start()
-    for copy in copies:
+    for copy in at_once(sources, scratch, refs[17]):
         copy.wait()
     present, spread_ref, ratio_ref, row_ref, col_ref, field_ref = scratch
     width = chunks * LANES
     spread = line(spread_ref, 0, chunks)
-    along_rows = line(ratio_ref, 0, chunks)
     along_columns = line(ratio_ref, chunks, chunks)
     here = stacked_planes(present, members, fields, chunks)
     here_ref[...] = here
     lane = lax.broadcasted_iota(jnp.int32, here.shape, 1)
     left = jnp.where(lane == 0, 0.0, pltpu.roll(here, 1, 1))
     right = jnp.where(lane == width - 1, 0.0, pltpu.roll(here, width - 1, 1))
-    part_ref[...] = (
-        here + spread * (right + left - 4.0 * here) - along_columns * (right - left) * 0.5
-    )
-    coefs_ref[0:1, :] = spread + along_rows * 0.5
-    coefs_ref[1:2, :] = spread - along_rows * 0.5
+    part = here + spread * (right + left - 4.0 * here) - along_columns * (right - left) * 0.5
+    part_ref[...] = part
 
     batches, count = row_ref.shape
     total = batches * count
     flat = lambda ref: jnp.concatenate([ref[b : b + 1, :] for b in range(batches)], axis=1)
     rows, cols, kinds = flat(row_ref), flat(col_ref), flat(field_ref)
     own_row = lax.axis_index("slab")
-    kinds_ref[0:1, :] = jnp.where(rows == own_row, kinds, -1)
+    seen = jnp.where(rows == own_row, kinds, -1)
+    kinds_ref[0:1, :] = jnp.where(rows == own_row + 1, kinds, -1)
     kinds_ref[1:2, :] = jnp.where(rows == own_row - 1, kinds, -1)
     at = lax.broadcasted_iota(jnp.int32, (width, total), 0).astype(F32) * 0.25
-    taps_ref[...] = jnp.maximum(0.5 - jnp.abs(at - cols.astype(F32) * 0.25), 0.0).astype(BF16)
+    taps = jnp.maximum(0.5 - jnp.abs(at - cols.astype(F32) * 0.25), 0.0).astype(BF16)
+    taps_ref[...] = taps
+    picked = picked_values(part, taps)
+    observed = jnp.zeros((members, total), F32)
+    for f in range(fields):
+        observed += jnp.where(seen == f, picked[f * members : (f + 1) * members], 0.0)
+    obs_ref[...] = observed
 
 
 def observe_kernel(
     members,
     fields,
-    chunks,
-    above_ref,
-    above_spread_ref,
-    above_ratio_ref,
-    part_ref,
+    inner_ref,
+    outer_ref,
+    part_obs_ref,
     here_ref,
-    coefs_ref,
     taps_ref,
     kinds_ref,
-    obs_ref,
-    partial_ref,
-    present_ref,
+    keep_ref,
+    send_ref,
+    again_ref,
 ):
-    above = stacked_planes(above_ref, members, fields, chunks)
+    even = lax.rem(lax.axis_index("slab"), 2) == 0
     here = here_ref[...]
-    partial = part_ref[...] + coefs_ref[0:1, :] * above
-    partial_ref[...] = partial
-    present_ref[...] = here
-    above_coef = line(above_spread_ref, 0, chunks) - line(above_ratio_ref, 0, chunks) * 0.5
-    handed = above_coef * here
-    taps = taps_ref[...]
-    picked = [
-        jnp.dot(part, taps, preferred_element_type=F32)
-        for part in split_three(jnp.concatenate([partial, handed], axis=0))
-    ]
-    picked = picked[2] + picked[1] + picked[0]
-    observed = None
+    again_ref[...] = here
+    below = jnp.where(even, inner_ref[0:1, :], outer_ref[0:1, :])
+    above = jnp.where(even, outer_ref[1:2, :], inner_ref[1:2, :])
+    picked = picked_values(
+        jnp.concatenate([below * here, above * here], axis=0), taps_ref[...]
+    )
+    observed = part_obs_ref[...]
     for side in range(2):
         kinds = kinds_ref[side : side + 1, :]
         for f in range(fields):
             start = (side * fields + f) * members
-            term = jnp.where(kinds == f, picked[start : start + members], 0.0)
-            observed = term if observed is None else observed + term
-    obs_ref[...] = observed
-
-
-def complete_kernel(obs_ref, other_ref, partial_ref, below_ref, coefs_ref, sum_ref, forecast_ref):
-    sum_ref[...] = obs_ref[...] + other_ref[...]
-    forecast_ref[...] = partial_ref[...] + coefs_ref[1:2, :] * below_ref[...]
+            observed += jnp.where(kinds == f, picked[start : start + members], 0.0)
+    half = observed.shape[1] // 2
+    first, second = observed[:, :half], observed[:, half:]
+    keep_ref[...] = jnp.where(even, first, second)
+    send_ref[...] = jnp.where(even, second, first)
+
+
+def complete_kernel(part_ref, inner_ref, outer_ref, coefs_ref, forecast_ref):
+    even = lax.rem(lax.axis_index("slab"), 2) == 0
+    inner, outer = inner_ref[...], outer_ref[...]
+    above, below = coefs_ref[0:1, :], coefs_ref[1:2, :]
+    forecast_ref[...] = (
+        part_ref[...]
+        + jnp.where(even, below, above) * inner
+        + jnp.where(even, above, below) * outer
+    )
 
 
 def solve_transposed(system, right_t, floor):
@@ -180,25 +203,22 @@
     return lax.while_loop(more, double, (eps, residual, answer))[2]
 
 
-def analysis_kernel(parts, *refs):
-    value_ref, error_ref, noise_ref, delayed_ref = refs[4 + 3 * parts : 8 + 3 * parts]
-    prior, sems = refs[8 + 3 * parts :]
-    copies = [
-        pltpu.make_async_copy(refs[i], refs[4 + 3 * parts + i], sems.at[i]) for i in range(4)
-    ]
-    for copy in copies:
-        copy.start()
-    refs = refs[4:]
-    prior_refs, forecast_refs = refs[:parts], refs[parts : 2 * parts]
-    delayed_refs = (delayed_ref,) + refs[2 * parts : 3 * parts - 1]
-    out_ref = refs[3 * parts - 1]
+def solve_kernel(parts, *refs):
+    sources, priors, mine_ref = refs[:3], refs[3 : 3 + 2 * parts], refs[3 + 2 * parts]
+    value_ref, error_ref, noise_ref, prior, sems = refs[4 + 2 * parts :]
+    copies = at_once(sources, (value_ref, error_ref, noise_ref), sems)
     batches, members, count = noise_ref.shape
     local = members // parts
     own = lax.axis_index("mem")
-    for d, ref in enumerate(prior_refs):
+    even = lax.rem(lax.axis_index("slab"), 2) == 0
+    half = batches * count // 2
+    for d in range(parts):
         owner = lax.rem(own + d, parts)
-        prior[pl.ds(pl.multiple_of(owner * local, local), local), :] = ref[...]
-    for copy in copies[:3]:
+        rows = pl.ds(pl.multiple_of(owner * local, local), local)
+        kept, received = priors[d][...], priors[parts + d][...]
+        prior[rows, :half] = jnp.where(even, kept, received)
+        prior[rows, half:] = jnp.where(even, received, kept)
+    for copy in copies:
         copy.wait()
     eye = (
         lax.broadcasted_iota(jnp.int32, (members, members), 0)
@@ -240,15 +260,17 @@
     source = lax.broadcasted_iota(jnp.int32, (members, members), 0)
     target = lax.broadcasted_iota(jnp.int32, (members, members), 1)
     turn = (source == lax.rem(target + own * local, members)).astype(F32)
-    mine = jnp.dot(mine, turn, precision=HIGHEST, preferred_element_type=F32)
-    high, low = split_two(mine)
+    mine_ref[...] = jnp.dot(mine, turn, precision=HIGHEST, preferred_element_type=F32)
+
+
+def combine_kernel(parts, fields, mine_ref, *refs):
+    forecast_refs, delayed_refs, out_ref = refs[:parts], refs[parts : 2 * parts], refs[2 * parts]
+    local = mine_ref.shape[0]
+    high, low = split_two(mine_ref[...])
     left = jnp.concatenate([high, high, low], axis=1)
-
-    fields = forecast_refs[0].shape[0] // local
     chunks = forecast_refs[0].shape[1] // LANES
-    lagged = delayed_ref.shape[0] // local
+    lagged = delayed_refs[0].shape[0] // local
     planes = fields * chunks + lagged
-    copies[3].wait()
     for start in range(0, planes, chunks):
         if start < fields * chunks:
             f = start // chunks
@@ -296,6 +318,13 @@
     total = batches * count
     planes = (1 + lagged) * fields * chunks
     stacked = (fields * members, width)
+    hbm = pl.BlockSpec(memory_space=pltpu.HBM)
+    vmem = pl.BlockSpec(memory_space=pltpu.VMEM)
+
+    def landing(sources):
+        return [pltpu.VMEM(s.shape, s.dtype) for s in sources], pltpu.SemaphoreType.DMA(
+            (len(sources),)
+        )
 
     def from_partners(array):
         return [
@@ -303,71 +332,91 @@
             for d in range(1, parts)
         ]
 
-    up = [(i, i + 1) for i in range(slabs - 1)]
-    down = [(j, i) for i, j in up]
+    def from_slab(array, bit):
+        return lax.ppermute(array, "slab", [(i, i ^ bit) for i in range(slabs)])
+
+    outer_pairs = [(i, i + 1) for i in range(1, slabs - 1, 2)]
+    outer_pairs += [(j, i) for i, j in outer_pairs]
+
+    def from_rows(array):
+        outer = lax.ppermute(array, "slab", outer_pairs)
+        return from_slab(array, 1), outer
+
     present, delayed = rows_of(present_ensemble), rows_of(delayed_ensemble)
     spread, ratios = rows_of(spreading_coefficient), rows_of(transport_ratios)
-    above = lax.ppermute(present, "slab", up)
-    above_spread = lax.ppermute(spread, "slab", up)
-    above_ratios = lax.ppermute(ratios, "slab", up)
-    sources = (present, spread, ratios, obs_row, obs_col, obs_field)
-    part, here, coefs, taps, kinds = pl.pallas_call(
+    sources = in_hbm((spread, ratios))
+    buffers, sems = landing(sources)
+    coefs = pl.pallas_call(
+        functools.partial(coefficient_kernel, chunks),
+        out_shape=shape_of((2, width)),
+        in_specs=[hbm] * len(sources),
+        scratch_shapes=[*buffers, sems],
+        compiler_params=PARAMS,
+        name="coefficients",
+    )(*sources)
+    inner_coefs, outer_coefs = from_rows(coefs)
+    sources = in_hbm((present, spread, ratios, obs_row, obs_col, obs_field))
+    buffers, sems = landing(sources)
+    part, here, taps, kinds, part_obs = pl.pallas_call(
         functools.partial(own_row_kernel, members, fields, chunks),
         out_shape=(
             shape_of(stacked),
             shape_of(stacked),
-            shape_of((2, width)),
             shape_of((width, total), BF16),
             shape_of((2, total), jnp.int32),
+            shape_of((members, total)),
         ),
-        in_specs=[pl.BlockSpec(memory_space=pltpu.HBM)] * len(sources),
-        scratch_shapes=[pltpu.VMEM(s.shape, s.dtype) for s in sources]
-        + [pltpu.SemaphoreType.DMA((len(sources),))],
+        in_specs=[hbm] * len(sources),
+        scratch_shapes=[*buffers, sems],
         compiler_params=PARAMS,
         name="own_row",
-    )(*in_hbm(sources))
+    )(*sources)
     others_delayed = from_partners(delayed)
-    terms, partial, present_again = pl.pallas_call(
-        functools.partial(observe_kernel, members, fields, chunks),
-        out_shape=(shape_of((members, total)), shape_of(stacked), shape_of(stacked)),
+    keep, send, again = pl.pallas_call(
+        functools.partial(observe_kernel, members, fields),
+        out_shape=(
+            shape_of((members, total // 2)),
+            shape_of((members, total // 2)),
+            shape_of(stacked),
+        ),
         compiler_params=PARAMS,
         name="observe",
-    )(above, above_spread, above_ratios, part, here, coefs, taps, kinds)
-
-    def from_slab(array, bit):
-        return lax.ppermute(array, "slab", [(i, i ^ bit) for i in range(slabs)])
-
-    other = from_slab(terms, 1)
-    below = lax.ppermute(present_again, "slab", down)
-    terms, forecast = pl.pallas_call(
+    )(inner_coefs, outer_coefs, part_obs, here, taps, kinds)
+
+    terms = keep + from_slab(send, 1)
+    inner_row, outer_row = from_rows(again)
+    forecast = pl.pallas_call(
         complete_kernel,
-        out_shape=(shape_of((members, total)), shape_of(stacked)),
+        out_shape=shape_of(stacked),
         compiler_params=PARAMS,
         name="complete",
-    )(terms, other, partial, below, coefs)
+    )(part, inner_row, outer_row, coefs)
     bit = 2
     while bit < slabs:
         terms = terms + from_slab(terms, bit)
         bit *= 2
-    sources = (obs_value, obs_error, obs_noise, delayed)
-    in_vmem = pl.BlockSpec(memory_space=pltpu.VMEM)
+    priors = [terms, *from_partners(terms)]
+    if parts == 2:
+        gathered = from_slab(jnp.concatenate(priors, axis=0), 1)
+        priors += [gathered[d * members : (d + 1) * members] for d in range(parts)]
+    else:
+        priors += [from_slab(prior, 1) for prior in priors]
+    sources = in_hbm((obs_value, obs_error, obs_noise))
+    buffers, sems = landing(sources)
+    mine = pl.pallas_call(
+        functools.partial(solve_kernel, parts),
+        out_shape=shape_of((members, all_members)),
+        in_specs=[hbm] * len(sources) + [vmem] * len(priors),
+        scratch_shapes=[*buffers, pltpu.VMEM((all_members, total), F32), sems],
+        compiler_params=PARAMS,
+        name="solve",
+    )(*sources, *priors)
     out = pl.pallas_call(
-        functools.partial(analysis_kernel, parts),
+        functools.partial(combine_kernel, parts, fields),
         out_shape=shape_of((members * planes, LANES)),
-        in_specs=[pl.BlockSpec(memory_space=pltpu.HBM)] * len(sources)
-        + [in_vmem] * (3 * parts - 1),
-        scratch_shapes=[pltpu.VMEM(s.shape, s.dtype) for s in sources]
-        + [pltpu.VMEM((all_members, total), F32), pltpu.SemaphoreType.DMA((len(sources),))],
-        compiler_params=PARAMS,
-        name="analysis",
-    )(
-        *in_hbm(sources),
-        terms,
-        *from_partners(terms),
-        forecast,
-        *from_partners(forecast),
-        *others_delayed,
-    )
+        compiler_params=PARAMS,
+        name="combine",
+    )(mine, forecast, *from_partners(forecast), delayed, *others_delayed)
     return out.reshape(members, 1 + lagged, fields, height, width)
 
 

time: 46.5 us -> 40.3 us (0.87)
  starting transfers between devices: 26.2 us -> 18.8 us
  Pallas kernels: 8.83 us -> 9.68 us
    ppermute x4 -> x2, starting transfers between devices: 10.2 us -> 1.31 us  [from_rows(): outer = lax.ppermute(array, 'slab', outer_pairs)]
    ppermute x3, waiting for transfers between devices: 2.78 us -> 4.95 us  [from_partners(): lax.ppermute(array, 'mem', [((i + d) % parts, i) for i in range(parts)])]
    ppermute x4 -> x7, waiting for transfers between devices: 8.34 us -> 6.5 us  [from_slab(): return lax.ppermute(array, 'slab', [(i, i ^ bit) for i in range(slabs)])]
    ppermute x4 -> x7, starting transfers between devices: 11.4 us -> 12.9 us  [from_slab(): return lax.ppermute(array, 'slab', [(i, i ^ bit) for i in range(slabs)])]
    pallas_call x3 -> x5, Pallas kernels: 7.25 us -> 7.98 us  [the longest x1 4.66 us: shards(): pl.pallas_call(functools.partial(solve_kernel, parts), out_shape=shape_of...]
  transfers between devices with their start and end apart: 11 -> 12, of which waited for: 5 -> 5; matrix products, arithmetic and copies ran while one was open for 0% -> 0% of each run, Pallas kernels for 4% -> 16%
where the time goes in v3:
time: 40.3 us; the launch traced here: 40.1 us
  starting transfers between devices  18.8 us (47%)
  waiting for transfers between devices  11.5 us (29%)
  Pallas kernels  9.68 us (24%)
    ppermute x7, starting transfers between devices, from_slab(): return lax.ppermute(array, 'slab', [(i, i ^ bit) for i in range(slabs)])  12.9 us
    ppermute x7, waiting for transfers between devices, from_slab(): return lax.ppermute(array, 'slab', [(i, i ^ bit) for i in range(slabs)])  6.5 us
    ppermute x3, waiting for transfers between devices, from_partners(): lax.ppermute(array, 'mem', [((i + d) % parts, i) for i in range(parts)])  4.95 us
    pallas_call x1, Pallas kernels, shards(): pl.pallas_call(functools.partial(solve_kernel, parts), out_shape=shape_of...  4.66 us
    ppermute x3, starting transfers between devices, from_partners(): lax.ppermute(array, 'mem', [((i + d) % parts, i) for i in range(parts)])  4.59 us
    pallas_call x1, Pallas kernels, shards(): pl.pallas_call(functools.partial(combine_kernel, parts, fields), out_shap...  1.92 us
    pallas_call x1, Pallas kernels, shards(): pl.pallas_call(functools.partial(own_row_kernel, members, fields, chunks)...  1.7 us
    ppermute x2, starting transfers between devices, from_rows(): outer = lax.ppermute(array, 'slab', outer_pairs)  1.31 us
  transfers between devices with their start and end apart: 12, of which 5 were waited for; matrix products, arithmetic and copies ran while one was open for 0% of the time, Pallas kernels for 16%

profile of v3, /device:TPU:0, one launch (start us, length us, event | category | flops | bytes accessed | tf_op | source)
XLA Modules:
  0.0 40.1 jit_solution(13318843059547567443)
XLA Ops:
  0.0 0.7 %coefficients.1.coefs_ref = f32[2,512]{1,0:T(2,128)S(1)} custom-call(f32[4,128]{1,0:T(4,128)} %bitcast.10, f32[8,128]{1,0:T(8,128)} %bitcast.8), custom_call_target="tpu_custom_call" | custom-call | tf_op jit(solution)/shard_map/coefficients/pallas_call | solution.py:349
  0.7 0.5 %collective-permute-start = (f32[2,512]{1,0:T(2,128)S(1)}, f32[2,512]{1,0:T(2,128)S(1)}, u32[]{:S(2)}, u32[]{:S(2)}) collective-permute-start(f32[2,512]{1,0:T(2,128)S(1)} %coefficients.1.coefs_ref), channel_id=1, source_target_pairs={{0,2},{2,0},{4,6},{6,4},{8,10},{10,8},{12,14},{14,12},{16,18},{18,... | collective-permute-start | bytes 12296 | tf_op jit(solution)/shard_map/ppermute | solution.py:336
  1.3 0.6 %collective-permute-start.1 = (f32[2,512]{1,0:T(2,128)S(1)}, f32[2,512]{1,0:T(2,128)S(1)}, u32[]{:S(2)}, u32[]{:S(2)}) collective-permute-start(f32[2,512]{1,0:T(2,128)S(1)} %coefficients.1.coefs_ref), channel_id=1, source_target_pairs={{2,4},{6,8},{10,12},{14,16},{18,20},{22,24},{26,28},{4,2},{8,6},{1... | collective-permute-start | bytes 12296 | tf_op jit(solution)/shard_map/ppermute | solution.py:342
  1.9 1.7 %own_row.1 = (f32[128,512]{1,0:T(8,128)S(1)}, f32[128,512]{1,0:T(8,128)S(1)}, bf16[512,512]{1,0:T(8,128)(2,1)S(1)}, s32[2,512]{1,0:T(2,128)S(1)}, f32[32,512]{1,0:T(8,128)S(1)}) custom-call(f32[512,128]{1,0:T(8,128)} %bitcast.7, f32[4,128]{1,0:T(4,128)} %bitcast.11, f32[8,128]{1,0:T(8,128)} %bitcast.9, s32[2,256]{1,0:T(2,128)} %refs_3_.1, s32[2,256]{1,0:T(2,128)} %refs_4_.1, ...), custom_call_target="tpu_custom_call" | custom-call | tf_op jit(solution)/shard_map/own_row/pallas_call | solution.py:360
  3.6 0.0 copy-start
  3.6 0.0 collective-permute-done.1.outer_ref
  3.6 0.6 %observe.1 = (f32[32,256]{1,0:T(8,128)S(1)}, f32[32,256]{1,0:T(8,128)S(1)}, f32[128,512]{1,0:T(8,128)S(1)}) custom-call(f32[2,512]{1,0:T(2,128)S(1)} %collective-permute-done.inner_ref, f32[2,512]{1,0:T(2,128)S(1)} %collective-permute-done.1.outer_ref, f32[32,512]{1,0:T(8,128)S(1)} %get-tuple-element.13.part_obs_ref, ...), custom_call_target="tpu_custom_call" | custom-call | tf_op jit(solution)/shard_map/observe/pallas_call | solution.py:375
  4.3 4.0 %collective-permute-start.2 = (f32[32,256]{1,0:T(8,128)S(1)}, f32[32,256]{1,0:T(8,128)S(1)}, u32[]{:S(2)}, u32[]{:S(2)}) collective-permute-start(f32[32,256]{1,0:T(8,128)S(1)} %get-tuple-element.18), channel_id=1, source_target_pairs={{0,2},{2,0},{4,6},{6,4},{8,10},{10,8},{12,14},{14,12},{16,18},{18,... | collective-permute-start | bytes 98312 | tf_op jit(solution)/shard_map/ppermute | solution.py:336
  8.2 0.9 %collective-permute-done.2 = f32[32,256]{1,0:T(8,128)S(1)} collective-permute-done((f32[32,256]{1,0:T(8,128)S(1)}, f32[32,256]{1,0:T(8,128)S(1)}, u32[]{:S(2)}, u32[]{:S(2)}) %collective-permute-start.2) | collective-permute-done | bytes 32800 | tf_op jit(solution)/shard_map/ppermute | solution.py:336
  9.1 2.6 %collective-permute-start.3 = (f32[32,256]{1,0:T(8,128)S(1)}, f32[32,256]{1,0:T(8,128)S(1)}, u32[]{:S(2)}, u32[]{:S(2)}) collective-permute-start(f32[32,256]{1,0:T(8,128)S(1)} %add.12), channel_id=1, source_target_pairs={{0,4},{2,6},{4,0},{6,2},{8,12},{10,14},{12,8},{14,10},{16,20},{18,... | collective-permute-start | bytes 98312 | tf_op jit(solution)/shard_map/ppermute | solution.py:336
  11.6 0.1 collective-permute-start.8
  11.7 0.7 %collective-permute-start.9 = (f32[128,512]{1,0:T(8,128)S(1)}, f32[128,512]{1,0:T(8,128)S(1)}, u32[]{:S(2)}, u32[]{:S(2)}) collective-permute-start(f32[128,512]{1,0:T(8,128)S(1)} %get-tuple-element.20), channel_id=1, source_target_pairs={{2,4},{6,8},{10,12},{14,16},{18,20},{22,24},{26,28},{4,2},{8,6},{1... | collective-permute-start | bytes 786440 | tf_op jit(solution)/shard_map/ppermute | solution.py:342
  12.4 1.6 %collective-permute-start.11 = (f32[1024,128]{1,0:T(8,128)S(1)}, f32[1024,128]{1,0:T(8,128)S(1)}, u32[]{:S(2)}, u32[]{:S(2)}) collective-permute-start(f32[1024,128]{1,0:T(8,128)S(1)} %bitcast.5), channel_id=1, source_target_pairs={{1,0},{0,1},{3,2},{2,3},{5,4},{4,5},{7,6},{6,7},{9,8},{8,9},{11,10... | collective-permute-start | bytes 1572872 | tf_op jit(solution)/shard_map/ppermute | solution.py:331
  14.0 2.9 %collective-permute-start.4 = (f32[32,256]{1,0:T(8,128)S(1)}, f32[32,256]{1,0:T(8,128)S(1)}, u32[]{:S(2)}, u32[]{:S(2)}) collective-permute-start(f32[32,256]{1,0:T(8,128)S(1)} %add.13), channel_id=1, source_target_pairs={{0,8},{2,10},{4,12},{6,14},{8,0},{10,2},{12,4},{14,6},{16,24},{18,... | collective-permute-start | bytes 98312 | tf_op jit(solution)/shard_map/ppermute | solution.py:336
  16.8 3.4 %collective-permute-done.4 = f32[32,256]{1,0:T(8,128)S(1)} collective-permute-done((f32[32,256]{1,0:T(8,128)S(1)}, f32[32,256]{1,0:T(8,128)S(1)}, u32[]{:S(2)}, u32[]{:S(2)}) %collective-permute-start.4) | collective-permute-done | bytes 32800 | tf_op jit(solution)/shard_map/ppermute | solution.py:336
  20.3 2.9 %collective-permute-start.5 = (f32[32,256]{1,0:T(8,128)S(1)}, f32[32,256]{1,0:T(8,128)S(1)}, u32[]{:S(2)}, u32[]{:S(2)}) collective-permute-start(f32[32,256]{1,0:T(8,128)S(1)} %add.14), channel_id=1, source_target_pairs={{0,16},{2,18},{4,20},{6,22},{8,24},{10,26},{12,28},{14,30},{16,0},... | collective-permute-start | bytes 98312 | tf_op jit(solution)/shard_map/ppermute | solution.py:336
  23.2 2.2 %collective-permute-done.5 = f32[32,256]{1,0:T(8,128)S(1)} collective-permute-done((f32[32,256]{1,0:T(8,128)S(1)}, f32[32,256]{1,0:T(8,128)S(1)}, u32[]{:S(2)}, u32[]{:S(2)}) %collective-permute-start.5) | collective-permute-done | bytes 32800 | tf_op jit(solution)/shard_map/ppermute | solution.py:336
  25.4 1.5 %collective-permute-start.6 = (f32[32,256]{1,0:T(8,128)S(1)}, f32[32,256]{1,0:T(8,128)S(1)}, u32[]{:S(2)}, u32[]{:S(2)}) collective-permute-start(f32[32,256]{1,0:T(8,128)S(1)} %add.15.refs_3_), channel_id=1, source_target_pairs={{1,0},{0,1},{3,2},{2,3},{5,4},{4,5},{7,6},{6,7},{9,8},{8,9},{11,10... | collective-permute-start | bytes 98312 | tf_op jit(solution)/shard_map/ppermute | solution.py:331
  26.9 2.4 %collective-permute-done.6.refs_4_ = f32[32,256]{1,0:T(8,128)S(1)} collective-permute-done((f32[32,256]{1,0:T(8,128)S(1)}, f32[32,256]{1,0:T(8,128)S(1)}, u32[]{:S(2)}, u32[]{:S(2)}) %collective-permute-start.6) | collective-permute-done | bytes 32800 | tf_op jit(solution)/shard_map/ppermute | solution.py:331
  29.3 0.1 complete.1.refs_0_
  29.4 1.5 %collective-permute-start.10 = (f32[128,512]{1,0:T(8,128)S(1)}, f32[128,512]{1,0:T(8,128)S(1)}, u32[]{:S(2)}, u32[]{:S(2)}) collective-permute-start(f32[128,512]{1,0:T(8,128)S(1)} %complete.1.refs_0_), channel_id=1, source_target_pairs={{1,0},{0,1},{3,2},{2,3},{5,4},{4,5},{7,6},{6,7},{9,8},{8,9},{11,10... | collective-permute-start | bytes 786440 | tf_op jit(solution)/shard_map/ppermute | solution.py:331
  30.9 4.7 %solve.1.mine_ref = f32[32,64]{1,0:T(8,128)S(1)} custom-call(f32[2,256]{1,0:T(2,128)} %refs_0_.1, f32[2,256]{1,0:T(2,128)} %refs_1_.1, f32[2,64,256]{2,1,0:T(8,128)} %refs_2_.1, f32[32,256]{1,0:T(8,128)S(1)} %add.15.refs_3_, f32[32,256]{1,0:T(8,128)S(1)} %collective-permute-done.6.refs_4_, f32[32,256]{1,0:T(8,128)S(1)} %get-tuple-element.22.refs_5_, ...), custom_call_target="tpu_custom_call" | custom-call | tf_op jit(solution)/shard_map/solve/pallas_call | solution.py:406
  35.6 2.5 %collective-permute-done.10.refs_1_ = f32[128,512]{1,0:T(8,128)S(1)} collective-permute-done((f32[128,512]{1,0:T(8,128)S(1)}, f32[128,512]{1,0:T(8,128)S(1)}, u32[]{:S(2)}, u32[]{:S(2)}) %collective-permute-start.10) | collective-permute-done | bytes 262176 | tf_op jit(solution)/shard_map/ppermute | solution.py:331
  38.1 1.9 %combine.1 = f32[1536,128]{1,0:T(8,128)} custom-call(f32[32,64]{1,0:T(8,128)S(1)} %solve.1.mine_ref, f32[128,512]{1,0:T(8,128)S(1)} %complete.1.refs_0_, f32[128,512]{1,0:T(8,128)S(1)} %collective-permute-done.10.refs_1_, f32[1024,128]{1,0:T(8,128)S(1)} %bitcast.6, f32[1024,128]{1,0:T(8,128)S(1)} %collective-permute-done.11.refs_3_), custom_call_target="tpu_custom_call" | custom-call | tf_op jit(solution)/shard_map/combine/pallas_call | solution.py:414
  (14 shorter events, 0.1 us)
Async XLA Ops:
  0.7 2.9 %collective-permute-start = (f32[2,512]{1,0:T(2,128)S(1)}, f32[2,512]{1,0:T(2,128)S(1)}, u32[]{:S(2)}, u32[]{:S(2)}) collective-permute-start(f32[2,512]{1,0:T(2,128)S(1)} %coefficients.1.coefs_ref), channel_id=1, source_target_pairs={{0,2},{2,0},{4,6},{6,4},{8,10},{10,8},{12,14},{14,12},{16,18},{18,... | collective-permute-start | bytes 12296 | tf_op jit(solution)/shard_map/ppermute | solution.py:336
  1.3 2.4 %collective-permute-start.1 = (f32[2,512]{1,0:T(2,128)S(1)}, f32[2,512]{1,0:T(2,128)S(1)}, u32[]{:S(2)}, u32[]{:S(2)}) collective-permute-start(f32[2,512]{1,0:T(2,128)S(1)} %coefficients.1.coefs_ref), channel_id=1, source_target_pairs={{2,4},{6,8},{10,12},{14,16},{18,20},{22,24},{26,28},{4,2},{8,6},{1... | collective-permute-start | bytes 12296 | tf_op jit(solution)/shard_map/ppermute | solution.py:342
  3.6 8.8 %copy-start = (f32[32,2,4,1,512]{4,3,2,1,0:T(1,128)S(1)}, f32[32,2,4,1,512]{4,3,2,1,0:T(1,128)}, u32[]{:S(2)}) copy-start(f32[32,2,4,1,512]{4,3,2,1,0:T(1,128)} %param.11) | copy-start | bytes 1572868
  4.3 4.8 %collective-permute-start.2 = (f32[32,256]{1,0:T(8,128)S(1)}, f32[32,256]{1,0:T(8,128)S(1)}, u32[]{:S(2)}, u32[]{:S(2)}) collective-permute-start(f32[32,256]{1,0:T(8,128)S(1)} %get-tuple-element.18), channel_id=1, source_target_pairs={{0,2},{2,0},{4,6},{6,4},{8,10},{10,8},{12,14},{14,12},{16,18},{18,... | collective-permute-start | bytes 98312 | tf_op jit(solution)/shard_map/ppermute | solution.py:336
  9.1 4.9 %collective-permute-start.3 = (f32[32,256]{1,0:T(8,128)S(1)}, f32[32,256]{1,0:T(8,128)S(1)}, u32[]{:S(2)}, u32[]{:S(2)}) collective-permute-start(f32[32,256]{1,0:T(8,128)S(1)} %add.12), channel_id=1, source_target_pairs={{0,4},{2,6},{4,0},{6,2},{8,12},{10,14},{12,8},{14,10},{16,20},{18,... | collective-permute-start | bytes 98312 | tf_op jit(solution)/shard_map/ppermute | solution.py:336
  11.6 17.7 %collective-permute-start.8 = (f32[128,512]{1,0:T(8,128)S(1)}, f32[128,512]{1,0:T(8,128)S(1)}, u32[]{:S(2)}, u32[]{:S(2)}) collective-permute-start(f32[128,512]{1,0:T(8,128)S(1)} %get-tuple-element.20), channel_id=1, source_target_pairs={{0,2},{2,0},{4,6},{6,4},{8,10},{10,8},{12,14},{14,12},{16,18},{18,... | collective-permute-start | bytes 786440 | tf_op jit(solution)/shard_map/ppermute | solution.py:336
  11.7 17.6 %collective-permute-start.9 = (f32[128,512]{1,0:T(8,128)S(1)}, f32[128,512]{1,0:T(8,128)S(1)}, u32[]{:S(2)}, u32[]{:S(2)}) collective-permute-start(f32[128,512]{1,0:T(8,128)S(1)} %get-tuple-element.20), channel_id=1, source_target_pairs={{2,4},{6,8},{10,12},{14,16},{18,20},{22,24},{26,28},{4,2},{8,6},{1... | collective-permute-start | bytes 786440 | tf_op jit(solution)/shard_map/ppermute | solution.py:342
  12.4 23.2 %collective-permute-start.11 = (f32[1024,128]{1,0:T(8,128)S(1)}, f32[1024,128]{1,0:T(8,128)S(1)}, u32[]{:S(2)}, u32[]{:S(2)}) collective-permute-start(f32[1024,128]{1,0:T(8,128)S(1)} %bitcast.5), channel_id=1, source_target_pairs={{1,0},{0,1},{3,2},{2,3},{5,4},{4,5},{7,6},{6,7},{9,8},{8,9},{11,10... | collective-permute-start | bytes 1572872 | tf_op jit(solution)/shard_map/ppermute | solution.py:331
  14.0 6.3 %collective-permute-start.4 = (f32[32,256]{1,0:T(8,128)S(1)}, f32[32,256]{1,0:T(8,128)S(1)}, u32[]{:S(2)}, u32[]{:S(2)}) collective-permute-start(f32[32,256]{1,0:T(8,128)S(1)} %add.13), channel_id=1, source_target_pairs={{0,8},{2,10},{4,12},{6,14},{8,0},{10,2},{12,4},{14,6},{16,24},{18,... | collective-permute-start | bytes 98312 | tf_op jit(solution)/shard_map/ppermute | solution.py:336
  20.3 5.1 %collective-permute-start.5 = (f32[32,256]{1,0:T(8,128)S(1)}, f32[32,256]{1,0:T(8,128)S(1)}, u32[]{:S(2)}, u32[]{:S(2)}) collective-permute-start(f32[32,256]{1,0:T(8,128)S(1)} %add.14), channel_id=1, source_target_pairs={{0,16},{2,18},{4,20},{6,22},{8,24},{10,26},{12,28},{14,30},{16,0},... | collective-permute-start | bytes 98312 | tf_op jit(solution)/shard_map/ppermute | solution.py:336
  25.4 3.9 %collective-permute-start.6 = (f32[32,256]{1,0:T(8,128)S(1)}, f32[32,256]{1,0:T(8,128)S(1)}, u32[]{:S(2)}, u32[]{:S(2)}) collective-permute-start(f32[32,256]{1,0:T(8,128)S(1)} %add.15.refs_3_), channel_id=1, source_target_pairs={{1,0},{0,1},{3,2},{2,3},{5,4},{4,5},{7,6},{6,7},{9,8},{8,9},{11,10... | collective-permute-start | bytes 98312 | tf_op jit(solution)/shard_map/ppermute | solution.py:331
  29.3 1.6 %collective-permute-start.7 = (f32[64,256]{1,0:T(8,128)S(1)}, f32[64,256]{1,0:T(8,128)S(1)}, u32[]{:S(2)}, u32[]{:S(2)}) collective-permute-start(f32[64,256]{1,0:T(8,128)S(1)} %pad_maximum_fusion), channel_id=1, source_target_pairs={{0,2},{2,0},{4,6},{6,4},{8,10},{10,8},{12,14},{14,12},{16,18},{18,... | collective-permute-start | bytes 196616 | tf_op jit(solution)/shard_map/ppermute | solution.py:336
  29.4 8.8 %collective-permute-start.10 = (f32[128,512]{1,0:T(8,128)S(1)}, f32[128,512]{1,0:T(8,128)S(1)}, u32[]{:S(2)}, u32[]{:S(2)}) collective-permute-start(f32[128,512]{1,0:T(8,128)S(1)} %complete.1.refs_0_), channel_id=1, source_target_pairs={{1,0},{0,1},{3,2},{2,3},{5,4},{4,5},{7,6},{6,7},{9,8},{8,9},{11,10... | collective-permute-start | bytes 786440 | tf_op jit(solution)/shard_map/ppermute | solution.py:331

commit v4 on v3

--- a/solution.py
+++ b/solution.py
@@ -12,6 +12,13 @@
 BF16 = jnp.bfloat16
 HIGHEST = lax.Precision.HIGHEST
 PARAMS = pltpu.CompilerParams(vmem_limit_bytes=48 * 1024 * 1024)
+
+
+OWN_FLOPS, SUM_FLOPS, GATHER_FLOPS, SOLVE_FLOPS = 10**11, 5*10**8, 10**9, 2*10**9
+
+
+def estimate(flops):
+    return pl.CostEstimate(flops=flops, transcendentals=0, bytes_accessed=0)
 
 
 def rows_of(array):
@@ -136,11 +143,9 @@
     kinds_ref,
     keep_ref,
     send_ref,
-    again_ref,
 ):
     even = lax.rem(lax.axis_index("slab"), 2) == 0
     here = here_ref[...]
-    again_ref[...] = here
     below = jnp.where(even, inner_ref[0:1, :], outer_ref[0:1, :])
     above = jnp.where(even, outer_ref[1:2, :], inner_ref[1:2, :])
     picked = picked_values(
@@ -158,15 +163,24 @@
     send_ref[...] = jnp.where(even, second, first)
 
 
-def complete_kernel(part_ref, inner_ref, outer_ref, coefs_ref, forecast_ref):
+def sum_kernel(terms_ref, other_ref, sum_ref):
+    sum_ref[...] = terms_ref[...] + other_ref[...]
+
+
+def complete_kernel(part_ref, inner_ref, outer_ref, coefs_ref, _, forecast_ref):
     even = lax.rem(lax.axis_index("slab"), 2) == 0
-    inner, outer = inner_ref[...], outer_ref[...]
     above, below = coefs_ref[0:1, :], coefs_ref[1:2, :]
     forecast_ref[...] = (
         part_ref[...]
-        + jnp.where(even, below, above) * inner
-        + jnp.where(even, above, below) * outer
-    )
+        + jnp.where(even, below, above) * inner_ref[...]
+        + jnp.where(even, above, below) * outer_ref[...]
+    )
+
+
+def gather_kernel(*refs):
+    local = refs[0].shape[0]
+    for d, ref in enumerate(refs[:-1]):
+        refs[-1][d * local : (d + 1) * local, :] = ref[...]
 
 
 def solve_transposed(system, right_t, floor):
@@ -204,8 +218,8 @@
 
 
 def solve_kernel(parts, *refs):
-    sources, priors, mine_ref = refs[:3], refs[3 : 3 + 2 * parts], refs[3 + 2 * parts]
-    value_ref, error_ref, noise_ref, prior, sems = refs[4 + 2 * parts :]
+    sources, kept_ref, received_ref, mine_ref = refs[:3], refs[3], refs[4], refs[5]
+    value_ref, error_ref, noise_ref, prior, sems = refs[6:]
     copies = at_once(sources, (value_ref, error_ref, noise_ref), sems)
     batches, members, count = noise_ref.shape
     local = members // parts
@@ -215,7 +229,8 @@
     for d in range(parts):
         owner = lax.rem(own + d, parts)
         rows = pl.ds(pl.multiple_of(owner * local, local), local)
-        kept, received = priors[d][...], priors[parts + d][...]
+        kept = kept_ref[d * local : (d + 1) * local, :]
+        received = received_ref[d * local : (d + 1) * local, :]
         prior[rows, :half] = jnp.where(even, kept, received)
         prior[rows, half:] = jnp.where(even, received, kept)
     for copy in copies:
@@ -313,7 +328,7 @@
     chunks = width // LANES
     lagged = delayed_ensemble.shape[1]
     slabs, parts = lax.axis_size("slab"), lax.axis_size("mem")
-    assert slabs & (slabs - 1) == 0
+    assert slabs & (slabs - 1) == 0 and slabs >= 8
     batches, all_members, count = obs_noise.shape
     total = batches * count
     planes = (1 + lagged) * fields * chunks
@@ -337,10 +352,6 @@
 
     outer_pairs = [(i, i + 1) for i in range(1, slabs - 1, 2)]
     outer_pairs += [(j, i) for i, j in outer_pairs]
-
-    def from_rows(array):
-        outer = lax.ppermute(array, "slab", outer_pairs)
-        return from_slab(array, 1), outer
 
     present, delayed = rows_of(present_ensemble), rows_of(delayed_ensemble)
     spread, ratios = rows_of(spreading_coefficient), rows_of(transport_ratios)
@@ -354,7 +365,8 @@
         compiler_params=PARAMS,
         name="coefficients",
     )(*sources)
-    inner_coefs, outer_coefs = from_rows(coefs)
+    outer_coefs = lax.ppermute(coefs, "slab", outer_pairs)
+    inner_coefs = from_slab(coefs, 1)
     sources = in_hbm((present, spread, ratios, obs_row, obs_col, obs_field))
     buffers, sems = landing(sources)
     part, here, taps, kinds, part_obs = pl.pallas_call(
@@ -369,46 +381,57 @@
         in_specs=[hbm] * len(sources),
         scratch_shapes=[*buffers, sems],
         compiler_params=PARAMS,
+        cost_estimate=estimate(OWN_FLOPS),
         name="own_row",
     )(*sources)
-    others_delayed = from_partners(delayed)
-    keep, send, again = pl.pallas_call(
+    others_delayed = from_partners(lax.optimization_barrier((delayed, coefs))[0])
+    keep, send = pl.pallas_call(
         functools.partial(observe_kernel, members, fields),
         out_shape=(
             shape_of((members, total // 2)),
             shape_of((members, total // 2)),
-            shape_of(stacked),
         ),
         compiler_params=PARAMS,
         name="observe",
     )(inner_coefs, outer_coefs, part_obs, here, taps, kinds)
 
+    def summed(terms, bit, flops):
+        return pl.pallas_call(
+            sum_kernel,
+            out_shape=shape_of(terms.shape),
+            cost_estimate=estimate(flops),
+            compiler_params=PARAMS,
+            name="sum",
+        )(terms, from_slab(terms, bit))
+
     terms = keep + from_slab(send, 1)
-    inner_row, outer_row = from_rows(again)
+    here, _ = lax.optimization_barrier((here, terms))
+    outer_row = lax.ppermute(here, "slab", outer_pairs)
+    inner_row = from_slab(here, 1)
     forecast = pl.pallas_call(
-        complete_kernel,
-        out_shape=shape_of(stacked),
-        compiler_params=PARAMS,
-        name="complete",
-    )(part, inner_row, outer_row, coefs)
-    bit = 2
-    while bit < slabs:
-        terms = terms + from_slab(terms, bit)
-        bit *= 2
-    priors = [terms, *from_partners(terms)]
-    if parts == 2:
-        gathered = from_slab(jnp.concatenate(priors, axis=0), 1)
-        priors += [gathered[d * members : (d + 1) * members] for d in range(parts)]
-    else:
-        priors += [from_slab(prior, 1) for prior in priors]
+        complete_kernel, out_shape=shape_of(stacked), compiler_params=PARAMS, name="complete"
+    )(part, inner_row, outer_row, coefs, others_delayed[0])
+    bit = slabs // 2
+    while bit > 1:
+        terms = summed(terms, bit, SUM_FLOPS)
+        bit //= 2
+    priors = pl.pallas_call(
+        gather_kernel,
+        out_shape=shape_of((all_members, total // 2)),
+        cost_estimate=estimate(GATHER_FLOPS),
+        compiler_params=PARAMS,
+        name="gather",
+    )(terms, *from_partners(terms))
+    priors = [priors, from_slab(priors, 1)]
     sources = in_hbm((obs_value, obs_error, obs_noise))
     buffers, sems = landing(sources)
     mine = pl.pallas_call(
         functools.partial(solve_kernel, parts),
         out_shape=shape_of((members, all_members)),
-        in_specs=[hbm] * len(sources) + [vmem] * len(priors),
+        in_specs=[hbm] * len(sources) + [vmem] * 2,
         scratch_shapes=[*buffers, pltpu.VMEM((all_members, total), F32), sems],
         compiler_params=PARAMS,
+        cost_estimate=estimate(SOLVE_FLOPS),
         name="solve",
     )(*sources, *priors)
     out = pl.pallas_call(

time: 40.3 us -> 38.9 us (0.965)
  starting transfers between devices: 18.8 us -> 15.9 us
  waiting for transfers between devices: 11.5 us -> 13 us
    ppermute x7, waiting for transfers between devices: 6.5 us -> 11.2 us  [from_slab(): return lax.ppermute(array, 'slab', [(i, i ^ bit) for i in range(slabs)])]
    ppermute x3, waiting for transfers between devices: 4.95 us -> 1.75 us  [from_partners(): lax.ppermute(array, 'mem', [((i + d) % parts, i) for i in range(parts)])]
    ppermute x7, starting transfers between devices: 12.9 us -> 11 us  [from_slab(): return lax.ppermute(array, 'slab', [(i, i ^ bit) for i in range(slabs)])]
    ppermute x3, starting transfers between devices: 4.59 us -> 3.58 us  [from_partners(): lax.ppermute(array, 'mem', [((i + d) % parts, i) for i in range(parts)])]
  transfers between devices with their start and end apart: 12 -> 12, of which waited for: 5 -> 5; matrix products, arithmetic and copies ran while one was open for 0% -> 0% of each run, Pallas kernels for 16% -> 18%
where the time goes in v4:
time: 38.9 us; the launch traced here: 38.6 us
  starting transfers between devices  15.9 us (41%)
  waiting for transfers between devices  13 us (33%)
  Pallas kernels  9.64 us (25%)
    ppermute x7, waiting for transfers between devices, from_slab(): return lax.ppermute(array, 'slab', [(i, i ^ bit) for i in range(slabs)])  11.2 us
    ppermute x7, starting transfers between devices, from_slab(): return lax.ppermute(array, 'slab', [(i, i ^ bit) for i in range(slabs)])  11 us
    pallas_call x1, Pallas kernels, shards(): pl.pallas_call(functools.partial(solve_kernel, parts), out_shape=shape_of...  4.66 us
    ppermute x3, starting transfers between devices, from_partners(): lax.ppermute(array, 'mem', [((i + d) % parts, i) for i in range(parts)])  3.58 us
    pallas_call x1, Pallas kernels, shards(): pl.pallas_call(functools.partial(combine_kernel, parts, fields), out_shap...  1.92 us
    ppermute x3, waiting for transfers between devices, from_partners(): lax.ppermute(array, 'mem', [((i + d) % parts, i) for i in range(parts)])  1.75 us
    pallas_call x1, Pallas kernels, shards(): pl.pallas_call(functools.partial(own_row_kernel, members, fields, chunks)...  1.67 us
  transfers between devices with their start and end apart: 12, of which 5 were waited for; matrix products, arithmetic and copies ran while one was open for 0% of the time, Pallas kernels for 18%

profile of v4, /device:TPU:0, one launch (start us, length us, event | category | flops | bytes accessed | tf_op | source)
XLA Modules:
  0.0 38.6 jit_solution(909851404328138610)
XLA Ops:
  0.0 0.7 %coefficients.1.coefs_ref = f32[2,512]{1,0:T(2,128)S(1)} custom-call(f32[4,128]{1,0:T(4,128)} %bitcast.9, f32[8,128]{1,0:T(8,128)} %bitcast.7), custom_call_target="tpu_custom_call" | custom-call | tf_op jit(solution)/shard_map/coefficients/pallas_call | solution.py:360
  0.7 0.7 %collective-permute-start.1 = (f32[2,512]{1,0:T(2,128)S(1)}, f32[2,512]{1,0:T(2,128)S(1)}, u32[]{:S(2)}, u32[]{:S(2)}) collective-permute-start(f32[2,512]{1,0:T(2,128)S(1)} %coefficients.1.coefs_ref), channel_id=1, source_target_pairs={{2,4},{6,8},{10,12},{14,16},{18,20},{22,24},{26,28},{4,2},{8,6},{1... | collective-permute-start | bytes 12296 | tf_op jit(solution)/shard_map/ppermute | solution.py:368
  1.4 4.4 %collective-permute-start = (f32[2,512]{1,0:T(2,128)S(1)}, f32[2,512]{1,0:T(2,128)S(1)}, u32[]{:S(2)}, u32[]{:S(2)}) collective-permute-start(f32[2,512]{1,0:T(2,128)S(1)} %coefficients.1.coefs_ref), channel_id=1, source_target_pairs={{0,2},{2,0},{4,6},{6,4},{8,10},{10,8},{12,14},{14,12},{16,18},{18,... | collective-permute-start | bytes 12296 | tf_op jit(solution)/shard_map/ppermute | solution.py:351
  5.8 1.5 %collective-permute-start.10 = (f32[1024,128]{1,0:T(8,128)}, f32[1024,128]{1,0:T(8,128)S(1)}, u32[]{:S(2)}, u32[]{:S(2)}) collective-permute-start(f32[1024,128]{1,0:T(8,128)} %bitcast.5), channel_id=1, source_target_pairs={{1,0},{0,1},{3,2},{2,3},{5,4},{4,5},{7,6},{6,7},{9,8},{8,9},{11,10... | collective-permute-start | bytes 1572872 | tf_op jit(solution)/shard_map/ppermute | solution.py:346
  7.3 1.7 %own_row.1 = (f32[128,512]{1,0:T(8,128)S(1)}, f32[128,512]{1,0:T(8,128)S(1)}, bf16[512,512]{1,0:T(8,128)(2,1)S(1)}, s32[2,512]{1,0:T(2,128)S(1)}, f32[32,512]{1,0:T(8,128)S(1)}) custom-call(f32[512,128]{1,0:T(8,128)} %bitcast.11, f32[4,128]{1,0:T(4,128)} %bitcast.10, f32[8,128]{1,0:T(8,128)} %bitcast.8, s32[2,256]{1,0:T(2,128)} %refs_3_.1, ...), custom_call_target="tpu_custom_call" | custom-call | flops 99999997952 | tf_op jit(solution)/shard_map/own_row/pallas_call | solution.py:372
  9.0 0.0 collective-permute-done.inner_ref
  9.0 0.6 %observe.1 = (f32[32,256]{1,0:T(8,128)S(1)}, f32[32,256]{1,0:T(8,128)S(1)}) custom-call(f32[2,512]{1,0:T(2,128)S(1)} %collective-permute-done.inner_ref, f32[2,512]{1,0:T(2,128)S(1)} %collective-permute-done.1.outer_ref, f32[32,512]{1,0:T(8,128)S(1)} %get-tuple-element.14.part_obs_ref, f32[128,512]{1,0:T(8,128)S(1)} %get-tuple-element.21.here_ref, ...), custom_call_target="tpu_custom_call" | custom-call | tf_op jit(solution)/shard_map/observe/pallas_call | solution.py:388
  9.6 0.1 collective-permute-start.2
  9.7 1.2 %collective-permute-done.2 = f32[32,256]{1,0:T(8,128)S(1)} collective-permute-done((f32[32,256]{1,0:T(8,128)S(1)}, f32[32,256]{1,0:T(8,128)S(1)}, u32[]{:S(2)}, u32[]{:S(2)}) %collective-permute-start.2) | collective-permute-done | bytes 32800 | tf_op jit(solution)/shard_map/ppermute | solution.py:351
  10.9 2.6 %collective-permute-start.3 = (f32[32,256]{1,0:T(8,128)S(1)}, f32[32,256]{1,0:T(8,128)S(1)}, u32[]{:S(2)}, u32[]{:S(2)}) collective-permute-start(f32[32,256]{1,0:T(8,128)S(1)} %add.3.terms_ref), channel_id=1, source_target_pairs={{0,16},{2,18},{4,20},{6,22},{8,24},{10,26},{12,28},{14,30},{16,0},... | collective-permute-start | bytes 98312 | tf_op jit(solution)/shard_map/ppermute | solution.py:351
  13.5 0.7 %collective-permute-start.9 = (f32[128,512]{1,0:T(8,128)S(1)}, f32[128,512]{1,0:T(8,128)S(1)}, u32[]{:S(2)}, u32[]{:S(2)}) collective-permute-start(f32[128,512]{1,0:T(8,128)S(1)} %get-tuple-element.21.here_ref), channel_id=1, source_target_pairs={{2,4},{6,8},{10,12},{14,16},{18,20},{22,24},{26,28},{4,2},{8,6},{1... | collective-permute-start | bytes 786440 | tf_op jit(solution)/shard_map/ppermute | solution.py:409
  14.1 2.9 %collective-permute-start.8 = (f32[128,512]{1,0:T(8,128)S(1)}, f32[128,512]{1,0:T(8,128)S(1)}, u32[]{:S(2)}, u32[]{:S(2)}) collective-permute-start(f32[128,512]{1,0:T(8,128)S(1)} %get-tuple-element.21.here_ref), channel_id=1, source_target_pairs={{0,2},{2,0},{4,6},{6,4},{8,10},{10,8},{12,14},{14,12},{16,18},{18,... | collective-permute-start | bytes 786440 | tf_op jit(solution)/shard_map/ppermute | solution.py:351
  17.1 0.0 collective-permute-done.3.other_ref
  17.1 0.9 %collective-permute-start.4 = (f32[32,256]{1,0:T(8,128)S(1)}, f32[32,256]{1,0:T(8,128)S(1)}, u32[]{:S(2)}, u32[]{:S(2)}) collective-permute-start(f32[32,256]{1,0:T(8,128)S(1)} %sum.3.terms_ref), channel_id=1, source_target_pairs={{0,8},{2,10},{4,12},{6,14},{8,0},{10,2},{12,4},{14,6},{16,24},{18,... | collective-permute-start | bytes 98312 | tf_op jit(solution)/shard_map/ppermute | solution.py:351
  18.0 4.9 %collective-permute-done.4.other_ref = f32[32,256]{1,0:T(8,128)S(1)} collective-permute-done((f32[32,256]{1,0:T(8,128)S(1)}, f32[32,256]{1,0:T(8,128)S(1)}, u32[]{:S(2)}, u32[]{:S(2)}) %collective-permute-start.4) | collective-permute-done | bytes 32800 | tf_op jit(solution)/shard_map/ppermute | solution.py:351
  22.9 3.9 %collective-permute-done.5.other_ref = f32[32,256]{1,0:T(8,128)S(1)} collective-permute-done((f32[32,256]{1,0:T(8,128)S(1)}, f32[32,256]{1,0:T(8,128)S(1)}, u32[]{:S(2)}, u32[]{:S(2)}) %collective-permute-start.5) | collective-permute-done | bytes 32800 | tf_op jit(solution)/shard_map/ppermute | solution.py:351
  26.8 0.5 %collective-permute-start.6 = (f32[32,256]{1,0:T(8,128)S(1)}, f32[32,256]{1,0:T(8,128)S(1)}, u32[]{:S(2)}, u32[]{:S(2)}) collective-permute-start(f32[32,256]{1,0:T(8,128)S(1)} %sum.5.refs_0_), channel_id=1, source_target_pairs={{1,0},{0,1},{3,2},{2,3},{5,4},{4,5},{7,6},{6,7},{9,8},{8,9},{11,10... | collective-permute-start | bytes 98312 | tf_op jit(solution)/shard_map/ppermute | solution.py:346
  27.3 0.1 complete.1.refs_0_
  27.4 1.6 %collective-permute-start.11 = (f32[128,512]{1,0:T(8,128)S(1)}, f32[128,512]{1,0:T(8,128)S(1)}, u32[]{:S(2)}, u32[]{:S(2)}) collective-permute-start(f32[128,512]{1,0:T(8,128)S(1)} %complete.1.refs_0_), channel_id=1, source_target_pairs={{1,0},{0,1},{3,2},{2,3},{5,4},{4,5},{7,6},{6,7},{9,8},{8,9},{11,10... | collective-permute-start | bytes 786440 | tf_op jit(solution)/shard_map/ppermute | solution.py:346
  29.0 1.7 %collective-permute-done.6.refs_1_ = f32[32,256]{1,0:T(8,128)S(1)} collective-permute-done((f32[32,256]{1,0:T(8,128)S(1)}, f32[32,256]{1,0:T(8,128)S(1)}, u32[]{:S(2)}, u32[]{:S(2)}) %collective-permute-start.6) | collective-permute-done | bytes 32800 | tf_op jit(solution)/shard_map/ppermute | solution.py:346
  30.7 0.1 collective-permute-start.7
  30.8 1.2 %collective-permute-done.7.refs_4_ = f32[64,256]{1,0:T(8,128)S(1)} collective-permute-done((f32[64,256]{1,0:T(8,128)S(1)}, f32[64,256]{1,0:T(8,128)S(1)}, u32[]{:S(2)}, u32[]{:S(2)}) %collective-permute-start.7) | collective-permute-done | bytes 65568 | tf_op jit(solution)/shard_map/ppermute | solution.py:351
  32.0 4.7 %solve.1.mine_ref = f32[32,64]{1,0:T(8,128)S(1)} custom-call(f32[2,256]{1,0:T(2,128)} %refs_0_.1, f32[2,256]{1,0:T(2,128)} %refs_1_.1, f32[2,64,256]{2,1,0:T(8,128)} %refs_2_.1, f32[64,256]{1,0:T(8,128)S(1)} %gather.1.refs_3_, f32[64,256]{1,0:T(8,128)S(1)} %collective-permute-done.7.refs_4_), custom_call_target="tpu_custom_call" | custom-call | flops 2000000000 | tf_op jit(solution)/shard_map/solve/pallas_call | solution.py:428
  36.7 1.9 %combine.1 = f32[1536,128]{1,0:T(8,128)} custom-call(f32[32,64]{1,0:T(8,128)S(1)} %solve.1.mine_ref, f32[128,512]{1,0:T(8,128)S(1)} %complete.1.refs_0_, f32[128,512]{1,0:T(8,128)S(1)} %collective-permute-done.11.refs_1_, f32[1024,128]{1,0:T(8,128)S(1)} %bitcast.6, f32[1024,128]{1,0:T(8,128)S(1)} %collective-permute-done.10._.refs_3_), custom_call_target="tpu_custom_call" | custom-call | tf_op jit(solution)/shard_map/combine/pallas_call | solution.py:437
  (13 shorter events, 0.0 us)
Async XLA Ops:
  0.7 8.2 %collective-permute-start.1 = (f32[2,512]{1,0:T(2,128)S(1)}, f32[2,512]{1,0:T(2,128)S(1)}, u32[]{:S(2)}, u32[]{:S(2)}) collective-permute-start(f32[2,512]{1,0:T(2,128)S(1)} %coefficients.1.coefs_ref), channel_id=1, source_target_pairs={{2,4},{6,8},{10,12},{14,16},{18,20},{22,24},{26,28},{4,2},{8,6},{1... | collective-permute-start | bytes 12296 | tf_op jit(solution)/shard_map/ppermute | solution.py:368
  1.4 7.6 %collective-permute-start = (f32[2,512]{1,0:T(2,128)S(1)}, f32[2,512]{1,0:T(2,128)S(1)}, u32[]{:S(2)}, u32[]{:S(2)}) collective-permute-start(f32[2,512]{1,0:T(2,128)S(1)} %coefficients.1.coefs_ref), channel_id=1, source_target_pairs={{0,2},{2,0},{4,6},{6,4},{8,10},{10,8},{12,14},{14,12},{16,18},{18,... | collective-permute-start | bytes 12296 | tf_op jit(solution)/shard_map/ppermute | solution.py:351
  5.8 21.5 %collective-permute-start.10 = (f32[1024,128]{1,0:T(8,128)}, f32[1024,128]{1,0:T(8,128)S(1)}, u32[]{:S(2)}, u32[]{:S(2)}) collective-permute-start(f32[1024,128]{1,0:T(8,128)} %bitcast.5), channel_id=1, source_target_pairs={{1,0},{0,1},{3,2},{2,3},{5,4},{4,5},{7,6},{6,7},{9,8},{8,9},{11,10... | collective-permute-start | bytes 1572872 | tf_op jit(solution)/shard_map/ppermute | solution.py:346
  9.6 1.3 %collective-permute-start.2 = (f32[32,256]{1,0:T(8,128)S(1)}, f32[32,256]{1,0:T(8,128)S(1)}, u32[]{:S(2)}, u32[]{:S(2)}) collective-permute-start(f32[32,256]{1,0:T(8,128)S(1)} %get-tuple-element.19), channel_id=1, source_target_pairs={{0,2},{2,0},{4,6},{6,4},{8,10},{10,8},{12,14},{14,12},{16,18},{18,... | collective-permute-start | bytes 98312 | tf_op jit(solution)/shard_map/ppermute | solution.py:351
  10.9 6.2 %collective-permute-start.3 = (f32[32,256]{1,0:T(8,128)S(1)}, f32[32,256]{1,0:T(8,128)S(1)}, u32[]{:S(2)}, u32[]{:S(2)}) collective-permute-start(f32[32,256]{1,0:T(8,128)S(1)} %add.3.terms_ref), channel_id=1, source_target_pairs={{0,16},{2,18},{4,20},{6,22},{8,24},{10,26},{12,28},{14,30},{16,0},... | collective-permute-start | bytes 98312 | tf_op jit(solution)/shard_map/ppermute | solution.py:351
  13.5 13.9 %collective-permute-start.9 = (f32[128,512]{1,0:T(8,128)S(1)}, f32[128,512]{1,0:T(8,128)S(1)}, u32[]{:S(2)}, u32[]{:S(2)}) collective-permute-start(f32[128,512]{1,0:T(8,128)S(1)} %get-tuple-element.21.here_ref), channel_id=1, source_target_pairs={{2,4},{6,8},{10,12},{14,16},{18,20},{22,24},{26,28},{4,2},{8,6},{1... | collective-permute-start | bytes 786440 | tf_op jit(solution)/shard_map/ppermute | solution.py:409
  14.1 13.2 %collective-permute-start.8 = (f32[128,512]{1,0:T(8,128)S(1)}, f32[128,512]{1,0:T(8,128)S(1)}, u32[]{:S(2)}, u32[]{:S(2)}) collective-permute-start(f32[128,512]{1,0:T(8,128)S(1)} %get-tuple-element.21.here_ref), channel_id=1, source_target_pairs={{0,2},{2,0},{4,6},{6,4},{8,10},{10,8},{12,14},{14,12},{16,18},{18,... | collective-permute-start | bytes 786440 | tf_op jit(solution)/shard_map/ppermute | solution.py:351
  17.1 5.8 %collective-permute-start.4 = (f32[32,256]{1,0:T(8,128)S(1)}, f32[32,256]{1,0:T(8,128)S(1)}, u32[]{:S(2)}, u32[]{:S(2)}) collective-permute-start(f32[32,256]{1,0:T(8,128)S(1)} %sum.3.terms_ref), channel_id=1, source_target_pairs={{0,8},{2,10},{4,12},{6,14},{8,0},{10,2},{12,4},{14,6},{16,24},{18,... | collective-permute-start | bytes 98312 | tf_op jit(solution)/shard_map/ppermute | solution.py:351
  22.9 3.9 %collective-permute-start.5 = (f32[32,256]{1,0:T(8,128)S(1)}, f32[32,256]{1,0:T(8,128)S(1)}, u32[]{:S(2)}, u32[]{:S(2)}) collective-permute-start(f32[32,256]{1,0:T(8,128)S(1)} %sum.4.terms_ref), channel_id=1, source_target_pairs={{0,4},{2,6},{4,0},{6,2},{8,12},{10,14},{12,8},{14,10},{16,20},{18,... | collective-permute-start | bytes 98312 | tf_op jit(solution)/shard_map/ppermute | solution.py:351
  26.8 3.9 %collective-permute-start.6 = (f32[32,256]{1,0:T(8,128)S(1)}, f32[32,256]{1,0:T(8,128)S(1)}, u32[]{:S(2)}, u32[]{:S(2)}) collective-permute-start(f32[32,256]{1,0:T(8,128)S(1)} %sum.5.refs_0_), channel_id=1, source_target_pairs={{1,0},{0,1},{3,2},{2,3},{5,4},{4,5},{7,6},{6,7},{9,8},{8,9},{11,10... | collective-permute-start | bytes 98312 | tf_op jit(solution)/shard_map/ppermute | solution.py:346
  27.4 9.3 %collective-permute-start.11 = (f32[128,512]{1,0:T(8,128)S(1)}, f32[128,512]{1,0:T(8,128)S(1)}, u32[]{:S(2)}, u32[]{:S(2)}) collective-permute-start(f32[128,512]{1,0:T(8,128)S(1)} %complete.1.refs_0_), channel_id=1, source_target_pairs={{1,0},{0,1},{3,2},{2,3},{5,4},{4,5},{7,6},{6,7},{9,8},{8,9},{11,10... | collective-permute-start | bytes 786440 | tf_op jit(solution)/shard_map/ppermute | solution.py:346
  30.7 6.0 %copy-start = (f32[32,2,4,1,512]{4,3,2,1,0:T(1,128)S(1)}, f32[32,2,4,1,512]{4,3,2,1,0:T(1,128)}, u32[]{:S(2)}) copy-start(f32[32,2,4,1,512]{4,3,2,1,0:T(1,128)} %param.11) | copy-start | bytes 1572868
  30.7 1.3 %collective-permute-start.7 = (f32[64,256]{1,0:T(8,128)S(1)}, f32[64,256]{1,0:T(8,128)S(1)}, u32[]{:S(2)}, u32[]{:S(2)}) collective-permute-start(f32[64,256]{1,0:T(8,128)S(1)} %gather.1.refs_3_), channel_id=1, source_target_pairs={{0,2},{2,0},{4,6},{6,4},{8,10},{10,8},{12,14},{14,12},{16,18},{18,... | collective-permute-start | bytes 196616 | tf_op jit(solution)/shard_map/ppermute | solution.py:351

commit v5 on v4

--- a/solution.py
+++ b/solution.py
@@ -14,7 +14,7 @@
 PARAMS = pltpu.CompilerParams(vmem_limit_bytes=48 * 1024 * 1024)
 
 
-OWN_FLOPS, SUM_FLOPS, GATHER_FLOPS, SOLVE_FLOPS = 10**11, 5*10**8, 10**9, 2*10**9
+OWN_FLOPS, SUM_FLOPS, GATHER_FLOPS, SOLVE_FLOPS = 10**11, 7*10**8, 10**9, 2*10**9
 
 
 def estimate(flops):
@@ -84,29 +84,42 @@
     return low + middle + high
 
 
-def coefficient_kernel(chunks, *refs):
-    sources, (coefs_ref,), scratch, sems = refs[:2], refs[2:3], refs[3:5], refs[5]
-    for copy in at_once(sources, scratch, sems):
+def load_kernel(chunks, *refs):
+    count = (len(refs) - 2) // 2
+    sources, held, packed_ref, coefs_ref, sems = refs[:count], refs[count:-3], *refs[-3:]
+    rows = sources[0].shape[0]
+    copies = at_once(sources, (packed_ref.at[:rows], *held), sems)
+    copies[1].wait()
+    copies[2].wait()
+    spread = held[0][...]
+    half = held[1][:chunks, :] * 0.5
+    for ref, start in ((packed_ref, rows), (coefs_ref, 0)):
+        ref[start : start + chunks, :] = spread + half
+        ref[start + chunks : start + 2 * chunks, :] = spread - half
+    for copy in (copies[0], *copies[3:]):
         copy.wait()
-    spread = line(scratch[0], 0, chunks)
-    half = line(scratch[1], 0, chunks) * 0.5
-    coefs_ref[0:1, :] = spread + half
-    coefs_ref[1:2, :] = spread - half
-
-
-def own_row_kernel(members, fields, chunks, *refs):
-    sources, (part_ref, here_ref, taps_ref, kinds_ref, obs_ref), scratch = (
-        refs[:6],
-        refs[6:11],
-        refs[11:17],
-    )
-    for copy in at_once(sources, scratch, refs[17]):
-        copy.wait()
-    present, spread_ref, ratio_ref, row_ref, col_ref, field_ref = scratch
+
+
+def own_row_kernel(
+    members,
+    fields,
+    chunks,
+    present_ref,
+    spread_ref,
+    ratio_ref,
+    row_ref,
+    col_ref,
+    field_ref,
+    part_ref,
+    here_ref,
+    taps_ref,
+    kinds_ref,
+    obs_ref,
+):
     width = chunks * LANES
     spread = line(spread_ref, 0, chunks)
     along_columns = line(ratio_ref, chunks, chunks)
-    here = stacked_planes(present, members, fields, chunks)
+    here = stacked_planes(present_ref, members, fields, chunks)
     here_ref[...] = here
     lane = lax.broadcasted_iota(jnp.int32, here.shape, 1)
     left = jnp.where(lane == 0, 0.0, pltpu.roll(here, 1, 1))
@@ -135,6 +148,7 @@
 def observe_kernel(
     members,
     fields,
+    chunks,
     inner_ref,
     outer_ref,
     part_obs_ref,
@@ -146,8 +160,11 @@
 ):
     even = lax.rem(lax.axis_index("slab"), 2) == 0
     here = here_ref[...]
-    below = jnp.where(even, inner_ref[0:1, :], outer_ref[0:1, :])
-    above = jnp.where(even, outer_ref[1:2, :], inner_ref[1:2, :])
+    rows = members * fields * chunks
+    inner_coefs = [line(inner_ref, rows + k * chunks, chunks) for k in range(2)]
+    outer_coefs = [line(outer_ref, k * chunks, chunks) for k in range(2)]
+    below = jnp.where(even, inner_coefs[0], outer_coefs[0])
+    above = jnp.where(even, outer_coefs[1], inner_coefs[1])
     picked = picked_values(
         jnp.concatenate([below * here, above * here], axis=0), taps_ref[...]
     )
@@ -167,12 +184,14 @@
     sum_ref[...] = terms_ref[...] + other_ref[...]
 
 
-def complete_kernel(part_ref, inner_ref, outer_ref, coefs_ref, _, forecast_ref):
+def complete_kernel(
+    members, fields, chunks, part_ref, inner_ref, outer_ref, coefs_ref, _, forecast_ref
+):
     even = lax.rem(lax.axis_index("slab"), 2) == 0
-    above, below = coefs_ref[0:1, :], coefs_ref[1:2, :]
+    above, below = line(coefs_ref, 0, chunks), line(coefs_ref, chunks, chunks)
     forecast_ref[...] = (
         part_ref[...]
-        + jnp.where(even, below, above) * inner_ref[...]
+        + jnp.where(even, below, above) * stacked_planes(inner_ref, members, fields, chunks)
         + jnp.where(even, above, below) * outer_ref[...]
     )
 
@@ -185,10 +204,7 @@
 
 def solve_transposed(system, right_t, floor):
     size = system.shape[0]
-    eye = (
-        lax.broadcasted_iota(jnp.int32, (size, size), 0)
-        == lax.broadcasted_iota(jnp.int32, (size, size), 1)
-    ).astype(F32)
+    eye = identity(size, size)
     top = jnp.max(jnp.sum(jnp.abs(system), axis=0, keepdims=True)) + 1.0
     scale = 2.0 / (top + floor)
     eps = (top - floor) / (top + floor)
@@ -217,13 +233,20 @@
     return lax.while_loop(more, double, (eps, residual, answer))[2]
 
 
-def solve_kernel(parts, *refs):
-    sources, kept_ref, received_ref, mine_ref = refs[:3], refs[3], refs[4], refs[5]
-    value_ref, error_ref, noise_ref, prior, sems = refs[6:]
-    copies = at_once(sources, (value_ref, error_ref, noise_ref), sems)
+def identity(rows, columns, shift=0):
+    return (
+        lax.broadcasted_iota(jnp.int32, (rows, columns), 0) + shift
+        == lax.broadcasted_iota(jnp.int32, (rows, columns), 1)
+    ).astype(F32)
+
+
+def solve_kernel(
+    parts, value_ref, error_ref, noise_ref, kept_ref, received_ref, mine_ref, prior, whole
+):
     batches, members, count = noise_ref.shape
     local = members // parts
     own = lax.axis_index("mem")
+    own_rows = pl.ds(pl.multiple_of(own * local, local), local)
     even = lax.rem(lax.axis_index("slab"), 2) == 0
     half = batches * count // 2
     for d in range(parts):
@@ -233,82 +256,104 @@
         received = received_ref[d * local : (d + 1) * local, :]
         prior[rows, :half] = jnp.where(even, kept, received)
         prior[rows, half:] = jnp.where(even, received, kept)
-    for copy in copies:
-        copy.wait()
-    eye = (
-        lax.broadcasted_iota(jnp.int32, (members, members), 0)
-        == lax.broadcasted_iota(jnp.int32, (members, members), 1)
-    ).astype(F32)
-    product_t = None
-    nt = (((1,), (1,)), ((), ()))
+    source = lax.broadcasted_iota(jnp.int32, (members, members), 0)
+    target = lax.broadcasted_iota(jnp.int32, (members, members), 1)
+    turn = (source == lax.rem(target + own * local, members)).astype(F32)
+    product_t = turned = None
     for b in range(batches):
+        last = b == batches - 1
         observed = prior[:, b * count : (b + 1) * count]
         if product_t is not None:
-            observed = jnp.dot(
-                product_t, observed, precision=HIGHEST, preferred_element_type=F32
+            both = jnp.dot(
+                product_t,
+                jnp.concatenate([observed, turn], axis=1) if last else observed,
+                precision=HIGHEST,
+                preferred_element_type=F32,
             )
-        errors = error_ref[b : b + 1, :]
-        scaled = (observed - jnp.mean(observed, axis=0, keepdims=True)) / errors
-        innovation = (value_ref[b : b + 1, :] - observed) / errors + noise_ref[b]
+            observed, turned = both[:, :count], both[:, count:]
+        share = 1.0 / error_ref[b : b + 1, :]
+        scaled = (observed - jnp.mean(observed, axis=0, keepdims=True)) * share
+        if last:
+            whole[...] = observed
+            innovation = (
+                value_ref[b : b + 1, :] * share + noise_ref[b, own_rows, :]
+            ) - whole[own_rows, :] * share
+            eye = identity(local, members, own * local)
+        else:
+            innovation = (value_ref[b : b + 1, :] * share + noise_ref[b]) - observed * share
+            eye = identity(members, members)
         both = lax.dot_general(
             jnp.concatenate([scaled, innovation], axis=0),
             scaled,
-            nt,
+            (((1,), (1,)), ((), ())),
             precision=HIGHEST,
             preferred_element_type=F32,
         )
-        system = both[:members] + (members - 1.0) * eye
+        system = both[:members] + (members - 1.0) * identity(members, members)
         weights_t = solve_transposed(system, both[members:], members - 1.0)
         matrix_t = eye + weights_t - jnp.mean(weights_t, axis=1, keepdims=True)
-        if product_t is None:
+        if last:
+            mine_ref[...] = jnp.dot(
+                matrix_t,
+                turn if turned is None else turned,
+                precision=HIGHEST,
+                preferred_element_type=F32,
+            )
+        elif product_t is None:
             product_t = matrix_t
         else:
             product_t = jnp.dot(
                 matrix_t, product_t, precision=HIGHEST, preferred_element_type=F32
             )
 
-    is_own = (
-        lax.broadcasted_iota(jnp.int32, (local, members), 0) + own * local
-        == lax.broadcasted_iota(jnp.int32, (local, members), 1)
-    ).astype(F32)
-    mine = jnp.dot(is_own, product_t, precision=HIGHEST, preferred_element_type=F32)
-    source = lax.broadcasted_iota(jnp.int32, (members, members), 0)
-    target = lax.broadcasted_iota(jnp.int32, (members, members), 1)
-    turn = (source == lax.rem(target + own * local, members)).astype(F32)
-    mine_ref[...] = jnp.dot(mine, turn, precision=HIGHEST, preferred_element_type=F32)
-
 
 def combine_kernel(parts, fields, mine_ref, *refs):
-    forecast_refs, delayed_refs, out_ref = refs[:parts], refs[parts : 2 * parts], refs[2 * parts]
+    forecast_refs, delayed_refs = refs[:parts], refs[parts : 2 * parts]
+    out_ref, done_ref, sems = refs[2 * parts :]
     local = mine_ref.shape[0]
     high, low = split_two(mine_ref[...])
     left = jnp.concatenate([high, high, low], axis=1)
     chunks = forecast_refs[0].shape[1] // LANES
+    level = fields * chunks
     lagged = delayed_refs[0].shape[0] // local
-    planes = fields * chunks + lagged
-    for start in range(0, planes, chunks):
-        if start < fields * chunks:
-            f = start // chunks
-            held = [ref[f * local : (f + 1) * local, :] for ref in forecast_refs]
-        else:
-            first = start - fields * chunks
-            held = [
-                jnp.concatenate(
-                    [ref[pl.ds(first + c, local, stride=lagged), :] for c in range(chunks)],
-                    axis=1,
-                )
-                for ref in delayed_refs
-            ]
-        held_high, held_low = split_two(jnp.concatenate(held, axis=0))
-        result = jnp.dot(
-            left,
-            jnp.concatenate([held_high, held_low, held_high], axis=0),
-            preferred_element_type=F32,
+    planes = level + lagged
+    copies = []
+    for first in [*range(level, planes, level), 0]:
+        for f in range(fields):
+            start = first + f * chunks
+            if first == 0:
+                held = [ref[f * local : (f + 1) * local, :] for ref in forecast_refs]
+            else:
+                held = [
+                    jnp.concatenate(
+                        [
+                            ref[pl.ds(start - level + c, local, stride=lagged), :]
+                            for c in range(chunks)
+                        ],
+                        axis=1,
+                    )
+                    for ref in delayed_refs
+                ]
+            held_high, held_low = split_two(jnp.concatenate(held, axis=0))
+            result = jnp.dot(
+                left,
+                jnp.concatenate([held_high, held_low, held_high], axis=0),
+                preferred_element_type=F32,
+            )
+            for c in range(chunks):
+                done_ref[pl.ds(start + c, local, stride=planes), :] = result[
+                    :, c * LANES : (c + 1) * LANES
+                ]
+        copies.append(
+            pltpu.make_async_copy(
+                done_ref.reshape(local, planes, LANES).at[:, first : first + level, :],
+                out_ref.at[:, first : first + level, :],
+                sems.at[len(copies)],
+            )
         )
-        for c in range(chunks):
-            out_ref[pl.ds(start + c, local, stride=planes), :] = result[
-                :, c * LANES : (c + 1) * LANES
-            ]
+        copies[-1].start()
+    for copy in copies:
+        copy.wait()
 
 
 def shards(
@@ -334,12 +379,6 @@
     planes = (1 + lagged) * fields * chunks
     stacked = (fields * members, width)
     hbm = pl.BlockSpec(memory_space=pltpu.HBM)
-    vmem = pl.BlockSpec(memory_space=pltpu.VMEM)
-
-    def landing(sources):
-        return [pltpu.VMEM(s.shape, s.dtype) for s in sources], pltpu.SemaphoreType.DMA(
-            (len(sources),)
-        )
 
     def from_partners(array):
         return [
@@ -355,20 +394,18 @@
 
     present, delayed = rows_of(present_ensemble), rows_of(delayed_ensemble)
     spread, ratios = rows_of(spreading_coefficient), rows_of(transport_ratios)
-    sources = in_hbm((spread, ratios))
-    buffers, sems = landing(sources)
-    coefs = pl.pallas_call(
-        functools.partial(coefficient_kernel, chunks),
-        out_shape=shape_of((2, width)),
+    sources = in_hbm((present, spread, ratios, obs_row, obs_col, obs_field))
+    *held, packed, coefs = pl.pallas_call(
+        functools.partial(load_kernel, chunks),
+        out_shape=[shape_of(x.shape, x.dtype) for x in sources[1:]]
+        + [shape_of((present.shape[0] + 2 * chunks, LANES)), shape_of((2 * chunks, LANES))],
         in_specs=[hbm] * len(sources),
-        scratch_shapes=[*buffers, sems],
-        compiler_params=PARAMS,
-        name="coefficients",
+        scratch_shapes=[pltpu.SemaphoreType.DMA((len(sources),))],
+        compiler_params=PARAMS,
+        name="load",
     )(*sources)
     outer_coefs = lax.ppermute(coefs, "slab", outer_pairs)
-    inner_coefs = from_slab(coefs, 1)
-    sources = in_hbm((present, spread, ratios, obs_row, obs_col, obs_field))
-    buffers, sems = landing(sources)
+    inner = from_slab(packed, 1)
     part, here, taps, kinds, part_obs = pl.pallas_call(
         functools.partial(own_row_kernel, members, fields, chunks),
         out_shape=(
@@ -378,22 +415,20 @@
             shape_of((2, total), jnp.int32),
             shape_of((members, total)),
         ),
-        in_specs=[hbm] * len(sources),
-        scratch_shapes=[*buffers, sems],
         compiler_params=PARAMS,
         cost_estimate=estimate(OWN_FLOPS),
         name="own_row",
-    )(*sources)
+    )(packed, *held)
     others_delayed = from_partners(lax.optimization_barrier((delayed, coefs))[0])
     keep, send = pl.pallas_call(
-        functools.partial(observe_kernel, members, fields),
+        functools.partial(observe_kernel, members, fields, chunks),
         out_shape=(
             shape_of((members, total // 2)),
             shape_of((members, total // 2)),
         ),
         compiler_params=PARAMS,
         name="observe",
-    )(inner_coefs, outer_coefs, part_obs, here, taps, kinds)
+    )(inner, outer_coefs, part_obs, here, taps, kinds)
 
     def summed(terms, bit, flops):
         return pl.pallas_call(
@@ -405,16 +440,18 @@
         )(terms, from_slab(terms, bit))
 
     terms = keep + from_slab(send, 1)
-    here, _ = lax.optimization_barrier((here, terms))
-    outer_row = lax.ppermute(here, "slab", outer_pairs)
-    inner_row = from_slab(here, 1)
+    outer_row = lax.ppermute(
+        lax.optimization_barrier((here, terms))[0], "slab", outer_pairs
+    )
+    order = [1 << k for k in reversed(range(1, slabs.bit_length() - 1))]
+    for bit in order:
+        terms = summed(terms, bit, SUM_FLOPS)
     forecast = pl.pallas_call(
-        complete_kernel, out_shape=shape_of(stacked), compiler_params=PARAMS, name="complete"
-    )(part, inner_row, outer_row, coefs, others_delayed[0])
-    bit = slabs // 2
-    while bit > 1:
-        terms = summed(terms, bit, SUM_FLOPS)
-        bit //= 2
+        functools.partial(complete_kernel, members, fields, chunks),
+        out_shape=shape_of(stacked),
+        compiler_params=PARAMS,
+        name="complete",
+    )(part, inner, outer_row, coefs, others_delayed[0])
     priors = pl.pallas_call(
         gather_kernel,
         out_shape=shape_of((all_members, total // 2)),
@@ -423,20 +460,25 @@
         name="gather",
     )(terms, *from_partners(terms))
     priors = [priors, from_slab(priors, 1)]
-    sources = in_hbm((obs_value, obs_error, obs_noise))
-    buffers, sems = landing(sources)
     mine = pl.pallas_call(
         functools.partial(solve_kernel, parts),
         out_shape=shape_of((members, all_members)),
-        in_specs=[hbm] * len(sources) + [vmem] * 2,
-        scratch_shapes=[*buffers, pltpu.VMEM((all_members, total), F32), sems],
+        scratch_shapes=[
+            pltpu.VMEM((all_members, total), F32),
+            pltpu.VMEM((all_members, count), F32),
+        ],
         compiler_params=PARAMS,
         cost_estimate=estimate(SOLVE_FLOPS),
         name="solve",
-    )(*sources, *priors)
+    )(obs_value, obs_error, obs_noise, *priors)
     out = pl.pallas_call(
         functools.partial(combine_kernel, parts, fields),
-        out_shape=shape_of((members * planes, LANES)),
+        out_shape=shape_of((members, planes, LANES)),
+        out_specs=hbm,
+        scratch_shapes=[
+            pltpu.VMEM((members * planes, LANES), F32),
+            pltpu.SemaphoreType.DMA((1 + lagged,)),
+        ],
         compiler_params=PARAMS,
         name="combine",
     )(mine, forecast, *from_partners(forecast), delayed, *others_delayed)

time: 38.9 us -> 37 us (0.951)
  Pallas kernels: 9.64 us -> 7.45 us
  waiting for transfers between devices: 13 us -> 13.8 us
  starting transfers between devices: 15.9 us -> 15.4 us
    ppermute x7 -> x6, starting transfers between devices: 11 us -> 9.39 us  [from_slab(): return lax.ppermute(array, 'slab', [(i, i ^ bit) for i in range(slabs)])]
    pallas_call x1, Pallas kernels: 4.66 us -> 3.3 us  [shards(): pl.pallas_call(functools.partial(solve_kernel, parts), out_shape=shape_of...]
    ppermute x3, starting transfers between devices: 3.58 us -> 4.67 us  [from_partners(): lax.ppermute(array, 'mem', [((i + d) % parts, i) for i in range(parts)])]
    pallas_call x1, Pallas kernels: 1.67 us -> 0.66 us  [shards(): pl.pallas_call(functools.partial(own_row_kernel, members, fields, chunks)...]
    ppermute x7 -> x6, waiting for transfers between devices: 11.2 us -> 12.2 us  [from_slab(): return lax.ppermute(array, 'slab', [(i, i ^ bit) for i in range(slabs)])]
  transfers between devices with their start and end apart: 12 -> 11, of which waited for: 5 -> 6; matrix products, arithmetic and copies ran while one was open for 0% -> 0% of each run, Pallas kernels for 18% -> 13%
where the time goes in v5:
time: 37 us; the launch traced here: 36.8 us
  starting transfers between devices  15.4 us (42%)
  waiting for transfers between devices  13.8 us (37%)
  Pallas kernels  7.45 us (20%)
    ppermute x6, waiting for transfers between devices, from_slab(): return lax.ppermute(array, 'slab', [(i, i ^ bit) for i in range(slabs)])  12.2 us
    ppermute x6, starting transfers between devices, from_slab(): return lax.ppermute(array, 'slab', [(i, i ^ bit) for i in range(slabs)])  9.39 us
    ppermute x3, starting transfers between devices, from_partners(): lax.ppermute(array, 'mem', [((i + d) % parts, i) for i in range(parts)])  4.67 us
    pallas_call x1, Pallas kernels, shards(): pl.pallas_call(functools.partial(solve_kernel, parts), out_shape=shape_of...  3.3 us
    pallas_call x1, Pallas kernels, shards(): pl.pallas_call(functools.partial(combine_kernel, parts, fields), out_shap...  1.71 us
    ppermute x3, waiting for transfers between devices, from_partners(): lax.ppermute(array, 'mem', [((i + d) % parts, i) for i in range(parts)])  1.66 us
    pallas_call x1, Pallas kernels, shards(): pl.pallas_call(functools.partial(load_kernel, chunks), out_shape=[shape_o...  1.01 us
  transfers between devices with their start and end apart: 11, of which 6 were waited for; matrix products, arithmetic and copies ran while one was open for 0% of the time, Pallas kernels for 13%

profile of v5, /device:TPU:0, one launch (start us, length us, event | category | flops | bytes accessed | tf_op | source)
XLA Modules:
  0.0 36.8 jit_solution(12673909372154853966)
XLA Ops:
  0.0 1.0 %load.1 = (f32[4,128]{1,0:T(4,128)S(1)}, f32[8,128]{1,0:T(8,128)S(1)}, s32[2,256]{1,0:T(2,128)S(1)}, s32[2,256]{1,0:T(2,128)S(1)}, s32[2,256]{1,0:T(2,128)S(1)},...) custom-call(f32[512,128]{1,0:T(8,128)} %bitcast.7, f32[4,128]{1,0:T(4,128)} %bitcast.9, f32[8,128]{1,0:T(8,128)} %bitcast.8, ...), custom_call_target="tpu_custom_call" | custom-call | tf_op jit(solution)/shard_map/load/pallas_call | solution.py:398
  1.0 0.5 %collective-permute-start = (f32[520,128]{1,0:T(8,128)S(1)}, f32[520,128]{1,0:T(8,128)S(1)}, u32[]{:S(2)}, u32[]{:S(2)}) collective-permute-start(f32[520,128]{1,0:T(8,128)S(1)} %get-tuple-element.21.present_ref), channel_id=1, source_target_pairs={{0,2},{2,0},{4,6},{6,4},{8,10},{10,8},{12,14},{14,12},{16,18},{18,... | collective-permute-start | bytes 798728 | tf_op jit(solution)/shard_map/ppermute | solution.py:390
  1.5 0.6 %collective-permute-start.1 = (f32[8,128]{1,0:T(8,128)S(1)}, f32[8,128]{1,0:T(8,128)S(1)}, u32[]{:S(2)}, u32[]{:S(2)}) collective-permute-start(f32[8,128]{1,0:T(8,128)S(1)} %get-tuple-element.22.coefs_ref), channel_id=1, source_target_pairs={{2,4},{6,8},{10,12},{14,16},{18,20},{22,24},{26,28},{4,2},{8,6},{1... | collective-permute-start | bytes 12296 | tf_op jit(solution)/shard_map/ppermute | solution.py:407
  2.2 2.6 %collective-permute-start.9 = (f32[1024,128]{1,0:T(8,128)}, f32[1024,128]{1,0:T(8,128)S(1)}, u32[]{:S(2)}, u32[]{:S(2)}) collective-permute-start(f32[1024,128]{1,0:T(8,128)} %bitcast.5), channel_id=1, source_target_pairs={{1,0},{0,1},{3,2},{2,3},{5,4},{4,5},{7,6},{6,7},{9,8},{8,9},{11,10... | collective-permute-start | bytes 1572872 | tf_op jit(solution)/shard_map/ppermute | solution.py:385
  4.8 0.7 %own_row.1 = (f32[128,512]{1,0:T(8,128)S(1)}, f32[128,512]{1,0:T(8,128)S(1)}, bf16[512,512]{1,0:T(8,128)(2,1)S(1)}, s32[2,512]{1,0:T(2,128)S(1)}, f32[32,512]{1,0:T(8,128)S(1)}) custom-call(f32[520,128]{1,0:T(8,128)S(1)} %get-tuple-element.21.present_ref, f32[4,128]{1,0:T(4,128)S(1)} %get-tuple-element.23.spread_ref, ...), custom_call_target="tpu_custom_call" | custom-call | flops 99999997952 | tf_op jit(solution)/shard_map/own_row/pallas_call | solution.py:409
  5.5 0.6 %observe.1 = (f32[32,256]{1,0:T(8,128)S(1)}, f32[32,256]{1,0:T(8,128)S(1)}) custom-call(f32[520,128]{1,0:T(8,128)S(1)} %collective-permute-done.inner_ref, f32[8,128]{1,0:T(8,128)S(1)} %collective-permute-done.1.outer_ref, f32[32,512]{1,0:T(8,128)S(1)} %get-tuple-element.28.part_obs_ref, f32[128,512]{1,0:T(8,128)S(1)} %get-tuple-element.35.here_ref, ...), custom_call_target="tpu_custom_call" | custom-call | tf_op jit(solution)/shard_map/observe/pallas_call | solution.py:423
  6.1 2.7 %collective-permute-start.2 = (f32[32,256]{1,0:T(8,128)S(1)}, f32[32,256]{1,0:T(8,128)S(1)}, u32[]{:S(2)}, u32[]{:S(2)}) collective-permute-start(f32[32,256]{1,0:T(8,128)S(1)} %get-tuple-element.33), channel_id=1, source_target_pairs={{0,2},{2,0},{4,6},{6,4},{8,10},{10,8},{12,14},{14,12},{16,18},{18,... | collective-permute-start | bytes 98312 | tf_op jit(solution)/shard_map/ppermute | solution.py:390
  8.8 0.9 %collective-permute-done.2 = f32[32,256]{1,0:T(8,128)S(1)} collective-permute-done((f32[32,256]{1,0:T(8,128)S(1)}, f32[32,256]{1,0:T(8,128)S(1)}, u32[]{:S(2)}, u32[]{:S(2)}) %collective-permute-start.2) | collective-permute-done | bytes 32800 | tf_op jit(solution)/shard_map/ppermute | solution.py:390
  9.6 3.2 %collective-permute-start.3 = (f32[32,256]{1,0:T(8,128)S(1)}, f32[32,256]{1,0:T(8,128)S(1)}, u32[]{:S(2)}, u32[]{:S(2)}) collective-permute-start(f32[32,256]{1,0:T(8,128)S(1)} %add.3.terms_ref), channel_id=1, source_target_pairs={{0,16},{2,18},{4,20},{6,22},{8,24},{10,26},{12,28},{14,30},{16,0},... | collective-permute-start | bytes 98312 | tf_op jit(solution)/shard_map/ppermute | solution.py:390
  12.9 0.7 %collective-permute-start.8 = (f32[128,512]{1,0:T(8,128)S(1)}, f32[128,512]{1,0:T(8,128)S(1)}, u32[]{:S(2)}, u32[]{:S(2)}) collective-permute-start(f32[128,512]{1,0:T(8,128)S(1)} %get-tuple-element.35.here_ref), channel_id=1, source_target_pairs={{2,4},{6,8},{10,12},{14,16},{18,20},{22,24},{26,28},{4,2},{8,6},{1... | collective-permute-start | bytes 786440 | tf_op jit(solution)/shard_map/ppermute | solution.py:443
  13.5 1.2 %collective-permute-done.3.other_ref = f32[32,256]{1,0:T(8,128)S(1)} collective-permute-done((f32[32,256]{1,0:T(8,128)S(1)}, f32[32,256]{1,0:T(8,128)S(1)}, u32[]{:S(2)}, u32[]{:S(2)}) %collective-permute-start.3) | collective-permute-done | bytes 32800 | tf_op jit(solution)/shard_map/ppermute | solution.py:390
  14.8 2.9 %collective-permute-start.4 = (f32[32,256]{1,0:T(8,128)S(1)}, f32[32,256]{1,0:T(8,128)S(1)}, u32[]{:S(2)}, u32[]{:S(2)}) collective-permute-start(f32[32,256]{1,0:T(8,128)S(1)} %sum.3.terms_ref), channel_id=1, source_target_pairs={{0,8},{2,10},{4,12},{6,14},{8,0},{10,2},{12,4},{14,6},{16,24},{18,... | collective-permute-start | bytes 98312 | tf_op jit(solution)/shard_map/ppermute | solution.py:390
  17.6 4.9 %collective-permute-done.4.other_ref = f32[32,256]{1,0:T(8,128)S(1)} collective-permute-done((f32[32,256]{1,0:T(8,128)S(1)}, f32[32,256]{1,0:T(8,128)S(1)}, u32[]{:S(2)}, u32[]{:S(2)}) %collective-permute-start.4) | collective-permute-done | bytes 32800 | tf_op jit(solution)/shard_map/ppermute | solution.py:390
  22.6 3.9 %collective-permute-done.5.other_ref = f32[32,256]{1,0:T(8,128)S(1)} collective-permute-done((f32[32,256]{1,0:T(8,128)S(1)}, f32[32,256]{1,0:T(8,128)S(1)}, u32[]{:S(2)}, u32[]{:S(2)}) %collective-permute-start.5) | collective-permute-done | bytes 32800 | tf_op jit(solution)/shard_map/ppermute | solution.py:390
  26.5 1.5 %collective-permute-start.6 = (f32[32,256]{1,0:T(8,128)S(1)}, f32[32,256]{1,0:T(8,128)S(1)}, u32[]{:S(2)}, u32[]{:S(2)}) collective-permute-start(f32[32,256]{1,0:T(8,128)S(1)} %sum.5.refs_0_), channel_id=1, source_target_pairs={{1,0},{0,1},{3,2},{2,3},{5,4},{4,5},{7,6},{6,7},{9,8},{8,9},{11,10... | collective-permute-start | bytes 98312 | tf_op jit(solution)/shard_map/ppermute | solution.py:385
  28.0 0.1 complete.1.refs_0_
  28.2 0.0 copy-start.2
  28.2 0.6 %collective-permute-start.10 = (f32[128,512]{1,0:T(8,128)S(1)}, f32[128,512]{1,0:T(8,128)S(1)}, u32[]{:S(2)}, u32[]{:S(2)}) collective-permute-start(f32[128,512]{1,0:T(8,128)S(1)} %complete.1.refs_0_), channel_id=1, source_target_pairs={{1,0},{0,1},{3,2},{2,3},{5,4},{4,5},{7,6},{6,7},{9,8},{8,9},{11,10... | collective-permute-start | bytes 786440 | tf_op jit(solution)/shard_map/ppermute | solution.py:385
  28.8 1.7 %collective-permute-done.6.refs_1_ = f32[32,256]{1,0:T(8,128)S(1)} collective-permute-done((f32[32,256]{1,0:T(8,128)S(1)}, f32[32,256]{1,0:T(8,128)S(1)}, u32[]{:S(2)}, u32[]{:S(2)}) %collective-permute-start.6) | collective-permute-done | bytes 32800 | tf_op jit(solution)/shard_map/ppermute | solution.py:385
  30.4 0.1 collective-permute-start.7
  30.5 1.2 %collective-permute-done.7.received_ref = f32[64,256]{1,0:T(8,128)S(1)} collective-permute-done((f32[64,256]{1,0:T(8,128)S(1)}, f32[64,256]{1,0:T(8,128)S(1)}, u32[]{:S(2)}, u32[]{:S(2)}) %collective-permute-start.7) | collective-permute-done | bytes 65568 | tf_op jit(solution)/shard_map/ppermute | solution.py:390
  31.8 3.3 %solve.1.mine_ref = f32[32,64]{1,0:T(8,128)S(1)} custom-call(f32[2,256]{1,0:T(2,128)S(1)} %copy-done.2, f32[2,256]{1,0:T(2,128)S(1)} %copy-done.3, f32[2,64,256]{2,1,0:T(8,128)S(1)} %copy-done.1, f32[64,256]{1,0:T(8,128)S(1)} %gather.1.kept_ref, f32[64,256]{1,0:T(8,128)S(1)} %collective-permute-done.7.received_ref), custom_call_target="tpu_custom_call" | custom-call | flops 2000000000 | tf_op jit(solution)/shard_map/solve/pallas_call | solution.py:463
  35.1 0.0 copy-done
  35.1 1.7 %combine.1 = f32[32,48,128]{2,1,0:T(8,128)} custom-call(f32[32,64]{1,0:T(8,128)S(1)} %solve.1.mine_ref, f32[128,512]{1,0:T(8,128)S(1)} %complete.1.refs_0_, f32[128,512]{1,0:T(8,128)S(1)} %collective-permute-done.10.refs_1_, f32[1024,128]{1,0:T(8,128)S(1)} %bitcast.6, f32[1024,128]{1,0:T(8,128)S(1)} %collective-permute-done.9._.refs_3_), custom_call_target="tpu_custom_call" | custom-call | tf_op jit(solution)/shard_map/combine/pallas_call | solution.py:474
  (17 shorter events, 0.1 us)
Async XLA Ops:
  1.0 4.4 %collective-permute-start = (f32[520,128]{1,0:T(8,128)S(1)}, f32[520,128]{1,0:T(8,128)S(1)}, u32[]{:S(2)}, u32[]{:S(2)}) collective-permute-start(f32[520,128]{1,0:T(8,128)S(1)} %get-tuple-element.21.present_ref), channel_id=1, source_target_pairs={{0,2},{2,0},{4,6},{6,4},{8,10},{10,8},{12,14},{14,12},{16,18},{18,... | collective-permute-start | bytes 798728 | tf_op jit(solution)/shard_map/ppermute | solution.py:390
  1.5 3.9 %collective-permute-start.1 = (f32[8,128]{1,0:T(8,128)S(1)}, f32[8,128]{1,0:T(8,128)S(1)}, u32[]{:S(2)}, u32[]{:S(2)}) collective-permute-start(f32[8,128]{1,0:T(8,128)S(1)} %get-tuple-element.22.coefs_ref), channel_id=1, source_target_pairs={{2,4},{6,8},{10,12},{14,16},{18,20},{22,24},{26,28},{4,2},{8,6},{1... | collective-permute-start | bytes 12296 | tf_op jit(solution)/shard_map/ppermute | solution.py:407
  2.2 25.8 %collective-permute-start.9 = (f32[1024,128]{1,0:T(8,128)}, f32[1024,128]{1,0:T(8,128)S(1)}, u32[]{:S(2)}, u32[]{:S(2)}) collective-permute-start(f32[1024,128]{1,0:T(8,128)} %bitcast.5), channel_id=1, source_target_pairs={{1,0},{0,1},{3,2},{2,3},{5,4},{4,5},{7,6},{6,7},{9,8},{8,9},{11,10... | collective-permute-start | bytes 1572872 | tf_op jit(solution)/shard_map/ppermute | solution.py:385
  6.1 3.5 %collective-permute-start.2 = (f32[32,256]{1,0:T(8,128)S(1)}, f32[32,256]{1,0:T(8,128)S(1)}, u32[]{:S(2)}, u32[]{:S(2)}) collective-permute-start(f32[32,256]{1,0:T(8,128)S(1)} %get-tuple-element.33), channel_id=1, source_target_pairs={{0,2},{2,0},{4,6},{6,4},{8,10},{10,8},{12,14},{14,12},{16,18},{18,... | collective-permute-start | bytes 98312 | tf_op jit(solution)/shard_map/ppermute | solution.py:390
  9.6 5.1 %collective-permute-start.3 = (f32[32,256]{1,0:T(8,128)S(1)}, f32[32,256]{1,0:T(8,128)S(1)}, u32[]{:S(2)}, u32[]{:S(2)}) collective-permute-start(f32[32,256]{1,0:T(8,128)S(1)} %add.3.terms_ref), channel_id=1, source_target_pairs={{0,16},{2,18},{4,20},{6,22},{8,24},{10,26},{12,28},{14,30},{16,0},... | collective-permute-start | bytes 98312 | tf_op jit(solution)/shard_map/ppermute | solution.py:390
  12.9 15.2 %collective-permute-start.8 = (f32[128,512]{1,0:T(8,128)S(1)}, f32[128,512]{1,0:T(8,128)S(1)}, u32[]{:S(2)}, u32[]{:S(2)}) collective-permute-start(f32[128,512]{1,0:T(8,128)S(1)} %get-tuple-element.35.here_ref), channel_id=1, source_target_pairs={{2,4},{6,8},{10,12},{14,16},{18,20},{22,24},{26,28},{4,2},{8,6},{1... | collective-permute-start | bytes 786440 | tf_op jit(solution)/shard_map/ppermute | solution.py:443
  14.8 7.8 %collective-permute-start.4 = (f32[32,256]{1,0:T(8,128)S(1)}, f32[32,256]{1,0:T(8,128)S(1)}, u32[]{:S(2)}, u32[]{:S(2)}) collective-permute-start(f32[32,256]{1,0:T(8,128)S(1)} %sum.3.terms_ref), channel_id=1, source_target_pairs={{0,8},{2,10},{4,12},{6,14},{8,0},{10,2},{12,4},{14,6},{16,24},{18,... | collective-permute-start | bytes 98312 | tf_op jit(solution)/shard_map/ppermute | solution.py:390
  22.6 3.9 %collective-permute-start.5 = (f32[32,256]{1,0:T(8,128)S(1)}, f32[32,256]{1,0:T(8,128)S(1)}, u32[]{:S(2)}, u32[]{:S(2)}) collective-permute-start(f32[32,256]{1,0:T(8,128)S(1)} %sum.4.terms_ref), channel_id=1, source_target_pairs={{0,4},{2,6},{4,0},{6,2},{8,12},{10,14},{12,8},{14,10},{16,20},{18,... | collective-permute-start | bytes 98312 | tf_op jit(solution)/shard_map/ppermute | solution.py:390
  26.5 3.9 %collective-permute-start.6 = (f32[32,256]{1,0:T(8,128)S(1)}, f32[32,256]{1,0:T(8,128)S(1)}, u32[]{:S(2)}, u32[]{:S(2)}) collective-permute-start(f32[32,256]{1,0:T(8,128)S(1)} %sum.5.refs_0_), channel_id=1, source_target_pairs={{1,0},{0,1},{3,2},{2,3},{5,4},{4,5},{7,6},{6,7},{9,8},{8,9},{11,10... | collective-permute-start | bytes 98312 | tf_op jit(solution)/shard_map/ppermute | solution.py:385
  28.1 3.6 %copy-start.1 = (f32[2,64,256]{2,1,0:T(8,128)S(1)}, f32[2,64,256]{2,1,0:T(8,128)}, u32[]{:S(2)}) copy-start(f32[2,64,256]{2,1,0:T(8,128)} %noise_ref.1) | copy-start | bytes 393220
  28.2 3.6 %copy-start.2 = (f32[2,256]{1,0:T(2,128)S(1)}, f32[2,256]{1,0:T(2,128)}, u32[]{:S(2)}) copy-start(f32[2,256]{1,0:T(2,128)} %value_ref.1) | copy-start | bytes 6148
  28.2 3.6 %copy-start.3 = (f32[2,256]{1,0:T(2,128)S(1)}, f32[2,256]{1,0:T(2,128)}, u32[]{:S(2)}) copy-start(f32[2,256]{1,0:T(2,128)} %error_ref.1) | copy-start | bytes 6148
  28.2 6.9 %collective-permute-start.10 = (f32[128,512]{1,0:T(8,128)S(1)}, f32[128,512]{1,0:T(8,128)S(1)}, u32[]{:S(2)}, u32[]{:S(2)}) collective-permute-start(f32[128,512]{1,0:T(8,128)S(1)} %complete.1.refs_0_), channel_id=1, source_target_pairs={{1,0},{0,1},{3,2},{2,3},{5,4},{4,5},{7,6},{6,7},{9,8},{8,9},{11,10... | collective-permute-start | bytes 786440 | tf_op jit(solution)/shard_map/ppermute | solution.py:385
  30.4 4.7 %copy-start = (f32[32,2,4,1,512]{4,3,2,1,0:T(1,128)S(1)}, f32[32,2,4,1,512]{4,3,2,1,0:T(1,128)}, u32[]{:S(2)}) copy-start(f32[32,2,4,1,512]{4,3,2,1,0:T(1,128)} %param.11) | copy-start | bytes 1572868
  30.4 1.3 %collective-permute-start.7 = (f32[64,256]{1,0:T(8,128)S(1)}, f32[64,256]{1,0:T(8,128)S(1)}, u32[]{:S(2)}, u32[]{:S(2)}) collective-permute-start(f32[64,256]{1,0:T(8,128)S(1)} %gather.1.kept_ref), channel_id=1, source_target_pairs={{0,2},{2,0},{4,6},{6,4},{8,10},{10,8},{12,14},{14,12},{16,18},{18,... | collective-permute-start | bytes 196616 | tf_op jit(solution)/shard_map/ppermute | solution.py:390

commit v6 on v5

--- a/solution.py
+++ b/solution.py
@@ -11,10 +11,11 @@
 F32 = jnp.float32
 BF16 = jnp.bfloat16
 HIGHEST = lax.Precision.HIGHEST
-PARAMS = pltpu.CompilerParams(vmem_limit_bytes=48 * 1024 * 1024)
-
-
-OWN_FLOPS, SUM_FLOPS, GATHER_FLOPS, SOLVE_FLOPS = 10**11, 7*10**8, 10**9, 2*10**9
+PARAMS = pltpu.CompilerParams(vmem_limit_bytes=16 * 1024 * 1024)
+
+
+SELECT_FLOPS = 1
+OWN_FLOPS, SUM_FLOPS, GATHER_FLOPS, SOLVE_FLOPS = 1, 10**8, 1, 10**9
 
 
 def estimate(flops):
@@ -85,63 +86,74 @@
 
 
 def load_kernel(chunks, *refs):
-    count = (len(refs) - 2) // 2
-    sources, held, packed_ref, coefs_ref, sems = refs[:count], refs[count:-3], *refs[-3:]
+    count = (len(refs) - 1) // 2
+    sources, packed_ref, held, sems = refs[:count], refs[count], refs[count + 1 : -1], refs[-1]
     rows = sources[0].shape[0]
     copies = at_once(sources, (packed_ref.at[:rows], *held), sems)
     copies[1].wait()
     copies[2].wait()
     spread = held[0][...]
     half = held[1][:chunks, :] * 0.5
-    for ref, start in ((packed_ref, rows), (coefs_ref, 0)):
-        ref[start : start + chunks, :] = spread + half
-        ref[start + chunks : start + 2 * chunks, :] = spread - half
+    packed_ref[rows : rows + chunks, :] = spread + half
+    packed_ref[rows + chunks : rows + 2 * chunks, :] = spread - half
     for copy in (copies[0], *copies[3:]):
         copy.wait()
+
+
+def weights(packed_ref, chunks):
+    rows = packed_ref.shape[0] - 2 * chunks
+    return line(packed_ref, rows, chunks), line(packed_ref, rows + chunks, chunks)
+
+
+def selector_kernel(row_ref, col_ref, field_ref, taps_ref, kinds_ref):
+    batches, count = row_ref.shape
+    shape = taps_ref.shape
+    flat = lambda ref: jnp.concatenate([ref[b : b + 1, :] for b in range(batches)], axis=1)
+    rows, cols, kinds = flat(row_ref), flat(col_ref), flat(field_ref)
+    own_row = lax.axis_index("slab")
+    for k, row in enumerate((own_row, own_row - 1)):
+        kinds_ref[k : k + 1, :] = jnp.where(rows == row, kinds, -1)
+    at = lax.broadcasted_iota(jnp.int32, shape, 0).astype(F32) * 0.25
+    taps_ref[...] = jnp.maximum(0.5 - jnp.abs(at - cols.astype(F32) * 0.25), 0.0).astype(BF16)
 
 
 def own_row_kernel(
     members,
     fields,
     chunks,
-    present_ref,
+    packed_ref,
+    inner_ref,
     spread_ref,
     ratio_ref,
-    row_ref,
-    col_ref,
-    field_ref,
+    taps_ref,
+    kinds_ref,
     part_ref,
     here_ref,
-    taps_ref,
-    kinds_ref,
     obs_ref,
 ):
     width = chunks * LANES
     spread = line(spread_ref, 0, chunks)
     along_columns = line(ratio_ref, chunks, chunks)
-    here = stacked_planes(present_ref, members, fields, chunks)
+    here = stacked_planes(packed_ref, members, fields, chunks)
     here_ref[...] = here
     lane = lax.broadcasted_iota(jnp.int32, here.shape, 1)
     left = jnp.where(lane == 0, 0.0, pltpu.roll(here, 1, 1))
     right = jnp.where(lane == width - 1, 0.0, pltpu.roll(here, width - 1, 1))
-    part = here + spread * (right + left - 4.0 * here) - along_columns * (right - left) * 0.5
+    even = lax.rem(lax.axis_index("slab"), 2) == 0
+    above, below = weights(packed_ref, chunks)
+    part = (
+        here
+        + spread * (right + left - 4.0 * here)
+        - along_columns * (right - left) * 0.5
+        + jnp.where(even, below, above) * stacked_planes(inner_ref, members, fields, chunks)
+    )
     part_ref[...] = part
-
-    batches, count = row_ref.shape
-    total = batches * count
-    flat = lambda ref: jnp.concatenate([ref[b : b + 1, :] for b in range(batches)], axis=1)
-    rows, cols, kinds = flat(row_ref), flat(col_ref), flat(field_ref)
-    own_row = lax.axis_index("slab")
-    seen = jnp.where(rows == own_row, kinds, -1)
-    kinds_ref[0:1, :] = jnp.where(rows == own_row + 1, kinds, -1)
-    kinds_ref[1:2, :] = jnp.where(rows == own_row - 1, kinds, -1)
-    at = lax.broadcasted_iota(jnp.int32, (width, total), 0).astype(F32) * 0.25
-    taps = jnp.maximum(0.5 - jnp.abs(at - cols.astype(F32) * 0.25), 0.0).astype(BF16)
-    taps_ref[...] = taps
-    picked = picked_values(part, taps)
-    observed = jnp.zeros((members, total), F32)
+    picked = picked_values(part, taps_ref[...])
+    observed = jnp.zeros(obs_ref.shape, F32)
     for f in range(fields):
-        observed += jnp.where(seen == f, picked[f * members : (f + 1) * members], 0.0)
+        observed += jnp.where(
+            kinds_ref[0:1, :] == f, picked[f * members : (f + 1) * members], 0.0
+        )
     obs_ref[...] = observed
 
 
@@ -149,56 +161,45 @@
     members,
     fields,
     chunks,
-    inner_ref,
+    packed_ref,
     outer_ref,
+    part_ref,
     part_obs_ref,
     here_ref,
     taps_ref,
     kinds_ref,
-    keep_ref,
-    send_ref,
+    obs_ref,
+    partial_ref,
 ):
-    even = lax.rem(lax.axis_index("slab"), 2) == 0
-    here = here_ref[...]
-    rows = members * fields * chunks
-    inner_coefs = [line(inner_ref, rows + k * chunks, chunks) for k in range(2)]
-    outer_coefs = [line(outer_ref, k * chunks, chunks) for k in range(2)]
-    below = jnp.where(even, inner_coefs[0], outer_coefs[0])
-    above = jnp.where(even, outer_coefs[1], inner_coefs[1])
-    picked = picked_values(
-        jnp.concatenate([below * here, above * here], axis=0), taps_ref[...]
-    )
+    above, _ = weights(packed_ref, chunks)
+    _, below_of_above = weights(outer_ref, chunks)
+    taken = above * stacked_planes(outer_ref, members, fields, chunks)
+    given = below_of_above * here_ref[...]
+    partial_ref[...] = part_ref[...] + taken
+    picked = picked_values(jnp.concatenate([taken, given], axis=0), taps_ref[...])
     observed = part_obs_ref[...]
     for side in range(2):
         kinds = kinds_ref[side : side + 1, :]
         for f in range(fields):
             start = (side * fields + f) * members
             observed += jnp.where(kinds == f, picked[start : start + members], 0.0)
-    half = observed.shape[1] // 2
-    first, second = observed[:, :half], observed[:, half:]
-    keep_ref[...] = jnp.where(even, first, second)
-    send_ref[...] = jnp.where(even, second, first)
-
-
-def sum_kernel(terms_ref, other_ref, sum_ref):
-    sum_ref[...] = terms_ref[...] + other_ref[...]
-
-
-def complete_kernel(
-    members, fields, chunks, part_ref, inner_ref, outer_ref, coefs_ref, _, forecast_ref
-):
-    even = lax.rem(lax.axis_index("slab"), 2) == 0
-    above, below = line(coefs_ref, 0, chunks), line(coefs_ref, chunks, chunks)
-    forecast_ref[...] = (
-        part_ref[...]
-        + jnp.where(even, below, above) * stacked_planes(inner_ref, members, fields, chunks)
-        + jnp.where(even, above, below) * outer_ref[...]
+    obs_ref[...] = observed
+
+
+def sum_kernel(terms_ref, other_ref, *refs):
+    refs[-1][...] = terms_ref[...] + other_ref[...]
+
+
+def complete_kernel(members, fields, chunks, partial_ref, outer_ref, packed_ref, forecast_ref):
+    _, below = weights(packed_ref, chunks)
+    forecast_ref[...] = partial_ref[...] + below * stacked_planes(
+        outer_ref, members, fields, chunks
     )
 
 
 def gather_kernel(*refs):
-    local = refs[0].shape[0]
-    for d, ref in enumerate(refs[:-1]):
+    local = refs[1].shape[0]
+    for d, ref in enumerate(refs[1:-1]):
         refs[-1][d * local : (d + 1) * local, :] = ref[...]
 
 
@@ -248,14 +249,12 @@
     own = lax.axis_index("mem")
     own_rows = pl.ds(pl.multiple_of(own * local, local), local)
     even = lax.rem(lax.axis_index("slab"), 2) == 0
-    half = batches * count // 2
     for d in range(parts):
         owner = lax.rem(own + d, parts)
-        rows = pl.ds(pl.multiple_of(owner * local, local), local)
-        kept = kept_ref[d * local : (d + 1) * local, :]
-        received = received_ref[d * local : (d + 1) * local, :]
-        prior[rows, :half] = jnp.where(even, kept, received)
-        prior[rows, half:] = jnp.where(even, received, kept)
+        block = slice(d * local, (d + 1) * local)
+        prior[pl.ds(pl.multiple_of(owner * local, local), local), :] = jnp.where(
+            even, received_ref[block, :], kept_ref[block, :]
+        )
     source = lax.broadcasted_iota(jnp.int32, (members, members), 0)
     target = lax.broadcasted_iota(jnp.int32, (members, members), 1)
     turn = (source == lax.rem(target + own * local, members)).astype(F32)
@@ -379,87 +378,90 @@
     planes = (1 + lagged) * fields * chunks
     stacked = (fields * members, width)
     hbm = pl.BlockSpec(memory_space=pltpu.HBM)
-
-    def from_partners(array):
+    sizes = (members, fields, chunks)
+
+    odd = range(1, slabs, 2)
+
+    def among_odd(array, bit):
+        return lax.ppermute(array, "slab", [(i, i ^ bit) for i in odd])
+
+    def from_partners(array, among):
         return [
-            lax.ppermute(array, "mem", [((i + d) % parts, i) for i in range(parts)])
+            lax.ppermute(
+                array,
+                ("slab", "mem"),
+                [(i * parts + (j + d) % parts, i * parts + j) for i in among for j in range(parts)],
+            )
             for d in range(1, parts)
         ]
-
-    def from_slab(array, bit):
-        return lax.ppermute(array, "slab", [(i, i ^ bit) for i in range(slabs)])
-
-    outer_pairs = [(i, i + 1) for i in range(1, slabs - 1, 2)]
-    outer_pairs += [(j, i) for i, j in outer_pairs]
 
     present, delayed = rows_of(present_ensemble), rows_of(delayed_ensemble)
     spread, ratios = rows_of(spreading_coefficient), rows_of(transport_ratios)
     sources = in_hbm((present, spread, ratios, obs_row, obs_col, obs_field))
-    *held, packed, coefs = pl.pallas_call(
+    packed, *held = pl.pallas_call(
         functools.partial(load_kernel, chunks),
-        out_shape=[shape_of(x.shape, x.dtype) for x in sources[1:]]
-        + [shape_of((present.shape[0] + 2 * chunks, LANES)), shape_of((2 * chunks, LANES))],
+        out_shape=[shape_of((present.shape[0] + 2 * chunks, LANES))]
+        + [shape_of(x.shape, x.dtype) for x in sources[1:]],
         in_specs=[hbm] * len(sources),
         scratch_shapes=[pltpu.SemaphoreType.DMA((len(sources),))],
         compiler_params=PARAMS,
         name="load",
     )(*sources)
-    outer_coefs = lax.ppermute(coefs, "slab", outer_pairs)
-    inner = from_slab(packed, 1)
-    part, here, taps, kinds, part_obs = pl.pallas_call(
-        functools.partial(own_row_kernel, members, fields, chunks),
-        out_shape=(
-            shape_of(stacked),
-            shape_of(stacked),
-            shape_of((width, total), BF16),
-            shape_of((2, total), jnp.int32),
-            shape_of((members, total)),
-        ),
+    outer_above = lax.ppermute(packed, "slab", [(i, i + 1) for i in odd[:-1]])
+    inner = lax.ppermute(packed, "slab", [(i, i ^ 1) for i in range(slabs)])
+    others_delayed = from_partners(
+        lax.optimization_barrier((in_hbm([delayed])[0], packed))[0], range(slabs)
+    )
+    outer_below = lax.ppermute(packed, "slab", [(i + 1, i) for i in odd[:-1]])
+    taps, kinds = pl.pallas_call(
+        selector_kernel,
+        out_shape=(shape_of((width, total), BF16), shape_of((2, total), jnp.int32)),
+        compiler_params=PARAMS,
+        cost_estimate=estimate(SELECT_FLOPS),
+        name="selector",
+    )(*held[2:])
+    part, here, part_obs = pl.pallas_call(
+        functools.partial(own_row_kernel, *sizes),
+        out_shape=(shape_of(stacked), shape_of(stacked), shape_of((members, total))),
         compiler_params=PARAMS,
         cost_estimate=estimate(OWN_FLOPS),
         name="own_row",
-    )(packed, *held)
-    others_delayed = from_partners(lax.optimization_barrier((delayed, coefs))[0])
-    keep, send = pl.pallas_call(
-        functools.partial(observe_kernel, members, fields, chunks),
-        out_shape=(
-            shape_of((members, total // 2)),
-            shape_of((members, total // 2)),
-        ),
+    )(packed, inner, *held[:2], taps, kinds)
+    terms, partial = pl.pallas_call(
+        functools.partial(observe_kernel, *sizes),
+        out_shape=(shape_of((members, total)), shape_of(stacked)),
         compiler_params=PARAMS,
         name="observe",
-    )(inner, outer_coefs, part_obs, here, taps, kinds)
-
-    def summed(terms, bit, flops):
+    )(packed, outer_above, part, part_obs, here, taps, kinds)
+    def summed(terms, other, flops, *arrived):
         return pl.pallas_call(
             sum_kernel,
             out_shape=shape_of(terms.shape),
             cost_estimate=estimate(flops),
             compiler_params=PARAMS,
             name="sum",
-        )(terms, from_slab(terms, bit))
-
-    terms = keep + from_slab(send, 1)
-    outer_row = lax.ppermute(
-        lax.optimization_barrier((here, terms))[0], "slab", outer_pairs
-    )
-    order = [1 << k for k in reversed(range(1, slabs.bit_length() - 1))]
-    for bit in order:
-        terms = summed(terms, bit, SUM_FLOPS)
+        )(terms, other, *arrived)
+
+    terms = summed(terms, lax.ppermute(terms, "slab", [(i - 1, i) for i in odd]), 1)
+    for bit in [1 << k for k in reversed(range(1, slabs.bit_length() - 1))]:
+        terms = summed(
+            terms, among_odd(terms, bit), SUM_FLOPS, *([outer_below] if bit == 4 else [])
+        )
     forecast = pl.pallas_call(
-        functools.partial(complete_kernel, members, fields, chunks),
+        functools.partial(complete_kernel, *sizes),
         out_shape=shape_of(stacked),
         compiler_params=PARAMS,
         name="complete",
-    )(part, inner, outer_row, coefs, others_delayed[0])
-    priors = pl.pallas_call(
+    )(lax.optimization_barrier((partial, terms))[0], outer_below, packed)
+
+    prior = pl.pallas_call(
         gather_kernel,
-        out_shape=shape_of((all_members, total // 2)),
+        out_shape=shape_of((all_members, total)),
         cost_estimate=estimate(GATHER_FLOPS),
         compiler_params=PARAMS,
         name="gather",
-    )(terms, *from_partners(terms))
-    priors = [priors, from_slab(priors, 1)]
+    )(others_delayed[0], terms, *from_partners(terms, odd))
+    received = lax.ppermute(prior, "slab", [(i, i - 1) for i in odd])
     mine = pl.pallas_call(
         functools.partial(solve_kernel, parts),
         out_shape=shape_of((members, all_members)),
@@ -470,7 +472,7 @@
         compiler_params=PARAMS,
         cost_estimate=estimate(SOLVE_FLOPS),
         name="solve",
-    )(obs_value, obs_error, obs_noise, *priors)
+    )(obs_value, obs_error, obs_noise, prior, received)
     out = pl.pallas_call(
         functools.partial(combine_kernel, parts, fields),
         out_shape=shape_of((members, planes, LANES)),
@@ -481,7 +483,7 @@
         ],
         compiler_params=PARAMS,
         name="combine",
-    )(mine, forecast, *from_partners(forecast), delayed, *others_delayed)
+    )(mine, forecast, *from_partners(forecast, range(slabs)), delayed, *others_delayed)
     return out.reshape(members, 1 + lagged, fields, height, width)
 
 

time: 37 us -> 45.1 us (1.22)
  waiting for transfers between devices: 13.8 us -> 18.8 us
  Pallas kernels: 7.45 us -> 9.7 us
  local copies, waits for them, and re-layouts: 0.03 us -> 0.83 us
    ppermute x11, waiting for transfers between devices: 13.8 us -> 18.8 us  [the longest x1 17.9 us: shards(): received = lax.ppermute(prior, 'slab', [(i, i - 1) for i in odd])]
    pallas_call x4 -> x5, Pallas kernels: 1.41 us -> 2.58 us  [the longest x1 1.05 us: shards(): pl.pallas_call(gather_kernel, out_shape=shape_of((all_members, total)), c...]
    pallas_call x1, Pallas kernels: 1.71 us -> 2.76 us  [shards(): pl.pallas_call(functools.partial(combine_kernel, parts, fields), out_shap...]
    unnamed x8 -> x10, local copies, waits for them, and re-layouts: 0.03 us -> 0.83 us
  transfers between devices with their start and end apart: 11 -> 11, of which waited for: 6 -> 2; matrix products, arithmetic and copies ran while one was open for 0% -> 0% of each run, Pallas kernels for 13% -> 13%
where the time goes in v6:
time: 45.1 us; the launch traced here: 44.7 us
  waiting for transfers between devices  18.8 us (42%)
  starting transfers between devices  15.1 us (33%)
  Pallas kernels  9.7 us (22%)
  local copies, waits for them, and re-layouts  0.83 us (2%)
    ppermute x1, waiting for transfers between devices, shards(): received = lax.ppermute(prior, 'slab', [(i, i - 1) for i in odd])  17.9 us
    ppermute x1, starting transfers between devices, shards(): lax.ppermute(terms, 'slab', [(i - 1, i) for i in odd])  5.12 us
    ppermute x3, starting transfers between devices, from_partners(): lax.ppermute(array, ('slab', 'mem'), [(i * parts + (j + d) % parts, i * p...  4.72 us
    pallas_call x1, Pallas kernels, shards(): pl.pallas_call(functools.partial(solve_kernel, parts), out_shape=shape_of...  3.31 us
    pallas_call x1, Pallas kernels, shards(): pl.pallas_call(functools.partial(combine_kernel, parts, fields), out_shap...  2.76 us
    ppermute x3, starting transfers between devices, among_odd(): return lax.ppermute(array, 'slab', [(i, i ^ bit) for i in odd])  1.99 us
    ppermute x1, starting transfers between devices, shards(): received = lax.ppermute(prior, 'slab', [(i, i - 1) for i in odd])  1.42 us
    pallas_call x1, Pallas kernels, shards(): pl.pallas_call(gather_kernel, out_shape=shape_of((all_members, total)), c...  1.05 us
  transfers between devices with their start and end apart: 11, of which 2 were waited for; matrix products, arithmetic and copies ran while one was open for 0% of the time, Pallas kernels for 13%

profile of v6, /device:TPU:0, one launch (start us, length us, event | category | flops | bytes accessed | tf_op | source)
XLA Modules:
  0.0 44.7 jit_solution(11993958566787499005)
XLA Ops:
  0.0 1.0 %load.1 = (f32[520,128]{1,0:T(8,128)S(1)}, f32[4,128]{1,0:T(4,128)S(1)}, f32[8,128]{1,0:T(8,128)S(1)}, s32[2,256]{1,0:T(2,128)S(1)}, s32[2,256]{1,0:T(2,128)S(1)}, /*index=5*/s32[2,256]{1,0:T(2,128)S(1)}) custom-call(f32[512,128]{1,0:T(8,128)} %bitcast.7, f32[4,128]{1,0:T(4,128)} %bitcast.9, f32[8,128]{1,0:T(8,128)} %bitcast.8, s32[2,256]{1,0:T(2,128)} %refs_3_.1, ...), custom_call_target="tpu_custom_call" | custom-call | tf_op jit(solution)/shard_map/load/pallas_call | solution.py:401
  1.0 0.5 %collective-permute-start.2 = (f32[520,128]{1,0:T(8,128)S(1)}, f32[520,128]{1,0:T(8,128)S(1)}, u32[]{:S(2)}, u32[]{:S(2)}) collective-permute-start(f32[520,128]{1,0:T(8,128)S(1)} %get-tuple-element.20.packed_ref), channel_id=1, source_target_pairs={{0,2},{2,0},{4,6},{6,4},{8,10},{10,8},{12,14},{14,12},{16,18},{18,... | collective-permute-start | bytes 798728 | tf_op jit(solution)/shard_map/ppermute | solution.py:411
  1.5 0.7 %collective-permute-start.1 = (f32[520,128]{1,0:T(8,128)S(1)}, f32[520,128]{1,0:T(8,128)S(1)}, u32[]{:S(2)}, u32[]{:S(2)}) collective-permute-start(f32[520,128]{1,0:T(8,128)S(1)} %get-tuple-element.20.packed_ref), channel_id=1, source_target_pairs={{2,4},{6,8},{10,12},{14,16},{18,20},{22,24},{26,28},{3,5},{7,9},{1... | collective-permute-start | bytes 798728 | tf_op jit(solution)/shard_map/ppermute | solution.py:410
  2.2 2.6 %collective-permute-start = (f32[1024,128]{1,0:T(8,128)}, f32[1024,128]{1,0:T(8,128)S(1)}, u32[]{:S(2)}, u32[]{:S(2)}) collective-permute-start(f32[1024,128]{1,0:T(8,128)} %bitcast.5), channel_id=1, source_target_pairs={{1,0},{0,1},{3,2},{2,3},{5,4},{4,5},{7,6},{6,7},{9,8},{8,9},{11,10... | collective-permute-start | bytes 1572872 | tf_op jit(solution)/shard_map/ppermute | solution.py:390
  4.8 0.7 %collective-permute-start.6 = (f32[520,128]{1,0:T(8,128)S(1)}, f32[520,128]{1,0:T(8,128)S(1)}, u32[]{:S(2)}, u32[]{:S(2)}) collective-permute-start(f32[520,128]{1,0:T(8,128)S(1)} %get-tuple-element.20.packed_ref), channel_id=1, source_target_pairs={{4,2},{8,6},{12,10},{16,14},{20,18},{24,22},{28,26},{5,3},{9,7},{1... | collective-permute-start | bytes 798728 | tf_op jit(solution)/shard_map/ppermute | solution.py:415
  5.5 0.2 selector.1
  5.7 0.6 %own_row.1 = (f32[128,512]{1,0:T(8,128)S(1)}, f32[128,512]{1,0:T(8,128)S(1)}, f32[32,512]{1,0:T(8,128)S(1)}) custom-call(f32[520,128]{1,0:T(8,128)S(1)} %get-tuple-element.20.packed_ref, f32[520,128]{1,0:T(8,128)S(1)} %collective-permute-done.2.inner_ref, f32[4,128]{1,0:T(4,128)S(1)} %get-tuple-element.22.spread_ref, ...), custom_call_target="tpu_custom_call" | custom-call | flops 1 | tf_op jit(solution)/shard_map/own_row/pallas_call | solution.py:423
  6.3 0.6 %observe.1 = (f32[32,512]{1,0:T(8,128)S(1)}, f32[128,512]{1,0:T(8,128)S(1)}) custom-call(f32[520,128]{1,0:T(8,128)S(1)} %get-tuple-element.20.packed_ref, f32[520,128]{1,0:T(8,128)S(1)} %collective-permute-done.1.outer_ref, f32[128,512]{1,0:T(8,128)S(1)} %get-tuple-element.29.part_ref, f32[32,512]{1,0:T(8,128)S(1)} %get-tuple-element.30.part_obs_ref, ...), custom_call_target="tpu_custom_call" | custom-call | tf_op jit(solution)/shard_map/observe/pallas_call | solution.py:430
  6.9 5.1 %collective-permute-start.3 = (f32[32,512]{1,0:T(8,128)S(1)}, f32[32,512]{1,0:T(8,128)S(1)}, u32[]{:S(2)}, u32[]{:S(2)}) collective-permute-start(f32[32,512]{1,0:T(8,128)S(1)} %get-tuple-element.32.terms_ref), channel_id=1, source_target_pairs={{0,2},{4,6},{8,10},{12,14},{16,18},{20,22},{24,26},{28,30},{1,3},{... | collective-permute-start | bytes 196616 | tf_op jit(solution)/shard_map/ppermute | solution.py:445
  12.1 0.9 %collective-permute-done.3.other_ref = f32[32,512]{1,0:T(8,128)S(1)} collective-permute-done((f32[32,512]{1,0:T(8,128)S(1)}, f32[32,512]{1,0:T(8,128)S(1)}, u32[]{:S(2)}, u32[]{:S(2)}) %collective-permute-start.3) | collective-permute-done | bytes 65568 | tf_op jit(solution)/shard_map/ppermute | solution.py:445
  13.0 0.7 %collective-permute-start.4 = (f32[32,512]{1,0:T(8,128)S(1)}, f32[32,512]{1,0:T(8,128)S(1)}, u32[]{:S(2)}, u32[]{:S(2)}) collective-permute-start(f32[32,512]{1,0:T(8,128)S(1)} %sum.4.terms_ref), channel_id=1, source_target_pairs={{2,18},{6,22},{10,26},{14,30},{18,2},{22,6},{26,10},{30,14},{3,19}... | collective-permute-start | bytes 196616 | tf_op jit(solution)/shard_map/ppermute | solution.py:386
  13.7 0.7 %collective-permute-start.5 = (f32[32,512]{1,0:T(8,128)S(1)}, f32[32,512]{1,0:T(8,128)S(1)}, u32[]{:S(2)}, u32[]{:S(2)}) collective-permute-start(f32[32,512]{1,0:T(8,128)S(1)} %sum.5.terms_ref), channel_id=1, source_target_pairs={{2,10},{6,14},{10,2},{14,6},{18,26},{22,30},{26,18},{30,22},{3,11}... | collective-permute-start | bytes 196616 | tf_op jit(solution)/shard_map/ppermute | solution.py:386
  14.4 0.7 %collective-permute-start.7 = (f32[32,512]{1,0:T(8,128)S(1)}, f32[32,512]{1,0:T(8,128)S(1)}, u32[]{:S(2)}, u32[]{:S(2)}) collective-permute-start(f32[32,512]{1,0:T(8,128)S(1)} %sum.6.terms_ref), channel_id=1, source_target_pairs={{2,6},{6,2},{10,14},{14,10},{18,22},{22,18},{26,30},{30,26},{3,7},... | collective-permute-start | bytes 196616 | tf_op jit(solution)/shard_map/ppermute | solution.py:386
  15.1 0.7 %collective-permute-start.8 = (f32[32,512]{1,0:T(8,128)S(1)}, f32[32,512]{1,0:T(8,128)S(1)}, u32[]{:S(2)}, u32[]{:S(2)}) collective-permute-start(f32[32,512]{1,0:T(8,128)S(1)} %sum.7.refs_1_), channel_id=1, source_target_pairs={{3,2},{2,3},{7,6},{6,7},{11,10},{10,11},{15,14},{14,15},{19,18},{1... | collective-permute-start | bytes 196616 | tf_op jit(solution)/shard_map/ppermute | solution.py:390
  15.7 0.1 complete.1.refs_0_
  15.9 0.0 copy-start.1
  15.9 1.5 %collective-permute-start.10 = (f32[128,512]{1,0:T(8,128)S(1)}, f32[128,512]{1,0:T(8,128)S(1)}, u32[]{:S(2)}, u32[]{:S(2)}) collective-permute-start(f32[128,512]{1,0:T(8,128)S(1)} %complete.1.refs_0_), channel_id=1, source_target_pairs={{1,0},{0,1},{3,2},{2,3},{5,4},{4,5},{7,6},{6,7},{9,8},{8,9},{11,10... | collective-permute-start | bytes 786440 | tf_op jit(solution)/shard_map/ppermute | solution.py:390
  17.4 0.8 %copy-done.4 = f32[1024,128]{1,0:T(8,128)} copy-done((f32[1024,128]{1,0:T(8,128)}, f32[1024,128]{1,0:T(8,128)S(1)}, u32[]{:S(2)}) %copy-start.4) | copy-done | bytes 524312
  18.2 1.1 %gather.1.kept_ref = f32[64,512]{1,0:T(8,128)S(1)} custom-call(f32[1024,128]{1,0:T(8,128)} %copy-done.4, f32[32,512]{1,0:T(8,128)S(1)} %sum.7.refs_1_, f32[32,512]{1,0:T(8,128)S(1)} %collective-permute-done.8.refs_2_), custom_call_target="tpu_custom_call" | custom-call | flops 1 | tf_op jit(solution)/shard_map/gather/pallas_call | solution.py:457
  19.2 1.4 %collective-permute-start.9 = (f32[64,512]{1,0:T(8,128)S(1)}, f32[64,512]{1,0:T(8,128)S(1)}, u32[]{:S(2)}, u32[]{:S(2)}) collective-permute-start(f32[64,512]{1,0:T(8,128)S(1)} %gather.1.kept_ref), channel_id=1, source_target_pairs={{2,0},{6,4},{10,8},{14,12},{18,16},{22,20},{26,24},{30,28},{3,1},{... | collective-permute-start | bytes 393224 | tf_op jit(solution)/shard_map/ppermute | solution.py:464
  20.7 17.9 %collective-permute-done.9.received_ref = f32[64,512]{1,0:T(8,128)S(1)} collective-permute-done((f32[64,512]{1,0:T(8,128)S(1)}, f32[64,512]{1,0:T(8,128)S(1)}, u32[]{:S(2)}, u32[]{:S(2)}) %collective-permute-start.9) | collective-permute-done | bytes 131104 | tf_op jit(solution)/shard_map/ppermute | solution.py:464
  38.6 3.3 %solve.1.mine_ref = f32[32,64]{1,0:T(8,128)S(1)} custom-call(f32[2,256]{1,0:T(2,128)S(1)} %copy-done.2, f32[2,256]{1,0:T(2,128)S(1)} %copy-done.3, f32[2,64,256]{2,1,0:T(8,128)S(1)} %copy-done.1, f32[64,512]{1,0:T(8,128)S(1)} %gather.1.kept_ref, f32[64,512]{1,0:T(8,128)S(1)} %collective-permute-done.9.received_ref), custom_call_target="tpu_custom_call" | custom-call | flops 1000000000 | tf_op jit(solution)/shard_map/solve/pallas_call | solution.py:465
  41.9 0.0 copy-done
  41.9 2.8 %combine.1 = f32[32,48,128]{2,1,0:T(8,128)} custom-call(f32[32,64]{1,0:T(8,128)S(1)} %solve.1.mine_ref, f32[128,512]{1,0:T(8,128)S(1)} %complete.1.refs_0_, f32[128,512]{1,0:T(8,128)S(1)} %collective-permute-done.10.refs_1_, f32[1024,128]{1,0:T(8,128)S(1)} %bitcast.6, f32[1024,128]{1,0:T(8,128)} %copy-done.4), custom_call_target="tpu_custom_call" | custom-call | tf_op jit(solution)/shard_map/combine/pallas_call | solution.py:476
  (20 shorter events, 0.1 us)
Async XLA Ops:
  1.0 4.6 %collective-permute-start.2 = (f32[520,128]{1,0:T(8,128)S(1)}, f32[520,128]{1,0:T(8,128)S(1)}, u32[]{:S(2)}, u32[]{:S(2)}) collective-permute-start(f32[520,128]{1,0:T(8,128)S(1)} %get-tuple-element.20.packed_ref), channel_id=1, source_target_pairs={{0,2},{2,0},{4,6},{6,4},{8,10},{10,8},{12,14},{14,12},{16,18},{18,... | collective-permute-start | bytes 798728 | tf_op jit(solution)/shard_map/ppermute | solution.py:411
  1.5 4.7 %collective-permute-start.1 = (f32[520,128]{1,0:T(8,128)S(1)}, f32[520,128]{1,0:T(8,128)S(1)}, u32[]{:S(2)}, u32[]{:S(2)}) collective-permute-start(f32[520,128]{1,0:T(8,128)S(1)} %get-tuple-element.20.packed_ref), channel_id=1, source_target_pairs={{2,4},{6,8},{10,12},{14,16},{18,20},{22,24},{26,28},{3,5},{7,9},{1... | collective-permute-start | bytes 798728 | tf_op jit(solution)/shard_map/ppermute | solution.py:410
  2.2 15.2 %collective-permute-start = (f32[1024,128]{1,0:T(8,128)}, f32[1024,128]{1,0:T(8,128)S(1)}, u32[]{:S(2)}, u32[]{:S(2)}) collective-permute-start(f32[1024,128]{1,0:T(8,128)} %bitcast.5), channel_id=1, source_target_pairs={{1,0},{0,1},{3,2},{2,3},{5,4},{4,5},{7,6},{6,7},{9,8},{8,9},{11,10... | collective-permute-start | bytes 1572872 | tf_op jit(solution)/shard_map/ppermute | solution.py:390
  4.8 9.5 %collective-permute-start.6 = (f32[520,128]{1,0:T(8,128)S(1)}, f32[520,128]{1,0:T(8,128)S(1)}, u32[]{:S(2)}, u32[]{:S(2)}) collective-permute-start(f32[520,128]{1,0:T(8,128)S(1)} %get-tuple-element.20.packed_ref), channel_id=1, source_target_pairs={{4,2},{8,6},{12,10},{16,14},{20,18},{24,22},{28,26},{5,3},{9,7},{1... | collective-permute-start | bytes 798728 | tf_op jit(solution)/shard_map/ppermute | solution.py:415
  6.9 6.0 %collective-permute-start.3 = (f32[32,512]{1,0:T(8,128)S(1)}, f32[32,512]{1,0:T(8,128)S(1)}, u32[]{:S(2)}, u32[]{:S(2)}) collective-permute-start(f32[32,512]{1,0:T(8,128)S(1)} %get-tuple-element.32.terms_ref), channel_id=1, source_target_pairs={{0,2},{4,6},{8,10},{12,14},{16,18},{20,22},{24,26},{28,30},{1,3},{... | collective-permute-start | bytes 196616 | tf_op jit(solution)/shard_map/ppermute | solution.py:445
  13.0 0.7 %collective-permute-start.4 = (f32[32,512]{1,0:T(8,128)S(1)}, f32[32,512]{1,0:T(8,128)S(1)}, u32[]{:S(2)}, u32[]{:S(2)}) collective-permute-start(f32[32,512]{1,0:T(8,128)S(1)} %sum.4.terms_ref), channel_id=1, source_target_pairs={{2,18},{6,22},{10,26},{14,30},{18,2},{22,6},{26,10},{30,14},{3,19}... | collective-permute-start | bytes 196616 | tf_op jit(solution)/shard_map/ppermute | solution.py:386
  13.7 0.7 %collective-permute-start.5 = (f32[32,512]{1,0:T(8,128)S(1)}, f32[32,512]{1,0:T(8,128)S(1)}, u32[]{:S(2)}, u32[]{:S(2)}) collective-permute-start(f32[32,512]{1,0:T(8,128)S(1)} %sum.5.terms_ref), channel_id=1, source_target_pairs={{2,10},{6,14},{10,2},{14,6},{18,26},{22,30},{26,18},{30,22},{3,11}... | collective-permute-start | bytes 196616 | tf_op jit(solution)/shard_map/ppermute | solution.py:386
  14.4 0.7 %collective-permute-start.7 = (f32[32,512]{1,0:T(8,128)S(1)}, f32[32,512]{1,0:T(8,128)S(1)}, u32[]{:S(2)}, u32[]{:S(2)}) collective-permute-start(f32[32,512]{1,0:T(8,128)S(1)} %sum.6.terms_ref), channel_id=1, source_target_pairs={{2,6},{6,2},{10,14},{14,10},{18,22},{22,18},{26,30},{30,26},{3,7},... | collective-permute-start | bytes 196616 | tf_op jit(solution)/shard_map/ppermute | solution.py:386
  15.1 2.3 %collective-permute-start.8 = (f32[32,512]{1,0:T(8,128)S(1)}, f32[32,512]{1,0:T(8,128)S(1)}, u32[]{:S(2)}, u32[]{:S(2)}) collective-permute-start(f32[32,512]{1,0:T(8,128)S(1)} %sum.7.refs_1_), channel_id=1, source_target_pairs={{3,2},{2,3},{7,6},{6,7},{11,10},{10,11},{15,14},{14,15},{19,18},{1... | collective-permute-start | bytes 196616 | tf_op jit(solution)/shard_map/ppermute | solution.py:390
  15.9 22.8 %copy-start.1 = (f32[2,64,256]{2,1,0:T(8,128)S(1)}, f32[2,64,256]{2,1,0:T(8,128)}, u32[]{:S(2)}) copy-start(f32[2,64,256]{2,1,0:T(8,128)} %noise_ref.1) | copy-start | bytes 393220
  15.9 22.8 %copy-start.2 = (f32[2,256]{1,0:T(2,128)S(1)}, f32[2,256]{1,0:T(2,128)}, u32[]{:S(2)}) copy-start(f32[2,256]{1,0:T(2,128)} %value_ref.1) | copy-start | bytes 6148
  15.9 22.7 %copy-start.3 = (f32[2,256]{1,0:T(2,128)S(1)}, f32[2,256]{1,0:T(2,128)}, u32[]{:S(2)}) copy-start(f32[2,256]{1,0:T(2,128)} %error_ref.1) | copy-start | bytes 6148
  15.9 26.0 %collective-permute-start.10 = (f32[128,512]{1,0:T(8,128)S(1)}, f32[128,512]{1,0:T(8,128)S(1)}, u32[]{:S(2)}, u32[]{:S(2)}) collective-permute-start(f32[128,512]{1,0:T(8,128)S(1)} %complete.1.refs_0_), channel_id=1, source_target_pairs={{1,0},{0,1},{3,2},{2,3},{5,4},{4,5},{7,6},{6,7},{9,8},{8,9},{11,10... | collective-permute-start | bytes 786440 | tf_op jit(solution)/shard_map/ppermute | solution.py:390
  17.4 0.8 %copy-start.4 = (f32[1024,128]{1,0:T(8,128)}, f32[1024,128]{1,0:T(8,128)S(1)}, u32[]{:S(2)}) copy-start(f32[1024,128]{1,0:T(8,128)S(1)} %collective-permute-done.refs_0_.refs_3_) | copy-start | bytes 1572868
  19.2 22.7 %copy-start = (f32[32,2,4,1,512]{4,3,2,1,0:T(1,128)S(1)}, f32[32,2,4,1,512]{4,3,2,1,0:T(1,128)}, u32[]{:S(2)}) copy-start(f32[32,2,4,1,512]{4,3,2,1,0:T(1,128)} %param.11) | copy-start | bytes 1572868
  19.2 19.4 %collective-permute-start.9 = (f32[64,512]{1,0:T(8,128)S(1)}, f32[64,512]{1,0:T(8,128)S(1)}, u32[]{:S(2)}, u32[]{:S(2)}) collective-permute-start(f32[64,512]{1,0:T(8,128)S(1)} %gather.1.kept_ref), channel_id=1, source_target_pairs={{2,0},{6,4},{10,8},{14,12},{18,16},{22,20},{26,24},{30,28},{3,1},{... | collective-permute-start | bytes 393224 | tf_op jit(solution)/shard_map/ppermute | solution.py:464

commit v7 on v6

--- a/solution.py
+++ b/solution.py
@@ -11,11 +11,11 @@
 F32 = jnp.float32
 BF16 = jnp.bfloat16
 HIGHEST = lax.Precision.HIGHEST
-PARAMS = pltpu.CompilerParams(vmem_limit_bytes=16 * 1024 * 1024)
+PARAMS = pltpu.CompilerParams(vmem_limit_bytes=48 * 1024 * 1024)
 
 
 SELECT_FLOPS = 1
-OWN_FLOPS, SUM_FLOPS, GATHER_FLOPS, SOLVE_FLOPS = 1, 10**8, 1, 10**9
+OWN_FLOPS, SUM_FLOPS, GATHER_FLOPS, SOLVE_FLOPS = 1, 5*10**8, 10**9, 2*10**9
 
 
 def estimate(flops):
@@ -168,7 +168,8 @@
     here_ref,
     taps_ref,
     kinds_ref,
-    obs_ref,
+    keep_ref,
+    send_ref,
     partial_ref,
 ):
     above, _ = weights(packed_ref, chunks)
@@ -183,14 +184,18 @@
         for f in range(fields):
             start = (side * fields + f) * members
             observed += jnp.where(kinds == f, picked[start : start + members], 0.0)
-    obs_ref[...] = observed
+    even = lax.rem(lax.axis_index("slab"), 2) == 0
+    half = observed.shape[1] // 2
+    first, second = observed[:, :half], observed[:, half:]
+    keep_ref[...] = jnp.where(even, first, second)
+    send_ref[...] = jnp.where(even, second, first)
 
 
 def sum_kernel(terms_ref, other_ref, *refs):
     refs[-1][...] = terms_ref[...] + other_ref[...]
 
 
-def complete_kernel(members, fields, chunks, partial_ref, outer_ref, packed_ref, forecast_ref):
+def complete_kernel(members, fields, chunks, partial_ref, outer_ref, packed_ref, _, forecast_ref):
     _, below = weights(packed_ref, chunks)
     forecast_ref[...] = partial_ref[...] + below * stacked_planes(
         outer_ref, members, fields, chunks
@@ -198,8 +203,8 @@
 
 
 def gather_kernel(*refs):
-    local = refs[1].shape[0]
-    for d, ref in enumerate(refs[1:-1]):
+    local = refs[0].shape[0]
+    for d, ref in enumerate(refs[:-1]):
         refs[-1][d * local : (d + 1) * local, :] = ref[...]
 
 
@@ -249,12 +254,14 @@
     own = lax.axis_index("mem")
     own_rows = pl.ds(pl.multiple_of(own * local, local), local)
     even = lax.rem(lax.axis_index("slab"), 2) == 0
+    half = batches * count // 2
     for d in range(parts):
         owner = lax.rem(own + d, parts)
-        block = slice(d * local, (d + 1) * local)
-        prior[pl.ds(pl.multiple_of(owner * local, local), local), :] = jnp.where(
-            even, received_ref[block, :], kept_ref[block, :]
-        )
+        rows = pl.ds(pl.multiple_of(owner * local, local), local)
+        kept = kept_ref[d * local : (d + 1) * local, :]
+        received = received_ref[d * local : (d + 1) * local, :]
+        prior[rows, :half] = jnp.where(even, kept, received)
+        prior[rows, half:] = jnp.where(even, received, kept)
     source = lax.broadcasted_iota(jnp.int32, (members, members), 0)
     target = lax.broadcasted_iota(jnp.int32, (members, members), 1)
     turn = (source == lax.rem(target + own * local, members)).astype(F32)
@@ -382,16 +389,12 @@
 
     odd = range(1, slabs, 2)
 
-    def among_odd(array, bit):
-        return lax.ppermute(array, "slab", [(i, i ^ bit) for i in odd])
-
-    def from_partners(array, among):
+    def from_slab(array, bit):
+        return lax.ppermute(array, "slab", [(i, i ^ bit) for i in range(slabs)])
+
+    def from_partners(array):
         return [
-            lax.ppermute(
-                array,
-                ("slab", "mem"),
-                [(i * parts + (j + d) % parts, i * parts + j) for i in among for j in range(parts)],
-            )
+            lax.ppermute(array, "mem", [((i + d) % parts, i) for i in range(parts)])
             for d in range(1, parts)
         ]
 
@@ -408,9 +411,9 @@
         name="load",
     )(*sources)
     outer_above = lax.ppermute(packed, "slab", [(i, i + 1) for i in odd[:-1]])
-    inner = lax.ppermute(packed, "slab", [(i, i ^ 1) for i in range(slabs)])
+    inner = from_slab(packed, 1)
     others_delayed = from_partners(
-        lax.optimization_barrier((in_hbm([delayed])[0], packed))[0], range(slabs)
+        lax.optimization_barrier((delayed, packed))[0]
     )
     outer_below = lax.ppermute(packed, "slab", [(i + 1, i) for i in odd[:-1]])
     taps, kinds = pl.pallas_call(
@@ -427,9 +430,13 @@
         cost_estimate=estimate(OWN_FLOPS),
         name="own_row",
     )(packed, inner, *held[:2], taps, kinds)
-    terms, partial = pl.pallas_call(
+    keep, send, partial = pl.pallas_call(
         functools.partial(observe_kernel, *sizes),
-        out_shape=(shape_of((members, total)), shape_of(stacked)),
+        out_shape=(
+            shape_of((members, total // 2)),
+            shape_of((members, total // 2)),
+            shape_of(stacked),
+        ),
         compiler_params=PARAMS,
         name="observe",
     )(packed, outer_above, part, part_obs, here, taps, kinds)
@@ -442,26 +449,27 @@
             name="sum",
         )(terms, other, *arrived)
 
-    terms = summed(terms, lax.ppermute(terms, "slab", [(i - 1, i) for i in odd]), 1)
+    terms = keep + from_slab(send, 1)
     for bit in [1 << k for k in reversed(range(1, slabs.bit_length() - 1))]:
         terms = summed(
-            terms, among_odd(terms, bit), SUM_FLOPS, *([outer_below] if bit == 4 else [])
+            terms, from_slab(terms, bit), SUM_FLOPS, *([outer_below] if bit == 4 else [])
         )
     forecast = pl.pallas_call(
         functools.partial(complete_kernel, *sizes),
         out_shape=shape_of(stacked),
         compiler_params=PARAMS,
         name="complete",
-    )(lax.optimization_barrier((partial, terms))[0], outer_below, packed)
+    )(
+        lax.optimization_barrier((partial, terms))[0], outer_below, packed, others_delayed[0]
+    )
 
     prior = pl.pallas_call(
         gather_kernel,
-        out_shape=shape_of((all_members, total)),
+        out_shape=shape_of((all_members, total // 2)),
         cost_estimate=estimate(GATHER_FLOPS),
         compiler_params=PARAMS,
         name="gather",
-    )(others_delayed[0], terms, *from_partners(terms, odd))
-    received = lax.ppermute(prior, "slab", [(i, i - 1) for i in odd])
+    )(terms, *from_partners(terms))
     mine = pl.pallas_call(
         functools.partial(solve_kernel, parts),
         out_shape=shape_of((members, all_members)),
@@ -472,7 +480,7 @@
         compiler_params=PARAMS,
         cost_estimate=estimate(SOLVE_FLOPS),
         name="solve",
-    )(obs_value, obs_error, obs_noise, prior, received)
+    )(obs_value, obs_error, obs_noise, prior, from_slab(prior, 1))
     out = pl.pallas_call(
         functools.partial(combine_kernel, parts, fields),
         out_shape=shape_of((members, planes, LANES)),
@@ -483,7 +491,7 @@
         ],
         compiler_params=PARAMS,
         name="combine",
-    )(mine, forecast, *from_partners(forecast, range(slabs)), delayed, *others_delayed)
+    )(mine, forecast, *from_partners(forecast), delayed, *others_delayed)
     return out.reshape(members, 1 + lagged, fields, height, width)
 
 

time: 45.1 us -> 36.4 us (0.81)
  waiting for transfers between devices: 18.8 us -> 11.8 us
  Pallas kernels: 9.7 us -> 7.57 us
  starting transfers between devices: 15.1 us -> 16.7 us
  local copies, waits for them, and re-layouts: 0.83 us -> 0.03 us
    ppermute x9, waiting for transfers between devices: 18.8 us -> 11.8 us  [the longest x6 10.1 us: from_slab(): return lax.ppermute(array, 'slab', [(i, i ^ bit) for i in range(slabs)])]
    ppermute x9, starting transfers between devices: 13.8 us -> 15.4 us  [the longest x6 10.7 us: from_slab(): return lax.ppermute(array, 'slab', [(i, i ^ bit) for i in range(slabs)])]
    pallas_call x1, Pallas kernels: 2.76 us -> 1.71 us  [shards(): pl.pallas_call(functools.partial(combine_kernel, parts, fields), out_shap...]
    pallas_call x1, Pallas kernels: 1.05 us -> 0.01 us  [shards(): pl.pallas_call(gather_kernel, out_shape=shape_of((all_members, total // 2...]
    unnamed x10 -> x8, local copies, waits for them, and re-layouts: 0.83 us -> 0.03 us
  transfers between devices with their start and end apart: 11 -> 11, of which waited for: 2 -> 6; matrix products, arithmetic and copies ran while one was open for 0% -> 0% of each run, Pallas kernels for 13% -> 13%
where the time goes in v7:
time: 36.4 us; the launch traced here: 36.2 us
  starting transfers between devices  16.7 us (46%)
  waiting for transfers between devices  11.8 us (32%)
  Pallas kernels  7.57 us (21%)
    ppermute x6, starting transfers between devices, from_slab(): return lax.ppermute(array, 'slab', [(i, i ^ bit) for i in range(slabs)])  10.7 us
    ppermute x6, waiting for transfers between devices, from_slab(): return lax.ppermute(array, 'slab', [(i, i ^ bit) for i in range(slabs)])  10.1 us
    ppermute x3, starting transfers between devices, from_partners(): lax.ppermute(array, 'mem', [((i + d) % parts, i) for i in range(parts)])  4.67 us
    pallas_call x1, Pallas kernels, shards(): pl.pallas_call(functools.partial(solve_kernel, parts), out_shape=shape_of...  3.3 us
    pallas_call x1, Pallas kernels, shards(): pl.pallas_call(functools.partial(combine_kernel, parts, fields), out_shap...  1.71 us
    ppermute x3, waiting for transfers between devices, from_partners(): lax.ppermute(array, 'mem', [((i + d) % parts, i) for i in range(parts)])  1.68 us
    pallas_call x1, Pallas kernels, shards(): pl.pallas_call(functools.partial(load_kernel, chunks), out_shape=[shape_o...  1.01 us
  transfers between devices with their start and end apart: 11, of which 6 were waited for; matrix products, arithmetic and copies ran while one was open for 0% of the time, Pallas kernels for 13%

profile of v7, /device:TPU:0, one launch (start us, length us, event | category | flops | bytes accessed | tf_op | source)
XLA Modules:
  0.0 36.2 jit_solution(66034461543347291)
XLA Ops:
  0.0 1.0 %load.1 = (f32[520,128]{1,0:T(8,128)S(1)}, f32[4,128]{1,0:T(4,128)S(1)}, f32[8,128]{1,0:T(8,128)S(1)}, s32[2,256]{1,0:T(2,128)S(1)}, s32[2,256]{1,0:T(2,128)S(1)}, /*index=5*/s32[2,256]{1,0:T(2,128)S(1)}) custom-call(f32[512,128]{1,0:T(8,128)} %bitcast.7, f32[4,128]{1,0:T(4,128)} %bitcast.9, f32[8,128]{1,0:T(8,128)} %bitcast.8, s32[2,256]{1,0:T(2,128)} %refs_3_.1, ...), custom_call_target="tpu_custom_call" | custom-call | tf_op jit(solution)/shard_map/load/pallas_call | solution.py:404
  1.0 0.5 %collective-permute-start.1 = (f32[520,128]{1,0:T(8,128)S(1)}, f32[520,128]{1,0:T(8,128)S(1)}, u32[]{:S(2)}, u32[]{:S(2)}) collective-permute-start(f32[520,128]{1,0:T(8,128)S(1)} %get-tuple-element.21.packed_ref), channel_id=1, source_target_pairs={{0,2},{2,0},{4,6},{6,4},{8,10},{10,8},{12,14},{14,12},{16,18},{18,... | collective-permute-start | bytes 798728 | tf_op jit(solution)/shard_map/ppermute | solution.py:393
  1.5 0.7 %collective-permute-start = (f32[520,128]{1,0:T(8,128)S(1)}, f32[520,128]{1,0:T(8,128)S(1)}, u32[]{:S(2)}, u32[]{:S(2)}) collective-permute-start(f32[520,128]{1,0:T(8,128)S(1)} %get-tuple-element.21.packed_ref), channel_id=1, source_target_pairs={{2,4},{6,8},{10,12},{14,16},{18,20},{22,24},{26,28},{3,5},{7,9},{1... | collective-permute-start | bytes 798728 | tf_op jit(solution)/shard_map/ppermute | solution.py:413
  2.2 2.6 %collective-permute-start.9 = (f32[1024,128]{1,0:T(8,128)}, f32[1024,128]{1,0:T(8,128)S(1)}, u32[]{:S(2)}, u32[]{:S(2)}) collective-permute-start(f32[1024,128]{1,0:T(8,128)} %bitcast.5), channel_id=1, source_target_pairs={{1,0},{0,1},{3,2},{2,3},{5,4},{4,5},{7,6},{6,7},{9,8},{8,9},{11,10... | collective-permute-start | bytes 1572872 | tf_op jit(solution)/shard_map/ppermute | solution.py:397
  4.8 0.7 %collective-permute-start.5 = (f32[520,128]{1,0:T(8,128)S(1)}, f32[520,128]{1,0:T(8,128)S(1)}, u32[]{:S(2)}, u32[]{:S(2)}) collective-permute-start(f32[520,128]{1,0:T(8,128)S(1)} %get-tuple-element.21.packed_ref), channel_id=1, source_target_pairs={{4,2},{8,6},{12,10},{16,14},{20,18},{24,22},{28,26},{5,3},{9,7},{1... | collective-permute-start | bytes 798728 | tf_op jit(solution)/shard_map/ppermute | solution.py:418
  5.5 0.2 selector.1
  5.7 0.6 %own_row.1 = (f32[128,512]{1,0:T(8,128)S(1)}, f32[128,512]{1,0:T(8,128)S(1)}, f32[32,512]{1,0:T(8,128)S(1)}) custom-call(f32[520,128]{1,0:T(8,128)S(1)} %get-tuple-element.21.packed_ref, f32[520,128]{1,0:T(8,128)S(1)} %collective-permute-done.1.inner_ref, f32[4,128]{1,0:T(4,128)S(1)} %get-tuple-element.22.spread_ref, ...), custom_call_target="tpu_custom_call" | custom-call | flops 1 | tf_op jit(solution)/shard_map/own_row/pallas_call | solution.py:426
  6.3 0.6 %observe.1 = (f32[32,256]{1,0:T(8,128)S(1)}, f32[32,256]{1,0:T(8,128)S(1)}, f32[128,512]{1,0:T(8,128)S(1)}) custom-call(f32[520,128]{1,0:T(8,128)S(1)} %get-tuple-element.21.packed_ref, f32[520,128]{1,0:T(8,128)S(1)} %collective-permute-done.outer_ref, f32[128,512]{1,0:T(8,128)S(1)} %get-tuple-element.29.part_ref, ...), custom_call_target="tpu_custom_call" | custom-call | tf_op jit(solution)/shard_map/observe/pallas_call | solution.py:433
  6.9 3.3 %collective-permute-start.2 = (f32[32,256]{1,0:T(8,128)S(1)}, f32[32,256]{1,0:T(8,128)S(1)}, u32[]{:S(2)}, u32[]{:S(2)}) collective-permute-start(f32[32,256]{1,0:T(8,128)S(1)} %get-tuple-element.33), channel_id=1, source_target_pairs={{0,2},{2,0},{4,6},{6,4},{8,10},{10,8},{12,14},{14,12},{16,18},{18,... | collective-permute-start | bytes 98312 | tf_op jit(solution)/shard_map/ppermute | solution.py:393
  10.2 0.9 %collective-permute-done.2 = f32[32,256]{1,0:T(8,128)S(1)} collective-permute-done((f32[32,256]{1,0:T(8,128)S(1)}, f32[32,256]{1,0:T(8,128)S(1)}, u32[]{:S(2)}, u32[]{:S(2)}) %collective-permute-start.2) | collective-permute-done | bytes 32800 | tf_op jit(solution)/shard_map/ppermute | solution.py:393
  11.1 4.6 %collective-permute-start.3 = (f32[32,256]{1,0:T(8,128)S(1)}, f32[32,256]{1,0:T(8,128)S(1)}, u32[]{:S(2)}, u32[]{:S(2)}) collective-permute-start(f32[32,256]{1,0:T(8,128)S(1)} %add.3.terms_ref), channel_id=1, source_target_pairs={{0,16},{2,18},{4,20},{6,22},{8,24},{10,26},{12,28},{14,30},{16,0},... | collective-permute-start | bytes 98312 | tf_op jit(solution)/shard_map/ppermute | solution.py:393
  15.7 2.4 %collective-permute-done.3.other_ref = f32[32,256]{1,0:T(8,128)S(1)} collective-permute-done((f32[32,256]{1,0:T(8,128)S(1)}, f32[32,256]{1,0:T(8,128)S(1)}, u32[]{:S(2)}, u32[]{:S(2)}) %collective-permute-start.3) | collective-permute-done | bytes 32800 | tf_op jit(solution)/shard_map/ppermute | solution.py:393
  18.1 1.4 %collective-permute-start.4 = (f32[32,256]{1,0:T(8,128)S(1)}, f32[32,256]{1,0:T(8,128)S(1)}, u32[]{:S(2)}, u32[]{:S(2)}) collective-permute-start(f32[32,256]{1,0:T(8,128)S(1)} %sum.3.terms_ref), channel_id=1, source_target_pairs={{0,8},{2,10},{4,12},{6,14},{8,0},{10,2},{12,4},{14,6},{16,24},{18,... | collective-permute-start | bytes 98312 | tf_op jit(solution)/shard_map/ppermute | solution.py:393
  19.5 2.5 %collective-permute-done.4.other_ref = f32[32,256]{1,0:T(8,128)S(1)} collective-permute-done((f32[32,256]{1,0:T(8,128)S(1)}, f32[32,256]{1,0:T(8,128)S(1)}, u32[]{:S(2)}, u32[]{:S(2)}) %collective-permute-start.4) | collective-permute-done | bytes 32800 | tf_op jit(solution)/shard_map/ppermute | solution.py:393
  22.0 0.8 %collective-permute-start.6 = (f32[32,256]{1,0:T(8,128)S(1)}, f32[32,256]{1,0:T(8,128)S(1)}, u32[]{:S(2)}, u32[]{:S(2)}) collective-permute-start(f32[32,256]{1,0:T(8,128)S(1)} %sum.4.terms_ref), channel_id=1, source_target_pairs={{0,4},{2,6},{4,0},{6,2},{8,12},{10,14},{12,8},{14,10},{16,20},{18,... | collective-permute-start | bytes 98312 | tf_op jit(solution)/shard_map/ppermute | solution.py:393
  22.8 3.1 %collective-permute-done.6.other_ref = f32[32,256]{1,0:T(8,128)S(1)} collective-permute-done((f32[32,256]{1,0:T(8,128)S(1)}, f32[32,256]{1,0:T(8,128)S(1)}, u32[]{:S(2)}, u32[]{:S(2)}) %collective-permute-start.6) | collective-permute-done | bytes 32800 | tf_op jit(solution)/shard_map/ppermute | solution.py:393
  25.9 1.0 %collective-permute-start.7 = (f32[32,256]{1,0:T(8,128)S(1)}, f32[32,256]{1,0:T(8,128)S(1)}, u32[]{:S(2)}, u32[]{:S(2)}) collective-permute-start(f32[32,256]{1,0:T(8,128)S(1)} %sum.5.refs_0_), channel_id=1, source_target_pairs={{1,0},{0,1},{3,2},{2,3},{5,4},{4,5},{7,6},{6,7},{9,8},{8,9},{11,10... | collective-permute-start | bytes 98312 | tf_op jit(solution)/shard_map/ppermute | solution.py:397
  26.9 0.1 complete.1.refs_0_
  27.1 1.1 %collective-permute-start.10 = (f32[128,512]{1,0:T(8,128)S(1)}, f32[128,512]{1,0:T(8,128)S(1)}, u32[]{:S(2)}, u32[]{:S(2)}) collective-permute-start(f32[128,512]{1,0:T(8,128)S(1)} %complete.1.refs_0_), channel_id=1, source_target_pairs={{1,0},{0,1},{3,2},{2,3},{5,4},{4,5},{7,6},{6,7},{9,8},{8,9},{11,10... | collective-permute-start | bytes 786440 | tf_op jit(solution)/shard_map/ppermute | solution.py:397
  28.2 1.7 %collective-permute-done.7.refs_1_ = f32[32,256]{1,0:T(8,128)S(1)} collective-permute-done((f32[32,256]{1,0:T(8,128)S(1)}, f32[32,256]{1,0:T(8,128)S(1)}, u32[]{:S(2)}, u32[]{:S(2)}) %collective-permute-start.7) | collective-permute-done | bytes 32800 | tf_op jit(solution)/shard_map/ppermute | solution.py:397
  29.9 0.1 collective-permute-start.8
  29.9 1.2 %collective-permute-done.8.received_ref = f32[64,256]{1,0:T(8,128)S(1)} collective-permute-done((f32[64,256]{1,0:T(8,128)S(1)}, f32[64,256]{1,0:T(8,128)S(1)}, u32[]{:S(2)}, u32[]{:S(2)}) %collective-permute-start.8) | collective-permute-done | bytes 65568 | tf_op jit(solution)/shard_map/ppermute | solution.py:393
  31.2 3.3 %solve.1.mine_ref = f32[32,64]{1,0:T(8,128)S(1)} custom-call(f32[2,256]{1,0:T(2,128)S(1)} %copy-done.2, f32[2,256]{1,0:T(2,128)S(1)} %copy-done.3, f32[2,64,256]{2,1,0:T(8,128)S(1)} %copy-done.1, f32[64,256]{1,0:T(8,128)S(1)} %gather.1.kept_ref, f32[64,256]{1,0:T(8,128)S(1)} %collective-permute-done.8.received_ref), custom_call_target="tpu_custom_call" | custom-call | flops 2000000000 | tf_op jit(solution)/shard_map/solve/pallas_call | solution.py:473
  34.5 1.7 %combine.1 = f32[32,48,128]{2,1,0:T(8,128)} custom-call(f32[32,64]{1,0:T(8,128)S(1)} %solve.1.mine_ref, f32[128,512]{1,0:T(8,128)S(1)} %complete.1.refs_0_, f32[128,512]{1,0:T(8,128)S(1)} %collective-permute-done.10.refs_1_, f32[1024,128]{1,0:T(8,128)S(1)} %bitcast.6, f32[1024,128]{1,0:T(8,128)S(1)} %collective-permute-done.9._.refs_3_), custom_call_target="tpu_custom_call" | custom-call | tf_op jit(solution)/shard_map/combine/pallas_call | solution.py:484
  (18 shorter events, 0.1 us)
Async XLA Ops:
  1.0 4.6 %collective-permute-start.1 = (f32[520,128]{1,0:T(8,128)S(1)}, f32[520,128]{1,0:T(8,128)S(1)}, u32[]{:S(2)}, u32[]{:S(2)}) collective-permute-start(f32[520,128]{1,0:T(8,128)S(1)} %get-tuple-element.21.packed_ref), channel_id=1, source_target_pairs={{0,2},{2,0},{4,6},{6,4},{8,10},{10,8},{12,14},{14,12},{16,18},{18,... | collective-permute-start | bytes 798728 | tf_op jit(solution)/shard_map/ppermute | solution.py:393
  1.5 4.7 %collective-permute-start = (f32[520,128]{1,0:T(8,128)S(1)}, f32[520,128]{1,0:T(8,128)S(1)}, u32[]{:S(2)}, u32[]{:S(2)}) collective-permute-start(f32[520,128]{1,0:T(8,128)S(1)} %get-tuple-element.21.packed_ref), channel_id=1, source_target_pairs={{2,4},{6,8},{10,12},{14,16},{18,20},{22,24},{26,28},{3,5},{7,9},{1... | collective-permute-start | bytes 798728 | tf_op jit(solution)/shard_map/ppermute | solution.py:413
  2.2 24.7 %collective-permute-start.9 = (f32[1024,128]{1,0:T(8,128)}, f32[1024,128]{1,0:T(8,128)S(1)}, u32[]{:S(2)}, u32[]{:S(2)}) collective-permute-start(f32[1024,128]{1,0:T(8,128)} %bitcast.5), channel_id=1, source_target_pairs={{1,0},{0,1},{3,2},{2,3},{5,4},{4,5},{7,6},{6,7},{9,8},{8,9},{11,10... | collective-permute-start | bytes 1572872 | tf_op jit(solution)/shard_map/ppermute | solution.py:397
  4.8 14.8 %collective-permute-start.5 = (f32[520,128]{1,0:T(8,128)S(1)}, f32[520,128]{1,0:T(8,128)S(1)}, u32[]{:S(2)}, u32[]{:S(2)}) collective-permute-start(f32[520,128]{1,0:T(8,128)S(1)} %get-tuple-element.21.packed_ref), channel_id=1, source_target_pairs={{4,2},{8,6},{12,10},{16,14},{20,18},{24,22},{28,26},{5,3},{9,7},{1... | collective-permute-start | bytes 798728 | tf_op jit(solution)/shard_map/ppermute | solution.py:418
  6.9 4.1 %collective-permute-start.2 = (f32[32,256]{1,0:T(8,128)S(1)}, f32[32,256]{1,0:T(8,128)S(1)}, u32[]{:S(2)}, u32[]{:S(2)}) collective-permute-start(f32[32,256]{1,0:T(8,128)S(1)} %get-tuple-element.33), channel_id=1, source_target_pairs={{0,2},{2,0},{4,6},{6,4},{8,10},{10,8},{12,14},{14,12},{16,18},{18,... | collective-permute-start | bytes 98312 | tf_op jit(solution)/shard_map/ppermute | solution.py:393
  11.1 7.0 %collective-permute-start.3 = (f32[32,256]{1,0:T(8,128)S(1)}, f32[32,256]{1,0:T(8,128)S(1)}, u32[]{:S(2)}, u32[]{:S(2)}) collective-permute-start(f32[32,256]{1,0:T(8,128)S(1)} %add.3.terms_ref), channel_id=1, source_target_pairs={{0,16},{2,18},{4,20},{6,22},{8,24},{10,26},{12,28},{14,30},{16,0},... | collective-permute-start | bytes 98312 | tf_op jit(solution)/shard_map/ppermute | solution.py:393
  18.1 3.9 %collective-permute-start.4 = (f32[32,256]{1,0:T(8,128)S(1)}, f32[32,256]{1,0:T(8,128)S(1)}, u32[]{:S(2)}, u32[]{:S(2)}) collective-permute-start(f32[32,256]{1,0:T(8,128)S(1)} %sum.3.terms_ref), channel_id=1, source_target_pairs={{0,8},{2,10},{4,12},{6,14},{8,0},{10,2},{12,4},{14,6},{16,24},{18,... | collective-permute-start | bytes 98312 | tf_op jit(solution)/shard_map/ppermute | solution.py:393
  22.0 3.9 %collective-permute-start.6 = (f32[32,256]{1,0:T(8,128)S(1)}, f32[32,256]{1,0:T(8,128)S(1)}, u32[]{:S(2)}, u32[]{:S(2)}) collective-permute-start(f32[32,256]{1,0:T(8,128)S(1)} %sum.4.terms_ref), channel_id=1, source_target_pairs={{0,4},{2,6},{4,0},{6,2},{8,12},{10,14},{12,8},{14,10},{16,20},{18,... | collective-permute-start | bytes 98312 | tf_op jit(solution)/shard_map/ppermute | solution.py:393
  25.9 3.9 %collective-permute-start.7 = (f32[32,256]{1,0:T(8,128)S(1)}, f32[32,256]{1,0:T(8,128)S(1)}, u32[]{:S(2)}, u32[]{:S(2)}) collective-permute-start(f32[32,256]{1,0:T(8,128)S(1)} %sum.5.refs_0_), channel_id=1, source_target_pairs={{1,0},{0,1},{3,2},{2,3},{5,4},{4,5},{7,6},{6,7},{9,8},{8,9},{11,10... | collective-permute-start | bytes 98312 | tf_op jit(solution)/shard_map/ppermute | solution.py:397
  27.0 4.2 %copy-start.1 = (f32[2,64,256]{2,1,0:T(8,128)S(1)}, f32[2,64,256]{2,1,0:T(8,128)}, u32[]{:S(2)}) copy-start(f32[2,64,256]{2,1,0:T(8,128)} %noise_ref.1) | copy-start | bytes 393220
  27.0 4.2 %copy-start.2 = (f32[2,256]{1,0:T(2,128)S(1)}, f32[2,256]{1,0:T(2,128)}, u32[]{:S(2)}) copy-start(f32[2,256]{1,0:T(2,128)} %value_ref.1) | copy-start | bytes 6148
  27.0 4.1 %copy-start.3 = (f32[2,256]{1,0:T(2,128)S(1)}, f32[2,256]{1,0:T(2,128)}, u32[]{:S(2)}) copy-start(f32[2,256]{1,0:T(2,128)} %error_ref.1) | copy-start | bytes 6148
  27.1 7.4 %collective-permute-start.10 = (f32[128,512]{1,0:T(8,128)S(1)}, f32[128,512]{1,0:T(8,128)S(1)}, u32[]{:S(2)}, u32[]{:S(2)}) collective-permute-start(f32[128,512]{1,0:T(8,128)S(1)} %complete.1.refs_0_), channel_id=1, source_target_pairs={{1,0},{0,1},{3,2},{2,3},{5,4},{4,5},{7,6},{6,7},{9,8},{8,9},{11,10... | collective-permute-start | bytes 786440 | tf_op jit(solution)/shard_map/ppermute | solution.py:397
  29.9 4.6 %copy-start = (f32[32,2,4,1,512]{4,3,2,1,0:T(1,128)S(1)}, f32[32,2,4,1,512]{4,3,2,1,0:T(1,128)}, u32[]{:S(2)}) copy-start(f32[32,2,4,1,512]{4,3,2,1,0:T(1,128)} %param.11) | copy-start | bytes 1572868
  29.9 1.3 %collective-permute-start.8 = (f32[64,256]{1,0:T(8,128)S(1)}, f32[64,256]{1,0:T(8,128)S(1)}, u32[]{:S(2)}, u32[]{:S(2)}) collective-permute-start(f32[64,256]{1,0:T(8,128)S(1)} %gather.1.kept_ref), channel_id=1, source_target_pairs={{0,2},{2,0},{4,6},{6,4},{8,10},{10,8},{12,14},{14,12},{16,18},{18,... | collective-permute-start | bytes 196616 | tf_op jit(solution)/shard_map/ppermute | solution.py:393

commit v8 on v7

--- a/solution.py
+++ b/solution.py
@@ -98,6 +98,15 @@
     packed_ref[rows + chunks : rows + 2 * chunks, :] = spread - half
     for copy in (copies[0], *copies[3:]):
         copy.wait()
+
+
+def keeps_first(parts):
+    rest = lax.axis_index("slab")
+    ones = lax.axis_index("mem") if parts == 2 else 0
+    for _ in range(lax.axis_size("slab").bit_length() - 1):
+        ones = ones + lax.rem(rest, 2)
+        rest = rest // 2
+    return lax.rem(ones, 2) == 0
 
 
 def weights(packed_ref, chunks):
@@ -158,6 +167,7 @@
 
 
 def observe_kernel(
+    parts,
     members,
     fields,
     chunks,
@@ -184,11 +194,11 @@
         for f in range(fields):
             start = (side * fields + f) * members
             observed += jnp.where(kinds == f, picked[start : start + members], 0.0)
-    even = lax.rem(lax.axis_index("slab"), 2) == 0
+    first_here = keeps_first(parts)
     half = observed.shape[1] // 2
     first, second = observed[:, :half], observed[:, half:]
-    keep_ref[...] = jnp.where(even, first, second)
-    send_ref[...] = jnp.where(even, second, first)
+    keep_ref[...] = jnp.where(first_here, first, second)
+    send_ref[...] = jnp.where(first_here, second, first)
 
 
 def sum_kernel(terms_ref, other_ref, *refs):
@@ -253,15 +263,15 @@
     local = members // parts
     own = lax.axis_index("mem")
     own_rows = pl.ds(pl.multiple_of(own * local, local), local)
-    even = lax.rem(lax.axis_index("slab"), 2) == 0
+    first_here = keeps_first(parts)
     half = batches * count // 2
     for d in range(parts):
         owner = lax.rem(own + d, parts)
         rows = pl.ds(pl.multiple_of(owner * local, local), local)
         kept = kept_ref[d * local : (d + 1) * local, :]
         received = received_ref[d * local : (d + 1) * local, :]
-        prior[rows, :half] = jnp.where(even, kept, received)
-        prior[rows, half:] = jnp.where(even, received, kept)
+        prior[rows, :half] = jnp.where(first_here, kept, received)
+        prior[rows, half:] = jnp.where(first_here, received, kept)
     source = lax.broadcasted_iota(jnp.int32, (members, members), 0)
     target = lax.broadcasted_iota(jnp.int32, (members, members), 1)
     turn = (source == lax.rem(target + own * local, members)).astype(F32)
@@ -392,6 +402,18 @@
     def from_slab(array, bit):
         return lax.ppermute(array, "slab", [(i, i ^ bit) for i in range(slabs)])
 
+    def from_other_pair(array, bit):
+        return from_slab(array, bit ^ 1)
+
+    def from_other_mem(array):
+        if parts != 2:
+            return from_partners(array)
+        return [
+            lax.ppermute(
+                array, ("slab", "mem"), [(i ^ 3, i) for i in range(slabs * parts)]
+            )
+        ]
+
     def from_partners(array):
         return [
             lax.ppermute(array, "mem", [((i + d) % parts, i) for i in range(parts)])
@@ -431,7 +453,7 @@
         name="own_row",
     )(packed, inner, *held[:2], taps, kinds)
     keep, send, partial = pl.pallas_call(
-        functools.partial(observe_kernel, *sizes),
+        functools.partial(observe_kernel, parts, *sizes),
         out_shape=(
             shape_of((members, total // 2)),
             shape_of((members, total // 2)),
@@ -452,7 +474,7 @@
     terms = keep + from_slab(send, 1)
     for bit in [1 << k for k in reversed(range(1, slabs.bit_length() - 1))]:
         terms = summed(
-            terms, from_slab(terms, bit), SUM_FLOPS, *([outer_below] if bit == 4 else [])
+            terms, from_other_pair(terms, bit), SUM_FLOPS, *([outer_below] if bit == 4 else [])
         )
     forecast = pl.pallas_call(
         functools.partial(complete_kernel, *sizes),
@@ -469,7 +491,7 @@
         cost_estimate=estimate(GATHER_FLOPS),
         compiler_params=PARAMS,
         name="gather",
-    )(terms, *from_partners(terms))
+    )(terms, *from_other_mem(terms))
     mine = pl.pallas_call(
         functools.partial(solve_kernel, parts),
         out_shape=shape_of((members, all_members)),

time: 36.4 us -> 35.6 us (0.978)
  waiting for transfers between devices: 11.8 us -> 11.4 us
    ppermute x6, waiting for transfers between devices: 10.1 us -> 8.61 us  [from_slab(): return lax.ppermute(array, 'slab', [(i, i ^ bit) for i in range(slabs)])]
    ppermute x3 -> x2, starting transfers between devices: 4.67 us -> 3.47 us  [from_partners(): lax.ppermute(array, 'mem', [((i + d) % parts, i) for i in range(parts)])]
    ppermute x0 -> x1, waiting for transfers between devices: none -> 1.16 us  [from_other_mem(): lax.ppermute(array, ('slab', 'mem'), [(i ^ 3, i) for i in range(slabs * p...]
    ppermute x0 -> x1, starting transfers between devices: none -> 1.14 us  [from_other_mem(): lax.ppermute(array, ('slab', 'mem'), [(i ^ 3, i) for i in range(slabs * p...]
    ppermute x3 -> x2, waiting for transfers between devices: 1.68 us -> 1.63 us  [from_partners(): lax.ppermute(array, 'mem', [((i + d) % parts, i) for i in range(parts)])]
  transfers between devices with their start and end apart: 11 -> 11, of which waited for: 6 -> 7; matrix products, arithmetic and copies ran while one was open for 0% -> 0% of each run, Pallas kernels for 13% -> 14%
where the time goes in v8:
time: 35.6 us; the launch traced here: 35.5 us
  starting transfers between devices  16.4 us (46%)
  waiting for transfers between devices  11.4 us (32%)
  Pallas kernels  7.59 us (21%)
    ppermute x6, starting transfers between devices, from_slab(): return lax.ppermute(array, 'slab', [(i, i ^ bit) for i in range(slabs)])  10.4 us
    ppermute x6, waiting for transfers between devices, from_slab(): return lax.ppermute(array, 'slab', [(i, i ^ bit) for i in range(slabs)])  8.61 us
    ppermute x2, starting transfers between devices, from_partners(): lax.ppermute(array, 'mem', [((i + d) % parts, i) for i in range(parts)])  3.47 us
    pallas_call x1, Pallas kernels, shards(): pl.pallas_call(functools.partial(solve_kernel, parts), out_shape=shape_of...  3.32 us
    pallas_call x1, Pallas kernels, shards(): pl.pallas_call(functools.partial(combine_kernel, parts, fields), out_shap...  1.71 us
    ppermute x2, waiting for transfers between devices, from_partners(): lax.ppermute(array, 'mem', [((i + d) % parts, i) for i in range(parts)])  1.63 us
    ppermute x1, waiting for transfers between devices, from_other_mem(): lax.ppermute(array, ('slab', 'mem'), [(i ^ 3, i) for i in range(slabs * p...  1.16 us
    ppermute x1, starting transfers between devices, from_other_mem(): lax.ppermute(array, ('slab', 'mem'), [(i ^ 3, i) for i in range(slabs * p...  1.14 us
  transfers between devices with their start and end apart: 11, of which 7 were waited for; matrix products, arithmetic and copies ran while one was open for 0% of the time, Pallas kernels for 14%

profile of v8, /device:TPU:0, one launch (start us, length us, event | category | flops | bytes accessed | tf_op | source)
XLA Modules:
  0.0 35.5 jit_solution(17280258860748195354)
XLA Ops:
  0.0 1.0 %load.1 = (f32[520,128]{1,0:T(8,128)S(1)}, f32[4,128]{1,0:T(4,128)S(1)}, f32[8,128]{1,0:T(8,128)S(1)}, s32[2,256]{1,0:T(2,128)S(1)}, s32[2,256]{1,0:T(2,128)S(1)}, /*index=5*/s32[2,256]{1,0:T(2,128)S(1)}) custom-call(f32[512,128]{1,0:T(8,128)} %bitcast.7, f32[4,128]{1,0:T(4,128)} %bitcast.9, f32[8,128]{1,0:T(8,128)} %bitcast.8, s32[2,256]{1,0:T(2,128)} %refs_3_.1, ...), custom_call_target="tpu_custom_call" | custom-call | tf_op jit(solution)/shard_map/load/pallas_call | solution.py:426
  1.0 0.5 %collective-permute-start.1 = (f32[520,128]{1,0:T(8,128)S(1)}, f32[520,128]{1,0:T(8,128)S(1)}, u32[]{:S(2)}, u32[]{:S(2)}) collective-permute-start(f32[520,128]{1,0:T(8,128)S(1)} %get-tuple-element.21.packed_ref), channel_id=1, source_target_pairs={{0,2},{2,0},{4,6},{6,4},{8,10},{10,8},{12,14},{14,12},{16,18},{18,... | collective-permute-start | bytes 798728 | tf_op jit(solution)/shard_map/ppermute | solution.py:403
  1.5 0.7 %collective-permute-start = (f32[520,128]{1,0:T(8,128)S(1)}, f32[520,128]{1,0:T(8,128)S(1)}, u32[]{:S(2)}, u32[]{:S(2)}) collective-permute-start(f32[520,128]{1,0:T(8,128)S(1)} %get-tuple-element.21.packed_ref), channel_id=1, source_target_pairs={{2,4},{6,8},{10,12},{14,16},{18,20},{22,24},{26,28},{3,5},{7,9},{1... | collective-permute-start | bytes 798728 | tf_op jit(solution)/shard_map/ppermute | solution.py:435
  2.2 2.6 %collective-permute-start.9 = (f32[1024,128]{1,0:T(8,128)}, f32[1024,128]{1,0:T(8,128)S(1)}, u32[]{:S(2)}, u32[]{:S(2)}) collective-permute-start(f32[1024,128]{1,0:T(8,128)} %bitcast.5), channel_id=1, source_target_pairs={{1,0},{0,1},{3,2},{2,3},{5,4},{4,5},{7,6},{6,7},{9,8},{8,9},{11,10... | collective-permute-start | bytes 1572872 | tf_op jit(solution)/shard_map/ppermute | solution.py:419
  4.8 0.7 %collective-permute-start.5 = (f32[520,128]{1,0:T(8,128)S(1)}, f32[520,128]{1,0:T(8,128)S(1)}, u32[]{:S(2)}, u32[]{:S(2)}) collective-permute-start(f32[520,128]{1,0:T(8,128)S(1)} %get-tuple-element.21.packed_ref), channel_id=1, source_target_pairs={{4,2},{8,6},{12,10},{16,14},{20,18},{24,22},{28,26},{5,3},{9,7},{1... | collective-permute-start | bytes 798728 | tf_op jit(solution)/shard_map/ppermute | solution.py:440
  5.5 0.2 selector.1
  5.7 0.6 %own_row.1 = (f32[128,512]{1,0:T(8,128)S(1)}, f32[128,512]{1,0:T(8,128)S(1)}, f32[32,512]{1,0:T(8,128)S(1)}) custom-call(f32[520,128]{1,0:T(8,128)S(1)} %get-tuple-element.21.packed_ref, f32[520,128]{1,0:T(8,128)S(1)} %collective-permute-done.1.inner_ref, f32[4,128]{1,0:T(4,128)S(1)} %get-tuple-element.22.spread_ref, ...), custom_call_target="tpu_custom_call" | custom-call | flops 1 | tf_op jit(solution)/shard_map/own_row/pallas_call | solution.py:448
  6.3 0.6 %observe.1 = (f32[32,256]{1,0:T(8,128)S(1)}, f32[32,256]{1,0:T(8,128)S(1)}, f32[128,512]{1,0:T(8,128)S(1)}) custom-call(f32[520,128]{1,0:T(8,128)S(1)} %get-tuple-element.21.packed_ref, f32[520,128]{1,0:T(8,128)S(1)} %collective-permute-done.outer_ref, f32[128,512]{1,0:T(8,128)S(1)} %get-tuple-element.29.part_ref, ...), custom_call_target="tpu_custom_call" | custom-call | tf_op jit(solution)/shard_map/observe/pallas_call | solution.py:455
  6.9 3.3 %collective-permute-start.2 = (f32[32,256]{1,0:T(8,128)S(1)}, f32[32,256]{1,0:T(8,128)S(1)}, u32[]{:S(2)}, u32[]{:S(2)}) collective-permute-start(f32[32,256]{1,0:T(8,128)S(1)} %get-tuple-element.33), channel_id=1, source_target_pairs={{0,2},{2,0},{4,6},{6,4},{8,10},{10,8},{12,14},{14,12},{16,18},{18,... | collective-permute-start | bytes 98312 | tf_op jit(solution)/shard_map/ppermute | solution.py:403
  10.2 0.9 %collective-permute-done.2 = f32[32,256]{1,0:T(8,128)S(1)} collective-permute-done((f32[32,256]{1,0:T(8,128)S(1)}, f32[32,256]{1,0:T(8,128)S(1)}, u32[]{:S(2)}, u32[]{:S(2)}) %collective-permute-start.2) | collective-permute-done | bytes 32800 | tf_op jit(solution)/shard_map/ppermute | solution.py:403
  11.1 4.4 %collective-permute-start.3 = (f32[32,256]{1,0:T(8,128)S(1)}, f32[32,256]{1,0:T(8,128)S(1)}, u32[]{:S(2)}, u32[]{:S(2)}) collective-permute-start(f32[32,256]{1,0:T(8,128)S(1)} %add.3.terms_ref), channel_id=1, source_target_pairs={{0,18},{2,16},{4,22},{6,20},{8,26},{10,24},{12,30},{14,28},{16,2},... | collective-permute-start | bytes 98312 | tf_op jit(solution)/shard_map/ppermute | solution.py:403
  15.4 2.0 %collective-permute-done.3.other_ref = f32[32,256]{1,0:T(8,128)S(1)} collective-permute-done((f32[32,256]{1,0:T(8,128)S(1)}, f32[32,256]{1,0:T(8,128)S(1)}, u32[]{:S(2)}, u32[]{:S(2)}) %collective-permute-start.3) | collective-permute-done | bytes 32800 | tf_op jit(solution)/shard_map/ppermute | solution.py:403
  17.5 1.6 %collective-permute-start.4 = (f32[32,256]{1,0:T(8,128)S(1)}, f32[32,256]{1,0:T(8,128)S(1)}, u32[]{:S(2)}, u32[]{:S(2)}) collective-permute-start(f32[32,256]{1,0:T(8,128)S(1)} %sum.3.terms_ref), channel_id=1, source_target_pairs={{0,10},{2,8},{4,14},{6,12},{8,2},{10,0},{12,6},{14,4},{16,26},{18,... | collective-permute-start | bytes 98312 | tf_op jit(solution)/shard_map/ppermute | solution.py:403
  19.0 1.8 %collective-permute-done.4.other_ref = f32[32,256]{1,0:T(8,128)S(1)} collective-permute-done((f32[32,256]{1,0:T(8,128)S(1)}, f32[32,256]{1,0:T(8,128)S(1)}, u32[]{:S(2)}, u32[]{:S(2)}) %collective-permute-start.4) | collective-permute-done | bytes 32800 | tf_op jit(solution)/shard_map/ppermute | solution.py:403
  20.8 0.3 collective-permute-start.6
  21.1 3.1 %collective-permute-done.6.other_ref = f32[32,256]{1,0:T(8,128)S(1)} collective-permute-done((f32[32,256]{1,0:T(8,128)S(1)}, f32[32,256]{1,0:T(8,128)S(1)}, u32[]{:S(2)}, u32[]{:S(2)}) %collective-permute-start.6) | collective-permute-done | bytes 32800 | tf_op jit(solution)/shard_map/ppermute | solution.py:403
  24.1 1.1 %collective-permute-start.7 = (f32[32,256]{1,0:T(8,128)S(1)}, f32[32,256]{1,0:T(8,128)S(1)}, u32[]{:S(2)}, u32[]{:S(2)}) collective-permute-start(f32[32,256]{1,0:T(8,128)S(1)} %sum.5.refs_0_), channel_id=1, source_target_pairs={{3,0},{2,1},{1,2},{0,3},{7,4},{6,5},{5,6},{4,7},{11,8},{10,9},{9,1... | collective-permute-start | bytes 98312 | tf_op jit(solution)/shard_map/ppermute | solution.py:412
  25.4 0.9 %collective-permute-start.10 = (f32[128,512]{1,0:T(8,128)S(1)}, f32[128,512]{1,0:T(8,128)S(1)}, u32[]{:S(2)}, u32[]{:S(2)}) collective-permute-start(f32[128,512]{1,0:T(8,128)S(1)} %complete.1.refs_0_), channel_id=1, source_target_pairs={{1,0},{0,1},{3,2},{2,3},{5,4},{4,5},{7,6},{6,7},{9,8},{8,9},{11,10... | collective-permute-start | bytes 786440 | tf_op jit(solution)/shard_map/ppermute | solution.py:419
  26.3 1.2 %collective-permute-done.7.refs_1_ = f32[32,256]{1,0:T(8,128)S(1)} collective-permute-done((f32[32,256]{1,0:T(8,128)S(1)}, f32[32,256]{1,0:T(8,128)S(1)}, u32[]{:S(2)}, u32[]{:S(2)}) %collective-permute-start.7) | collective-permute-done | bytes 32800 | tf_op jit(solution)/shard_map/ppermute | solution.py:412
  27.5 0.4 %collective-permute-start.8 = (f32[64,256]{1,0:T(8,128)S(1)}, f32[64,256]{1,0:T(8,128)S(1)}, u32[]{:S(2)}, u32[]{:S(2)}) collective-permute-start(f32[64,256]{1,0:T(8,128)S(1)} %gather.1.kept_ref), channel_id=1, source_target_pairs={{0,2},{2,0},{4,6},{6,4},{8,10},{10,8},{12,14},{14,12},{16,18},{18,... | collective-permute-start | bytes 196616 | tf_op jit(solution)/shard_map/ppermute | solution.py:403
  27.9 0.9 %collective-permute-done.8.received_ref = f32[64,256]{1,0:T(8,128)S(1)} collective-permute-done((f32[64,256]{1,0:T(8,128)S(1)}, f32[64,256]{1,0:T(8,128)S(1)}, u32[]{:S(2)}, u32[]{:S(2)}) %collective-permute-start.8) | collective-permute-done | bytes 65568 | tf_op jit(solution)/shard_map/ppermute | solution.py:403
  28.8 3.3 %solve.1.mine_ref = f32[32,64]{1,0:T(8,128)S(1)} custom-call(f32[2,256]{1,0:T(2,128)S(1)} %copy-done.2, f32[2,256]{1,0:T(2,128)S(1)} %copy-done.3, f32[2,64,256]{2,1,0:T(8,128)S(1)} %copy-done.1, f32[64,256]{1,0:T(8,128)S(1)} %gather.1.kept_ref, f32[64,256]{1,0:T(8,128)S(1)} %collective-permute-done.8.received_ref), custom_call_target="tpu_custom_call" | custom-call | flops 2000000000 | tf_op jit(solution)/shard_map/solve/pallas_call | solution.py:495
  32.1 1.6 %collective-permute-done.10.refs_1_ = f32[128,512]{1,0:T(8,128)S(1)} collective-permute-done((f32[128,512]{1,0:T(8,128)S(1)}, f32[128,512]{1,0:T(8,128)S(1)}, u32[]{:S(2)}, u32[]{:S(2)}) %collective-permute-start.10) | collective-permute-done | bytes 262176 | tf_op jit(solution)/shard_map/ppermute | solution.py:419
  33.8 1.7 %combine.1 = f32[32,48,128]{2,1,0:T(8,128)} custom-call(f32[32,64]{1,0:T(8,128)S(1)} %solve.1.mine_ref, f32[128,512]{1,0:T(8,128)S(1)} %complete.1.refs_0_, f32[128,512]{1,0:T(8,128)S(1)} %collective-permute-done.10.refs_1_, f32[1024,128]{1,0:T(8,128)S(1)} %bitcast.6, f32[1024,128]{1,0:T(8,128)S(1)} %collective-permute-done.9._.refs_3_), custom_call_target="tpu_custom_call" | custom-call | tf_op jit(solution)/shard_map/combine/pallas_call | solution.py:506
  (18 shorter events, 0.2 us)
Async XLA Ops:
  1.0 4.6 %collective-permute-start.1 = (f32[520,128]{1,0:T(8,128)S(1)}, f32[520,128]{1,0:T(8,128)S(1)}, u32[]{:S(2)}, u32[]{:S(2)}) collective-permute-start(f32[520,128]{1,0:T(8,128)S(1)} %get-tuple-element.21.packed_ref), channel_id=1, source_target_pairs={{0,2},{2,0},{4,6},{6,4},{8,10},{10,8},{12,14},{14,12},{16,18},{18,... | collective-permute-start | bytes 798728 | tf_op jit(solution)/shard_map/ppermute | solution.py:403
  1.5 4.7 %collective-permute-start = (f32[520,128]{1,0:T(8,128)S(1)}, f32[520,128]{1,0:T(8,128)S(1)}, u32[]{:S(2)}, u32[]{:S(2)}) collective-permute-start(f32[520,128]{1,0:T(8,128)S(1)} %get-tuple-element.21.packed_ref), channel_id=1, source_target_pairs={{2,4},{6,8},{10,12},{14,16},{18,20},{22,24},{26,28},{3,5},{7,9},{1... | collective-permute-start | bytes 798728 | tf_op jit(solution)/shard_map/ppermute | solution.py:435
  2.2 23.1 %collective-permute-start.9 = (f32[1024,128]{1,0:T(8,128)}, f32[1024,128]{1,0:T(8,128)S(1)}, u32[]{:S(2)}, u32[]{:S(2)}) collective-permute-start(f32[1024,128]{1,0:T(8,128)} %bitcast.5), channel_id=1, source_target_pairs={{1,0},{0,1},{3,2},{2,3},{5,4},{4,5},{7,6},{6,7},{9,8},{8,9},{11,10... | collective-permute-start | bytes 1572872 | tf_op jit(solution)/shard_map/ppermute | solution.py:419
  4.8 14.3 %collective-permute-start.5 = (f32[520,128]{1,0:T(8,128)S(1)}, f32[520,128]{1,0:T(8,128)S(1)}, u32[]{:S(2)}, u32[]{:S(2)}) collective-permute-start(f32[520,128]{1,0:T(8,128)S(1)} %get-tuple-element.21.packed_ref), channel_id=1, source_target_pairs={{4,2},{8,6},{12,10},{16,14},{20,18},{24,22},{28,26},{5,3},{9,7},{1... | collective-permute-start | bytes 798728 | tf_op jit(solution)/shard_map/ppermute | solution.py:440
  6.9 4.1 %collective-permute-start.2 = (f32[32,256]{1,0:T(8,128)S(1)}, f32[32,256]{1,0:T(8,128)S(1)}, u32[]{:S(2)}, u32[]{:S(2)}) collective-permute-start(f32[32,256]{1,0:T(8,128)S(1)} %get-tuple-element.33), channel_id=1, source_target_pairs={{0,2},{2,0},{4,6},{6,4},{8,10},{10,8},{12,14},{14,12},{16,18},{18,... | collective-permute-start | bytes 98312 | tf_op jit(solution)/shard_map/ppermute | solution.py:403
  11.1 6.4 %collective-permute-start.3 = (f32[32,256]{1,0:T(8,128)S(1)}, f32[32,256]{1,0:T(8,128)S(1)}, u32[]{:S(2)}, u32[]{:S(2)}) collective-permute-start(f32[32,256]{1,0:T(8,128)S(1)} %add.3.terms_ref), channel_id=1, source_target_pairs={{0,18},{2,16},{4,22},{6,20},{8,26},{10,24},{12,30},{14,28},{16,2},... | collective-permute-start | bytes 98312 | tf_op jit(solution)/shard_map/ppermute | solution.py:403
  17.5 3.3 %collective-permute-start.4 = (f32[32,256]{1,0:T(8,128)S(1)}, f32[32,256]{1,0:T(8,128)S(1)}, u32[]{:S(2)}, u32[]{:S(2)}) collective-permute-start(f32[32,256]{1,0:T(8,128)S(1)} %sum.3.terms_ref), channel_id=1, source_target_pairs={{0,10},{2,8},{4,14},{6,12},{8,2},{10,0},{12,6},{14,4},{16,26},{18,... | collective-permute-start | bytes 98312 | tf_op jit(solution)/shard_map/ppermute | solution.py:403
  20.8 3.3 %collective-permute-start.6 = (f32[32,256]{1,0:T(8,128)S(1)}, f32[32,256]{1,0:T(8,128)S(1)}, u32[]{:S(2)}, u32[]{:S(2)}) collective-permute-start(f32[32,256]{1,0:T(8,128)S(1)} %sum.4.terms_ref), channel_id=1, source_target_pairs={{0,6},{2,4},{4,2},{6,0},{8,14},{10,12},{12,10},{14,8},{16,22},{18,... | collective-permute-start | bytes 98312 | tf_op jit(solution)/shard_map/ppermute | solution.py:403
  24.1 3.3 %collective-permute-start.7 = (f32[32,256]{1,0:T(8,128)S(1)}, f32[32,256]{1,0:T(8,128)S(1)}, u32[]{:S(2)}, u32[]{:S(2)}) collective-permute-start(f32[32,256]{1,0:T(8,128)S(1)} %sum.5.refs_0_), channel_id=1, source_target_pairs={{3,0},{2,1},{1,2},{0,3},{7,4},{6,5},{5,6},{4,7},{11,8},{10,9},{9,1... | collective-permute-start | bytes 98312 | tf_op jit(solution)/shard_map/ppermute | solution.py:412
  25.4 3.4 %copy-start.1 = (f32[2,64,256]{2,1,0:T(8,128)S(1)}, f32[2,64,256]{2,1,0:T(8,128)}, u32[]{:S(2)}) copy-start(f32[2,64,256]{2,1,0:T(8,128)} %noise_ref.1) | copy-start | bytes 393220
  25.4 3.4 %copy-start.2 = (f32[2,256]{1,0:T(2,128)S(1)}, f32[2,256]{1,0:T(2,128)}, u32[]{:S(2)}) copy-start(f32[2,256]{1,0:T(2,128)} %value_ref.1) | copy-start | bytes 6148
  25.4 3.4 %copy-start.3 = (f32[2,256]{1,0:T(2,128)S(1)}, f32[2,256]{1,0:T(2,128)}, u32[]{:S(2)}) copy-start(f32[2,256]{1,0:T(2,128)} %error_ref.1) | copy-start | bytes 6148
  25.4 8.3 %collective-permute-start.10 = (f32[128,512]{1,0:T(8,128)S(1)}, f32[128,512]{1,0:T(8,128)S(1)}, u32[]{:S(2)}, u32[]{:S(2)}) collective-permute-start(f32[128,512]{1,0:T(8,128)S(1)} %complete.1.refs_0_), channel_id=1, source_target_pairs={{1,0},{0,1},{3,2},{2,3},{5,4},{4,5},{7,6},{6,7},{9,8},{8,9},{11,10... | collective-permute-start | bytes 786440 | tf_op jit(solution)/shard_map/ppermute | solution.py:419
  27.5 6.3 %copy-start = (f32[32,2,4,1,512]{4,3,2,1,0:T(1,128)S(1)}, f32[32,2,4,1,512]{4,3,2,1,0:T(1,128)}, u32[]{:S(2)}) copy-start(f32[32,2,4,1,512]{4,3,2,1,0:T(1,128)} %param.11) | copy-start | bytes 1572868
  27.5 1.3 %collective-permute-start.8 = (f32[64,256]{1,0:T(8,128)S(1)}, f32[64,256]{1,0:T(8,128)S(1)}, u32[]{:S(2)}, u32[]{:S(2)}) collective-permute-start(f32[64,256]{1,0:T(8,128)S(1)} %gather.1.kept_ref), channel_id=1, source_target_pairs={{0,2},{2,0},{4,6},{6,4},{8,10},{10,8},{12,14},{14,12},{16,18},{18,... | collective-permute-start | bytes 196616 | tf_op jit(solution)/shard_map/ppermute | solution.py:403

commit v9 on v8

--- a/solution.py
+++ b/solution.py
@@ -15,7 +15,7 @@
 
 
 SELECT_FLOPS = 1
-OWN_FLOPS, SUM_FLOPS, GATHER_FLOPS, SOLVE_FLOPS = 1, 5*10**8, 10**9, 2*10**9
+OWN_FLOPS, SUM_FLOPS, GATHER_FLOPS, SOLVE_FLOPS = 1, (8*10**8,8*10**8,1), 10**8, 5*10**8
 
 
 def estimate(flops):
@@ -131,7 +131,6 @@
     fields,
     chunks,
     packed_ref,
-    inner_ref,
     spread_ref,
     ratio_ref,
     taps_ref,
@@ -148,13 +147,10 @@
     lane = lax.broadcasted_iota(jnp.int32, here.shape, 1)
     left = jnp.where(lane == 0, 0.0, pltpu.roll(here, 1, 1))
     right = jnp.where(lane == width - 1, 0.0, pltpu.roll(here, width - 1, 1))
-    even = lax.rem(lax.axis_index("slab"), 2) == 0
-    above, below = weights(packed_ref, chunks)
     part = (
         here
         + spread * (right + left - 4.0 * here)
         - along_columns * (right - left) * 0.5
-        + jnp.where(even, below, above) * stacked_planes(inner_ref, members, fields, chunks)
     )
     part_ref[...] = part
     picked = picked_values(part, taps_ref[...])
@@ -172,6 +168,7 @@
     fields,
     chunks,
     packed_ref,
+    inner_ref,
     outer_ref,
     part_ref,
     part_obs_ref,
@@ -182,9 +179,12 @@
     send_ref,
     partial_ref,
 ):
-    above, _ = weights(packed_ref, chunks)
+    even = lax.rem(lax.axis_index("slab"), 2) == 0
+    above, below = weights(packed_ref, chunks)
     _, below_of_above = weights(outer_ref, chunks)
-    taken = above * stacked_planes(outer_ref, members, fields, chunks)
+    taken = jnp.where(even, below, above) * stacked_planes(
+        inner_ref, members, fields, chunks
+    ) + above * stacked_planes(outer_ref, members, fields, chunks)
     given = below_of_above * here_ref[...]
     partial_ref[...] = part_ref[...] + taken
     picked = picked_values(jnp.concatenate([taken, given], axis=0), taps_ref[...])
@@ -205,7 +205,7 @@
     refs[-1][...] = terms_ref[...] + other_ref[...]
 
 
-def complete_kernel(members, fields, chunks, partial_ref, outer_ref, packed_ref, _, forecast_ref):
+def complete_kernel(members, fields, chunks, partial_ref, outer_ref, packed_ref, forecast_ref):
     _, below = weights(packed_ref, chunks)
     forecast_ref[...] = partial_ref[...] + below * stacked_planes(
         outer_ref, members, fields, chunks
@@ -433,7 +433,6 @@
         name="load",
     )(*sources)
     outer_above = lax.ppermute(packed, "slab", [(i, i + 1) for i in odd[:-1]])
-    inner = from_slab(packed, 1)
     others_delayed = from_partners(
         lax.optimization_barrier((delayed, packed))[0]
     )
@@ -451,7 +450,8 @@
         compiler_params=PARAMS,
         cost_estimate=estimate(OWN_FLOPS),
         name="own_row",
-    )(packed, inner, *held[:2], taps, kinds)
+    )(packed, *held[:2], taps, kinds)
+    inner = from_slab(packed, 1)
     keep, send, partial = pl.pallas_call(
         functools.partial(observe_kernel, parts, *sizes),
         out_shape=(
@@ -461,7 +461,7 @@
         ),
         compiler_params=PARAMS,
         name="observe",
-    )(packed, outer_above, part, part_obs, here, taps, kinds)
+    )(packed, inner, outer_above, part, part_obs, here, taps, kinds)
     def summed(terms, other, flops, *arrived):
         return pl.pallas_call(
             sum_kernel,
@@ -474,15 +474,20 @@
     terms = keep + from_slab(send, 1)
     for bit in [1 << k for k in reversed(range(1, slabs.bit_length() - 1))]:
         terms = summed(
-            terms, from_other_pair(terms, bit), SUM_FLOPS, *([outer_below] if bit == 4 else [])
+            terms,
+            from_other_pair(terms, bit),
+            SUM_FLOPS[min(slabs // 2 // bit, 4) // 2],
+            *([others_delayed[0]] if bit == 2 else []),
         )
+        if bit == slabs // 2:
+            after_far = terms
     forecast = pl.pallas_call(
         functools.partial(complete_kernel, *sizes),
         out_shape=shape_of(stacked),
         compiler_params=PARAMS,
         name="complete",
     )(
-        lax.optimization_barrier((partial, terms))[0], outer_below, packed, others_delayed[0]
+        lax.optimization_barrier((partial, after_far))[0], outer_below, packed
     )
 
     prior = pl.pallas_call(

time: 35.6 us -> 34.7 us (0.975)
  waiting for transfers between devices: 11.4 us -> 9.77 us
  starting transfers between devices: 16.4 us -> 17 us
    ppermute x2, waiting for transfers between devices: 1.63 us -> 0.01 us  [from_partners(): lax.ppermute(array, 'mem', [((i + d) % parts, i) for i in range(parts)])]
    ppermute x6, waiting for transfers between devices: 8.61 us -> 7.41 us  [from_slab(): return lax.ppermute(array, 'slab', [(i, i ^ bit) for i in range(slabs)])]
    ppermute x1, waiting for transfers between devices: 1.16 us -> 2.35 us  [from_other_mem(): lax.ppermute(array, ('slab', 'mem'), [(i ^ 3, i) for i in range(slabs * p...]
    ppermute x2, starting transfers between devices: 3.47 us -> 3.91 us  [from_partners(): lax.ppermute(array, 'mem', [((i + d) % parts, i) for i in range(parts)])]
  transfers between devices with their start and end apart: 11 -> 11, of which waited for: 7 -> 6; matrix products, arithmetic and copies ran while one was open for 0% -> 0% of each run, Pallas kernels for 14% -> 14%
where the time goes in v9:
time: 34.7 us; the launch traced here: 34.5 us
  starting transfers between devices  17 us (49%)
  waiting for transfers between devices  9.77 us (28%)
  Pallas kernels  7.65 us (22%)
    ppermute x6, starting transfers between devices, from_slab(): return lax.ppermute(array, 'slab', [(i, i ^ bit) for i in range(slabs)])  10.3 us
    ppermute x6, waiting for transfers between devices, from_slab(): return lax.ppermute(array, 'slab', [(i, i ^ bit) for i in range(slabs)])  7.41 us
    ppermute x2, starting transfers between devices, from_partners(): lax.ppermute(array, 'mem', [((i + d) % parts, i) for i in range(parts)])  3.91 us
    pallas_call x1, Pallas kernels, shards(): pl.pallas_call(functools.partial(solve_kernel, parts), out_shape=shape_of...  3.32 us
    ppermute x1, waiting for transfers between devices, from_other_mem(): lax.ppermute(array, ('slab', 'mem'), [(i ^ 3, i) for i in range(slabs * p...  2.35 us
    pallas_call x1, Pallas kernels, shards(): pl.pallas_call(functools.partial(combine_kernel, parts, fields), out_shap...  1.71 us
    ppermute x1, starting transfers between devices, from_other_mem(): lax.ppermute(array, ('slab', 'mem'), [(i ^ 3, i) for i in range(slabs * p...  1.47 us
    pallas_call x1, Pallas kernels, shards(): pl.pallas_call(functools.partial(load_kernel, chunks), out_shape=[shape_o...  1.01 us
  transfers between devices with their start and end apart: 11, of which 6 were waited for; matrix products, arithmetic and copies ran while one was open for 0% of the time, Pallas kernels for 14%

profile of v9, /device:TPU:0, one launch (start us, length us, event | category | flops | bytes accessed | tf_op | source)
XLA Modules:
  0.0 34.5 jit_solution(5325493407942920065)
XLA Ops:
  0.0 1.0 %load.1 = (f32[520,128]{1,0:T(8,128)S(1)}, f32[4,128]{1,0:T(4,128)S(1)}, f32[8,128]{1,0:T(8,128)S(1)}, s32[2,256]{1,0:T(2,128)S(1)}, s32[2,256]{1,0:T(2,128)S(1)}, /*index=5*/s32[2,256]{1,0:T(2,128)S(1)}) custom-call(f32[512,128]{1,0:T(8,128)} %bitcast.7, f32[4,128]{1,0:T(4,128)} %bitcast.9, f32[8,128]{1,0:T(8,128)} %bitcast.8, s32[2,256]{1,0:T(2,128)} %refs_3_.1, ...), custom_call_target="tpu_custom_call" | custom-call | tf_op jit(solution)/shard_map/load/pallas_call | solution.py:426
  1.0 0.5 %collective-permute-start = (f32[520,128]{1,0:T(8,128)S(1)}, f32[520,128]{1,0:T(8,128)S(1)}, u32[]{:S(2)}, u32[]{:S(2)}) collective-permute-start(f32[520,128]{1,0:T(8,128)S(1)} %get-tuple-element.21.packed_ref), channel_id=1, source_target_pairs={{0,2},{2,0},{4,6},{6,4},{8,10},{10,8},{12,14},{14,12},{16,18},{18,... | collective-permute-start | bytes 798728 | tf_op jit(solution)/shard_map/ppermute | solution.py:403
  1.5 0.7 %collective-permute-start.1 = (f32[520,128]{1,0:T(8,128)S(1)}, f32[520,128]{1,0:T(8,128)S(1)}, u32[]{:S(2)}, u32[]{:S(2)}) collective-permute-start(f32[520,128]{1,0:T(8,128)S(1)} %get-tuple-element.21.packed_ref), channel_id=1, source_target_pairs={{2,4},{6,8},{10,12},{14,16},{18,20},{22,24},{26,28},{3,5},{7,9},{1... | collective-permute-start | bytes 798728 | tf_op jit(solution)/shard_map/ppermute | solution.py:435
  2.2 2.6 %collective-permute-start.6 = (f32[1024,128]{1,0:T(8,128)}, f32[1024,128]{1,0:T(8,128)S(1)}, u32[]{:S(2)}, u32[]{:S(2)}) collective-permute-start(f32[1024,128]{1,0:T(8,128)} %bitcast.5), channel_id=1, source_target_pairs={{1,0},{0,1},{3,2},{2,3},{5,4},{4,5},{7,6},{6,7},{9,8},{8,9},{11,10... | collective-permute-start | bytes 1572872 | tf_op jit(solution)/shard_map/ppermute | solution.py:419
  4.8 0.7 %collective-permute-start.9 = (f32[520,128]{1,0:T(8,128)S(1)}, f32[520,128]{1,0:T(8,128)S(1)}, u32[]{:S(2)}, u32[]{:S(2)}) collective-permute-start(f32[520,128]{1,0:T(8,128)S(1)} %get-tuple-element.21.packed_ref), channel_id=1, source_target_pairs={{4,2},{8,6},{12,10},{16,14},{20,18},{24,22},{28,26},{5,3},{9,7},{1... | collective-permute-start | bytes 798728 | tf_op jit(solution)/shard_map/ppermute | solution.py:439
  5.5 0.2 selector.1
  5.7 0.5 %own_row.1 = (f32[128,512]{1,0:T(8,128)S(1)}, f32[128,512]{1,0:T(8,128)S(1)}, f32[32,512]{1,0:T(8,128)S(1)}) custom-call(f32[520,128]{1,0:T(8,128)S(1)} %get-tuple-element.21.packed_ref, f32[4,128]{1,0:T(4,128)S(1)} %get-tuple-element.22.spread_ref, f32[8,128]{1,0:T(8,128)S(1)} %get-tuple-element.23.ratio_ref, ...), custom_call_target="tpu_custom_call" | custom-call | flops 1 | tf_op jit(solution)/shard_map/own_row/pallas_call | solution.py:447
  6.2 0.8 %observe.1 = (f32[32,256]{1,0:T(8,128)S(1)}, f32[32,256]{1,0:T(8,128)S(1)}, f32[128,512]{1,0:T(8,128)S(1)}) custom-call(f32[520,128]{1,0:T(8,128)S(1)} %get-tuple-element.21.packed_ref, f32[520,128]{1,0:T(8,128)S(1)} %collective-permute-done.inner_ref, f32[520,128]{1,0:T(8,128)S(1)} %collective-permute-done.1.outer_ref, ...), custom_call_target="tpu_custom_call" | custom-call | tf_op jit(solution)/shard_map/observe/pallas_call | solution.py:455
  7.0 3.3 %collective-permute-start.2 = (f32[32,256]{1,0:T(8,128)S(1)}, f32[32,256]{1,0:T(8,128)S(1)}, u32[]{:S(2)}, u32[]{:S(2)}) collective-permute-start(f32[32,256]{1,0:T(8,128)S(1)} %get-tuple-element.33), channel_id=1, source_target_pairs={{0,2},{2,0},{4,6},{6,4},{8,10},{10,8},{12,14},{14,12},{16,18},{18,... | collective-permute-start | bytes 98312 | tf_op jit(solution)/shard_map/ppermute | solution.py:403
  10.3 0.9 %collective-permute-done.2 = f32[32,256]{1,0:T(8,128)S(1)} collective-permute-done((f32[32,256]{1,0:T(8,128)S(1)}, f32[32,256]{1,0:T(8,128)S(1)}, u32[]{:S(2)}, u32[]{:S(2)}) %collective-permute-start.2) | collective-permute-done | bytes 32800 | tf_op jit(solution)/shard_map/ppermute | solution.py:403
  11.1 4.4 %collective-permute-start.3 = (f32[32,256]{1,0:T(8,128)S(1)}, f32[32,256]{1,0:T(8,128)S(1)}, u32[]{:S(2)}, u32[]{:S(2)}) collective-permute-start(f32[32,256]{1,0:T(8,128)S(1)} %add.3.terms_ref), channel_id=1, source_target_pairs={{0,18},{2,16},{4,22},{6,20},{8,26},{10,24},{12,30},{14,28},{16,2},... | collective-permute-start | bytes 98312 | tf_op jit(solution)/shard_map/ppermute | solution.py:403
  15.6 2.0 %collective-permute-done.3.other_ref = f32[32,256]{1,0:T(8,128)S(1)} collective-permute-done((f32[32,256]{1,0:T(8,128)S(1)}, f32[32,256]{1,0:T(8,128)S(1)}, u32[]{:S(2)}, u32[]{:S(2)}) %collective-permute-start.3) | collective-permute-done | bytes 32800 | tf_op jit(solution)/shard_map/ppermute | solution.py:403
  17.6 1.4 %collective-permute-start.4 = (f32[32,256]{1,0:T(8,128)S(1)}, f32[32,256]{1,0:T(8,128)S(1)}, u32[]{:S(2)}, u32[]{:S(2)}) collective-permute-start(f32[32,256]{1,0:T(8,128)S(1)} %sum.3.terms_ref), channel_id=1, source_target_pairs={{0,10},{2,8},{4,14},{6,12},{8,2},{10,0},{12,6},{14,4},{16,26},{18,... | collective-permute-start | bytes 98312 | tf_op jit(solution)/shard_map/ppermute | solution.py:403
  19.1 0.1 complete.1.refs_0_
  19.2 1.3 %collective-permute-start.10 = (f32[128,512]{1,0:T(8,128)S(1)}, f32[128,512]{1,0:T(8,128)S(1)}, u32[]{:S(2)}, u32[]{:S(2)}) collective-permute-start(f32[128,512]{1,0:T(8,128)S(1)} %complete.1.refs_0_), channel_id=1, source_target_pairs={{1,0},{0,1},{3,2},{2,3},{5,4},{4,5},{7,6},{6,7},{9,8},{8,9},{11,10... | collective-permute-start | bytes 786440 | tf_op jit(solution)/shard_map/ppermute | solution.py:419
  20.5 0.4 %collective-permute-done.4.other_ref = f32[32,256]{1,0:T(8,128)S(1)} collective-permute-done((f32[32,256]{1,0:T(8,128)S(1)}, f32[32,256]{1,0:T(8,128)S(1)}, u32[]{:S(2)}, u32[]{:S(2)}) %collective-permute-start.4) | collective-permute-done | bytes 32800 | tf_op jit(solution)/shard_map/ppermute | solution.py:403
  21.0 0.3 collective-permute-start.5
  21.2 3.1 %collective-permute-done.5.other_ref = f32[32,256]{1,0:T(8,128)S(1)} collective-permute-done((f32[32,256]{1,0:T(8,128)S(1)}, f32[32,256]{1,0:T(8,128)S(1)}, u32[]{:S(2)}, u32[]{:S(2)}) %collective-permute-start.5) | collective-permute-done | bytes 32800 | tf_op jit(solution)/shard_map/ppermute | solution.py:403
  24.3 1.5 %collective-permute-start.7 = (f32[32,256]{1,0:T(8,128)S(1)}, f32[32,256]{1,0:T(8,128)S(1)}, u32[]{:S(2)}, u32[]{:S(2)}) collective-permute-start(f32[32,256]{1,0:T(8,128)S(1)} %sum.5.refs_0_), channel_id=1, source_target_pairs={{3,0},{2,1},{1,2},{0,3},{7,4},{6,5},{5,6},{4,7},{11,8},{10,9},{9,1... | collective-permute-start | bytes 98312 | tf_op jit(solution)/shard_map/ppermute | solution.py:412
  25.8 2.3 %collective-permute-done.7.refs_1_ = f32[32,256]{1,0:T(8,128)S(1)} collective-permute-done((f32[32,256]{1,0:T(8,128)S(1)}, f32[32,256]{1,0:T(8,128)S(1)}, u32[]{:S(2)}, u32[]{:S(2)}) %collective-permute-start.7) | collective-permute-done | bytes 32800 | tf_op jit(solution)/shard_map/ppermute | solution.py:412
  28.2 0.3 collective-permute-start.8
  28.5 1.0 %collective-permute-done.8.received_ref = f32[64,256]{1,0:T(8,128)S(1)} collective-permute-done((f32[64,256]{1,0:T(8,128)S(1)}, f32[64,256]{1,0:T(8,128)S(1)}, u32[]{:S(2)}, u32[]{:S(2)}) %collective-permute-start.8) | collective-permute-done | bytes 65568 | tf_op jit(solution)/shard_map/ppermute | solution.py:403
  29.5 3.3 %solve.1.mine_ref = f32[32,64]{1,0:T(8,128)S(1)} custom-call(f32[2,256]{1,0:T(2,128)S(1)} %copy-done.2, f32[2,256]{1,0:T(2,128)S(1)} %copy-done.3, f32[2,64,256]{2,1,0:T(8,128)S(1)} %copy-done.1, f32[64,256]{1,0:T(8,128)S(1)} %gather.1.kept_ref, f32[64,256]{1,0:T(8,128)S(1)} %collective-permute-done.8.received_ref), custom_call_target="tpu_custom_call" | custom-call | flops 500000000 | tf_op jit(solution)/shard_map/solve/pallas_call | solution.py:500
  32.8 1.7 %combine.1 = f32[32,48,128]{2,1,0:T(8,128)} custom-call(f32[32,64]{1,0:T(8,128)S(1)} %solve.1.mine_ref, f32[128,512]{1,0:T(8,128)S(1)} %complete.1.refs_0_, f32[128,512]{1,0:T(8,128)S(1)} %collective-permute-done.10.refs_1_, f32[1024,128]{1,0:T(8,128)S(1)} %bitcast.6, f32[1024,128]{1,0:T(8,128)S(1)} %collective-permute-done.6.refs_0_.refs_3_), custom_call_target="tpu_custom_call" | custom-call | tf_op jit(solution)/shard_map/combine/pallas_call | solution.py:511
  (18 shorter events, 0.1 us)
Async XLA Ops:
  1.0 5.2 %collective-permute-start = (f32[520,128]{1,0:T(8,128)S(1)}, f32[520,128]{1,0:T(8,128)S(1)}, u32[]{:S(2)}, u32[]{:S(2)}) collective-permute-start(f32[520,128]{1,0:T(8,128)S(1)} %get-tuple-element.21.packed_ref), channel_id=1, source_target_pairs={{0,2},{2,0},{4,6},{6,4},{8,10},{10,8},{12,14},{14,12},{16,18},{18,... | collective-permute-start | bytes 798728 | tf_op jit(solution)/shard_map/ppermute | solution.py:403
  1.5 4.7 %collective-permute-start.1 = (f32[520,128]{1,0:T(8,128)S(1)}, f32[520,128]{1,0:T(8,128)S(1)}, u32[]{:S(2)}, u32[]{:S(2)}) collective-permute-start(f32[520,128]{1,0:T(8,128)S(1)} %get-tuple-element.21.packed_ref), channel_id=1, source_target_pairs={{2,4},{6,8},{10,12},{14,16},{18,20},{22,24},{26,28},{3,5},{7,9},{1... | collective-permute-start | bytes 798728 | tf_op jit(solution)/shard_map/ppermute | solution.py:435
  2.2 22.1 %collective-permute-start.6 = (f32[1024,128]{1,0:T(8,128)}, f32[1024,128]{1,0:T(8,128)S(1)}, u32[]{:S(2)}, u32[]{:S(2)}) collective-permute-start(f32[1024,128]{1,0:T(8,128)} %bitcast.5), channel_id=1, source_target_pairs={{1,0},{0,1},{3,2},{2,3},{5,4},{4,5},{7,6},{6,7},{9,8},{8,9},{11,10... | collective-permute-start | bytes 1572872 | tf_op jit(solution)/shard_map/ppermute | solution.py:419
  4.8 14.3 %collective-permute-start.9 = (f32[520,128]{1,0:T(8,128)S(1)}, f32[520,128]{1,0:T(8,128)S(1)}, u32[]{:S(2)}, u32[]{:S(2)}) collective-permute-start(f32[520,128]{1,0:T(8,128)S(1)} %get-tuple-element.21.packed_ref), channel_id=1, source_target_pairs={{4,2},{8,6},{12,10},{16,14},{20,18},{24,22},{28,26},{5,3},{9,7},{1... | collective-permute-start | bytes 798728 | tf_op jit(solution)/shard_map/ppermute | solution.py:439
  7.0 4.1 %collective-permute-start.2 = (f32[32,256]{1,0:T(8,128)S(1)}, f32[32,256]{1,0:T(8,128)S(1)}, u32[]{:S(2)}, u32[]{:S(2)}) collective-permute-start(f32[32,256]{1,0:T(8,128)S(1)} %get-tuple-element.33), channel_id=1, source_target_pairs={{0,2},{2,0},{4,6},{6,4},{8,10},{10,8},{12,14},{14,12},{16,18},{18,... | collective-permute-start | bytes 98312 | tf_op jit(solution)/shard_map/ppermute | solution.py:403
  11.1 6.5 %collective-permute-start.3 = (f32[32,256]{1,0:T(8,128)S(1)}, f32[32,256]{1,0:T(8,128)S(1)}, u32[]{:S(2)}, u32[]{:S(2)}) collective-permute-start(f32[32,256]{1,0:T(8,128)S(1)} %add.3.terms_ref), channel_id=1, source_target_pairs={{0,18},{2,16},{4,22},{6,20},{8,26},{10,24},{12,30},{14,28},{16,2},... | collective-permute-start | bytes 98312 | tf_op jit(solution)/shard_map/ppermute | solution.py:403
  17.6 3.3 %collective-permute-start.4 = (f32[32,256]{1,0:T(8,128)S(1)}, f32[32,256]{1,0:T(8,128)S(1)}, u32[]{:S(2)}, u32[]{:S(2)}) collective-permute-start(f32[32,256]{1,0:T(8,128)S(1)} %sum.3.terms_ref), channel_id=1, source_target_pairs={{0,10},{2,8},{4,14},{6,12},{8,2},{10,0},{12,6},{14,4},{16,26},{18,... | collective-permute-start | bytes 98312 | tf_op jit(solution)/shard_map/ppermute | solution.py:403
  19.2 13.7 %collective-permute-start.10 = (f32[128,512]{1,0:T(8,128)S(1)}, f32[128,512]{1,0:T(8,128)S(1)}, u32[]{:S(2)}, u32[]{:S(2)}) collective-permute-start(f32[128,512]{1,0:T(8,128)S(1)} %complete.1.refs_0_), channel_id=1, source_target_pairs={{1,0},{0,1},{3,2},{2,3},{5,4},{4,5},{7,6},{6,7},{9,8},{8,9},{11,10... | collective-permute-start | bytes 786440 | tf_op jit(solution)/shard_map/ppermute | solution.py:419
  21.0 3.3 %collective-permute-start.5 = (f32[32,256]{1,0:T(8,128)S(1)}, f32[32,256]{1,0:T(8,128)S(1)}, u32[]{:S(2)}, u32[]{:S(2)}) collective-permute-start(f32[32,256]{1,0:T(8,128)S(1)} %sum.4.terms_ref), channel_id=1, source_target_pairs={{0,6},{2,4},{4,2},{6,0},{8,14},{10,12},{12,10},{14,8},{16,22},{18,... | collective-permute-start | bytes 98312 | tf_op jit(solution)/shard_map/ppermute | solution.py:403
  24.3 5.2 %copy-start.1 = (f32[2,64,256]{2,1,0:T(8,128)S(1)}, f32[2,64,256]{2,1,0:T(8,128)}, u32[]{:S(2)}) copy-start(f32[2,64,256]{2,1,0:T(8,128)} %noise_ref.1) | copy-start | bytes 393220
  24.3 5.2 %copy-start.2 = (f32[2,256]{1,0:T(2,128)S(1)}, f32[2,256]{1,0:T(2,128)}, u32[]{:S(2)}) copy-start(f32[2,256]{1,0:T(2,128)} %value_ref.1) | copy-start | bytes 6148
  24.3 5.2 %copy-start.3 = (f32[2,256]{1,0:T(2,128)S(1)}, f32[2,256]{1,0:T(2,128)}, u32[]{:S(2)}) copy-start(f32[2,256]{1,0:T(2,128)} %error_ref.1) | copy-start | bytes 6148
  24.3 3.8 %collective-permute-start.7 = (f32[32,256]{1,0:T(8,128)S(1)}, f32[32,256]{1,0:T(8,128)S(1)}, u32[]{:S(2)}, u32[]{:S(2)}) collective-permute-start(f32[32,256]{1,0:T(8,128)S(1)} %sum.5.refs_0_), channel_id=1, source_target_pairs={{3,0},{2,1},{1,2},{0,3},{7,4},{6,5},{5,6},{4,7},{11,8},{10,9},{9,1... | collective-permute-start | bytes 98312 | tf_op jit(solution)/shard_map/ppermute | solution.py:412
  28.2 4.7 %copy-start = (f32[32,2,4,1,512]{4,3,2,1,0:T(1,128)S(1)}, f32[32,2,4,1,512]{4,3,2,1,0:T(1,128)}, u32[]{:S(2)}) copy-start(f32[32,2,4,1,512]{4,3,2,1,0:T(1,128)} %param.11) | copy-start | bytes 1572868
  28.2 1.3 %collective-permute-start.8 = (f32[64,256]{1,0:T(8,128)S(1)}, f32[64,256]{1,0:T(8,128)S(1)}, u32[]{:S(2)}, u32[]{:S(2)}) collective-permute-start(f32[64,256]{1,0:T(8,128)S(1)} %gather.1.kept_ref), channel_id=1, source_target_pairs={{0,2},{2,0},{4,6},{6,4},{8,10},{10,8},{12,14},{14,12},{16,18},{18,... | collective-permute-start | bytes 196616 | tf_op jit(solution)/shard_map/ppermute | solution.py:403

commit v10 on v9

--- a/solution.py
+++ b/solution.py
@@ -15,7 +15,8 @@
 
 
 SELECT_FLOPS = 1
-OWN_FLOPS, SUM_FLOPS, GATHER_FLOPS, SOLVE_FLOPS = 1, (8*10**8,8*10**8,1), 10**8, 5*10**8
+STEPS = 5
+OWN_FLOPS, SUM_FLOPS, GATHER_FLOPS, SOLVE_FLOPS = 1, (7*10**8,7*10**8,1), 10**8, 5*10**8
 
 
 def estimate(flops):
@@ -218,26 +219,34 @@
         refs[-1][d * local : (d + 1) * local, :] = ref[...]
 
 
+def identity(rows, columns):
+    return (
+        lax.broadcasted_iota(jnp.int32, (rows, columns), 0)
+        == lax.broadcasted_iota(jnp.int32, (rows, columns), 1)
+    ).astype(F32)
+
+
+def precise(x, y):
+    return jnp.dot(x, y, precision=HIGHEST, preferred_element_type=F32)
+
+
+def three_pass(x, y):
+    x_high, x_low = split_two(x)
+    y_high, y_low = split_two(y)
+    dot = functools.partial(jnp.dot, preferred_element_type=F32)
+    return dot(x_low, y_high) + dot(x_high, y_low) + dot(x_high, y_high)
+
+
 def solve_transposed(system, right_t, floor):
     size = system.shape[0]
     eye = identity(size, size)
     top = jnp.max(jnp.sum(jnp.abs(system), axis=0, keepdims=True)) + 1.0
     scale = 2.0 / (top + floor)
-    eps = (top - floor) / (top + floor)
-    residual = eye - scale * system
-    answer = scale * right_t
-
-    def more(carry):
-        return carry[0] > 1e-6
-
-    def double(carry):
+    start = ((top - floor) / (top + floor), eye - scale * system, scale * right_t)
+
+    def double(product, carry):
         eps, residual, answer = carry
-        both = jnp.dot(
-            jnp.concatenate([residual, answer], axis=0),
-            residual,
-            precision=HIGHEST,
-            preferred_element_type=F32,
-        )
+        both = product(jnp.concatenate([residual, answer], axis=0), residual)
         square = eps * eps
         share = 1.0 / (2.0 - square)
         return (
@@ -246,58 +255,50 @@
             (answer + both[size:]) * (2.0 * share),
         )
 
-    return lax.while_loop(more, double, (eps, residual, answer))[2]
-
-
-def identity(rows, columns, shift=0):
-    return (
-        lax.broadcasted_iota(jnp.int32, (rows, columns), 0) + shift
-        == lax.broadcasted_iota(jnp.int32, (rows, columns), 1)
-    ).astype(F32)
+    def more(carry):
+        return carry[0] > 1e-6
+
+    def well_conditioned():
+        carry = start
+        for _ in range(STEPS):
+            carry = double(three_pass, carry)
+        return lax.while_loop(more, functools.partial(double, three_pass), carry)[2]
+
+    def otherwise():
+        return lax.while_loop(more, functools.partial(double, precise), start)[2]
+
+    return lax.cond(top < 32.0 * floor, well_conditioned, otherwise)
 
 
 def solve_kernel(
-    parts, value_ref, error_ref, noise_ref, kept_ref, received_ref, mine_ref, prior, whole
+    parts, value_ref, error_ref, noise_ref, kept_ref, received_ref, mine_ref
 ):
     batches, members, count = noise_ref.shape
     local = members // parts
     own = lax.axis_index("mem")
-    own_rows = pl.ds(pl.multiple_of(own * local, local), local)
     first_here = keeps_first(parts)
-    half = batches * count // 2
-    for d in range(parts):
-        owner = lax.rem(own + d, parts)
-        rows = pl.ds(pl.multiple_of(owner * local, local), local)
-        kept = kept_ref[d * local : (d + 1) * local, :]
-        received = received_ref[d * local : (d + 1) * local, :]
-        prior[rows, :half] = jnp.where(first_here, kept, received)
-        prior[rows, half:] = jnp.where(first_here, received, kept)
-    source = lax.broadcasted_iota(jnp.int32, (members, members), 0)
-    target = lax.broadcasted_iota(jnp.int32, (members, members), 1)
-    turn = (source == lax.rem(target + own * local, members)).astype(F32)
-    product_t = turned = None
+    halves = [
+        jnp.where(first_here, kept_ref[...], received_ref[...]),
+        jnp.where(first_here, received_ref[...], kept_ref[...]),
+    ]
+    prior = jnp.concatenate(halves, axis=1)
+    product_t = None
     for b in range(batches):
         last = b == batches - 1
+        wanted = local if last else members
         observed = prior[:, b * count : (b + 1) * count]
         if product_t is not None:
-            both = jnp.dot(
-                product_t,
-                jnp.concatenate([observed, turn], axis=1) if last else observed,
-                precision=HIGHEST,
-                preferred_element_type=F32,
-            )
-            observed, turned = both[:, :count], both[:, count:]
+            observed = precise(product_t, observed)
         share = 1.0 / error_ref[b : b + 1, :]
         scaled = (observed - jnp.mean(observed, axis=0, keepdims=True)) * share
-        if last:
-            whole[...] = observed
-            innovation = (
-                value_ref[b : b + 1, :] * share + noise_ref[b, own_rows, :]
-            ) - whole[own_rows, :] * share
-            eye = identity(local, members, own * local)
-        else:
-            innovation = (value_ref[b : b + 1, :] * share + noise_ref[b]) - observed * share
-            eye = identity(members, members)
+        blocks = []
+        for d in range(wanted // local):
+            owner = lax.rem(own + d, parts)
+            blocks.append(
+                noise_ref[b, pl.ds(pl.multiple_of(owner * local, local), local), :]
+            )
+        noise = jnp.concatenate(blocks, axis=0)
+        innovation = (value_ref[b : b + 1, :] * share + noise) - observed[:wanted] * share
         both = lax.dot_general(
             jnp.concatenate([scaled, innovation], axis=0),
             scaled,
@@ -307,50 +308,49 @@
         )
         system = both[:members] + (members - 1.0) * identity(members, members)
         weights_t = solve_transposed(system, both[members:], members - 1.0)
-        matrix_t = eye + weights_t - jnp.mean(weights_t, axis=1, keepdims=True)
-        if last:
-            mine_ref[...] = jnp.dot(
-                matrix_t,
-                turn if turned is None else turned,
-                precision=HIGHEST,
-                preferred_element_type=F32,
-            )
-        elif product_t is None:
-            product_t = matrix_t
-        else:
-            product_t = jnp.dot(
-                matrix_t, product_t, precision=HIGHEST, preferred_element_type=F32
-            )
+        matrix_t = (
+            identity(wanted, members) + weights_t - jnp.mean(weights_t, axis=1, keepdims=True)
+        )
+        product_t = matrix_t if product_t is None else precise(matrix_t, product_t)
+    mine_ref[...] = product_t
+
+
+def prepare_kernel(parts, *refs):
+    sources, high_ref, low_ref = refs[:parts], refs[parts], refs[parts + 1]
+    lagged = high_ref.shape[1] // LANES
+    local = high_ref.shape[0] // parts
+    for k in range(lagged):
+        held = jnp.concatenate(
+            [ref[pl.ds(k, local, stride=lagged), :] for ref in sources], axis=0
+        )
+        high, low = split_two(held)
+        high_ref[:, k * LANES : (k + 1) * LANES] = high
+        low_ref[:, k * LANES : (k + 1) * LANES] = low
 
 
 def combine_kernel(parts, fields, mine_ref, *refs):
-    forecast_refs, delayed_refs = refs[:parts], refs[parts : 2 * parts]
-    out_ref, done_ref, sems = refs[2 * parts :]
+    forecast_refs = refs[:parts]
+    lagged_high_ref, lagged_low_ref, out_ref, done_ref, sems = refs[parts:]
     local = mine_ref.shape[0]
     high, low = split_two(mine_ref[...])
     left = jnp.concatenate([high, high, low], axis=1)
-    chunks = forecast_refs[0].shape[1] // LANES
+    width = forecast_refs[0].shape[1]
+    chunks = width // LANES
     level = fields * chunks
-    lagged = delayed_refs[0].shape[0] // local
-    planes = level + lagged
+    planes = level + lagged_high_ref.shape[1] // LANES
     copies = []
     for first in [*range(level, planes, level), 0]:
         for f in range(fields):
             start = first + f * chunks
             if first == 0:
-                held = [ref[f * local : (f + 1) * local, :] for ref in forecast_refs]
+                held_high, held_low = split_two(
+                    jnp.concatenate(
+                        [ref[f * local : (f + 1) * local, :] for ref in forecast_refs], axis=0
+                    )
+                )
             else:
-                held = [
-                    jnp.concatenate(
-                        [
-                            ref[pl.ds(start - level + c, local, stride=lagged), :]
-                            for c in range(chunks)
-                        ],
-                        axis=1,
-                    )
-                    for ref in delayed_refs
-                ]
-            held_high, held_low = split_two(jnp.concatenate(held, axis=0))
+                lanes = slice((start - level) * LANES, (start - level) * LANES + width)
+                held_high, held_low = lagged_high_ref[:, lanes], lagged_low_ref[:, lanes]
             result = jnp.dot(
                 left,
                 jnp.concatenate([held_high, held_low, held_high], axis=0),
@@ -500,14 +500,16 @@
     mine = pl.pallas_call(
         functools.partial(solve_kernel, parts),
         out_shape=shape_of((members, all_members)),
-        scratch_shapes=[
-            pltpu.VMEM((all_members, total), F32),
-            pltpu.VMEM((all_members, count), F32),
-        ],
         compiler_params=PARAMS,
         cost_estimate=estimate(SOLVE_FLOPS),
         name="solve",
     )(obs_value, obs_error, obs_noise, prior, from_slab(prior, 1))
+    lagged_parts = pl.pallas_call(
+        functools.partial(prepare_kernel, parts),
+        out_shape=[shape_of((all_members, delayed.size // members), BF16)] * 2,
+        compiler_params=PARAMS,
+        name="prepare",
+    )(delayed, *others_delayed)
     out = pl.pallas_call(
         functools.partial(combine_kernel, parts, fields),
         out_shape=shape_of((members, planes, LANES)),
@@ -518,7 +520,7 @@
         ],
         compiler_params=PARAMS,
         name="combine",
-    )(mine, forecast, *from_partners(forecast), delayed, *others_delayed)
+    )(mine, forecast, *from_partners(forecast), *lagged_parts)
     return out.reshape(members, 1 + lagged, fields, height, width)
 
 

time: 34.7 us -> 34.2 us (0.986)
  waiting for transfers between devices: 9.77 us -> 9.09 us
    pallas_call x0 -> x1, Pallas kernels: none -> 0.71 us  [shards(): pl.pallas_call(functools.partial(prepare_kernel, parts), out_shape=[shape...]
    ppermute x6, waiting for transfers between devices: 7.41 us -> 6.73 us  [from_slab(): return lax.ppermute(array, 'slab', [(i, i ^ bit) for i in range(slabs)])]
  transfers between devices with their start and end apart: 11 -> 11, of which waited for: 6 -> 6; matrix products, arithmetic and copies ran while one was open for 0% -> 0% of each run, Pallas kernels for 14% -> 16%
where the time goes in v10:
time: 34.2 us; the launch traced here: 34 us
  starting transfers between devices  17 us (50%)
  waiting for transfers between devices  9.09 us (27%)
  Pallas kernels  7.77 us (23%)
    ppermute x6, starting transfers between devices, from_slab(): return lax.ppermute(array, 'slab', [(i, i ^ bit) for i in range(slabs)])  10.3 us
    ppermute x6, waiting for transfers between devices, from_slab(): return lax.ppermute(array, 'slab', [(i, i ^ bit) for i in range(slabs)])  6.73 us
    ppermute x2, starting transfers between devices, from_partners(): lax.ppermute(array, 'mem', [((i + d) % parts, i) for i in range(parts)])  3.91 us
    pallas_call x1, Pallas kernels, shards(): pl.pallas_call(functools.partial(solve_kernel, parts), out_shape=shape_of...  3.07 us
    ppermute x1, waiting for transfers between devices, from_other_mem(): lax.ppermute(array, ('slab', 'mem'), [(i ^ 3, i) for i in range(slabs * p...  2.35 us
    ppermute x1, starting transfers between devices, from_other_mem(): lax.ppermute(array, ('slab', 'mem'), [(i ^ 3, i) for i in range(slabs * p...  1.47 us
    pallas_call x1, Pallas kernels, shards(): pl.pallas_call(functools.partial(combine_kernel, parts, fields), out_shap...  1.37 us
    pallas_call x1, Pallas kernels, shards(): pl.pallas_call(functools.partial(load_kernel, chunks), out_shape=[shape_o...  1.01 us
  transfers between devices with their start and end apart: 11, of which 6 were waited for; matrix products, arithmetic and copies ran while one was open for 0% of the time, Pallas kernels for 16%

profile of v10, /device:TPU:0, one launch (start us, length us, event | category | flops | bytes accessed | tf_op | source)
XLA Modules:
  0.0 34.0 jit_solution(17321177936290467178)
XLA Ops:
  0.0 1.0 %load.1 = (f32[520,128]{1,0:T(8,128)S(1)}, f32[4,128]{1,0:T(4,128)S(1)}, f32[8,128]{1,0:T(8,128)S(1)}, s32[2,256]{1,0:T(2,128)S(1)}, s32[2,256]{1,0:T(2,128)S(1)}, /*index=5*/s32[2,256]{1,0:T(2,128)S(1)}) custom-call(f32[512,128]{1,0:T(8,128)} %bitcast.7, f32[4,128]{1,0:T(4,128)} %bitcast.9, f32[8,128]{1,0:T(8,128)} %bitcast.8, s32[2,256]{1,0:T(2,128)} %refs_3_.1, ...), custom_call_target="tpu_custom_call" | custom-call | tf_op jit(solution)/shard_map/load/pallas_call | solution.py:426
  1.0 0.5 %collective-permute-start = (f32[520,128]{1,0:T(8,128)S(1)}, f32[520,128]{1,0:T(8,128)S(1)}, u32[]{:S(2)}, u32[]{:S(2)}) collective-permute-start(f32[520,128]{1,0:T(8,128)S(1)} %get-tuple-element.23.packed_ref), channel_id=1, source_target_pairs={{0,2},{2,0},{4,6},{6,4},{8,10},{10,8},{12,14},{14,12},{16,18},{18,... | collective-permute-start | bytes 798728 | tf_op jit(solution)/shard_map/ppermute | solution.py:403
  1.5 0.7 %collective-permute-start.1 = (f32[520,128]{1,0:T(8,128)S(1)}, f32[520,128]{1,0:T(8,128)S(1)}, u32[]{:S(2)}, u32[]{:S(2)}) collective-permute-start(f32[520,128]{1,0:T(8,128)S(1)} %get-tuple-element.23.packed_ref), channel_id=1, source_target_pairs={{2,4},{6,8},{10,12},{14,16},{18,20},{22,24},{26,28},{3,5},{7,9},{1... | collective-permute-start | bytes 798728 | tf_op jit(solution)/shard_map/ppermute | solution.py:435
  2.2 2.6 %collective-permute-start.6 = (f32[1024,128]{1,0:T(8,128)}, f32[1024,128]{1,0:T(8,128)S(1)}, u32[]{:S(2)}, u32[]{:S(2)}) collective-permute-start(f32[1024,128]{1,0:T(8,128)} %bitcast.5), channel_id=1, source_target_pairs={{1,0},{0,1},{3,2},{2,3},{5,4},{4,5},{7,6},{6,7},{9,8},{8,9},{11,10... | collective-permute-start | bytes 1572872 | tf_op jit(solution)/shard_map/ppermute | solution.py:419
  4.8 0.7 %collective-permute-start.9 = (f32[520,128]{1,0:T(8,128)S(1)}, f32[520,128]{1,0:T(8,128)S(1)}, u32[]{:S(2)}, u32[]{:S(2)}) collective-permute-start(f32[520,128]{1,0:T(8,128)S(1)} %get-tuple-element.23.packed_ref), channel_id=1, source_target_pairs={{4,2},{8,6},{12,10},{16,14},{20,18},{24,22},{28,26},{5,3},{9,7},{1... | collective-permute-start | bytes 798728 | tf_op jit(solution)/shard_map/ppermute | solution.py:439
  5.5 0.2 selector.1
  5.7 0.5 %own_row.1 = (f32[128,512]{1,0:T(8,128)S(1)}, f32[128,512]{1,0:T(8,128)S(1)}, f32[32,512]{1,0:T(8,128)S(1)}) custom-call(f32[520,128]{1,0:T(8,128)S(1)} %get-tuple-element.23.packed_ref, f32[4,128]{1,0:T(4,128)S(1)} %get-tuple-element.24.spread_ref, f32[8,128]{1,0:T(8,128)S(1)} %get-tuple-element.25.ratio_ref, ...), custom_call_target="tpu_custom_call" | custom-call | flops 1 | tf_op jit(solution)/shard_map/own_row/pallas_call | solution.py:447
  6.2 0.8 %observe.1 = (f32[32,256]{1,0:T(8,128)S(1)}, f32[32,256]{1,0:T(8,128)S(1)}, f32[128,512]{1,0:T(8,128)S(1)}) custom-call(f32[520,128]{1,0:T(8,128)S(1)} %get-tuple-element.23.packed_ref, f32[520,128]{1,0:T(8,128)S(1)} %collective-permute-done.inner_ref, f32[520,128]{1,0:T(8,128)S(1)} %collective-permute-done.1.outer_ref, ...), custom_call_target="tpu_custom_call" | custom-call | tf_op jit(solution)/shard_map/observe/pallas_call | solution.py:455
  7.0 3.3 %collective-permute-start.2 = (f32[32,256]{1,0:T(8,128)S(1)}, f32[32,256]{1,0:T(8,128)S(1)}, u32[]{:S(2)}, u32[]{:S(2)}) collective-permute-start(f32[32,256]{1,0:T(8,128)S(1)} %get-tuple-element.35), channel_id=1, source_target_pairs={{0,2},{2,0},{4,6},{6,4},{8,10},{10,8},{12,14},{14,12},{16,18},{18,... | collective-permute-start | bytes 98312 | tf_op jit(solution)/shard_map/ppermute | solution.py:403
  10.3 0.9 %collective-permute-done.2 = f32[32,256]{1,0:T(8,128)S(1)} collective-permute-done((f32[32,256]{1,0:T(8,128)S(1)}, f32[32,256]{1,0:T(8,128)S(1)}, u32[]{:S(2)}, u32[]{:S(2)}) %collective-permute-start.2) | collective-permute-done | bytes 32800 | tf_op jit(solution)/shard_map/ppermute | solution.py:403
  11.1 4.4 %collective-permute-start.3 = (f32[32,256]{1,0:T(8,128)S(1)}, f32[32,256]{1,0:T(8,128)S(1)}, u32[]{:S(2)}, u32[]{:S(2)}) collective-permute-start(f32[32,256]{1,0:T(8,128)S(1)} %add.3.terms_ref), channel_id=1, source_target_pairs={{0,18},{2,16},{4,22},{6,20},{8,26},{10,24},{12,30},{14,28},{16,2},... | collective-permute-start | bytes 98312 | tf_op jit(solution)/shard_map/ppermute | solution.py:403
  15.6 2.0 %collective-permute-done.3.other_ref = f32[32,256]{1,0:T(8,128)S(1)} collective-permute-done((f32[32,256]{1,0:T(8,128)S(1)}, f32[32,256]{1,0:T(8,128)S(1)}, u32[]{:S(2)}, u32[]{:S(2)}) %collective-permute-start.3) | collective-permute-done | bytes 32800 | tf_op jit(solution)/shard_map/ppermute | solution.py:403
  17.6 1.4 %collective-permute-start.4 = (f32[32,256]{1,0:T(8,128)S(1)}, f32[32,256]{1,0:T(8,128)S(1)}, u32[]{:S(2)}, u32[]{:S(2)}) collective-permute-start(f32[32,256]{1,0:T(8,128)S(1)} %sum.3.terms_ref), channel_id=1, source_target_pairs={{0,10},{2,8},{4,14},{6,12},{8,2},{10,0},{12,6},{14,4},{16,26},{18,... | collective-permute-start | bytes 98312 | tf_op jit(solution)/shard_map/ppermute | solution.py:403
  19.2 1.3 %collective-permute-start.10 = (f32[128,512]{1,0:T(8,128)S(1)}, f32[128,512]{1,0:T(8,128)S(1)}, u32[]{:S(2)}, u32[]{:S(2)}) collective-permute-start(f32[128,512]{1,0:T(8,128)S(1)} %complete.1.refs_0_), channel_id=1, source_target_pairs={{1,0},{0,1},{3,2},{2,3},{5,4},{4,5},{7,6},{6,7},{9,8},{8,9},{11,10... | collective-permute-start | bytes 786440 | tf_op jit(solution)/shard_map/ppermute | solution.py:419
  20.5 0.4 %collective-permute-done.4.other_ref = f32[32,256]{1,0:T(8,128)S(1)} collective-permute-done((f32[32,256]{1,0:T(8,128)S(1)}, f32[32,256]{1,0:T(8,128)S(1)}, u32[]{:S(2)}, u32[]{:S(2)}) %collective-permute-start.4) | collective-permute-done | bytes 32800 | tf_op jit(solution)/shard_map/ppermute | solution.py:403
  21.0 0.3 collective-permute-start.5
  21.3 3.1 %collective-permute-done.5.other_ref = f32[32,256]{1,0:T(8,128)S(1)} collective-permute-done((f32[32,256]{1,0:T(8,128)S(1)}, f32[32,256]{1,0:T(8,128)S(1)}, u32[]{:S(2)}, u32[]{:S(2)}) %collective-permute-start.5) | collective-permute-done | bytes 32800 | tf_op jit(solution)/shard_map/ppermute | solution.py:403
  24.4 1.5 %collective-permute-start.7 = (f32[32,256]{1,0:T(8,128)S(1)}, f32[32,256]{1,0:T(8,128)S(1)}, u32[]{:S(2)}, u32[]{:S(2)}) collective-permute-start(f32[32,256]{1,0:T(8,128)S(1)} %sum.5.refs_0_), channel_id=1, source_target_pairs={{3,0},{2,1},{1,2},{0,3},{7,4},{6,5},{5,6},{4,7},{11,8},{10,9},{9,1... | collective-permute-start | bytes 98312 | tf_op jit(solution)/shard_map/ppermute | solution.py:412
  25.8 2.3 %collective-permute-done.7.refs_1_ = f32[32,256]{1,0:T(8,128)S(1)} collective-permute-done((f32[32,256]{1,0:T(8,128)S(1)}, f32[32,256]{1,0:T(8,128)S(1)}, u32[]{:S(2)}, u32[]{:S(2)}) %collective-permute-start.7) | collective-permute-done | bytes 32800 | tf_op jit(solution)/shard_map/ppermute | solution.py:412
  28.2 0.3 collective-permute-start.8
  28.5 0.7 %prepare.1 = (bf16[64,4096]{1,0:T(8,128)(2,1)S(1)}, bf16[64,4096]{1,0:T(8,128)(2,1)S(1)}) custom-call(f32[1024,128]{1,0:T(8,128)S(1)} %bitcast.6, f32[1024,128]{1,0:T(8,128)S(1)} %collective-permute-done.6.refs_0_.refs_1_), custom_call_target="tpu_custom_call" | custom-call | tf_op jit(solution)/shard_map/prepare/pallas_call | solution.py:507
  29.2 0.3 %collective-permute-done.8.received_ref = f32[64,256]{1,0:T(8,128)S(1)} collective-permute-done((f32[64,256]{1,0:T(8,128)S(1)}, f32[64,256]{1,0:T(8,128)S(1)}, u32[]{:S(2)}, u32[]{:S(2)}) %collective-permute-start.8) | collective-permute-done | bytes 65568 | tf_op jit(solution)/shard_map/ppermute | solution.py:403
  29.6 3.1 %solve.1.mine_ref = f32[32,64]{1,0:T(8,128)S(1)} custom-call(f32[2,256]{1,0:T(2,128)S(1)} %copy-done.2, f32[2,256]{1,0:T(2,128)S(1)} %copy-done.3, f32[2,64,256]{2,1,0:T(8,128)S(1)} %copy-done.1, f32[64,256]{1,0:T(8,128)S(1)} %gather.1.kept_ref, f32[64,256]{1,0:T(8,128)S(1)} %collective-permute-done.8.received_ref), custom_call_target="tpu_custom_call" | custom-call | flops 500000000 | tf_op jit(solution)/shard_map/solve/pallas_call | solution.py:500
  32.6 1.4 %combine.1 = f32[32,48,128]{2,1,0:T(8,128)} custom-call(f32[32,64]{1,0:T(8,128)S(1)} %solve.1.mine_ref, f32[128,512]{1,0:T(8,128)S(1)} %complete.1.refs_0_, f32[128,512]{1,0:T(8,128)S(1)} %collective-permute-done.10.refs_1_, bf16[64,4096]{1,0:T(8,128)(2,1)S(1)} %get-tuple-element.39.refs_2_, bf16[64,4096]{1,0:T(8,128)(2,1)S(1)} %get-tuple-element.40.refs_3_), custom_call_target="tpu_custom_call" | custom-call | tf_op jit(solution)/shard_map/combine/pallas_call | solution.py:513
  (19 shorter events, 0.2 us)
Async XLA Ops:
  1.0 5.2 %collective-permute-start = (f32[520,128]{1,0:T(8,128)S(1)}, f32[520,128]{1,0:T(8,128)S(1)}, u32[]{:S(2)}, u32[]{:S(2)}) collective-permute-start(f32[520,128]{1,0:T(8,128)S(1)} %get-tuple-element.23.packed_ref), channel_id=1, source_target_pairs={{0,2},{2,0},{4,6},{6,4},{8,10},{10,8},{12,14},{14,12},{16,18},{18,... | collective-permute-start | bytes 798728 | tf_op jit(solution)/shard_map/ppermute | solution.py:403
  1.5 4.7 %collective-permute-start.1 = (f32[520,128]{1,0:T(8,128)S(1)}, f32[520,128]{1,0:T(8,128)S(1)}, u32[]{:S(2)}, u32[]{:S(2)}) collective-permute-start(f32[520,128]{1,0:T(8,128)S(1)} %get-tuple-element.23.packed_ref), channel_id=1, source_target_pairs={{2,4},{6,8},{10,12},{14,16},{18,20},{22,24},{26,28},{3,5},{7,9},{1... | collective-permute-start | bytes 798728 | tf_op jit(solution)/shard_map/ppermute | solution.py:435
  2.2 22.2 %collective-permute-start.6 = (f32[1024,128]{1,0:T(8,128)}, f32[1024,128]{1,0:T(8,128)S(1)}, u32[]{:S(2)}, u32[]{:S(2)}) collective-permute-start(f32[1024,128]{1,0:T(8,128)} %bitcast.5), channel_id=1, source_target_pairs={{1,0},{0,1},{3,2},{2,3},{5,4},{4,5},{7,6},{6,7},{9,8},{8,9},{11,10... | collective-permute-start | bytes 1572872 | tf_op jit(solution)/shard_map/ppermute | solution.py:419
  4.8 14.3 %collective-permute-start.9 = (f32[520,128]{1,0:T(8,128)S(1)}, f32[520,128]{1,0:T(8,128)S(1)}, u32[]{:S(2)}, u32[]{:S(2)}) collective-permute-start(f32[520,128]{1,0:T(8,128)S(1)} %get-tuple-element.23.packed_ref), channel_id=1, source_target_pairs={{4,2},{8,6},{12,10},{16,14},{20,18},{24,22},{28,26},{5,3},{9,7},{1... | collective-permute-start | bytes 798728 | tf_op jit(solution)/shard_map/ppermute | solution.py:439
  7.0 4.1 %collective-permute-start.2 = (f32[32,256]{1,0:T(8,128)S(1)}, f32[32,256]{1,0:T(8,128)S(1)}, u32[]{:S(2)}, u32[]{:S(2)}) collective-permute-start(f32[32,256]{1,0:T(8,128)S(1)} %get-tuple-element.35), channel_id=1, source_target_pairs={{0,2},{2,0},{4,6},{6,4},{8,10},{10,8},{12,14},{14,12},{16,18},{18,... | collective-permute-start | bytes 98312 | tf_op jit(solution)/shard_map/ppermute | solution.py:403
  11.1 6.5 %collective-permute-start.3 = (f32[32,256]{1,0:T(8,128)S(1)}, f32[32,256]{1,0:T(8,128)S(1)}, u32[]{:S(2)}, u32[]{:S(2)}) collective-permute-start(f32[32,256]{1,0:T(8,128)S(1)} %add.3.terms_ref), channel_id=1, source_target_pairs={{0,18},{2,16},{4,22},{6,20},{8,26},{10,24},{12,30},{14,28},{16,2},... | collective-permute-start | bytes 98312 | tf_op jit(solution)/shard_map/ppermute | solution.py:403
  17.6 3.3 %collective-permute-start.4 = (f32[32,256]{1,0:T(8,128)S(1)}, f32[32,256]{1,0:T(8,128)S(1)}, u32[]{:S(2)}, u32[]{:S(2)}) collective-permute-start(f32[32,256]{1,0:T(8,128)S(1)} %sum.3.terms_ref), channel_id=1, source_target_pairs={{0,10},{2,8},{4,14},{6,12},{8,2},{10,0},{12,6},{14,4},{16,26},{18,... | collective-permute-start | bytes 98312 | tf_op jit(solution)/shard_map/ppermute | solution.py:403
  19.2 13.5 %collective-permute-start.10 = (f32[128,512]{1,0:T(8,128)S(1)}, f32[128,512]{1,0:T(8,128)S(1)}, u32[]{:S(2)}, u32[]{:S(2)}) collective-permute-start(f32[128,512]{1,0:T(8,128)S(1)} %complete.1.refs_0_), channel_id=1, source_target_pairs={{1,0},{0,1},{3,2},{2,3},{5,4},{4,5},{7,6},{6,7},{9,8},{8,9},{11,10... | collective-permute-start | bytes 786440 | tf_op jit(solution)/shard_map/ppermute | solution.py:419
  21.0 7.5 %copy-start = (f32[32,2,4,1,512]{4,3,2,1,0:T(1,128)S(1)}, f32[32,2,4,1,512]{4,3,2,1,0:T(1,128)}, u32[]{:S(2)}) copy-start(f32[32,2,4,1,512]{4,3,2,1,0:T(1,128)} %param.11) | copy-start | bytes 1572868
  21.0 3.4 %collective-permute-start.5 = (f32[32,256]{1,0:T(8,128)S(1)}, f32[32,256]{1,0:T(8,128)S(1)}, u32[]{:S(2)}, u32[]{:S(2)}) collective-permute-start(f32[32,256]{1,0:T(8,128)S(1)} %sum.4.terms_ref), channel_id=1, source_target_pairs={{0,6},{2,4},{4,2},{6,0},{8,14},{10,12},{12,10},{14,8},{16,22},{18,... | collective-permute-start | bytes 98312 | tf_op jit(solution)/shard_map/ppermute | solution.py:403
  24.4 3.8 %collective-permute-start.7 = (f32[32,256]{1,0:T(8,128)S(1)}, f32[32,256]{1,0:T(8,128)S(1)}, u32[]{:S(2)}, u32[]{:S(2)}) collective-permute-start(f32[32,256]{1,0:T(8,128)S(1)} %sum.5.refs_0_), channel_id=1, source_target_pairs={{3,0},{2,1},{1,2},{0,3},{7,4},{6,5},{5,6},{4,7},{11,8},{10,9},{9,1... | collective-permute-start | bytes 98312 | tf_op jit(solution)/shard_map/ppermute | solution.py:412
  28.2 1.4 %copy-start.1 = (f32[2,64,256]{2,1,0:T(8,128)S(1)}, f32[2,64,256]{2,1,0:T(8,128)}, u32[]{:S(2)}) copy-start(f32[2,64,256]{2,1,0:T(8,128)} %noise_ref.1) | copy-start | bytes 393220
  28.2 1.3 %copy-start.2 = (f32[2,256]{1,0:T(2,128)S(1)}, f32[2,256]{1,0:T(2,128)}, u32[]{:S(2)}) copy-start(f32[2,256]{1,0:T(2,128)} %value_ref.1) | copy-start | bytes 6148
  28.2 1.3 %copy-start.3 = (f32[2,256]{1,0:T(2,128)S(1)}, f32[2,256]{1,0:T(2,128)}, u32[]{:S(2)}) copy-start(f32[2,256]{1,0:T(2,128)} %error_ref.1) | copy-start | bytes 6148
  28.2 1.3 %collective-permute-start.8 = (f32[64,256]{1,0:T(8,128)S(1)}, f32[64,256]{1,0:T(8,128)S(1)}, u32[]{:S(2)}, u32[]{:S(2)}) collective-permute-start(f32[64,256]{1,0:T(8,128)S(1)} %gather.1.kept_ref), channel_id=1, source_target_pairs={{0,2},{2,0},{4,6},{6,4},{8,10},{10,8},{12,14},{14,12},{16,18},{18,... | collective-permute-start | bytes 196616 | tf_op jit(solution)/shard_map/ppermute | solution.py:403

commit v11 on v10

--- a/solution.py
+++ b/solution.py
@@ -15,7 +15,6 @@
 
 
 SELECT_FLOPS = 1
-STEPS = 5
 OWN_FLOPS, SUM_FLOPS, GATHER_FLOPS, SOLVE_FLOPS = 1, (7*10**8,7*10**8,1), 10**8, 5*10**8
 
 
@@ -240,9 +239,10 @@
 def solve_transposed(system, right_t, floor):
     size = system.shape[0]
     eye = identity(size, size)
-    top = jnp.max(jnp.sum(jnp.abs(system), axis=0, keepdims=True)) + 1.0
+    sums = jnp.sum(jnp.abs(system), axis=0, keepdims=True)
+    top = jnp.max(sums, axis=1, keepdims=True) + 1.0
     scale = 2.0 / (top + floor)
-    start = ((top - floor) / (top + floor), eye - scale * system, scale * right_t)
+    start = (1.0 - floor * scale, eye - scale * system, scale * right_t)
 
     def double(product, carry):
         eps, residual, answer = carry
@@ -255,24 +255,32 @@
             (answer + both[size:]) * (2.0 * share),
         )
 
-    def more(carry):
-        return carry[0] > 1e-6
-
-    def well_conditioned():
+    def steps(count):
         carry = start
-        for _ in range(STEPS):
+        for _ in range(count):
             carry = double(three_pass, carry)
-        return lax.while_loop(more, functools.partial(double, three_pass), carry)[2]
-
-    def otherwise():
-        return lax.while_loop(more, functools.partial(double, precise), start)[2]
-
-    return lax.cond(top < 32.0 * floor, well_conditioned, otherwise)
-
-
-def solve_kernel(
-    parts, value_ref, error_ref, noise_ref, kept_ref, received_ref, mine_ref
-):
+        return carry[2]
+
+    def loop():
+        return lax.while_loop(
+            lambda carry: jnp.max(carry[0]) > 1e-6, functools.partial(double, precise), start
+        )[2]
+
+    condition = jnp.max(top) / floor
+    return lax.cond(
+        condition < 20.0,
+        lambda: steps(5),
+        lambda: lax.cond(condition < 78.0, lambda: steps(6), loop),
+    )
+
+
+def precise_nt(x, y):
+    return lax.dot_general(
+        x, y, (((1,), (1,)), ((), ())), precision=HIGHEST, preferred_element_type=F32
+    )
+
+
+def solve_kernel(parts, value_ref, error_ref, noise_ref, kept_ref, received_ref, mine_ref):
     batches, members, count = noise_ref.shape
     local = members // parts
     own = lax.axis_index("mem")
@@ -282,32 +290,36 @@
         jnp.where(first_here, received_ref[...], kept_ref[...]),
     ]
     prior = jnp.concatenate(halves, axis=1)
-    product_t = None
+    grams = []
     for b in range(batches):
-        last = b == batches - 1
-        wanted = local if last else members
+        wanted = local if b == batches - 1 else members
         observed = prior[:, b * count : (b + 1) * count]
-        if product_t is not None:
-            observed = precise(product_t, observed)
         share = 1.0 / error_ref[b : b + 1, :]
-        scaled = (observed - jnp.mean(observed, axis=0, keepdims=True)) * share
+        mean = jnp.mean(observed, axis=0, keepdims=True)
+        anomalies = (observed - mean) * share
         blocks = []
         for d in range(wanted // local):
             owner = lax.rem(own + d, parts)
             blocks.append(
                 noise_ref[b, pl.ds(pl.multiple_of(owner * local, local), local), :]
             )
-        noise = jnp.concatenate(blocks, axis=0)
-        innovation = (value_ref[b : b + 1, :] * share + noise) - observed[:wanted] * share
-        both = lax.dot_general(
-            jnp.concatenate([scaled, innovation], axis=0),
-            scaled,
-            (((1,), (1,)), ((), ())),
-            precision=HIGHEST,
-            preferred_element_type=F32,
-        )
-        system = both[:members] + (members - 1.0) * identity(members, members)
-        weights_t = solve_transposed(system, both[members:], members - 1.0)
+        innovation = (value_ref[b : b + 1, :] - mean) * share + jnp.concatenate(blocks, axis=0)
+        both = precise_nt(jnp.concatenate([anomalies, innovation], axis=0), anomalies)
+        grams.append((both[:members], both[members:]))
+    diagonal = (members - 1.0) * identity(members, members)
+    product_t = None
+    for b, (gram, cross) in enumerate(grams):
+        wanted = cross.shape[0]
+        if product_t is None:
+            system, right_t = gram, cross - gram[:wanted]
+        else:
+            centred = product_t - jnp.mean(product_t, axis=0, keepdims=True)
+            both = precise(jnp.concatenate([centred, product_t[:wanted]], axis=0), gram)
+            both = precise_nt(
+                jnp.concatenate([both[:members], cross - both[members:]], axis=0), centred
+            )
+            system, right_t = both[:members], both[members:]
+        weights_t = solve_transposed(system + diagonal, right_t, members - 1.0)
         matrix_t = (
             identity(wanted, members) + weights_t - jnp.mean(weights_t, axis=1, keepdims=True)
         )

time: 34.2 us -> 34 us (level)
  no operation moved by 1% of the time
where the time goes in v11:
time: 34 us; the launch traced here: 33.9 us
  starting transfers between devices  17 us (50%)
  waiting for transfers between devices  9.09 us (27%)
  Pallas kernels  7.64 us (22%)
    ppermute x6, starting transfers between devices, from_slab(): return lax.ppermute(array, 'slab', [(i, i ^ bit) for i in range(slabs)])  10.3 us
    ppermute x6, waiting for transfers between devices, from_slab(): return lax.ppermute(array, 'slab', [(i, i ^ bit) for i in range(slabs)])  6.73 us
    ppermute x2, starting transfers between devices, from_partners(): lax.ppermute(array, 'mem', [((i + d) % parts, i) for i in range(parts)])  3.91 us
    pallas_call x1, Pallas kernels, shards(): pl.pallas_call(functools.partial(solve_kernel, parts), out_shape=shape_of...  2.94 us
    ppermute x1, waiting for transfers between devices, from_other_mem(): lax.ppermute(array, ('slab', 'mem'), [(i ^ 3, i) for i in range(slabs * p...  2.35 us
    ppermute x1, starting transfers between devices, from_other_mem(): lax.ppermute(array, ('slab', 'mem'), [(i ^ 3, i) for i in range(slabs * p...  1.47 us
    pallas_call x1, Pallas kernels, shards(): pl.pallas_call(functools.partial(combine_kernel, parts, fields), out_shap...  1.37 us
    pallas_call x1, Pallas kernels, shards(): pl.pallas_call(functools.partial(load_kernel, chunks), out_shape=[shape_o...  1.01 us
  transfers between devices with their start and end apart: 11, of which 6 were waited for; matrix products, arithmetic and copies ran while one was open for 0% of the time, Pallas kernels for 16%

profile of v11, /device:TPU:0, one launch (start us, length us, event | category | flops | bytes accessed | tf_op | source)
XLA Modules:
  0.0 33.9 jit_solution(11642065345748620721)
XLA Ops:
  0.0 1.0 %load.1 = (f32[520,128]{1,0:T(8,128)S(1)}, f32[4,128]{1,0:T(4,128)S(1)}, f32[8,128]{1,0:T(8,128)S(1)}, s32[2,256]{1,0:T(2,128)S(1)}, s32[2,256]{1,0:T(2,128)S(1)}, /*index=5*/s32[2,256]{1,0:T(2,128)S(1)}) custom-call(f32[512,128]{1,0:T(8,128)} %bitcast.7, f32[4,128]{1,0:T(4,128)} %bitcast.9, f32[8,128]{1,0:T(8,128)} %bitcast.8, s32[2,256]{1,0:T(2,128)} %refs_3_.1, ...), custom_call_target="tpu_custom_call" | custom-call | tf_op jit(solution)/shard_map/load/pallas_call | solution.py:438
  1.0 0.5 %collective-permute-start = (f32[520,128]{1,0:T(8,128)S(1)}, f32[520,128]{1,0:T(8,128)S(1)}, u32[]{:S(2)}, u32[]{:S(2)}) collective-permute-start(f32[520,128]{1,0:T(8,128)S(1)} %get-tuple-element.23.packed_ref), channel_id=1, source_target_pairs={{0,2},{2,0},{4,6},{6,4},{8,10},{10,8},{12,14},{14,12},{16,18},{18,... | collective-permute-start | bytes 798728 | tf_op jit(solution)/shard_map/ppermute | solution.py:415
  1.5 0.7 %collective-permute-start.1 = (f32[520,128]{1,0:T(8,128)S(1)}, f32[520,128]{1,0:T(8,128)S(1)}, u32[]{:S(2)}, u32[]{:S(2)}) collective-permute-start(f32[520,128]{1,0:T(8,128)S(1)} %get-tuple-element.23.packed_ref), channel_id=1, source_target_pairs={{2,4},{6,8},{10,12},{14,16},{18,20},{22,24},{26,28},{3,5},{7,9},{1... | collective-permute-start | bytes 798728 | tf_op jit(solution)/shard_map/ppermute | solution.py:447
  2.2 2.6 %collective-permute-start.6 = (f32[1024,128]{1,0:T(8,128)}, f32[1024,128]{1,0:T(8,128)S(1)}, u32[]{:S(2)}, u32[]{:S(2)}) collective-permute-start(f32[1024,128]{1,0:T(8,128)} %bitcast.5), channel_id=1, source_target_pairs={{1,0},{0,1},{3,2},{2,3},{5,4},{4,5},{7,6},{6,7},{9,8},{8,9},{11,10... | collective-permute-start | bytes 1572872 | tf_op jit(solution)/shard_map/ppermute | solution.py:431
  4.8 0.7 %collective-permute-start.9 = (f32[520,128]{1,0:T(8,128)S(1)}, f32[520,128]{1,0:T(8,128)S(1)}, u32[]{:S(2)}, u32[]{:S(2)}) collective-permute-start(f32[520,128]{1,0:T(8,128)S(1)} %get-tuple-element.23.packed_ref), channel_id=1, source_target_pairs={{4,2},{8,6},{12,10},{16,14},{20,18},{24,22},{28,26},{5,3},{9,7},{1... | collective-permute-start | bytes 798728 | tf_op jit(solution)/shard_map/ppermute | solution.py:451
  5.5 0.2 selector.1
  5.7 0.5 %own_row.1 = (f32[128,512]{1,0:T(8,128)S(1)}, f32[128,512]{1,0:T(8,128)S(1)}, f32[32,512]{1,0:T(8,128)S(1)}) custom-call(f32[520,128]{1,0:T(8,128)S(1)} %get-tuple-element.23.packed_ref, f32[4,128]{1,0:T(4,128)S(1)} %get-tuple-element.24.spread_ref, f32[8,128]{1,0:T(8,128)S(1)} %get-tuple-element.25.ratio_ref, ...), custom_call_target="tpu_custom_call" | custom-call | flops 1 | tf_op jit(solution)/shard_map/own_row/pallas_call | solution.py:459
  6.2 0.8 %observe.1 = (f32[32,256]{1,0:T(8,128)S(1)}, f32[32,256]{1,0:T(8,128)S(1)}, f32[128,512]{1,0:T(8,128)S(1)}) custom-call(f32[520,128]{1,0:T(8,128)S(1)} %get-tuple-element.23.packed_ref, f32[520,128]{1,0:T(8,128)S(1)} %collective-permute-done.inner_ref, f32[520,128]{1,0:T(8,128)S(1)} %collective-permute-done.1.outer_ref, ...), custom_call_target="tpu_custom_call" | custom-call | tf_op jit(solution)/shard_map/observe/pallas_call | solution.py:467
  7.0 3.3 %collective-permute-start.2 = (f32[32,256]{1,0:T(8,128)S(1)}, f32[32,256]{1,0:T(8,128)S(1)}, u32[]{:S(2)}, u32[]{:S(2)}) collective-permute-start(f32[32,256]{1,0:T(8,128)S(1)} %get-tuple-element.35), channel_id=1, source_target_pairs={{0,2},{2,0},{4,6},{6,4},{8,10},{10,8},{12,14},{14,12},{16,18},{18,... | collective-permute-start | bytes 98312 | tf_op jit(solution)/shard_map/ppermute | solution.py:415
  10.3 0.9 %collective-permute-done.2 = f32[32,256]{1,0:T(8,128)S(1)} collective-permute-done((f32[32,256]{1,0:T(8,128)S(1)}, f32[32,256]{1,0:T(8,128)S(1)}, u32[]{:S(2)}, u32[]{:S(2)}) %collective-permute-start.2) | collective-permute-done | bytes 32800 | tf_op jit(solution)/shard_map/ppermute | solution.py:415
  11.1 4.4 %collective-permute-start.3 = (f32[32,256]{1,0:T(8,128)S(1)}, f32[32,256]{1,0:T(8,128)S(1)}, u32[]{:S(2)}, u32[]{:S(2)}) collective-permute-start(f32[32,256]{1,0:T(8,128)S(1)} %add.3.terms_ref), channel_id=1, source_target_pairs={{0,18},{2,16},{4,22},{6,20},{8,26},{10,24},{12,30},{14,28},{16,2},... | collective-permute-start | bytes 98312 | tf_op jit(solution)/shard_map/ppermute | solution.py:415
  15.6 2.0 %collective-permute-done.3.other_ref = f32[32,256]{1,0:T(8,128)S(1)} collective-permute-done((f32[32,256]{1,0:T(8,128)S(1)}, f32[32,256]{1,0:T(8,128)S(1)}, u32[]{:S(2)}, u32[]{:S(2)}) %collective-permute-start.3) | collective-permute-done | bytes 32800 | tf_op jit(solution)/shard_map/ppermute | solution.py:415
  17.6 1.4 %collective-permute-start.4 = (f32[32,256]{1,0:T(8,128)S(1)}, f32[32,256]{1,0:T(8,128)S(1)}, u32[]{:S(2)}, u32[]{:S(2)}) collective-permute-start(f32[32,256]{1,0:T(8,128)S(1)} %sum.3.terms_ref), channel_id=1, source_target_pairs={{0,10},{2,8},{4,14},{6,12},{8,2},{10,0},{12,6},{14,4},{16,26},{18,... | collective-permute-start | bytes 98312 | tf_op jit(solution)/shard_map/ppermute | solution.py:415
  19.2 1.3 %collective-permute-start.10 = (f32[128,512]{1,0:T(8,128)S(1)}, f32[128,512]{1,0:T(8,128)S(1)}, u32[]{:S(2)}, u32[]{:S(2)}) collective-permute-start(f32[128,512]{1,0:T(8,128)S(1)} %complete.1.refs_0_), channel_id=1, source_target_pairs={{1,0},{0,1},{3,2},{2,3},{5,4},{4,5},{7,6},{6,7},{9,8},{8,9},{11,10... | collective-permute-start | bytes 786440 | tf_op jit(solution)/shard_map/ppermute | solution.py:431
  20.5 0.4 %collective-permute-done.4.other_ref = f32[32,256]{1,0:T(8,128)S(1)} collective-permute-done((f32[32,256]{1,0:T(8,128)S(1)}, f32[32,256]{1,0:T(8,128)S(1)}, u32[]{:S(2)}, u32[]{:S(2)}) %collective-permute-start.4) | collective-permute-done | bytes 32800 | tf_op jit(solution)/shard_map/ppermute | solution.py:415
  21.0 0.3 collective-permute-start.5
  21.3 3.1 %collective-permute-done.5.other_ref = f32[32,256]{1,0:T(8,128)S(1)} collective-permute-done((f32[32,256]{1,0:T(8,128)S(1)}, f32[32,256]{1,0:T(8,128)S(1)}, u32[]{:S(2)}, u32[]{:S(2)}) %collective-permute-start.5) | collective-permute-done | bytes 32800 | tf_op jit(solution)/shard_map/ppermute | solution.py:415
  24.4 1.5 %collective-permute-start.7 = (f32[32,256]{1,0:T(8,128)S(1)}, f32[32,256]{1,0:T(8,128)S(1)}, u32[]{:S(2)}, u32[]{:S(2)}) collective-permute-start(f32[32,256]{1,0:T(8,128)S(1)} %sum.5.refs_0_), channel_id=1, source_target_pairs={{3,0},{2,1},{1,2},{0,3},{7,4},{6,5},{5,6},{4,7},{11,8},{10,9},{9,1... | collective-permute-start | bytes 98312 | tf_op jit(solution)/shard_map/ppermute | solution.py:424
  25.8 2.3 %collective-permute-done.7.refs_1_ = f32[32,256]{1,0:T(8,128)S(1)} collective-permute-done((f32[32,256]{1,0:T(8,128)S(1)}, f32[32,256]{1,0:T(8,128)S(1)}, u32[]{:S(2)}, u32[]{:S(2)}) %collective-permute-start.7) | collective-permute-done | bytes 32800 | tf_op jit(solution)/shard_map/ppermute | solution.py:424
  28.2 0.3 collective-permute-start.8
  28.5 0.7 %prepare.1 = (bf16[64,4096]{1,0:T(8,128)(2,1)S(1)}, bf16[64,4096]{1,0:T(8,128)(2,1)S(1)}) custom-call(f32[1024,128]{1,0:T(8,128)S(1)} %bitcast.6, f32[1024,128]{1,0:T(8,128)S(1)} %collective-permute-done.6.refs_0_.refs_1_), custom_call_target="tpu_custom_call" | custom-call | tf_op jit(solution)/shard_map/prepare/pallas_call | solution.py:519
  29.2 0.3 %collective-permute-done.8.received_ref = f32[64,256]{1,0:T(8,128)S(1)} collective-permute-done((f32[64,256]{1,0:T(8,128)S(1)}, f32[64,256]{1,0:T(8,128)S(1)}, u32[]{:S(2)}, u32[]{:S(2)}) %collective-permute-start.8) | collective-permute-done | bytes 65568 | tf_op jit(solution)/shard_map/ppermute | solution.py:415
  29.6 2.9 %solve.1.mine_ref = f32[32,64]{1,0:T(8,128)S(1)} custom-call(f32[2,256]{1,0:T(2,128)S(1)} %copy-done.2, f32[2,256]{1,0:T(2,128)S(1)} %copy-done.3, f32[2,64,256]{2,1,0:T(8,128)S(1)} %copy-done.1, f32[64,256]{1,0:T(8,128)S(1)} %gather.1.kept_ref, f32[64,256]{1,0:T(8,128)S(1)} %collective-permute-done.8.received_ref), custom_call_target="tpu_custom_call" | custom-call | flops 500000000 | tf_op jit(solution)/shard_map/solve/pallas_call | solution.py:512
  32.5 1.4 %combine.1 = f32[32,48,128]{2,1,0:T(8,128)} custom-call(f32[32,64]{1,0:T(8,128)S(1)} %solve.1.mine_ref, f32[128,512]{1,0:T(8,128)S(1)} %complete.1.refs_0_, f32[128,512]{1,0:T(8,128)S(1)} %collective-permute-done.10.refs_1_, bf16[64,4096]{1,0:T(8,128)(2,1)S(1)} %get-tuple-element.39.refs_2_, bf16[64,4096]{1,0:T(8,128)(2,1)S(1)} %get-tuple-element.40.refs_3_), custom_call_target="tpu_custom_call" | custom-call | tf_op jit(solution)/shard_map/combine/pallas_call | solution.py:525
  (19 shorter events, 0.2 us)
Async XLA Ops:
  1.0 5.2 %collective-permute-start = (f32[520,128]{1,0:T(8,128)S(1)}, f32[520,128]{1,0:T(8,128)S(1)}, u32[]{:S(2)}, u32[]{:S(2)}) collective-permute-start(f32[520,128]{1,0:T(8,128)S(1)} %get-tuple-element.23.packed_ref), channel_id=1, source_target_pairs={{0,2},{2,0},{4,6},{6,4},{8,10},{10,8},{12,14},{14,12},{16,18},{18,... | collective-permute-start | bytes 798728 | tf_op jit(solution)/shard_map/ppermute | solution.py:415
  1.5 4.7 %collective-permute-start.1 = (f32[520,128]{1,0:T(8,128)S(1)}, f32[520,128]{1,0:T(8,128)S(1)}, u32[]{:S(2)}, u32[]{:S(2)}) collective-permute-start(f32[520,128]{1,0:T(8,128)S(1)} %get-tuple-element.23.packed_ref), channel_id=1, source_target_pairs={{2,4},{6,8},{10,12},{14,16},{18,20},{22,24},{26,28},{3,5},{7,9},{1... | collective-permute-start | bytes 798728 | tf_op jit(solution)/shard_map/ppermute | solution.py:447
  2.2 22.2 %collective-permute-start.6 = (f32[1024,128]{1,0:T(8,128)}, f32[1024,128]{1,0:T(8,128)S(1)}, u32[]{:S(2)}, u32[]{:S(2)}) collective-permute-start(f32[1024,128]{1,0:T(8,128)} %bitcast.5), channel_id=1, source_target_pairs={{1,0},{0,1},{3,2},{2,3},{5,4},{4,5},{7,6},{6,7},{9,8},{8,9},{11,10... | collective-permute-start | bytes 1572872 | tf_op jit(solution)/shard_map/ppermute | solution.py:431
  4.8 14.3 %collective-permute-start.9 = (f32[520,128]{1,0:T(8,128)S(1)}, f32[520,128]{1,0:T(8,128)S(1)}, u32[]{:S(2)}, u32[]{:S(2)}) collective-permute-start(f32[520,128]{1,0:T(8,128)S(1)} %get-tuple-element.23.packed_ref), channel_id=1, source_target_pairs={{4,2},{8,6},{12,10},{16,14},{20,18},{24,22},{28,26},{5,3},{9,7},{1... | collective-permute-start | bytes 798728 | tf_op jit(solution)/shard_map/ppermute | solution.py:451
  7.0 4.1 %collective-permute-start.2 = (f32[32,256]{1,0:T(8,128)S(1)}, f32[32,256]{1,0:T(8,128)S(1)}, u32[]{:S(2)}, u32[]{:S(2)}) collective-permute-start(f32[32,256]{1,0:T(8,128)S(1)} %get-tuple-element.35), channel_id=1, source_target_pairs={{0,2},{2,0},{4,6},{6,4},{8,10},{10,8},{12,14},{14,12},{16,18},{18,... | collective-permute-start | bytes 98312 | tf_op jit(solution)/shard_map/ppermute | solution.py:415
  11.1 6.5 %collective-permute-start.3 = (f32[32,256]{1,0:T(8,128)S(1)}, f32[32,256]{1,0:T(8,128)S(1)}, u32[]{:S(2)}, u32[]{:S(2)}) collective-permute-start(f32[32,256]{1,0:T(8,128)S(1)} %add.3.terms_ref), channel_id=1, source_target_pairs={{0,18},{2,16},{4,22},{6,20},{8,26},{10,24},{12,30},{14,28},{16,2},... | collective-permute-start | bytes 98312 | tf_op jit(solution)/shard_map/ppermute | solution.py:415
  17.6 3.3 %collective-permute-start.4 = (f32[32,256]{1,0:T(8,128)S(1)}, f32[32,256]{1,0:T(8,128)S(1)}, u32[]{:S(2)}, u32[]{:S(2)}) collective-permute-start(f32[32,256]{1,0:T(8,128)S(1)} %sum.3.terms_ref), channel_id=1, source_target_pairs={{0,10},{2,8},{4,14},{6,12},{8,2},{10,0},{12,6},{14,4},{16,26},{18,... | collective-permute-start | bytes 98312 | tf_op jit(solution)/shard_map/ppermute | solution.py:415
  19.2 13.3 %collective-permute-start.10 = (f32[128,512]{1,0:T(8,128)S(1)}, f32[128,512]{1,0:T(8,128)S(1)}, u32[]{:S(2)}, u32[]{:S(2)}) collective-permute-start(f32[128,512]{1,0:T(8,128)S(1)} %complete.1.refs_0_), channel_id=1, source_target_pairs={{1,0},{0,1},{3,2},{2,3},{5,4},{4,5},{7,6},{6,7},{9,8},{8,9},{11,10... | collective-permute-start | bytes 786440 | tf_op jit(solution)/shard_map/ppermute | solution.py:431
  21.0 7.5 %copy-start = (f32[32,2,4,1,512]{4,3,2,1,0:T(1,128)S(1)}, f32[32,2,4,1,512]{4,3,2,1,0:T(1,128)}, u32[]{:S(2)}) copy-start(f32[32,2,4,1,512]{4,3,2,1,0:T(1,128)} %param.11) | copy-start | bytes 1572868
  21.0 3.4 %collective-permute-start.5 = (f32[32,256]{1,0:T(8,128)S(1)}, f32[32,256]{1,0:T(8,128)S(1)}, u32[]{:S(2)}, u32[]{:S(2)}) collective-permute-start(f32[32,256]{1,0:T(8,128)S(1)} %sum.4.terms_ref), channel_id=1, source_target_pairs={{0,6},{2,4},{4,2},{6,0},{8,14},{10,12},{12,10},{14,8},{16,22},{18,... | collective-permute-start | bytes 98312 | tf_op jit(solution)/shard_map/ppermute | solution.py:415
  24.4 3.8 %collective-permute-start.7 = (f32[32,256]{1,0:T(8,128)S(1)}, f32[32,256]{1,0:T(8,128)S(1)}, u32[]{:S(2)}, u32[]{:S(2)}) collective-permute-start(f32[32,256]{1,0:T(8,128)S(1)} %sum.5.refs_0_), channel_id=1, source_target_pairs={{3,0},{2,1},{1,2},{0,3},{7,4},{6,5},{5,6},{4,7},{11,8},{10,9},{9,1... | collective-permute-start | bytes 98312 | tf_op jit(solution)/shard_map/ppermute | solution.py:424
  28.2 1.4 %copy-start.1 = (f32[2,64,256]{2,1,0:T(8,128)S(1)}, f32[2,64,256]{2,1,0:T(8,128)}, u32[]{:S(2)}) copy-start(f32[2,64,256]{2,1,0:T(8,128)} %noise_ref.1) | copy-start | bytes 393220
  28.2 1.3 %copy-start.2 = (f32[2,256]{1,0:T(2,128)S(1)}, f32[2,256]{1,0:T(2,128)}, u32[]{:S(2)}) copy-start(f32[2,256]{1,0:T(2,128)} %value_ref.1) | copy-start | bytes 6148
  28.2 1.3 %copy-start.3 = (f32[2,256]{1,0:T(2,128)S(1)}, f32[2,256]{1,0:T(2,128)}, u32[]{:S(2)}) copy-start(f32[2,256]{1,0:T(2,128)} %error_ref.1) | copy-start | bytes 6148
  28.2 1.3 %collective-permute-start.8 = (f32[64,256]{1,0:T(8,128)S(1)}, f32[64,256]{1,0:T(8,128)S(1)}, u32[]{:S(2)}, u32[]{:S(2)}) collective-permute-start(f32[64,256]{1,0:T(8,128)S(1)} %gather.1.kept_ref), channel_id=1, source_target_pairs={{0,2},{2,0},{4,6},{6,4},{8,10},{10,8},{12,14},{14,12},{16,18},{18,... | collective-permute-start | bytes 196616 | tf_op jit(solution)/shard_map/ppermute | solution.py:415

commit v12 on v11

--- a/solution.py
+++ b/solution.py
@@ -168,8 +168,7 @@
     fields,
     chunks,
     packed_ref,
-    inner_ref,
-    outer_ref,
+    up_ref,
     part_ref,
     part_obs_ref,
     here_ref,
@@ -179,12 +178,9 @@
     send_ref,
     partial_ref,
 ):
-    even = lax.rem(lax.axis_index("slab"), 2) == 0
-    above, below = weights(packed_ref, chunks)
-    _, below_of_above = weights(outer_ref, chunks)
-    taken = jnp.where(even, below, above) * stacked_planes(
-        inner_ref, members, fields, chunks
-    ) + above * stacked_planes(outer_ref, members, fields, chunks)
+    above, _ = weights(packed_ref, chunks)
+    _, below_of_above = weights(up_ref, chunks)
+    taken = above * stacked_planes(up_ref, members, fields, chunks)
     given = below_of_above * here_ref[...]
     partial_ref[...] = part_ref[...] + taken
     picked = picked_values(jnp.concatenate([taken, given], axis=0), taps_ref[...])
@@ -205,10 +201,10 @@
     refs[-1][...] = terms_ref[...] + other_ref[...]
 
 
-def complete_kernel(members, fields, chunks, partial_ref, outer_ref, packed_ref, forecast_ref):
+def complete_kernel(members, fields, chunks, partial_ref, down_ref, packed_ref, forecast_ref):
     _, below = weights(packed_ref, chunks)
     forecast_ref[...] = partial_ref[...] + below * stacked_planes(
-        outer_ref, members, fields, chunks
+        down_ref, members, fields, chunks
     )
 
 
@@ -409,8 +405,6 @@
     hbm = pl.BlockSpec(memory_space=pltpu.HBM)
     sizes = (members, fields, chunks)
 
-    odd = range(1, slabs, 2)
-
     def from_slab(array, bit):
         return lax.ppermute(array, "slab", [(i, i ^ bit) for i in range(slabs)])
 
@@ -444,11 +438,12 @@
         compiler_params=PARAMS,
         name="load",
     )(*sources)
-    outer_above = lax.ppermute(packed, "slab", [(i, i + 1) for i in odd[:-1]])
+    up = [(i, i + 1) for i in range(slabs - 1)]
+    from_above = lax.ppermute(packed, "slab", up)
     others_delayed = from_partners(
         lax.optimization_barrier((delayed, packed))[0]
     )
-    outer_below = lax.ppermute(packed, "slab", [(i + 1, i) for i in odd[:-1]])
+    from_below = lax.ppermute(packed, "slab", [(j, i) for i, j in up])
     taps, kinds = pl.pallas_call(
         selector_kernel,
         out_shape=(shape_of((width, total), BF16), shape_of((2, total), jnp.int32)),
@@ -463,7 +458,6 @@
         cost_estimate=estimate(OWN_FLOPS),
         name="own_row",
     )(packed, *held[:2], taps, kinds)
-    inner = from_slab(packed, 1)
     keep, send, partial = pl.pallas_call(
         functools.partial(observe_kernel, parts, *sizes),
         out_shape=(
@@ -473,7 +467,7 @@
         ),
         compiler_params=PARAMS,
         name="observe",
-    )(packed, inner, outer_above, part, part_obs, here, taps, kinds)
+    )(packed, from_above, part, part_obs, here, taps, kinds)
     def summed(terms, other, flops, *arrived):
         return pl.pallas_call(
             sum_kernel,
@@ -499,7 +493,7 @@
         compiler_params=PARAMS,
         name="complete",
     )(
-        lax.optimization_barrier((partial, after_far))[0], outer_below, packed
+        lax.optimization_barrier((partial, after_far))[0], from_below, packed
     )
 
     prior = pl.pallas_call(

time: 34 us -> 33.9 us (level)
    ppermute x2, starting transfers between devices: 1.33 us -> 3.65 us  [the longest x1 2.37 us: shards(): from_above = lax.ppermute(packed, 'slab', up)]
    ppermute x6 -> x5, starting transfers between devices: 10.3 us -> 8.33 us  [from_slab(): return lax.ppermute(array, 'slab', [(i, i ^ bit) for i in range(slabs)])]
    ppermute x6 -> x5, waiting for transfers between devices: 6.73 us -> 6.63 us  [from_slab(): return lax.ppermute(array, 'slab', [(i, i ^ bit) for i in range(slabs)])]
  transfers between devices with their start and end apart: 11 -> 10, of which waited for: 6 -> 6; matrix products, arithmetic and copies ran while one was open for 0% -> 0% of each run, Pallas kernels for 16% -> 15%
where the time goes in v12:
time: 33.9 us; the launch traced here: 33.7 us
  starting transfers between devices  17 us (50%)
  waiting for transfers between devices  9.01 us (27%)
  Pallas kernels  7.47 us (22%)
    ppermute x5, starting transfers between devices, from_slab(): return lax.ppermute(array, 'slab', [(i, i ^ bit) for i in range(slabs)])  8.33 us
    ppermute x5, waiting for transfers between devices, from_slab(): return lax.ppermute(array, 'slab', [(i, i ^ bit) for i in range(slabs)])  6.63 us
    ppermute x2, starting transfers between devices, from_partners(): lax.ppermute(array, 'mem', [((i + d) % parts, i) for i in range(parts)])  3.59 us
    pallas_call x1, Pallas kernels, shards(): pl.pallas_call(functools.partial(solve_kernel, parts), out_shape=shape_of...  2.94 us
    ppermute x1, starting transfers between devices, shards(): from_above = lax.ppermute(packed, 'slab', up)  2.37 us
    ppermute x1, waiting for transfers between devices, from_other_mem(): lax.ppermute(array, ('slab', 'mem'), [(i ^ 3, i) for i in range(slabs * p...  2.37 us
    ppermute x1, starting transfers between devices, from_other_mem(): lax.ppermute(array, ('slab', 'mem'), [(i ^ 3, i) for i in range(slabs * p...  1.47 us
    pallas_call x1, Pallas kernels, shards(): pl.pallas_call(functools.partial(combine_kernel, parts, fields), out_shap...  1.36 us
  transfers between devices with their start and end apart: 10, of which 6 were waited for; matrix products, arithmetic and copies ran while one was open for 0% of the time, Pallas kernels for 15%

profile of v12, /device:TPU:0, one launch (start us, length us, event | category | flops | bytes accessed | tf_op | source)
XLA Modules:
  0.0 33.7 jit_solution(7130096044006221534)
XLA Ops:
  0.0 1.0 %load.1 = (f32[520,128]{1,0:T(8,128)S(1)}, f32[4,128]{1,0:T(4,128)S(1)}, f32[8,128]{1,0:T(8,128)S(1)}, s32[2,256]{1,0:T(2,128)S(1)}, s32[2,256]{1,0:T(2,128)S(1)}, /*index=5*/s32[2,256]{1,0:T(2,128)S(1)}) custom-call(f32[512,128]{1,0:T(8,128)} %bitcast.7, f32[4,128]{1,0:T(4,128)} %bitcast.9, f32[8,128]{1,0:T(8,128)} %bitcast.8, s32[2,256]{1,0:T(2,128)} %refs_3_.1, ...), custom_call_target="tpu_custom_call" | custom-call | tf_op jit(solution)/shard_map/load/pallas_call | solution.py:432
  1.0 2.4 %collective-permute-start = (f32[520,128]{1,0:T(8,128)S(1)}, f32[520,128]{1,0:T(8,128)S(1)}, u32[]{:S(2)}, u32[]{:S(2)}) collective-permute-start(f32[520,128]{1,0:T(8,128)S(1)} %get-tuple-element.23.packed_ref), channel_id=1, source_target_pairs={{0,2},{2,4},{4,6},{6,8},{8,10},{10,12},{12,14},{14,16},{16,18},{18... | collective-permute-start | bytes 798728 | tf_op jit(solution)/shard_map/ppermute | solution.py:442
  3.4 2.4 %collective-permute-start.5 = (f32[1024,128]{1,0:T(8,128)}, f32[1024,128]{1,0:T(8,128)S(1)}, u32[]{:S(2)}, u32[]{:S(2)}) collective-permute-start(f32[1024,128]{1,0:T(8,128)} %bitcast.5), channel_id=1, source_target_pairs={{1,0},{0,1},{3,2},{2,3},{5,4},{4,5},{7,6},{6,7},{9,8},{8,9},{11,10... | collective-permute-start | bytes 1572872 | tf_op jit(solution)/shard_map/ppermute | solution.py:425
  5.8 1.3 %collective-permute-start.8 = (f32[520,128]{1,0:T(8,128)S(1)}, f32[520,128]{1,0:T(8,128)S(1)}, u32[]{:S(2)}, u32[]{:S(2)}) collective-permute-start(f32[520,128]{1,0:T(8,128)S(1)} %get-tuple-element.23.packed_ref), channel_id=1, source_target_pairs={{2,0},{4,2},{6,4},{8,6},{10,8},{12,10},{14,12},{16,14},{18,16},{20... | collective-permute-start | bytes 798728 | tf_op jit(solution)/shard_map/ppermute | solution.py:446
  7.1 0.2 selector.1
  7.3 0.5 %own_row.1 = (f32[128,512]{1,0:T(8,128)S(1)}, f32[128,512]{1,0:T(8,128)S(1)}, f32[32,512]{1,0:T(8,128)S(1)}) custom-call(f32[520,128]{1,0:T(8,128)S(1)} %get-tuple-element.23.packed_ref, f32[4,128]{1,0:T(4,128)S(1)} %get-tuple-element.24.spread_ref, f32[8,128]{1,0:T(8,128)S(1)} %get-tuple-element.25.ratio_ref, ...), custom_call_target="tpu_custom_call" | custom-call | flops 1 | tf_op jit(solution)/shard_map/own_row/pallas_call | solution.py:454
  7.8 0.6 %observe.1 = (f32[32,256]{1,0:T(8,128)S(1)}, f32[32,256]{1,0:T(8,128)S(1)}, f32[128,512]{1,0:T(8,128)S(1)}) custom-call(f32[520,128]{1,0:T(8,128)S(1)} %get-tuple-element.23.packed_ref, f32[520,128]{1,0:T(8,128)S(1)} %collective-permute-done.up_ref, f32[128,512]{1,0:T(8,128)S(1)} %get-tuple-element.31.part_ref, ...), custom_call_target="tpu_custom_call" | custom-call | tf_op jit(solution)/shard_map/observe/pallas_call | solution.py:461
  8.4 2.2 %collective-permute-start.1 = (f32[32,256]{1,0:T(8,128)S(1)}, f32[32,256]{1,0:T(8,128)S(1)}, u32[]{:S(2)}, u32[]{:S(2)}) collective-permute-start(f32[32,256]{1,0:T(8,128)S(1)} %get-tuple-element.35), channel_id=1, source_target_pairs={{0,2},{2,0},{4,6},{6,4},{8,10},{10,8},{12,14},{14,12},{16,18},{18,... | collective-permute-start | bytes 98312 | tf_op jit(solution)/shard_map/ppermute | solution.py:409
  10.6 0.9 %collective-permute-done.1 = f32[32,256]{1,0:T(8,128)S(1)} collective-permute-done((f32[32,256]{1,0:T(8,128)S(1)}, f32[32,256]{1,0:T(8,128)S(1)}, u32[]{:S(2)}, u32[]{:S(2)}) %collective-permute-start.1) | collective-permute-done | bytes 32800 | tf_op jit(solution)/shard_map/ppermute | solution.py:409
  11.5 3.9 %collective-permute-start.2 = (f32[32,256]{1,0:T(8,128)S(1)}, f32[32,256]{1,0:T(8,128)S(1)}, u32[]{:S(2)}, u32[]{:S(2)}) collective-permute-start(f32[32,256]{1,0:T(8,128)S(1)} %add.3.terms_ref), channel_id=1, source_target_pairs={{0,18},{2,16},{4,22},{6,20},{8,26},{10,24},{12,30},{14,28},{16,2},... | collective-permute-start | bytes 98312 | tf_op jit(solution)/shard_map/ppermute | solution.py:409
  15.4 2.0 %collective-permute-done.2.other_ref = f32[32,256]{1,0:T(8,128)S(1)} collective-permute-done((f32[32,256]{1,0:T(8,128)S(1)}, f32[32,256]{1,0:T(8,128)S(1)}, u32[]{:S(2)}, u32[]{:S(2)}) %collective-permute-start.2) | collective-permute-done | bytes 32800 | tf_op jit(solution)/shard_map/ppermute | solution.py:409
  17.4 1.6 %collective-permute-start.3 = (f32[32,256]{1,0:T(8,128)S(1)}, f32[32,256]{1,0:T(8,128)S(1)}, u32[]{:S(2)}, u32[]{:S(2)}) collective-permute-start(f32[32,256]{1,0:T(8,128)S(1)} %sum.3.terms_ref), channel_id=1, source_target_pairs={{0,10},{2,8},{4,14},{6,12},{8,2},{10,0},{12,6},{14,4},{16,26},{18,... | collective-permute-start | bytes 98312 | tf_op jit(solution)/shard_map/ppermute | solution.py:409
  19.0 0.1 complete.1.refs_0_
  19.1 1.2 %collective-permute-start.9 = (f32[128,512]{1,0:T(8,128)S(1)}, f32[128,512]{1,0:T(8,128)S(1)}, u32[]{:S(2)}, u32[]{:S(2)}) collective-permute-start(f32[128,512]{1,0:T(8,128)S(1)} %complete.1.refs_0_), channel_id=1, source_target_pairs={{1,0},{0,1},{3,2},{2,3},{5,4},{4,5},{7,6},{6,7},{9,8},{8,9},{11,10... | collective-permute-start | bytes 786440 | tf_op jit(solution)/shard_map/ppermute | solution.py:425
  20.3 0.5 %collective-permute-done.3.other_ref = f32[32,256]{1,0:T(8,128)S(1)} collective-permute-done((f32[32,256]{1,0:T(8,128)S(1)}, f32[32,256]{1,0:T(8,128)S(1)}, u32[]{:S(2)}, u32[]{:S(2)}) %collective-permute-start.3) | collective-permute-done | bytes 32800 | tf_op jit(solution)/shard_map/ppermute | solution.py:409
  20.7 0.3 %collective-permute-start.4 = (f32[32,256]{1,0:T(8,128)S(1)}, f32[32,256]{1,0:T(8,128)S(1)}, u32[]{:S(2)}, u32[]{:S(2)}) collective-permute-start(f32[32,256]{1,0:T(8,128)S(1)} %sum.4.terms_ref), channel_id=1, source_target_pairs={{0,6},{2,4},{4,2},{6,0},{8,14},{10,12},{12,10},{14,8},{16,22},{18,... | collective-permute-start | bytes 98312 | tf_op jit(solution)/shard_map/ppermute | solution.py:409
  21.1 3.1 %collective-permute-done.4.other_ref = f32[32,256]{1,0:T(8,128)S(1)} collective-permute-done((f32[32,256]{1,0:T(8,128)S(1)}, f32[32,256]{1,0:T(8,128)S(1)}, u32[]{:S(2)}, u32[]{:S(2)}) %collective-permute-start.4) | collective-permute-done | bytes 32800 | tf_op jit(solution)/shard_map/ppermute | solution.py:409
  24.1 1.5 %collective-permute-start.6 = (f32[32,256]{1,0:T(8,128)S(1)}, f32[32,256]{1,0:T(8,128)S(1)}, u32[]{:S(2)}, u32[]{:S(2)}) collective-permute-start(f32[32,256]{1,0:T(8,128)S(1)} %sum.5.refs_0_), channel_id=1, source_target_pairs={{3,0},{2,1},{1,2},{0,3},{7,4},{6,5},{5,6},{4,7},{11,8},{10,9},{9,1... | collective-permute-start | bytes 98312 | tf_op jit(solution)/shard_map/ppermute | solution.py:418
  25.6 2.4 %collective-permute-done.6.refs_1_ = f32[32,256]{1,0:T(8,128)S(1)} collective-permute-done((f32[32,256]{1,0:T(8,128)S(1)}, f32[32,256]{1,0:T(8,128)S(1)}, u32[]{:S(2)}, u32[]{:S(2)}) %collective-permute-start.6) | collective-permute-done | bytes 32800 | tf_op jit(solution)/shard_map/ppermute | solution.py:418
  28.0 0.4 %collective-permute-start.7 = (f32[64,256]{1,0:T(8,128)S(1)}, f32[64,256]{1,0:T(8,128)S(1)}, u32[]{:S(2)}, u32[]{:S(2)}) collective-permute-start(f32[64,256]{1,0:T(8,128)S(1)} %gather.1.kept_ref), channel_id=1, source_target_pairs={{0,2},{2,0},{4,6},{6,4},{8,10},{10,8},{12,14},{14,12},{16,18},{18,... | collective-permute-start | bytes 196616 | tf_op jit(solution)/shard_map/ppermute | solution.py:409
  28.4 0.7 %prepare.1 = (bf16[64,4096]{1,0:T(8,128)(2,1)S(1)}, bf16[64,4096]{1,0:T(8,128)(2,1)S(1)}) custom-call(f32[1024,128]{1,0:T(8,128)S(1)} %bitcast.6, f32[1024,128]{1,0:T(8,128)S(1)} %collective-permute-done.5.refs_0_.refs_1_), custom_call_target="tpu_custom_call" | custom-call | tf_op jit(solution)/shard_map/prepare/pallas_call | solution.py:513
  29.1 0.2 collective-permute-done.7.received_ref
  29.3 2.9 %solve.1.mine_ref = f32[32,64]{1,0:T(8,128)S(1)} custom-call(f32[2,256]{1,0:T(2,128)S(1)} %copy-done.2, f32[2,256]{1,0:T(2,128)S(1)} %copy-done.3, f32[2,64,256]{2,1,0:T(8,128)S(1)} %copy-done.1, f32[64,256]{1,0:T(8,128)S(1)} %gather.1.kept_ref, f32[64,256]{1,0:T(8,128)S(1)} %collective-permute-done.7.received_ref), custom_call_target="tpu_custom_call" | custom-call | flops 500000000 | tf_op jit(solution)/shard_map/solve/pallas_call | solution.py:506
  32.3 1.4 %combine.1 = f32[32,48,128]{2,1,0:T(8,128)} custom-call(f32[32,64]{1,0:T(8,128)S(1)} %solve.1.mine_ref, f32[128,512]{1,0:T(8,128)S(1)} %complete.1.refs_0_, f32[128,512]{1,0:T(8,128)S(1)} %collective-permute-done.9.refs_1_, bf16[64,4096]{1,0:T(8,128)(2,1)S(1)} %get-tuple-element.39.refs_2_, bf16[64,4096]{1,0:T(8,128)(2,1)S(1)} %get-tuple-element.40.refs_3_), custom_call_target="tpu_custom_call" | custom-call | tf_op jit(solution)/shard_map/combine/pallas_call | solution.py:519
  (17 shorter events, 0.1 us)
Async XLA Ops:
  1.0 6.8 %collective-permute-start = (f32[520,128]{1,0:T(8,128)S(1)}, f32[520,128]{1,0:T(8,128)S(1)}, u32[]{:S(2)}, u32[]{:S(2)}) collective-permute-start(f32[520,128]{1,0:T(8,128)S(1)} %get-tuple-element.23.packed_ref), channel_id=1, source_target_pairs={{0,2},{2,4},{4,6},{6,8},{8,10},{10,12},{12,14},{14,16},{16,18},{18... | collective-permute-start | bytes 798728 | tf_op jit(solution)/shard_map/ppermute | solution.py:442
  3.4 20.7 %collective-permute-start.5 = (f32[1024,128]{1,0:T(8,128)}, f32[1024,128]{1,0:T(8,128)S(1)}, u32[]{:S(2)}, u32[]{:S(2)}) collective-permute-start(f32[1024,128]{1,0:T(8,128)} %bitcast.5), channel_id=1, source_target_pairs={{1,0},{0,1},{3,2},{2,3},{5,4},{4,5},{7,6},{6,7},{9,8},{8,9},{11,10... | collective-permute-start | bytes 1572872 | tf_op jit(solution)/shard_map/ppermute | solution.py:425
  5.8 13.2 %collective-permute-start.8 = (f32[520,128]{1,0:T(8,128)S(1)}, f32[520,128]{1,0:T(8,128)S(1)}, u32[]{:S(2)}, u32[]{:S(2)}) collective-permute-start(f32[520,128]{1,0:T(8,128)S(1)} %get-tuple-element.23.packed_ref), channel_id=1, source_target_pairs={{2,0},{4,2},{6,4},{8,6},{10,8},{12,10},{14,12},{16,14},{18,16},{20... | collective-permute-start | bytes 798728 | tf_op jit(solution)/shard_map/ppermute | solution.py:446
  8.4 3.1 %collective-permute-start.1 = (f32[32,256]{1,0:T(8,128)S(1)}, f32[32,256]{1,0:T(8,128)S(1)}, u32[]{:S(2)}, u32[]{:S(2)}) collective-permute-start(f32[32,256]{1,0:T(8,128)S(1)} %get-tuple-element.35), channel_id=1, source_target_pairs={{0,2},{2,0},{4,6},{6,4},{8,10},{10,8},{12,14},{14,12},{16,18},{18,... | collective-permute-start | bytes 98312 | tf_op jit(solution)/shard_map/ppermute | solution.py:409
  11.5 5.9 %collective-permute-start.2 = (f32[32,256]{1,0:T(8,128)S(1)}, f32[32,256]{1,0:T(8,128)S(1)}, u32[]{:S(2)}, u32[]{:S(2)}) collective-permute-start(f32[32,256]{1,0:T(8,128)S(1)} %add.3.terms_ref), channel_id=1, source_target_pairs={{0,18},{2,16},{4,22},{6,20},{8,26},{10,24},{12,30},{14,28},{16,2},... | collective-permute-start | bytes 98312 | tf_op jit(solution)/shard_map/ppermute | solution.py:409
  17.4 3.3 %collective-permute-start.3 = (f32[32,256]{1,0:T(8,128)S(1)}, f32[32,256]{1,0:T(8,128)S(1)}, u32[]{:S(2)}, u32[]{:S(2)}) collective-permute-start(f32[32,256]{1,0:T(8,128)S(1)} %sum.3.terms_ref), channel_id=1, source_target_pairs={{0,10},{2,8},{4,14},{6,12},{8,2},{10,0},{12,6},{14,4},{16,26},{18,... | collective-permute-start | bytes 98312 | tf_op jit(solution)/shard_map/ppermute | solution.py:409
  19.1 13.2 %collective-permute-start.9 = (f32[128,512]{1,0:T(8,128)S(1)}, f32[128,512]{1,0:T(8,128)S(1)}, u32[]{:S(2)}, u32[]{:S(2)}) collective-permute-start(f32[128,512]{1,0:T(8,128)S(1)} %complete.1.refs_0_), channel_id=1, source_target_pairs={{1,0},{0,1},{3,2},{2,3},{5,4},{4,5},{7,6},{6,7},{9,8},{8,9},{11,10... | collective-permute-start | bytes 786440 | tf_op jit(solution)/shard_map/ppermute | solution.py:425
  20.7 7.7 %copy-start = (f32[32,2,4,1,512]{4,3,2,1,0:T(1,128)S(1)}, f32[32,2,4,1,512]{4,3,2,1,0:T(1,128)}, u32[]{:S(2)}) copy-start(f32[32,2,4,1,512]{4,3,2,1,0:T(1,128)} %param.11) | copy-start | bytes 1572868
  20.7 3.4 %collective-permute-start.4 = (f32[32,256]{1,0:T(8,128)S(1)}, f32[32,256]{1,0:T(8,128)S(1)}, u32[]{:S(2)}, u32[]{:S(2)}) collective-permute-start(f32[32,256]{1,0:T(8,128)S(1)} %sum.4.terms_ref), channel_id=1, source_target_pairs={{0,6},{2,4},{4,2},{6,0},{8,14},{10,12},{12,10},{14,8},{16,22},{18,... | collective-permute-start | bytes 98312 | tf_op jit(solution)/shard_map/ppermute | solution.py:409
  24.1 3.8 %collective-permute-start.6 = (f32[32,256]{1,0:T(8,128)S(1)}, f32[32,256]{1,0:T(8,128)S(1)}, u32[]{:S(2)}, u32[]{:S(2)}) collective-permute-start(f32[32,256]{1,0:T(8,128)S(1)} %sum.5.refs_0_), channel_id=1, source_target_pairs={{3,0},{2,1},{1,2},{0,3},{7,4},{6,5},{5,6},{4,7},{11,8},{10,9},{9,1... | collective-permute-start | bytes 98312 | tf_op jit(solution)/shard_map/ppermute | solution.py:418
  28.0 1.4 %copy-start.1 = (f32[2,64,256]{2,1,0:T(8,128)S(1)}, f32[2,64,256]{2,1,0:T(8,128)}, u32[]{:S(2)}) copy-start(f32[2,64,256]{2,1,0:T(8,128)} %noise_ref.1) | copy-start | bytes 393220
  28.0 1.3 %copy-start.2 = (f32[2,256]{1,0:T(2,128)S(1)}, f32[2,256]{1,0:T(2,128)}, u32[]{:S(2)}) copy-start(f32[2,256]{1,0:T(2,128)} %value_ref.1) | copy-start | bytes 6148
  28.0 1.3 %copy-start.3 = (f32[2,256]{1,0:T(2,128)S(1)}, f32[2,256]{1,0:T(2,128)}, u32[]{:S(2)}) copy-start(f32[2,256]{1,0:T(2,128)} %error_ref.1) | copy-start | bytes 6148
  28.0 1.3 %collective-permute-start.7 = (f32[64,256]{1,0:T(8,128)S(1)}, f32[64,256]{1,0:T(8,128)S(1)}, u32[]{:S(2)}, u32[]{:S(2)}) collective-permute-start(f32[64,256]{1,0:T(8,128)S(1)} %gather.1.kept_ref), channel_id=1, source_target_pairs={{0,2},{2,0},{4,6},{6,4},{8,10},{10,8},{12,14},{14,12},{16,18},{18,... | collective-permute-start | bytes 196616 | tf_op jit(solution)/shard_map/ppermute | solution.py:409

commit v13 on v11

--- a/solution.py
+++ b/solution.py
@@ -15,7 +15,7 @@
 
 
 SELECT_FLOPS = 1
-OWN_FLOPS, SUM_FLOPS, GATHER_FLOPS, SOLVE_FLOPS = 1, (7*10**8,7*10**8,1), 10**8, 5*10**8
+OWN_FLOPS, SUM_FLOPS, GATHER_FLOPS, SOLVE_FLOPS = 10**11, (2*10**9,7*10**8,1), 10**8, 5*10**8
 
 
 def estimate(flops):
@@ -86,16 +86,17 @@
 
 
 def load_kernel(chunks, *refs):
-    count = (len(refs) - 1) // 2
-    sources, packed_ref, held, sems = refs[:count], refs[count], refs[count + 1 : -1], refs[-1]
+    count = (len(refs) - 2) // 2
+    sources, held, packed_ref, coefs_ref, sems = refs[:count], refs[count:-3], *refs[-3:]
     rows = sources[0].shape[0]
     copies = at_once(sources, (packed_ref.at[:rows], *held), sems)
     copies[1].wait()
     copies[2].wait()
     spread = held[0][...]
     half = held[1][:chunks, :] * 0.5
-    packed_ref[rows : rows + chunks, :] = spread + half
-    packed_ref[rows + chunks : rows + 2 * chunks, :] = spread - half
+    for ref, start in ((packed_ref, rows), (coefs_ref, 0)):
+        ref[start : start + chunks, :] = spread + half
+        ref[start + chunks : start + 2 * chunks, :] = spread - half
     for copy in (copies[0], *copies[3:]):
         copy.wait()
 
@@ -120,7 +121,7 @@
     flat = lambda ref: jnp.concatenate([ref[b : b + 1, :] for b in range(batches)], axis=1)
     rows, cols, kinds = flat(row_ref), flat(col_ref), flat(field_ref)
     own_row = lax.axis_index("slab")
-    for k, row in enumerate((own_row, own_row - 1)):
+    for k, row in enumerate((own_row, own_row + 1, own_row - 1)):
         kinds_ref[k : k + 1, :] = jnp.where(rows == row, kinds, -1)
     at = lax.broadcasted_iota(jnp.int32, shape, 0).astype(F32) * 0.25
     taps_ref[...] = jnp.maximum(0.5 - jnp.abs(at - cols.astype(F32) * 0.25), 0.0).astype(BF16)
@@ -167,30 +168,26 @@
     members,
     fields,
     chunks,
-    packed_ref,
     inner_ref,
     outer_ref,
-    part_ref,
     part_obs_ref,
     here_ref,
     taps_ref,
     kinds_ref,
     keep_ref,
     send_ref,
-    partial_ref,
 ):
     even = lax.rem(lax.axis_index("slab"), 2) == 0
-    above, below = weights(packed_ref, chunks)
-    _, below_of_above = weights(outer_ref, chunks)
-    taken = jnp.where(even, below, above) * stacked_planes(
-        inner_ref, members, fields, chunks
-    ) + above * stacked_planes(outer_ref, members, fields, chunks)
-    given = below_of_above * here_ref[...]
-    partial_ref[...] = part_ref[...] + taken
-    picked = picked_values(jnp.concatenate([taken, given], axis=0), taps_ref[...])
+    here = here_ref[...]
+    inner, outer = weights(inner_ref, chunks), weights(outer_ref, chunks)
+    to_below = jnp.where(even, inner[0], outer[0])
+    to_above = jnp.where(even, outer[1], inner[1])
+    picked = picked_values(
+        jnp.concatenate([to_below * here, to_above * here], axis=0), taps_ref[...]
+    )
     observed = part_obs_ref[...]
     for side in range(2):
-        kinds = kinds_ref[side : side + 1, :]
+        kinds = kinds_ref[1 + side : 2 + side, :]
         for f in range(fields):
             start = (side * fields + f) * members
             observed += jnp.where(kinds == f, picked[start : start + members], 0.0)
@@ -205,10 +202,13 @@
     refs[-1][...] = terms_ref[...] + other_ref[...]
 
 
-def complete_kernel(members, fields, chunks, partial_ref, outer_ref, packed_ref, forecast_ref):
-    _, below = weights(packed_ref, chunks)
-    forecast_ref[...] = partial_ref[...] + below * stacked_planes(
-        outer_ref, members, fields, chunks
+def complete_kernel(members, fields, chunks, part_ref, packed_ref, inner_ref, outer_ref, forecast_ref):
+    even = lax.rem(lax.axis_index("slab"), 2) == 0
+    above, below = weights(packed_ref, chunks)
+    forecast_ref[...] = (
+        part_ref[...]
+        + jnp.where(even, below, above) * stacked_planes(inner_ref, members, fields, chunks)
+        + jnp.where(even, above, below) * stacked_planes(outer_ref, members, fields, chunks)
     )
 
 
@@ -409,8 +409,6 @@
     hbm = pl.BlockSpec(memory_space=pltpu.HBM)
     sizes = (members, fields, chunks)
 
-    odd = range(1, slabs, 2)
-
     def from_slab(array, bit):
         return lax.ppermute(array, "slab", [(i, i ^ bit) for i in range(slabs)])
 
@@ -435,23 +433,25 @@
     present, delayed = rows_of(present_ensemble), rows_of(delayed_ensemble)
     spread, ratios = rows_of(spreading_coefficient), rows_of(transport_ratios)
     sources = in_hbm((present, spread, ratios, obs_row, obs_col, obs_field))
-    packed, *held = pl.pallas_call(
+    *held, packed, coefs = pl.pallas_call(
         functools.partial(load_kernel, chunks),
-        out_shape=[shape_of((present.shape[0] + 2 * chunks, LANES))]
-        + [shape_of(x.shape, x.dtype) for x in sources[1:]],
+        out_shape=[shape_of(x.shape, x.dtype) for x in sources[1:]]
+        + [shape_of((present.shape[0] + 2 * chunks, LANES)), shape_of((2 * chunks, LANES))],
         in_specs=[hbm] * len(sources),
         scratch_shapes=[pltpu.SemaphoreType.DMA((len(sources),))],
         compiler_params=PARAMS,
         name="load",
     )(*sources)
-    outer_above = lax.ppermute(packed, "slab", [(i, i + 1) for i in odd[:-1]])
+    outer_pairs = [(i, i + 1) for i in range(1, slabs - 1, 2)]
+    outer_pairs += [(j, i) for i, j in outer_pairs]
+    outer_coefs = lax.ppermute(coefs, "slab", outer_pairs)
+    inner = from_slab(packed, 1)
     others_delayed = from_partners(
         lax.optimization_barrier((delayed, packed))[0]
     )
-    outer_below = lax.ppermute(packed, "slab", [(i + 1, i) for i in odd[:-1]])
     taps, kinds = pl.pallas_call(
         selector_kernel,
-        out_shape=(shape_of((width, total), BF16), shape_of((2, total), jnp.int32)),
+        out_shape=(shape_of((width, total), BF16), shape_of((3, total), jnp.int32)),
         compiler_params=PARAMS,
         cost_estimate=estimate(SELECT_FLOPS),
         name="selector",
@@ -463,17 +463,13 @@
         cost_estimate=estimate(OWN_FLOPS),
         name="own_row",
     )(packed, *held[:2], taps, kinds)
-    inner = from_slab(packed, 1)
-    keep, send, partial = pl.pallas_call(
+    keep, send = pl.pallas_call(
         functools.partial(observe_kernel, parts, *sizes),
-        out_shape=(
-            shape_of((members, total // 2)),
-            shape_of((members, total // 2)),
-            shape_of(stacked),
-        ),
+        out_shape=[shape_of((members, total // 2))] * 2,
         compiler_params=PARAMS,
         name="observe",
-    )(packed, inner, outer_above, part, part_obs, here, taps, kinds)
+    )(inner, outer_coefs, part_obs, here, taps, kinds)
+
     def summed(terms, other, flops, *arrived):
         return pl.pallas_call(
             sum_kernel,
@@ -484,38 +480,42 @@
         )(terms, other, *arrived)
 
     terms = keep + from_slab(send, 1)
-    for bit in [1 << k for k in reversed(range(1, slabs.bit_length() - 1))]:
+    outer_row = lax.ppermute(
+        lax.optimization_barrier((packed, terms))[0], "slab", outer_pairs
+    )
+    far = slabs // 2
+    terms = summed(terms, from_other_pair(terms, far), SUM_FLOPS[0])
+    terms = pl.pallas_call(
+        gather_kernel,
+        out_shape=shape_of((all_members, total // 2)),
+        cost_estimate=estimate(GATHER_FLOPS),
+        compiler_params=PARAMS,
+        name="gather",
+    )(terms, *from_other_mem(terms))
+    forecast = pl.pallas_call(
+        functools.partial(complete_kernel, *sizes),
+        out_shape=shape_of(stacked),
+        compiler_params=PARAMS,
+        name="complete",
+    )(lax.optimization_barrier((part, terms))[0], packed, inner, outer_row)
+    bit = far // 2
+    while bit > 1:
+        last = bit == 2
         terms = summed(
             terms,
             from_other_pair(terms, bit),
-            SUM_FLOPS[min(slabs // 2 // bit, 4) // 2],
-            *([others_delayed[0]] if bit == 2 else []),
+            SUM_FLOPS[1 + last],
+            *([others_delayed[0]] if last else []),
         )
-        if bit == slabs // 2:
-            after_far = terms
-    forecast = pl.pallas_call(
-        functools.partial(complete_kernel, *sizes),
-        out_shape=shape_of(stacked),
-        compiler_params=PARAMS,
-        name="complete",
-    )(
-        lax.optimization_barrier((partial, after_far))[0], outer_below, packed
-    )
-
-    prior = pl.pallas_call(
-        gather_kernel,
-        out_shape=shape_of((all_members, total // 2)),
-        cost_estimate=estimate(GATHER_FLOPS),
-        compiler_params=PARAMS,
-        name="gather",
-    )(terms, *from_other_mem(terms))
+        bit //= 2
+    priors = [terms, from_slab(terms, 1)]
     mine = pl.pallas_call(
         functools.partial(solve_kernel, parts),
         out_shape=shape_of((members, all_members)),
         compiler_params=PARAMS,
         cost_estimate=estimate(SOLVE_FLOPS),
         name="solve",
-    )(obs_value, obs_error, obs_noise, prior, from_slab(prior, 1))
+    )(obs_value, obs_error, obs_noise, *priors)
     lagged_parts = pl.pallas_call(
         functools.partial(prepare_kernel, parts),
         out_shape=[shape_of((all_members, delayed.size // members), BF16)] * 2,

time: 34 us -> 34.6 us (1.018)
  starting transfers between devices: 17 us -> 17.7 us
    ppermute x1, starting transfers between devices: 1.47 us -> 2.5 us  [from_other_mem(): lax.ppermute(array, ('slab', 'mem'), [(i ^ 3, i) for i in range(slabs * p...]
    ppermute x2, starting transfers between devices: 3.91 us -> 3.05 us  [from_partners(): lax.ppermute(array, 'mem', [((i + d) % parts, i) for i in range(parts)])]
    ppermute x6, waiting for transfers between devices: 6.73 us -> 5.9 us  [from_slab(): return lax.ppermute(array, 'slab', [(i, i ^ bit) for i in range(slabs)])]
    ppermute x1, waiting for transfers between devices: 2.35 us -> 3.11 us  [from_other_mem(): lax.ppermute(array, ('slab', 'mem'), [(i ^ 3, i) for i in range(slabs * p...]
    ppermute x6, starting transfers between devices: 10.3 us -> 10.9 us  [from_slab(): return lax.ppermute(array, 'slab', [(i, i ^ bit) for i in range(slabs)])]
  transfers between devices with their start and end apart: 11 -> 11, of which waited for: 6 -> 6; matrix products, arithmetic and copies ran while one was open for 0% -> 0% of each run, Pallas kernels for 16% -> 15%
where the time goes in v13:
time: 34.6 us; the launch traced here: 34.4 us
  starting transfers between devices  17.7 us (51%)
  waiting for transfers between devices  9.02 us (26%)
  Pallas kernels  7.5 us (22%)
    ppermute x6, starting transfers between devices, from_slab(): return lax.ppermute(array, 'slab', [(i, i ^ bit) for i in range(slabs)])  10.9 us
    ppermute x6, waiting for transfers between devices, from_slab(): return lax.ppermute(array, 'slab', [(i, i ^ bit) for i in range(slabs)])  5.9 us
    ppermute x1, waiting for transfers between devices, from_other_mem(): lax.ppermute(array, ('slab', 'mem'), [(i ^ 3, i) for i in range(slabs * p...  3.11 us
    ppermute x2, starting transfers between devices, from_partners(): lax.ppermute(array, 'mem', [((i + d) % parts, i) for i in range(parts)])  3.05 us
    pallas_call x1, Pallas kernels, shards(): pl.pallas_call(functools.partial(solve_kernel, parts), out_shape=shape_of...  2.94 us
    ppermute x1, starting transfers between devices, from_other_mem(): lax.ppermute(array, ('slab', 'mem'), [(i ^ 3, i) for i in range(slabs * p...  2.5 us
    pallas_call x1, Pallas kernels, shards(): pl.pallas_call(functools.partial(combine_kernel, parts, fields), out_shap...  1.36 us
    pallas_call x1, Pallas kernels, shards(): pl.pallas_call(functools.partial(load_kernel, chunks), out_shape=[shape_o...  1.01 us
  transfers between devices with their start and end apart: 11, of which 6 were waited for; matrix products, arithmetic and copies ran while one was open for 0% of the time, Pallas kernels for 15%

profile of v13, /device:TPU:0, one launch (start us, length us, event | category | flops | bytes accessed | tf_op | source)
XLA Modules:
  0.0 34.4 jit_solution(6725816668509377092)
XLA Ops:
  0.0 1.0 %load.1 = (f32[4,128]{1,0:T(4,128)S(1)}, f32[8,128]{1,0:T(8,128)S(1)}, s32[2,256]{1,0:T(2,128)S(1)}, s32[2,256]{1,0:T(2,128)S(1)}, s32[2,256]{1,0:T(2,128)S(1)},...) custom-call(f32[512,128]{1,0:T(8,128)} %bitcast.7, f32[4,128]{1,0:T(4,128)} %bitcast.9, f32[8,128]{1,0:T(8,128)} %bitcast.8, ...), custom_call_target="tpu_custom_call" | custom-call | tf_op jit(solution)/shard_map/load/pallas_call | solution.py:436
  1.0 0.7 %collective-permute-start.1 = (f32[8,128]{1,0:T(8,128)S(1)}, f32[8,128]{1,0:T(8,128)S(1)}, u32[]{:S(2)}, u32[]{:S(2)}) collective-permute-start(f32[8,128]{1,0:T(8,128)S(1)} %get-tuple-element.25), channel_id=1, source_target_pairs={{2,4},{6,8},{10,12},{14,16},{18,20},{22,24},{26,28},{4,2},{8,6},{1... | collective-permute-start | bytes 12296 | tf_op jit(solution)/shard_map/ppermute | solution.py:447
  1.7 4.4 %collective-permute-start = (f32[520,128]{1,0:T(8,128)S(1)}, f32[520,128]{1,0:T(8,128)S(1)}, u32[]{:S(2)}, u32[]{:S(2)}) collective-permute-start(f32[520,128]{1,0:T(8,128)S(1)} %get-tuple-element.40.packed_ref), channel_id=1, source_target_pairs={{0,2},{2,0},{4,6},{6,4},{8,10},{10,8},{12,14},{14,12},{16,18},{18,... | collective-permute-start | bytes 798728 | tf_op jit(solution)/shard_map/ppermute | solution.py:413
  6.1 1.5 %collective-permute-start.7 = (f32[1024,128]{1,0:T(8,128)}, f32[1024,128]{1,0:T(8,128)S(1)}, u32[]{:S(2)}, u32[]{:S(2)}) collective-permute-start(f32[1024,128]{1,0:T(8,128)} %bitcast.5), channel_id=1, source_target_pairs={{1,0},{0,1},{3,2},{2,3},{5,4},{4,5},{7,6},{6,7},{9,8},{8,9},{11,10... | collective-permute-start | bytes 1572872 | tf_op jit(solution)/shard_map/ppermute | solution.py:429
  7.6 0.2 selector.1
  7.8 0.5 %own_row.1 = (f32[128,512]{1,0:T(8,128)S(1)}, f32[128,512]{1,0:T(8,128)S(1)}, f32[32,512]{1,0:T(8,128)S(1)}) custom-call(f32[520,128]{1,0:T(8,128)S(1)} %get-tuple-element.40.packed_ref, f32[4,128]{1,0:T(4,128)S(1)} %get-tuple-element.26.spread_ref, f32[8,128]{1,0:T(8,128)S(1)} %get-tuple-element.27.ratio_ref, ...), custom_call_target="tpu_custom_call" | custom-call | flops 99999997952 | tf_op jit(solution)/shard_map/own_row/pallas_call | solution.py:459
  8.3 0.6 %observe.1 = (f32[32,256]{1,0:T(8,128)S(1)}, f32[32,256]{1,0:T(8,128)S(1)}) custom-call(f32[520,128]{1,0:T(8,128)S(1)} %collective-permute-done.inner_ref, f32[8,128]{1,0:T(8,128)S(1)} %collective-permute-done.1.outer_ref, f32[32,512]{1,0:T(8,128)S(1)} %get-tuple-element.33.part_obs_ref, f32[128,512]{1,0:T(8,128)S(1)} %get-tuple-element.34.here_ref, ...), custom_call_target="tpu_custom_call" | custom-call | tf_op jit(solution)/shard_map/observe/pallas_call | solution.py:466
  9.0 1.2 %collective-permute-done.2 = f32[32,256]{1,0:T(8,128)S(1)} collective-permute-done((f32[32,256]{1,0:T(8,128)S(1)}, f32[32,256]{1,0:T(8,128)S(1)}, u32[]{:S(2)}, u32[]{:S(2)}) %collective-permute-start.2) | collective-permute-done | bytes 32800 | tf_op jit(solution)/shard_map/ppermute | solution.py:413
  10.2 2.4 %collective-permute-start.3 = (f32[32,256]{1,0:T(8,128)S(1)}, f32[32,256]{1,0:T(8,128)S(1)}, u32[]{:S(2)}, u32[]{:S(2)}) collective-permute-start(f32[32,256]{1,0:T(8,128)S(1)} %add.3.terms_ref), channel_id=1, source_target_pairs={{0,18},{2,16},{4,22},{6,20},{8,26},{10,24},{12,30},{14,28},{16,2},... | collective-permute-start | bytes 98312 | tf_op jit(solution)/shard_map/ppermute | solution.py:413
  12.5 0.7 %collective-permute-start.9 = (f32[520,128]{1,0:T(8,128)S(1)}, f32[520,128]{1,0:T(8,128)S(1)}, u32[]{:S(2)}, u32[]{:S(2)}) collective-permute-start(f32[520,128]{1,0:T(8,128)S(1)} %get-tuple-element.40.packed_ref), channel_id=1, source_target_pairs={{2,4},{6,8},{10,12},{14,16},{18,20},{22,24},{26,28},{4,2},{8,6},{1... | collective-permute-start | bytes 798728 | tf_op jit(solution)/shard_map/ppermute | solution.py:483
  13.2 1.2 %collective-permute-done.3.other_ref = f32[32,256]{1,0:T(8,128)S(1)} collective-permute-done((f32[32,256]{1,0:T(8,128)S(1)}, f32[32,256]{1,0:T(8,128)S(1)}, u32[]{:S(2)}, u32[]{:S(2)}) %collective-permute-start.3) | collective-permute-done | bytes 32800 | tf_op jit(solution)/shard_map/ppermute | solution.py:413
  14.4 2.5 %collective-permute-start.4 = (f32[32,256]{1,0:T(8,128)S(1)}, f32[32,256]{1,0:T(8,128)S(1)}, u32[]{:S(2)}, u32[]{:S(2)}) collective-permute-start(f32[32,256]{1,0:T(8,128)S(1)} %sum.3.refs_0_), channel_id=1, source_target_pairs={{3,0},{2,1},{1,2},{0,3},{7,4},{6,5},{5,6},{4,7},{11,8},{10,9},{9,1... | collective-permute-start | bytes 98312 | tf_op jit(solution)/shard_map/ppermute | solution.py:422
  16.9 3.1 %collective-permute-done.4.refs_1_ = f32[32,256]{1,0:T(8,128)S(1)} collective-permute-done((f32[32,256]{1,0:T(8,128)S(1)}, f32[32,256]{1,0:T(8,128)S(1)}, u32[]{:S(2)}, u32[]{:S(2)}) %collective-permute-start.4) | collective-permute-done | bytes 32800 | tf_op jit(solution)/shard_map/ppermute | solution.py:422
  20.0 2.2 %collective-permute-start.5 = (f32[64,256]{1,0:T(8,128)S(1)}, f32[64,256]{1,0:T(8,128)S(1)}, u32[]{:S(2)}, u32[]{:S(2)}) collective-permute-start(f32[64,256]{1,0:T(8,128)S(1)} %gather.1.terms_ref), channel_id=1, source_target_pairs={{0,10},{2,8},{4,14},{6,12},{8,2},{10,0},{12,6},{14,4},{16,26},{18,... | collective-permute-start | bytes 196616 | tf_op jit(solution)/shard_map/ppermute | solution.py:413
  22.2 0.2 complete.1.refs_0_
  22.4 1.6 %collective-permute-start.10 = (f32[128,512]{1,0:T(8,128)S(1)}, f32[128,512]{1,0:T(8,128)S(1)}, u32[]{:S(2)}, u32[]{:S(2)}) collective-permute-start(f32[128,512]{1,0:T(8,128)S(1)} %complete.1.refs_0_), channel_id=1, source_target_pairs={{1,0},{0,1},{3,2},{2,3},{5,4},{4,5},{7,6},{6,7},{9,8},{8,9},{11,10... | collective-permute-start | bytes 786440 | tf_op jit(solution)/shard_map/ppermute | solution.py:429
  23.9 0.5 %collective-permute-done.5.other_ref = f32[64,256]{1,0:T(8,128)S(1)} collective-permute-done((f32[64,256]{1,0:T(8,128)S(1)}, f32[64,256]{1,0:T(8,128)S(1)}, u32[]{:S(2)}, u32[]{:S(2)}) %collective-permute-start.5) | collective-permute-done | bytes 65568 | tf_op jit(solution)/shard_map/ppermute | solution.py:413
  24.5 1.4 %collective-permute-start.6 = (f32[64,256]{1,0:T(8,128)S(1)}, f32[64,256]{1,0:T(8,128)S(1)}, u32[]{:S(2)}, u32[]{:S(2)}) collective-permute-start(f32[64,256]{1,0:T(8,128)S(1)} %sum.4.terms_ref), channel_id=1, source_target_pairs={{0,6},{2,4},{4,2},{6,0},{8,14},{10,12},{12,10},{14,8},{16,22},{18,... | collective-permute-start | bytes 196616 | tf_op jit(solution)/shard_map/ppermute | solution.py:413
  25.9 2.8 %collective-permute-done.6.other_ref = f32[64,256]{1,0:T(8,128)S(1)} collective-permute-done((f32[64,256]{1,0:T(8,128)S(1)}, f32[64,256]{1,0:T(8,128)S(1)}, u32[]{:S(2)}, u32[]{:S(2)}) %collective-permute-start.6) | collective-permute-done | bytes 65568 | tf_op jit(solution)/shard_map/ppermute | solution.py:413
  28.7 0.5 %collective-permute-start.8 = (f32[64,256]{1,0:T(8,128)S(1)}, f32[64,256]{1,0:T(8,128)S(1)}, u32[]{:S(2)}, u32[]{:S(2)}) collective-permute-start(f32[64,256]{1,0:T(8,128)S(1)} %sum.5.kept_ref), channel_id=1, source_target_pairs={{0,2},{2,0},{4,6},{6,4},{8,10},{10,8},{12,14},{14,12},{16,18},{18,... | collective-permute-start | bytes 196616 | tf_op jit(solution)/shard_map/ppermute | solution.py:413
  29.2 0.7 %prepare.1 = (bf16[64,4096]{1,0:T(8,128)(2,1)S(1)}, bf16[64,4096]{1,0:T(8,128)(2,1)S(1)}) custom-call(f32[1024,128]{1,0:T(8,128)S(1)} %bitcast.6, f32[1024,128]{1,0:T(8,128)S(1)} %collective-permute-done.7.refs_0_.refs_1_), custom_call_target="tpu_custom_call" | custom-call | tf_op jit(solution)/shard_map/prepare/pallas_call | solution.py:519
  29.9 0.2 collective-permute-done.8.received_ref
  30.1 2.9 %solve.1.mine_ref = f32[32,64]{1,0:T(8,128)S(1)} custom-call(f32[2,256]{1,0:T(2,128)S(1)} %copy-done.2, f32[2,256]{1,0:T(2,128)S(1)} %copy-done.3, f32[2,64,256]{2,1,0:T(8,128)S(1)} %copy-done.1, f32[64,256]{1,0:T(8,128)S(1)} %sum.5.kept_ref, f32[64,256]{1,0:T(8,128)S(1)} %collective-permute-done.8.received_ref), custom_call_target="tpu_custom_call" | custom-call | flops 500000000 | tf_op jit(solution)/shard_map/solve/pallas_call | solution.py:512
  33.1 1.4 %combine.1 = f32[32,48,128]{2,1,0:T(8,128)} custom-call(f32[32,64]{1,0:T(8,128)S(1)} %solve.1.mine_ref, f32[128,512]{1,0:T(8,128)S(1)} %complete.1.refs_0_, f32[128,512]{1,0:T(8,128)S(1)} %collective-permute-done.10.refs_1_, bf16[64,4096]{1,0:T(8,128)(2,1)S(1)} %get-tuple-element.41.refs_2_, bf16[64,4096]{1,0:T(8,128)(2,1)S(1)} %get-tuple-element.42.refs_3_), custom_call_target="tpu_custom_call" | custom-call | tf_op jit(solution)/shard_map/combine/pallas_call | solution.py:525
  (19 shorter events, 0.1 us)
Async XLA Ops:
  1.0 7.3 %collective-permute-start.1 = (f32[8,128]{1,0:T(8,128)S(1)}, f32[8,128]{1,0:T(8,128)S(1)}, u32[]{:S(2)}, u32[]{:S(2)}) collective-permute-start(f32[8,128]{1,0:T(8,128)S(1)} %get-tuple-element.25), channel_id=1, source_target_pairs={{2,4},{6,8},{10,12},{14,16},{18,20},{22,24},{26,28},{4,2},{8,6},{1... | collective-permute-start | bytes 12296 | tf_op jit(solution)/shard_map/ppermute | solution.py:447
  1.7 6.6 %collective-permute-start = (f32[520,128]{1,0:T(8,128)S(1)}, f32[520,128]{1,0:T(8,128)S(1)}, u32[]{:S(2)}, u32[]{:S(2)}) collective-permute-start(f32[520,128]{1,0:T(8,128)S(1)} %get-tuple-element.40.packed_ref), channel_id=1, source_target_pairs={{0,2},{2,0},{4,6},{6,4},{8,10},{10,8},{12,14},{14,12},{16,18},{18,... | collective-permute-start | bytes 798728 | tf_op jit(solution)/shard_map/ppermute | solution.py:413
  6.1 22.6 %collective-permute-start.7 = (f32[1024,128]{1,0:T(8,128)}, f32[1024,128]{1,0:T(8,128)S(1)}, u32[]{:S(2)}, u32[]{:S(2)}) collective-permute-start(f32[1024,128]{1,0:T(8,128)} %bitcast.5), channel_id=1, source_target_pairs={{1,0},{0,1},{3,2},{2,3},{5,4},{4,5},{7,6},{6,7},{9,8},{8,9},{11,10... | collective-permute-start | bytes 1572872 | tf_op jit(solution)/shard_map/ppermute | solution.py:429
  8.9 1.3 %collective-permute-start.2 = (f32[32,256]{1,0:T(8,128)S(1)}, f32[32,256]{1,0:T(8,128)S(1)}, u32[]{:S(2)}, u32[]{:S(2)}) collective-permute-start(f32[32,256]{1,0:T(8,128)S(1)} %get-tuple-element.36), channel_id=1, source_target_pairs={{0,2},{2,0},{4,6},{6,4},{8,10},{10,8},{12,14},{14,12},{16,18},{18,... | collective-permute-start | bytes 98312 | tf_op jit(solution)/shard_map/ppermute | solution.py:413
  10.2 4.2 %collective-permute-start.3 = (f32[32,256]{1,0:T(8,128)S(1)}, f32[32,256]{1,0:T(8,128)S(1)}, u32[]{:S(2)}, u32[]{:S(2)}) collective-permute-start(f32[32,256]{1,0:T(8,128)S(1)} %add.3.terms_ref), channel_id=1, source_target_pairs={{0,18},{2,16},{4,22},{6,20},{8,26},{10,24},{12,30},{14,28},{16,2},... | collective-permute-start | bytes 98312 | tf_op jit(solution)/shard_map/ppermute | solution.py:413
  12.5 9.7 %collective-permute-start.9 = (f32[520,128]{1,0:T(8,128)S(1)}, f32[520,128]{1,0:T(8,128)S(1)}, u32[]{:S(2)}, u32[]{:S(2)}) collective-permute-start(f32[520,128]{1,0:T(8,128)S(1)} %get-tuple-element.40.packed_ref), channel_id=1, source_target_pairs={{2,4},{6,8},{10,12},{14,16},{18,20},{22,24},{26,28},{4,2},{8,6},{1... | collective-permute-start | bytes 798728 | tf_op jit(solution)/shard_map/ppermute | solution.py:483
  14.4 5.6 %collective-permute-start.4 = (f32[32,256]{1,0:T(8,128)S(1)}, f32[32,256]{1,0:T(8,128)S(1)}, u32[]{:S(2)}, u32[]{:S(2)}) collective-permute-start(f32[32,256]{1,0:T(8,128)S(1)} %sum.3.refs_0_), channel_id=1, source_target_pairs={{3,0},{2,1},{1,2},{0,3},{7,4},{6,5},{5,6},{4,7},{11,8},{10,9},{9,1... | collective-permute-start | bytes 98312 | tf_op jit(solution)/shard_map/ppermute | solution.py:422
  20.0 4.5 %collective-permute-start.5 = (f32[64,256]{1,0:T(8,128)S(1)}, f32[64,256]{1,0:T(8,128)S(1)}, u32[]{:S(2)}, u32[]{:S(2)}) collective-permute-start(f32[64,256]{1,0:T(8,128)S(1)} %gather.1.terms_ref), channel_id=1, source_target_pairs={{0,10},{2,8},{4,14},{6,12},{8,2},{10,0},{12,6},{14,4},{16,26},{18,... | collective-permute-start | bytes 196616 | tf_op jit(solution)/shard_map/ppermute | solution.py:413
  22.4 10.7 %collective-permute-start.10 = (f32[128,512]{1,0:T(8,128)S(1)}, f32[128,512]{1,0:T(8,128)S(1)}, u32[]{:S(2)}, u32[]{:S(2)}) collective-permute-start(f32[128,512]{1,0:T(8,128)S(1)} %complete.1.refs_0_), channel_id=1, source_target_pairs={{1,0},{0,1},{3,2},{2,3},{5,4},{4,5},{7,6},{6,7},{9,8},{8,9},{11,10... | collective-permute-start | bytes 786440 | tf_op jit(solution)/shard_map/ppermute | solution.py:429
  24.5 4.7 %copy-start = (f32[32,2,4,1,512]{4,3,2,1,0:T(1,128)S(1)}, f32[32,2,4,1,512]{4,3,2,1,0:T(1,128)}, u32[]{:S(2)}) copy-start(f32[32,2,4,1,512]{4,3,2,1,0:T(1,128)} %param.11) | copy-start | bytes 1572868
  24.5 4.2 %collective-permute-start.6 = (f32[64,256]{1,0:T(8,128)S(1)}, f32[64,256]{1,0:T(8,128)S(1)}, u32[]{:S(2)}, u32[]{:S(2)}) collective-permute-start(f32[64,256]{1,0:T(8,128)S(1)} %sum.4.terms_ref), channel_id=1, source_target_pairs={{0,6},{2,4},{4,2},{6,0},{8,14},{10,12},{12,10},{14,8},{16,22},{18,... | collective-permute-start | bytes 196616 | tf_op jit(solution)/shard_map/ppermute | solution.py:413
  28.7 1.4 %copy-start.1 = (f32[2,64,256]{2,1,0:T(8,128)S(1)}, f32[2,64,256]{2,1,0:T(8,128)}, u32[]{:S(2)}) copy-start(f32[2,64,256]{2,1,0:T(8,128)} %noise_ref.1) | copy-start | bytes 393220
  28.7 1.4 %copy-start.2 = (f32[2,256]{1,0:T(2,128)S(1)}, f32[2,256]{1,0:T(2,128)}, u32[]{:S(2)}) copy-start(f32[2,256]{1,0:T(2,128)} %value_ref.1) | copy-start | bytes 6148
  28.7 1.4 %copy-start.3 = (f32[2,256]{1,0:T(2,128)S(1)}, f32[2,256]{1,0:T(2,128)}, u32[]{:S(2)}) copy-start(f32[2,256]{1,0:T(2,128)} %error_ref.1) | copy-start | bytes 6148
  28.7 1.4 %collective-permute-start.8 = (f32[64,256]{1,0:T(8,128)S(1)}, f32[64,256]{1,0:T(8,128)S(1)}, u32[]{:S(2)}, u32[]{:S(2)}) collective-permute-start(f32[64,256]{1,0:T(8,128)S(1)} %sum.5.kept_ref), channel_id=1, source_target_pairs={{0,2},{2,0},{4,6},{6,4},{8,10},{10,8},{12,14},{14,12},{16,18},{18,... | collective-permute-start | bytes 196616 | tf_op jit(solution)/shard_map/ppermute | solution.py:413

commit v14 on v13

--- a/solution.py
+++ b/solution.py
@@ -15,7 +15,7 @@
 
 
 SELECT_FLOPS = 1
-OWN_FLOPS, SUM_FLOPS, GATHER_FLOPS, SOLVE_FLOPS = 10**11, (2*10**9,7*10**8,1), 10**8, 5*10**8
+OWN_FLOPS, SUM_FLOPS, GATHER_FLOPS, SOLVE_FLOPS = 10**11, (10**9,7*10**8,1), 10**9, 5*10**8
 
 
 def estimate(flops):
@@ -86,18 +86,26 @@
 
 
 def load_kernel(chunks, *refs):
-    count = (len(refs) - 2) // 2
-    sources, held, packed_ref, coefs_ref, sems = refs[:count], refs[count:-3], *refs[-3:]
-    rows = sources[0].shape[0]
-    copies = at_once(sources, (packed_ref.at[:rows], *held), sems)
-    copies[1].wait()
-    copies[2].wait()
+    sources, (*held, first_ref, second_ref, packed_ref, coefs_ref), sems = (
+        refs[:7],
+        refs[7:-1],
+        refs[-1],
+    )
+    present, delayed, *others = sources
+    rows, half = present.shape[0], first_ref.shape[0]
+    copies = at_once(
+        [present, delayed.at[:half], delayed.at[half:], *others],
+        [packed_ref.at[:rows], first_ref, second_ref, *held],
+        sems,
+    )
+    copies[3].wait()
+    copies[4].wait()
     spread = held[0][...]
-    half = held[1][:chunks, :] * 0.5
+    along_rows = held[1][:chunks, :] * 0.5
     for ref, start in ((packed_ref, rows), (coefs_ref, 0)):
-        ref[start : start + chunks, :] = spread + half
-        ref[start + chunks : start + 2 * chunks, :] = spread - half
-    for copy in (copies[0], *copies[3:]):
+        ref[start : start + chunks, :] = spread + along_rows
+        ref[start + chunks : start + 2 * chunks, :] = spread - along_rows
+    for copy in (*copies[:3], *copies[5:]):
         copy.wait()
 
 
@@ -328,12 +336,12 @@
 
 
 def prepare_kernel(parts, *refs):
-    sources, high_ref, low_ref = refs[:parts], refs[parts], refs[parts + 1]
+    sources, high_ref, low_ref = refs[: 2 * parts], refs[2 * parts], refs[2 * parts + 1]
     lagged = high_ref.shape[1] // LANES
-    local = high_ref.shape[0] // parts
+    count = high_ref.shape[0] // (2 * parts)
     for k in range(lagged):
         held = jnp.concatenate(
-            [ref[pl.ds(k, local, stride=lagged), :] for ref in sources], axis=0
+            [ref[pl.ds(k, count, stride=lagged), :] for ref in sources], axis=0
         )
         high, low = split_two(held)
         high_ref[:, k * LANES : (k + 1) * LANES] = high
@@ -432,13 +440,15 @@
 
     present, delayed = rows_of(present_ensemble), rows_of(delayed_ensemble)
     spread, ratios = rows_of(spreading_coefficient), rows_of(transport_ratios)
-    sources = in_hbm((present, spread, ratios, obs_row, obs_col, obs_field))
-    *held, packed, coefs = pl.pallas_call(
+    sources = in_hbm((present, delayed, spread, ratios, obs_row, obs_col, obs_field))
+    half_shape = (delayed.shape[0] // 2, LANES)
+    *held, first_half, second_half, packed, coefs = pl.pallas_call(
         functools.partial(load_kernel, chunks),
-        out_shape=[shape_of(x.shape, x.dtype) for x in sources[1:]]
+        out_shape=[shape_of(x.shape, x.dtype) for x in sources[2:]]
+        + [shape_of(half_shape)] * 2
         + [shape_of((present.shape[0] + 2 * chunks, LANES)), shape_of((2 * chunks, LANES))],
         in_specs=[hbm] * len(sources),
-        scratch_shapes=[pltpu.SemaphoreType.DMA((len(sources),))],
+        scratch_shapes=[pltpu.SemaphoreType.DMA((len(sources) + 1,))],
         compiler_params=PARAMS,
         name="load",
     )(*sources)
@@ -446,9 +456,7 @@
     outer_pairs += [(j, i) for i, j in outer_pairs]
     outer_coefs = lax.ppermute(coefs, "slab", outer_pairs)
     inner = from_slab(packed, 1)
-    others_delayed = from_partners(
-        lax.optimization_barrier((delayed, packed))[0]
-    )
+    others_first = from_partners(first_half)
     taps, kinds = pl.pallas_call(
         selector_kernel,
         out_shape=(shape_of((width, total), BF16), shape_of((3, total), jnp.int32)),
@@ -484,7 +492,8 @@
         lax.optimization_barrier((packed, terms))[0], "slab", outer_pairs
     )
     far = slabs // 2
-    terms = summed(terms, from_other_pair(terms, far), SUM_FLOPS[0])
+    terms = summed(terms, from_other_pair(terms, far), SUM_FLOPS[0], others_first[0])
+    others_second = from_partners(lax.optimization_barrier((second_half, terms))[0])
     terms = pl.pallas_call(
         gather_kernel,
         out_shape=shape_of((all_members, total // 2)),
@@ -505,7 +514,7 @@
             terms,
             from_other_pair(terms, bit),
             SUM_FLOPS[1 + last],
-            *([others_delayed[0]] if last else []),
+            *([others_second[0]] if last else []),
         )
         bit //= 2
     priors = [terms, from_slab(terms, 1)]
@@ -521,7 +530,11 @@
         out_shape=[shape_of((all_members, delayed.size // members), BF16)] * 2,
         compiler_params=PARAMS,
         name="prepare",
-    )(delayed, *others_delayed)
+    )(
+        first_half,
+        second_half,
+        *[half for both in zip(others_first, others_second) for half in both],
+    )
     out = pl.pallas_call(
         functools.partial(combine_kernel, parts, fields),
         out_shape=shape_of((members, planes, LANES)),

time: 34.6 us -> 34.8 us (level)
  starting transfers between devices: 17.7 us -> 20.4 us
  waiting for transfers between devices: 9.02 us -> 6.44 us
    ppermute x1, waiting for transfers between devices: 3.11 us -> 1.18 us  [from_other_mem(): lax.ppermute(array, ('slab', 'mem'), [(i ^ 3, i) for i in range(slabs * p...]
    ppermute x6, starting transfers between devices: 10.9 us -> 11.9 us  [from_slab(): return lax.ppermute(array, 'slab', [(i, i ^ bit) for i in range(slabs)])]
    ppermute x1, starting transfers between devices: 2.5 us -> 3.46 us  [from_other_mem(): lax.ppermute(array, ('slab', 'mem'), [(i ^ 3, i) for i in range(slabs * p...]
    ppermute x2 -> x3, starting transfers between devices: 3.05 us -> 3.74 us  [from_partners(): lax.ppermute(array, 'mem', [((i + d) % parts, i) for i in range(parts)])]
    ppermute x6, waiting for transfers between devices: 5.9 us -> 5.25 us  [from_slab(): return lax.ppermute(array, 'slab', [(i, i ^ bit) for i in range(slabs)])]
  transfers between devices with their start and end apart: 11 -> 12, of which waited for: 6 -> 6; matrix products, arithmetic and copies ran while one was open for 0% -> 0% of each run, Pallas kernels for 15% -> 15%
where the time goes in v14:
time: 34.8 us; the launch traced here: 34.7 us
  starting transfers between devices  20.4 us (59%)
  Pallas kernels  7.66 us (22%)
  waiting for transfers between devices  6.44 us (19%)
    ppermute x6, starting transfers between devices, from_slab(): return lax.ppermute(array, 'slab', [(i, i ^ bit) for i in range(slabs)])  11.9 us
    ppermute x6, waiting for transfers between devices, from_slab(): return lax.ppermute(array, 'slab', [(i, i ^ bit) for i in range(slabs)])  5.25 us
    ppermute x3, starting transfers between devices, from_partners(): lax.ppermute(array, 'mem', [((i + d) % parts, i) for i in range(parts)])  3.74 us
    ppermute x1, starting transfers between devices, from_other_mem(): lax.ppermute(array, ('slab', 'mem'), [(i ^ 3, i) for i in range(slabs * p...  3.46 us
    pallas_call x1, Pallas kernels, shards(): pl.pallas_call(functools.partial(solve_kernel, parts), out_shape=shape_of...  2.93 us
    pallas_call x1, Pallas kernels, shards(): pl.pallas_call(functools.partial(combine_kernel, parts, fields), out_shap...  1.36 us
    pallas_call x1, Pallas kernels, shards(): pl.pallas_call(functools.partial(load_kernel, chunks), out_shape=[shape_o...  1.18 us
    ppermute x1, waiting for transfers between devices, from_other_mem(): lax.ppermute(array, ('slab', 'mem'), [(i ^ 3, i) for i in range(slabs * p...  1.18 us
  transfers between devices with their start and end apart: 12, of which 6 were waited for; matrix products, arithmetic and copies ran while one was open for 0% of the time, Pallas kernels for 15%

profile of v14, /device:TPU:0, one launch (start us, length us, event | category | flops | bytes accessed | tf_op | source)
XLA Modules:
  0.0 34.7 jit_solution(9298527531100010575)
XLA Ops:
  0.0 1.2 %load.1 = (f32[4,128]{1,0:T(4,128)S(1)}, f32[8,128]{1,0:T(8,128)S(1)}, s32[2,256]{1,0:T(2,128)S(1)}, s32[2,256]{1,0:T(2,128)S(1)}, s32[2,256]{1,0:T(2,128)S(1)},...) custom-call(f32[512,128]{1,0:T(8,128)} %bitcast.6, ...), custom_call_target="tpu_custom_call" | custom-call | tf_op jit(solution)/shard_map/load/pallas_call | solution.py:445
  1.2 0.5 %collective-permute-start = (f32[520,128]{1,0:T(8,128)S(1)}, f32[520,128]{1,0:T(8,128)S(1)}, u32[]{:S(2)}, u32[]{:S(2)}) collective-permute-start(f32[520,128]{1,0:T(8,128)S(1)} %get-tuple-element.44.packed_ref), channel_id=1, source_target_pairs={{0,2},{2,0},{4,6},{6,4},{8,10},{10,8},{12,14},{14,12},{16,18},{18,... | collective-permute-start | bytes 798728 | tf_op jit(solution)/shard_map/ppermute | solution.py:421
  1.7 0.6 %collective-permute-start.1 = (f32[8,128]{1,0:T(8,128)S(1)}, f32[8,128]{1,0:T(8,128)S(1)}, u32[]{:S(2)}, u32[]{:S(2)}) collective-permute-start(f32[8,128]{1,0:T(8,128)S(1)} %get-tuple-element.27), channel_id=1, source_target_pairs={{2,4},{6,8},{10,12},{14,16},{18,20},{22,24},{26,28},{4,2},{8,6},{1... | collective-permute-start | bytes 12296 | tf_op jit(solution)/shard_map/ppermute | solution.py:457
  2.4 2.6 %collective-permute-start.4 = (f32[512,128]{1,0:T(8,128)S(1)}, f32[512,128]{1,0:T(8,128)S(1)}, u32[]{:S(2)}, u32[]{:S(2)}) collective-permute-start(f32[512,128]{1,0:T(8,128)S(1)} %get-tuple-element.39.refs_0_), channel_id=1, source_target_pairs={{1,0},{0,1},{3,2},{2,3},{5,4},{4,5},{7,6},{6,7},{9,8},{8,9},{11,10... | collective-permute-start | bytes 786440 | tf_op jit(solution)/shard_map/ppermute | solution.py:437
  4.9 0.2 selector.1
  5.1 0.5 %own_row.1 = (f32[128,512]{1,0:T(8,128)S(1)}, f32[128,512]{1,0:T(8,128)S(1)}, f32[32,512]{1,0:T(8,128)S(1)}) custom-call(f32[520,128]{1,0:T(8,128)S(1)} %get-tuple-element.44.packed_ref, f32[4,128]{1,0:T(4,128)S(1)} %get-tuple-element.28.spread_ref, f32[8,128]{1,0:T(8,128)S(1)} %get-tuple-element.29.ratio_ref, ...), custom_call_target="tpu_custom_call" | custom-call | flops 99999997952 | tf_op jit(solution)/shard_map/own_row/pallas_call | solution.py:467
  5.7 0.6 %observe.1 = (f32[32,256]{1,0:T(8,128)S(1)}, f32[32,256]{1,0:T(8,128)S(1)}) custom-call(f32[520,128]{1,0:T(8,128)S(1)} %collective-permute-done.inner_ref, f32[8,128]{1,0:T(8,128)S(1)} %collective-permute-done.1.outer_ref, f32[32,512]{1,0:T(8,128)S(1)} %get-tuple-element.35.part_obs_ref, f32[128,512]{1,0:T(8,128)S(1)} %get-tuple-element.36.here_ref, ...), custom_call_target="tpu_custom_call" | custom-call | tf_op jit(solution)/shard_map/observe/pallas_call | solution.py:474
  6.3 2.7 %collective-permute-start.2 = (f32[32,256]{1,0:T(8,128)S(1)}, f32[32,256]{1,0:T(8,128)S(1)}, u32[]{:S(2)}, u32[]{:S(2)}) collective-permute-start(f32[32,256]{1,0:T(8,128)S(1)} %get-tuple-element.38), channel_id=1, source_target_pairs={{0,2},{2,0},{4,6},{6,4},{8,10},{10,8},{12,14},{14,12},{16,18},{18,... | collective-permute-start | bytes 98312 | tf_op jit(solution)/shard_map/ppermute | solution.py:421
  8.9 0.9 %collective-permute-done.2 = f32[32,256]{1,0:T(8,128)S(1)} collective-permute-done((f32[32,256]{1,0:T(8,128)S(1)}, f32[32,256]{1,0:T(8,128)S(1)}, u32[]{:S(2)}, u32[]{:S(2)}) %collective-permute-start.2) | collective-permute-done | bytes 32800 | tf_op jit(solution)/shard_map/ppermute | solution.py:421
  9.8 3.0 %collective-permute-start.3 = (f32[32,256]{1,0:T(8,128)S(1)}, f32[32,256]{1,0:T(8,128)S(1)}, u32[]{:S(2)}, u32[]{:S(2)}) collective-permute-start(f32[32,256]{1,0:T(8,128)S(1)} %add.3.terms_ref), channel_id=1, source_target_pairs={{0,18},{2,16},{4,22},{6,20},{8,26},{10,24},{12,30},{14,28},{16,2},... | collective-permute-start | bytes 98312 | tf_op jit(solution)/shard_map/ppermute | solution.py:421
  12.8 0.7 %collective-permute-start.10 = (f32[520,128]{1,0:T(8,128)S(1)}, f32[520,128]{1,0:T(8,128)S(1)}, u32[]{:S(2)}, u32[]{:S(2)}) collective-permute-start(f32[520,128]{1,0:T(8,128)S(1)} %get-tuple-element.44.packed_ref), channel_id=1, source_target_pairs={{2,4},{6,8},{10,12},{14,16},{18,20},{22,24},{26,28},{4,2},{8,6},{1... | collective-permute-start | bytes 798728 | tf_op jit(solution)/shard_map/ppermute | solution.py:491
  13.5 0.9 %collective-permute-done.3.other_ref = f32[32,256]{1,0:T(8,128)S(1)} collective-permute-done((f32[32,256]{1,0:T(8,128)S(1)}, f32[32,256]{1,0:T(8,128)S(1)}, u32[]{:S(2)}, u32[]{:S(2)}) %collective-permute-start.3) | collective-permute-done | bytes 32800 | tf_op jit(solution)/shard_map/ppermute | solution.py:421
  14.4 3.5 %collective-permute-start.5 = (f32[32,256]{1,0:T(8,128)S(1)}, f32[32,256]{1,0:T(8,128)S(1)}, u32[]{:S(2)}, u32[]{:S(2)}) collective-permute-start(f32[32,256]{1,0:T(8,128)S(1)} %sum.3.refs_0_), channel_id=1, source_target_pairs={{3,0},{2,1},{1,2},{0,3},{7,4},{6,5},{5,6},{4,7},{11,8},{10,9},{9,1... | collective-permute-start | bytes 98312 | tf_op jit(solution)/shard_map/ppermute | solution.py:430
  17.8 0.5 %collective-permute-start.8 = (f32[512,128]{1,0:T(8,128)S(1)}, f32[512,128]{1,0:T(8,128)S(1)}, u32[]{:S(2)}, u32[]{:S(2)}) collective-permute-start(f32[512,128]{1,0:T(8,128)S(1)} %get-tuple-element.41.refs_1_), channel_id=1, source_target_pairs={{1,0},{0,1},{3,2},{2,3},{5,4},{4,5},{7,6},{6,7},{9,8},{8,9},{11,10... | collective-permute-start | bytes 786440 | tf_op jit(solution)/shard_map/ppermute | solution.py:437
  18.4 1.2 %collective-permute-done.5.refs_1_ = f32[32,256]{1,0:T(8,128)S(1)} collective-permute-done((f32[32,256]{1,0:T(8,128)S(1)}, f32[32,256]{1,0:T(8,128)S(1)}, u32[]{:S(2)}, u32[]{:S(2)}) %collective-permute-start.5) | collective-permute-done | bytes 32800 | tf_op jit(solution)/shard_map/ppermute | solution.py:430
  19.5 1.7 %collective-permute-start.6 = (f32[64,256]{1,0:T(8,128)S(1)}, f32[64,256]{1,0:T(8,128)S(1)}, u32[]{:S(2)}, u32[]{:S(2)}) collective-permute-start(f32[64,256]{1,0:T(8,128)S(1)} %gather.1.terms_ref), channel_id=1, source_target_pairs={{0,10},{2,8},{4,14},{6,12},{8,2},{10,0},{12,6},{14,4},{16,26},{18,... | collective-permute-start | bytes 196616 | tf_op jit(solution)/shard_map/ppermute | solution.py:421
  21.4 0.6 %collective-permute-start.11 = (f32[128,512]{1,0:T(8,128)S(1)}, f32[128,512]{1,0:T(8,128)S(1)}, u32[]{:S(2)}, u32[]{:S(2)}) collective-permute-start(f32[128,512]{1,0:T(8,128)S(1)} %complete.1.refs_0_), channel_id=1, source_target_pairs={{1,0},{0,1},{3,2},{2,3},{5,4},{4,5},{7,6},{6,7},{9,8},{8,9},{11,10... | collective-permute-start | bytes 786440 | tf_op jit(solution)/shard_map/ppermute | solution.py:437
  22.1 1.3 %collective-permute-done.6.other_ref = f32[64,256]{1,0:T(8,128)S(1)} collective-permute-done((f32[64,256]{1,0:T(8,128)S(1)}, f32[64,256]{1,0:T(8,128)S(1)}, u32[]{:S(2)}, u32[]{:S(2)}) %collective-permute-start.6) | collective-permute-done | bytes 65568 | tf_op jit(solution)/shard_map/ppermute | solution.py:421
  23.4 2.2 %collective-permute-start.7 = (f32[64,256]{1,0:T(8,128)S(1)}, f32[64,256]{1,0:T(8,128)S(1)}, u32[]{:S(2)}, u32[]{:S(2)}) collective-permute-start(f32[64,256]{1,0:T(8,128)S(1)} %sum.4.terms_ref), channel_id=1, source_target_pairs={{0,6},{2,4},{4,2},{6,0},{8,14},{10,12},{12,10},{14,8},{16,22},{18,... | collective-permute-start | bytes 196616 | tf_op jit(solution)/shard_map/ppermute | solution.py:421
  25.6 2.0 %collective-permute-done.7.other_ref = f32[64,256]{1,0:T(8,128)S(1)} collective-permute-done((f32[64,256]{1,0:T(8,128)S(1)}, f32[64,256]{1,0:T(8,128)S(1)}, u32[]{:S(2)}, u32[]{:S(2)}) %collective-permute-start.7) | collective-permute-done | bytes 65568 | tf_op jit(solution)/shard_map/ppermute | solution.py:421
  27.6 1.9 %collective-permute-start.9 = (f32[64,256]{1,0:T(8,128)S(1)}, f32[64,256]{1,0:T(8,128)S(1)}, u32[]{:S(2)}, u32[]{:S(2)}) collective-permute-start(f32[64,256]{1,0:T(8,128)S(1)} %sum.5.kept_ref), channel_id=1, source_target_pairs={{0,2},{2,0},{4,6},{6,4},{8,10},{10,8},{12,14},{14,12},{16,18},{18,... | collective-permute-start | bytes 196616 | tf_op jit(solution)/shard_map/ppermute | solution.py:421
  29.5 0.7 %prepare.1 = (bf16[64,4096]{1,0:T(8,128)(2,1)S(1)}, bf16[64,4096]{1,0:T(8,128)(2,1)S(1)}) custom-call(f32[512,128]{1,0:T(8,128)S(1)} %get-tuple-element.39.refs_0_, f32[512,128]{1,0:T(8,128)S(1)} %get-tuple-element.41.refs_1_, f32[512,128]{1,0:T(8,128)S(1)} %collective-permute-done.4.refs_0_.refs_2_, f32[512,128]{1,0:T(8,128)S(1)} %collective-permute-done.8.refs_0_.refs_3_), custom_call_target="tpu_custom_call" | custom-call | tf_op jit(solution)/shard_map/prepare/pallas_call | solution.py:528
  30.4 2.9 %solve.1.mine_ref = f32[32,64]{1,0:T(8,128)S(1)} custom-call(f32[2,256]{1,0:T(2,128)S(1)} %copy-done.1, f32[2,256]{1,0:T(2,128)S(1)} %copy-done.2, f32[2,64,256]{2,1,0:T(8,128)S(1)} %copy-done, f32[64,256]{1,0:T(8,128)S(1)} %sum.5.kept_ref, f32[64,256]{1,0:T(8,128)S(1)} %collective-permute-done.9.received_ref), custom_call_target="tpu_custom_call" | custom-call | flops 500000000 | tf_op jit(solution)/shard_map/solve/pallas_call | solution.py:521
  33.3 1.4 %combine.1 = f32[32,48,128]{2,1,0:T(8,128)} custom-call(f32[32,64]{1,0:T(8,128)S(1)} %solve.1.mine_ref, f32[128,512]{1,0:T(8,128)S(1)} %complete.1.refs_0_, f32[128,512]{1,0:T(8,128)S(1)} %collective-permute-done.11.refs_1_, bf16[64,4096]{1,0:T(8,128)(2,1)S(1)} %get-tuple-element.45.refs_2_, bf16[64,4096]{1,0:T(8,128)(2,1)S(1)} %get-tuple-element.46.refs_3_), custom_call_target="tpu_custom_call" | custom-call | tf_op jit(solution)/shard_map/combine/pallas_call | solution.py:538
  (19 shorter events, 0.4 us)
Async XLA Ops:
  1.2 4.5 %collective-permute-start = (f32[520,128]{1,0:T(8,128)S(1)}, f32[520,128]{1,0:T(8,128)S(1)}, u32[]{:S(2)}, u32[]{:S(2)}) collective-permute-start(f32[520,128]{1,0:T(8,128)S(1)} %get-tuple-element.44.packed_ref), channel_id=1, source_target_pairs={{0,2},{2,0},{4,6},{6,4},{8,10},{10,8},{12,14},{14,12},{16,18},{18,... | collective-permute-start | bytes 798728 | tf_op jit(solution)/shard_map/ppermute | solution.py:421
  1.7 3.9 %collective-permute-start.1 = (f32[8,128]{1,0:T(8,128)S(1)}, f32[8,128]{1,0:T(8,128)S(1)}, u32[]{:S(2)}, u32[]{:S(2)}) collective-permute-start(f32[8,128]{1,0:T(8,128)S(1)} %get-tuple-element.27), channel_id=1, source_target_pairs={{2,4},{6,8},{10,12},{14,16},{18,20},{22,24},{26,28},{4,2},{8,6},{1... | collective-permute-start | bytes 12296 | tf_op jit(solution)/shard_map/ppermute | solution.py:457
  2.4 11.1 %collective-permute-start.4 = (f32[512,128]{1,0:T(8,128)S(1)}, f32[512,128]{1,0:T(8,128)S(1)}, u32[]{:S(2)}, u32[]{:S(2)}) collective-permute-start(f32[512,128]{1,0:T(8,128)S(1)} %get-tuple-element.39.refs_0_), channel_id=1, source_target_pairs={{1,0},{0,1},{3,2},{2,3},{5,4},{4,5},{7,6},{6,7},{9,8},{8,9},{11,10... | collective-permute-start | bytes 786440 | tf_op jit(solution)/shard_map/ppermute | solution.py:437
  6.3 3.5 %collective-permute-start.2 = (f32[32,256]{1,0:T(8,128)S(1)}, f32[32,256]{1,0:T(8,128)S(1)}, u32[]{:S(2)}, u32[]{:S(2)}) collective-permute-start(f32[32,256]{1,0:T(8,128)S(1)} %get-tuple-element.38), channel_id=1, source_target_pairs={{0,2},{2,0},{4,6},{6,4},{8,10},{10,8},{12,14},{14,12},{16,18},{18,... | collective-permute-start | bytes 98312 | tf_op jit(solution)/shard_map/ppermute | solution.py:421
  9.8 4.6 %collective-permute-start.3 = (f32[32,256]{1,0:T(8,128)S(1)}, f32[32,256]{1,0:T(8,128)S(1)}, u32[]{:S(2)}, u32[]{:S(2)}) collective-permute-start(f32[32,256]{1,0:T(8,128)S(1)} %add.3.terms_ref), channel_id=1, source_target_pairs={{0,18},{2,16},{4,22},{6,20},{8,26},{10,24},{12,30},{14,28},{16,2},... | collective-permute-start | bytes 98312 | tf_op jit(solution)/shard_map/ppermute | solution.py:421
  12.8 8.5 %collective-permute-start.10 = (f32[520,128]{1,0:T(8,128)S(1)}, f32[520,128]{1,0:T(8,128)S(1)}, u32[]{:S(2)}, u32[]{:S(2)}) collective-permute-start(f32[520,128]{1,0:T(8,128)S(1)} %get-tuple-element.44.packed_ref), channel_id=1, source_target_pairs={{2,4},{6,8},{10,12},{14,16},{18,20},{22,24},{26,28},{4,2},{8,6},{1... | collective-permute-start | bytes 798728 | tf_op jit(solution)/shard_map/ppermute | solution.py:491
  14.4 5.2 %collective-permute-start.5 = (f32[32,256]{1,0:T(8,128)S(1)}, f32[32,256]{1,0:T(8,128)S(1)}, u32[]{:S(2)}, u32[]{:S(2)}) collective-permute-start(f32[32,256]{1,0:T(8,128)S(1)} %sum.3.refs_0_), channel_id=1, source_target_pairs={{3,0},{2,1},{1,2},{0,3},{7,4},{6,5},{5,6},{4,7},{11,8},{10,9},{9,1... | collective-permute-start | bytes 98312 | tf_op jit(solution)/shard_map/ppermute | solution.py:430
  17.8 9.7 %collective-permute-start.8 = (f32[512,128]{1,0:T(8,128)S(1)}, f32[512,128]{1,0:T(8,128)S(1)}, u32[]{:S(2)}, u32[]{:S(2)}) collective-permute-start(f32[512,128]{1,0:T(8,128)S(1)} %get-tuple-element.41.refs_1_), channel_id=1, source_target_pairs={{1,0},{0,1},{3,2},{2,3},{5,4},{4,5},{7,6},{6,7},{9,8},{8,9},{11,10... | collective-permute-start | bytes 786440 | tf_op jit(solution)/shard_map/ppermute | solution.py:437
  19.5 3.9 %collective-permute-start.6 = (f32[64,256]{1,0:T(8,128)S(1)}, f32[64,256]{1,0:T(8,128)S(1)}, u32[]{:S(2)}, u32[]{:S(2)}) collective-permute-start(f32[64,256]{1,0:T(8,128)S(1)} %gather.1.terms_ref), channel_id=1, source_target_pairs={{0,10},{2,8},{4,14},{6,12},{8,2},{10,0},{12,6},{14,4},{16,26},{18,... | collective-permute-start | bytes 196616 | tf_op jit(solution)/shard_map/ppermute | solution.py:421
  21.4 11.9 %collective-permute-start.11 = (f32[128,512]{1,0:T(8,128)S(1)}, f32[128,512]{1,0:T(8,128)S(1)}, u32[]{:S(2)}, u32[]{:S(2)}) collective-permute-start(f32[128,512]{1,0:T(8,128)S(1)} %complete.1.refs_0_), channel_id=1, source_target_pairs={{1,0},{0,1},{3,2},{2,3},{5,4},{4,5},{7,6},{6,7},{9,8},{8,9},{11,10... | collective-permute-start | bytes 786440 | tf_op jit(solution)/shard_map/ppermute | solution.py:437
  23.4 4.1 %collective-permute-start.7 = (f32[64,256]{1,0:T(8,128)S(1)}, f32[64,256]{1,0:T(8,128)S(1)}, u32[]{:S(2)}, u32[]{:S(2)}) collective-permute-start(f32[64,256]{1,0:T(8,128)S(1)} %sum.4.terms_ref), channel_id=1, source_target_pairs={{0,6},{2,4},{4,2},{6,0},{8,14},{10,12},{12,10},{14,8},{16,22},{18,... | collective-permute-start | bytes 196616 | tf_op jit(solution)/shard_map/ppermute | solution.py:421
  27.6 2.8 %copy-start = (f32[2,64,256]{2,1,0:T(8,128)S(1)}, f32[2,64,256]{2,1,0:T(8,128)}, u32[]{:S(2)}) copy-start(f32[2,64,256]{2,1,0:T(8,128)} %noise_ref.1) | copy-start | bytes 393220
  27.6 2.8 %copy-start.1 = (f32[2,256]{1,0:T(2,128)S(1)}, f32[2,256]{1,0:T(2,128)}, u32[]{:S(2)}) copy-start(f32[2,256]{1,0:T(2,128)} %value_ref.1) | copy-start | bytes 6148
  27.6 2.8 %copy-start.2 = (f32[2,256]{1,0:T(2,128)S(1)}, f32[2,256]{1,0:T(2,128)}, u32[]{:S(2)}) copy-start(f32[2,256]{1,0:T(2,128)} %error_ref.1) | copy-start | bytes 6148
  27.6 2.8 %collective-permute-start.9 = (f32[64,256]{1,0:T(8,128)S(1)}, f32[64,256]{1,0:T(8,128)S(1)}, u32[]{:S(2)}, u32[]{:S(2)}) collective-permute-start(f32[64,256]{1,0:T(8,128)S(1)} %sum.5.kept_ref), channel_id=1, source_target_pairs={{0,2},{2,0},{4,6},{6,4},{8,10},{10,8},{12,14},{14,12},{16,18},{18,... | collective-permute-start | bytes 196616 | tf_op jit(solution)/shard_map/ppermute | solution.py:421

commit v15 on v14

--- a/solution.py
+++ b/solution.py
@@ -15,7 +15,7 @@
 
 
 SELECT_FLOPS = 1
-OWN_FLOPS, SUM_FLOPS, GATHER_FLOPS, SOLVE_FLOPS = 10**11, (10**9,7*10**8,1), 10**9, 5*10**8
+OWN_FLOPS, SUM_FLOPS, GATHER_FLOPS, SOLVE_FLOPS = 10**11, (3*10**9,1,5*10**8), 1, 10**9
 
 
 def estimate(flops):
@@ -288,7 +288,9 @@
     )
 
 
-def solve_kernel(parts, value_ref, error_ref, noise_ref, kept_ref, received_ref, mine_ref):
+def solve_kernel(
+    parts, value_ref, error_ref, noise_ref, kept_ref, received_ref, _high, _low, mine_ref
+):
     batches, members, count = noise_ref.shape
     local = members // parts
     own = lax.axis_index("mem")
@@ -348,48 +350,68 @@
         low_ref[:, k * LANES : (k + 1) * LANES] = low
 
 
-def combine_kernel(parts, fields, mine_ref, *refs):
-    forecast_refs = refs[:parts]
-    lagged_high_ref, lagged_low_ref, out_ref, done_ref, sems = refs[parts:]
-    local = mine_ref.shape[0]
-    high, low = split_two(mine_ref[...])
+def write_level(mine, parts_of, first, fields, chunks, done_ref, out_ref, sem):
+    local, planes = out_ref.shape[:2]
+    high, low = split_two(mine)
     left = jnp.concatenate([high, high, low], axis=1)
-    width = forecast_refs[0].shape[1]
-    chunks = width // LANES
     level = fields * chunks
-    planes = level + lagged_high_ref.shape[1] // LANES
+    for f in range(fields):
+        held_high, held_low = parts_of(f)
+        result = jnp.dot(
+            left,
+            jnp.concatenate([held_high, held_low, held_high], axis=0),
+            preferred_element_type=F32,
+        )
+        for c in range(chunks):
+            done_ref[pl.ds(f * chunks + c, local, stride=level), :] = result[
+                :, c * LANES : (c + 1) * LANES
+            ]
+    copy = pltpu.make_async_copy(
+        done_ref.reshape(local, level, LANES), out_ref.at[:, first : first + level, :], sem
+    )
+    copy.start()
+    return copy
+
+
+def combine_lagged_kernel(fields, chunks, mine_ref, high_ref, low_ref, out_ref, done_ref, sems):
+    level = fields * chunks
     copies = []
-    for first in [*range(level, planes, level), 0]:
-        for f in range(fields):
-            start = first + f * chunks
-            if first == 0:
-                held_high, held_low = split_two(
-                    jnp.concatenate(
-                        [ref[f * local : (f + 1) * local, :] for ref in forecast_refs], axis=0
-                    )
-                )
-            else:
-                lanes = slice((start - level) * LANES, (start - level) * LANES + width)
-                held_high, held_low = lagged_high_ref[:, lanes], lagged_low_ref[:, lanes]
-            result = jnp.dot(
-                left,
-                jnp.concatenate([held_high, held_low, held_high], axis=0),
-                preferred_element_type=F32,
+    for k in range(done_ref.shape[0]):
+
+        def parts_of(f):
+            start = (k * level + f * chunks) * LANES
+            lanes = slice(start, start + chunks * LANES)
+            return high_ref[:, lanes], low_ref[:, lanes]
+
+        copies.append(
+            write_level(
+                mine_ref[...],
+                parts_of,
+                (1 + k) * level,
+                fields,
+                chunks,
+                done_ref.at[k],
+                out_ref,
+                sems.at[k],
             )
-            for c in range(chunks):
-                done_ref[pl.ds(start + c, local, stride=planes), :] = result[
-                    :, c * LANES : (c + 1) * LANES
-                ]
-        copies.append(
-            pltpu.make_async_copy(
-                done_ref.reshape(local, planes, LANES).at[:, first : first + level, :],
-                out_ref.at[:, first : first + level, :],
-                sems.at[len(copies)],
-            )
-        )
-        copies[-1].start()
+        )
     for copy in copies:
         copy.wait()
+
+
+def combine_forecast_kernel(parts, fields, chunks, mine_ref, *refs):
+    forecast_refs = refs[:parts]
+    _, out_ref, done_ref, sem = refs[parts:]
+    local = mine_ref.shape[0]
+
+    def parts_of(f):
+        return split_two(
+            jnp.concatenate(
+                [ref[f * local : (f + 1) * local, :] for ref in forecast_refs], axis=0
+            )
+        )
+
+    write_level(mine_ref[...], parts_of, 0, fields, chunks, done_ref, out_ref, sem).wait()
 
 
 def shards(
@@ -501,30 +523,23 @@
         compiler_params=PARAMS,
         name="gather",
     )(terms, *from_other_mem(terms))
-    forecast = pl.pallas_call(
-        functools.partial(complete_kernel, *sizes),
-        out_shape=shape_of(stacked),
-        compiler_params=PARAMS,
-        name="complete",
-    )(lax.optimization_barrier((part, terms))[0], packed, inner, outer_row)
     bit = far // 2
     while bit > 1:
         last = bit == 2
+        before_last = terms
         terms = summed(
             terms,
             from_other_pair(terms, bit),
             SUM_FLOPS[1 + last],
-            *([others_second[0]] if last else []),
         )
         bit //= 2
+    forecast = pl.pallas_call(
+        functools.partial(complete_kernel, *sizes),
+        out_shape=shape_of(stacked),
+        compiler_params=PARAMS,
+        name="complete",
+    )(lax.optimization_barrier((part, before_last))[0], packed, inner, outer_row)
     priors = [terms, from_slab(terms, 1)]
-    mine = pl.pallas_call(
-        functools.partial(solve_kernel, parts),
-        out_shape=shape_of((members, all_members)),
-        compiler_params=PARAMS,
-        cost_estimate=estimate(SOLVE_FLOPS),
-        name="solve",
-    )(obs_value, obs_error, obs_noise, *priors)
     lagged_parts = pl.pallas_call(
         functools.partial(prepare_kernel, parts),
         out_shape=[shape_of((all_members, delayed.size // members), BF16)] * 2,
@@ -535,17 +550,35 @@
         second_half,
         *[half for both in zip(others_first, others_second) for half in both],
     )
+    mine = pl.pallas_call(
+        functools.partial(solve_kernel, parts),
+        out_shape=shape_of((members, all_members)),
+        compiler_params=PARAMS,
+        cost_estimate=estimate(SOLVE_FLOPS),
+        name="solve",
+    )(obs_value, obs_error, obs_noise, *priors, *lagged_parts)
+    level = fields * chunks
     out = pl.pallas_call(
-        functools.partial(combine_kernel, parts, fields),
+        functools.partial(combine_lagged_kernel, fields, chunks),
         out_shape=shape_of((members, planes, LANES)),
         out_specs=hbm,
         scratch_shapes=[
-            pltpu.VMEM((members * planes, LANES), F32),
-            pltpu.SemaphoreType.DMA((1 + lagged,)),
+            pltpu.VMEM((lagged, members * level, LANES), F32),
+            pltpu.SemaphoreType.DMA((lagged,)),
         ],
         compiler_params=PARAMS,
-        name="combine",
-    )(mine, forecast, *from_partners(forecast), *lagged_parts)
+        name="combine_lagged",
+    )(mine, *lagged_parts)
+    out = pl.pallas_call(
+        functools.partial(combine_forecast_kernel, parts, fields, chunks),
+        out_shape=shape_of((members, planes, LANES)),
+        in_specs=[pl.BlockSpec(memory_space=pltpu.VMEM)] * (1 + parts) + [hbm],
+        out_specs=hbm,
+        input_output_aliases={1 + parts: 0},
+        scratch_shapes=[pltpu.VMEM((members * level, LANES), F32), pltpu.SemaphoreType.DMA],
+        compiler_params=PARAMS,
+        name="combine_forecast",
+    )(mine, forecast, *from_partners(forecast), out)
     return out.reshape(members, 1 + lagged, fields, height, width)
 
 

time: 34.8 us -> 35 us (level)
  waiting for transfers between devices: 6.44 us -> 5.57 us
  Pallas kernels: 7.66 us -> 8.5 us
  local copies, waits for them, and re-layouts: 0.02 us -> 0.51 us
    ppermute x6, starting transfers between devices: 11.9 us -> 10.7 us  [from_slab(): return lax.ppermute(array, 'slab', [(i, i ^ bit) for i in range(slabs)])]
    ppermute x6, waiting for transfers between devices: 5.25 us -> 4.38 us  [from_slab(): return lax.ppermute(array, 'slab', [(i, i ^ bit) for i in range(slabs)])]
    pallas_call x1 -> x2, Pallas kernels: 1.36 us -> 2.22 us  [the longest x1 1.2 us: shards(): pl.pallas_call(functools.partial(combine_lagged_kernel, fields, chunks),...]
    ppermute x3, starting transfers between devices: 3.74 us -> 4.59 us  [from_partners(): lax.ppermute(array, 'mem', [((i + d) % parts, i) for i in range(parts)])]
    unnamed x6, local copies, waits for them, and re-layouts: 0.02 us -> 0.51 us
  transfers between devices with their start and end apart: 12 -> 12, of which waited for: 6 -> 6; matrix products, arithmetic and copies ran while one was open for 0% -> 0% of each run, Pallas kernels for 15% -> 18%
where the time goes in v15:
time: 35 us; the launch traced here: 34.8 us
  starting transfers between devices  20.1 us (57%)
  Pallas kernels  8.5 us (24%)
  waiting for transfers between devices  5.57 us (16%)
  local copies, waits for them, and re-layouts  0.51 us (1%)
    ppermute x6, starting transfers between devices, from_slab(): return lax.ppermute(array, 'slab', [(i, i ^ bit) for i in range(slabs)])  10.7 us
    ppermute x3, starting transfers between devices, from_partners(): lax.ppermute(array, 'mem', [((i + d) % parts, i) for i in range(parts)])  4.59 us
    ppermute x6, waiting for transfers between devices, from_slab(): return lax.ppermute(array, 'slab', [(i, i ^ bit) for i in range(slabs)])  4.38 us
    ppermute x1, starting transfers between devices, from_other_mem(): lax.ppermute(array, ('slab', 'mem'), [(i ^ 3, i) for i in range(slabs * p...  3.46 us
    pallas_call x1, Pallas kernels, shards(): pl.pallas_call(functools.partial(solve_kernel, parts), out_shape=shape_of...  2.92 us
    pallas_call x1, Pallas kernels, shards(): pl.pallas_call(functools.partial(combine_lagged_kernel, fields, chunks),...  1.2 us
    pallas_call x1, Pallas kernels, shards(): pl.pallas_call(functools.partial(load_kernel, chunks), out_shape=[shape_o...  1.18 us
    ppermute x1, waiting for transfers between devices, from_other_mem(): lax.ppermute(array, ('slab', 'mem'), [(i ^ 3, i) for i in range(slabs * p...  1.18 us
  transfers between devices with their start and end apart: 12, of which 6 were waited for; matrix products, arithmetic and copies ran while one was open for 0% of the time, Pallas kernels for 18%

profile of v15, /device:TPU:0, one launch (start us, length us, event | category | flops | bytes accessed | tf_op | source)
XLA Modules:
  0.0 34.8 jit_solution(442360477017960965)
XLA Ops:
  0.0 1.2 %load.1 = (f32[4,128]{1,0:T(4,128)S(1)}, f32[8,128]{1,0:T(8,128)S(1)}, s32[2,256]{1,0:T(2,128)S(1)}, s32[2,256]{1,0:T(2,128)S(1)}, s32[2,256]{1,0:T(2,128)S(1)},...) custom-call(f32[512,128]{1,0:T(8,128)} %bitcast.6, ...), custom_call_target="tpu_custom_call" | custom-call | tf_op jit(solution)/shard_map/load/pallas_call | solution.py:467
  1.2 0.5 %collective-permute-start = (f32[520,128]{1,0:T(8,128)S(1)}, f32[520,128]{1,0:T(8,128)S(1)}, u32[]{:S(2)}, u32[]{:S(2)}) collective-permute-start(f32[520,128]{1,0:T(8,128)S(1)} %get-tuple-element.46.packed_ref), channel_id=1, source_target_pairs={{0,2},{2,0},{4,6},{6,4},{8,10},{10,8},{12,14},{14,12},{16,18},{18,... | collective-permute-start | bytes 798728 | tf_op jit(solution)/shard_map/ppermute | solution.py:443
  1.7 0.6 %collective-permute-start.1 = (f32[8,128]{1,0:T(8,128)S(1)}, f32[8,128]{1,0:T(8,128)S(1)}, u32[]{:S(2)}, u32[]{:S(2)}) collective-permute-start(f32[8,128]{1,0:T(8,128)S(1)} %get-tuple-element.27), channel_id=1, source_target_pairs={{2,4},{6,8},{10,12},{14,16},{18,20},{22,24},{26,28},{4,2},{8,6},{1... | collective-permute-start | bytes 12296 | tf_op jit(solution)/shard_map/ppermute | solution.py:479
  2.4 2.6 %collective-permute-start.4 = (f32[512,128]{1,0:T(8,128)S(1)}, f32[512,128]{1,0:T(8,128)S(1)}, u32[]{:S(2)}, u32[]{:S(2)}) collective-permute-start(f32[512,128]{1,0:T(8,128)S(1)} %get-tuple-element.39.refs_0_), channel_id=1, source_target_pairs={{1,0},{0,1},{3,2},{2,3},{5,4},{4,5},{7,6},{6,7},{9,8},{8,9},{11,10... | collective-permute-start | bytes 786440 | tf_op jit(solution)/shard_map/ppermute | solution.py:459
  5.1 0.5 %own_row.1 = (f32[128,512]{1,0:T(8,128)S(1)}, f32[128,512]{1,0:T(8,128)S(1)}, f32[32,512]{1,0:T(8,128)S(1)}) custom-call(f32[520,128]{1,0:T(8,128)S(1)} %get-tuple-element.46.packed_ref, f32[4,128]{1,0:T(4,128)S(1)} %get-tuple-element.28.spread_ref, f32[8,128]{1,0:T(8,128)S(1)} %get-tuple-element.29.ratio_ref, ...), custom_call_target="tpu_custom_call" | custom-call | flops 99999997952 | tf_op jit(solution)/shard_map/own_row/pallas_call | solution.py:489
  5.7 0.6 %observe.1 = (f32[32,256]{1,0:T(8,128)S(1)}, f32[32,256]{1,0:T(8,128)S(1)}) custom-call(f32[520,128]{1,0:T(8,128)S(1)} %collective-permute-done.inner_ref, f32[8,128]{1,0:T(8,128)S(1)} %collective-permute-done.1.outer_ref, f32[32,512]{1,0:T(8,128)S(1)} %get-tuple-element.35.part_obs_ref, f32[128,512]{1,0:T(8,128)S(1)} %get-tuple-element.36.here_ref, ...), custom_call_target="tpu_custom_call" | custom-call | tf_op jit(solution)/shard_map/observe/pallas_call | solution.py:496
  6.3 2.7 %collective-permute-start.2 = (f32[32,256]{1,0:T(8,128)S(1)}, f32[32,256]{1,0:T(8,128)S(1)}, u32[]{:S(2)}, u32[]{:S(2)}) collective-permute-start(f32[32,256]{1,0:T(8,128)S(1)} %get-tuple-element.38), channel_id=1, source_target_pairs={{0,2},{2,0},{4,6},{6,4},{8,10},{10,8},{12,14},{14,12},{16,18},{18,... | collective-permute-start | bytes 98312 | tf_op jit(solution)/shard_map/ppermute | solution.py:443
  8.9 0.9 %collective-permute-done.2 = f32[32,256]{1,0:T(8,128)S(1)} collective-permute-done((f32[32,256]{1,0:T(8,128)S(1)}, f32[32,256]{1,0:T(8,128)S(1)}, u32[]{:S(2)}, u32[]{:S(2)}) %collective-permute-start.2) | collective-permute-done | bytes 32800 | tf_op jit(solution)/shard_map/ppermute | solution.py:443
  9.8 3.0 %collective-permute-start.3 = (f32[32,256]{1,0:T(8,128)S(1)}, f32[32,256]{1,0:T(8,128)S(1)}, u32[]{:S(2)}, u32[]{:S(2)}) collective-permute-start(f32[32,256]{1,0:T(8,128)S(1)} %add.3.terms_ref), channel_id=1, source_target_pairs={{0,18},{2,16},{4,22},{6,20},{8,26},{10,24},{12,30},{14,28},{16,2},... | collective-permute-start | bytes 98312 | tf_op jit(solution)/shard_map/ppermute | solution.py:443
  12.8 0.7 %collective-permute-start.10 = (f32[520,128]{1,0:T(8,128)S(1)}, f32[520,128]{1,0:T(8,128)S(1)}, u32[]{:S(2)}, u32[]{:S(2)}) collective-permute-start(f32[520,128]{1,0:T(8,128)S(1)} %get-tuple-element.46.packed_ref), channel_id=1, source_target_pairs={{2,4},{6,8},{10,12},{14,16},{18,20},{22,24},{26,28},{4,2},{8,6},{1... | collective-permute-start | bytes 798728 | tf_op jit(solution)/shard_map/ppermute | solution.py:513
  13.5 0.9 %collective-permute-done.3.other_ref = f32[32,256]{1,0:T(8,128)S(1)} collective-permute-done((f32[32,256]{1,0:T(8,128)S(1)}, f32[32,256]{1,0:T(8,128)S(1)}, u32[]{:S(2)}, u32[]{:S(2)}) %collective-permute-start.3) | collective-permute-done | bytes 32800 | tf_op jit(solution)/shard_map/ppermute | solution.py:443
  14.4 3.5 %collective-permute-start.5 = (f32[32,256]{1,0:T(8,128)S(1)}, f32[32,256]{1,0:T(8,128)S(1)}, u32[]{:S(2)}, u32[]{:S(2)}) collective-permute-start(f32[32,256]{1,0:T(8,128)S(1)} %sum.3.refs_0_), channel_id=1, source_target_pairs={{3,0},{2,1},{1,2},{0,3},{7,4},{6,5},{5,6},{4,7},{11,8},{10,9},{9,1... | collective-permute-start | bytes 98312 | tf_op jit(solution)/shard_map/ppermute | solution.py:452
  17.8 0.5 %collective-permute-start.9 = (f32[512,128]{1,0:T(8,128)S(1)}, f32[512,128]{1,0:T(8,128)S(1)}, u32[]{:S(2)}, u32[]{:S(2)}) collective-permute-start(f32[512,128]{1,0:T(8,128)S(1)} %get-tuple-element.41.refs_1_), channel_id=1, source_target_pairs={{1,0},{0,1},{3,2},{2,3},{5,4},{4,5},{7,6},{6,7},{9,8},{8,9},{11,10... | collective-permute-start | bytes 786440 | tf_op jit(solution)/shard_map/ppermute | solution.py:459
  18.4 1.2 %collective-permute-done.5.refs_1_ = f32[32,256]{1,0:T(8,128)S(1)} collective-permute-done((f32[32,256]{1,0:T(8,128)S(1)}, f32[32,256]{1,0:T(8,128)S(1)}, u32[]{:S(2)}, u32[]{:S(2)}) %collective-permute-start.5) | collective-permute-done | bytes 32800 | tf_op jit(solution)/shard_map/ppermute | solution.py:452
  19.5 1.7 %collective-permute-start.6 = (f32[64,256]{1,0:T(8,128)S(1)}, f32[64,256]{1,0:T(8,128)S(1)}, u32[]{:S(2)}, u32[]{:S(2)}) collective-permute-start(f32[64,256]{1,0:T(8,128)S(1)} %gather.1.terms_ref), channel_id=1, source_target_pairs={{0,10},{2,8},{4,14},{6,12},{8,2},{10,0},{12,6},{14,4},{16,26},{18,... | collective-permute-start | bytes 196616 | tf_op jit(solution)/shard_map/ppermute | solution.py:443
  21.3 2.1 %collective-permute-done.6.other_ref = f32[64,256]{1,0:T(8,128)S(1)} collective-permute-done((f32[64,256]{1,0:T(8,128)S(1)}, f32[64,256]{1,0:T(8,128)S(1)}, u32[]{:S(2)}, u32[]{:S(2)}) %collective-permute-start.6) | collective-permute-done | bytes 65568 | tf_op jit(solution)/shard_map/ppermute | solution.py:443
  23.4 2.2 %collective-permute-start.7 = (f32[64,256]{1,0:T(8,128)S(1)}, f32[64,256]{1,0:T(8,128)S(1)}, u32[]{:S(2)}, u32[]{:S(2)}) collective-permute-start(f32[64,256]{1,0:T(8,128)S(1)} %sum.4.terms_ref), channel_id=1, source_target_pairs={{0,6},{2,4},{4,2},{6,0},{8,14},{10,12},{12,10},{14,8},{16,22},{18,... | collective-permute-start | bytes 196616 | tf_op jit(solution)/shard_map/ppermute | solution.py:443
  25.8 1.5 %collective-permute-start.11 = (f32[128,512]{1,0:T(8,128)S(1)}, f32[128,512]{1,0:T(8,128)S(1)}, u32[]{:S(2)}, u32[]{:S(2)}) collective-permute-start(f32[128,512]{1,0:T(8,128)S(1)} %complete.1.refs_0_), channel_id=1, source_target_pairs={{1,0},{0,1},{3,2},{2,3},{5,4},{4,5},{7,6},{6,7},{9,8},{8,9},{11,10... | collective-permute-start | bytes 786440 | tf_op jit(solution)/shard_map/ppermute | solution.py:459
  27.6 0.7 %collective-permute-start.8 = (f32[64,256]{1,0:T(8,128)S(1)}, f32[64,256]{1,0:T(8,128)S(1)}, u32[]{:S(2)}, u32[]{:S(2)}) collective-permute-start(f32[64,256]{1,0:T(8,128)S(1)} %sum.5.kept_ref), channel_id=1, source_target_pairs={{0,2},{2,0},{4,6},{6,4},{8,10},{10,8},{12,14},{14,12},{16,18},{18,... | collective-permute-start | bytes 196616 | tf_op jit(solution)/shard_map/ppermute | solution.py:443
  28.2 0.7 %prepare.1 = (bf16[64,4096]{1,0:T(8,128)(2,1)S(1)}, bf16[64,4096]{1,0:T(8,128)(2,1)S(1)}) custom-call(f32[512,128]{1,0:T(8,128)S(1)} %get-tuple-element.39.refs_0_, f32[512,128]{1,0:T(8,128)S(1)} %get-tuple-element.41.refs_1_, f32[512,128]{1,0:T(8,128)S(1)} %collective-permute-done.4.refs_0_.refs_2_, f32[512,128]{1,0:T(8,128)S(1)} %collective-permute-done.9.refs_3_), custom_call_target="tpu_custom_call" | custom-call | tf_op jit(solution)/shard_map/prepare/pallas_call | solution.py:543
  29.1 0.5 %copy-done.1 = f32[2,256]{1,0:T(2,128)S(1)} copy-done((f32[2,256]{1,0:T(2,128)S(1)}, f32[2,256]{1,0:T(2,128)}, u32[]{:S(2)}) %copy-start.1) | copy-done | bytes 2072
  29.6 2.9 %solve.1.mine_ref = f32[32,64]{1,0:T(8,128)S(1)} custom-call(f32[2,256]{1,0:T(2,128)S(1)} %copy-done.1, f32[2,256]{1,0:T(2,128)S(1)} %copy-done.2, f32[2,64,256]{2,1,0:T(8,128)S(1)} %copy-done, f32[64,256]{1,0:T(8,128)S(1)} %sum.5.kept_ref, f32[64,256]{1,0:T(8,128)S(1)} %collective-permute-done.8.received_ref, ...), custom_call_target="tpu_custom_call" | custom-call | flops 1000000000 | tf_op jit(solution)/shard_map/solve/pallas_call | solution.py:553
  32.6 1.2 %combine_lagged.1.refs_2_ = f32[32,48,128]{2,1,0:T(8,128)} custom-call(f32[32,64]{1,0:T(8,128)S(1)} %solve.1.mine_ref, bf16[64,4096]{1,0:T(8,128)(2,1)S(1)} %get-tuple-element.42._high.high_ref, bf16[64,4096]{1,0:T(8,128)(2,1)S(1)} %get-tuple-element.43._low.low_ref), custom_call_target="tpu_custom_call" | custom-call | tf_op jit(solution)/shard_map/combine_lagged/pallas_call | solution.py:561
  33.8 1.0 %combine_forecast.1 = f32[32,48,128]{2,1,0:T(8,128)} custom-call(f32[32,64]{1,0:T(8,128)S(1)} %solve.1.mine_ref, f32[128,512]{1,0:T(8,128)S(1)} %complete.1.refs_0_, f32[128,512]{1,0:T(8,128)S(1)} %collective-permute-done.11.refs_1_, f32[32,48,128]{2,1,0:T(8,128)} %combine_lagged.1.refs_2_), custom_call_target="tpu_custom_call", output_to_operand_aliasing={{}: (3, {})} | custom-call | tf_op jit(solution)/shard_map/combine_forecast/pallas_call | solution.py:572
  (20 shorter events, 0.9 us)
Async XLA Ops:
  1.2 4.5 %collective-permute-start = (f32[520,128]{1,0:T(8,128)S(1)}, f32[520,128]{1,0:T(8,128)S(1)}, u32[]{:S(2)}, u32[]{:S(2)}) collective-permute-start(f32[520,128]{1,0:T(8,128)S(1)} %get-tuple-element.46.packed_ref), channel_id=1, source_target_pairs={{0,2},{2,0},{4,6},{6,4},{8,10},{10,8},{12,14},{14,12},{16,18},{18,... | collective-permute-start | bytes 798728 | tf_op jit(solution)/shard_map/ppermute | solution.py:443
  1.7 3.9 %collective-permute-start.1 = (f32[8,128]{1,0:T(8,128)S(1)}, f32[8,128]{1,0:T(8,128)S(1)}, u32[]{:S(2)}, u32[]{:S(2)}) collective-permute-start(f32[8,128]{1,0:T(8,128)S(1)} %get-tuple-element.27), channel_id=1, source_target_pairs={{2,4},{6,8},{10,12},{14,16},{18,20},{22,24},{26,28},{4,2},{8,6},{1... | collective-permute-start | bytes 12296 | tf_op jit(solution)/shard_map/ppermute | solution.py:479
  2.4 11.1 %collective-permute-start.4 = (f32[512,128]{1,0:T(8,128)S(1)}, f32[512,128]{1,0:T(8,128)S(1)}, u32[]{:S(2)}, u32[]{:S(2)}) collective-permute-start(f32[512,128]{1,0:T(8,128)S(1)} %get-tuple-element.39.refs_0_), channel_id=1, source_target_pairs={{1,0},{0,1},{3,2},{2,3},{5,4},{4,5},{7,6},{6,7},{9,8},{8,9},{11,10... | collective-permute-start | bytes 786440 | tf_op jit(solution)/shard_map/ppermute | solution.py:459
  6.3 3.5 %collective-permute-start.2 = (f32[32,256]{1,0:T(8,128)S(1)}, f32[32,256]{1,0:T(8,128)S(1)}, u32[]{:S(2)}, u32[]{:S(2)}) collective-permute-start(f32[32,256]{1,0:T(8,128)S(1)} %get-tuple-element.38), channel_id=1, source_target_pairs={{0,2},{2,0},{4,6},{6,4},{8,10},{10,8},{12,14},{14,12},{16,18},{18,... | collective-permute-start | bytes 98312 | tf_op jit(solution)/shard_map/ppermute | solution.py:443
  9.8 4.6 %collective-permute-start.3 = (f32[32,256]{1,0:T(8,128)S(1)}, f32[32,256]{1,0:T(8,128)S(1)}, u32[]{:S(2)}, u32[]{:S(2)}) collective-permute-start(f32[32,256]{1,0:T(8,128)S(1)} %add.3.terms_ref), channel_id=1, source_target_pairs={{0,18},{2,16},{4,22},{6,20},{8,26},{10,24},{12,30},{14,28},{16,2},... | collective-permute-start | bytes 98312 | tf_op jit(solution)/shard_map/ppermute | solution.py:443
  12.8 12.8 %collective-permute-start.10 = (f32[520,128]{1,0:T(8,128)S(1)}, f32[520,128]{1,0:T(8,128)S(1)}, u32[]{:S(2)}, u32[]{:S(2)}) collective-permute-start(f32[520,128]{1,0:T(8,128)S(1)} %get-tuple-element.46.packed_ref), channel_id=1, source_target_pairs={{2,4},{6,8},{10,12},{14,16},{18,20},{22,24},{26,28},{4,2},{8,6},{1... | collective-permute-start | bytes 798728 | tf_op jit(solution)/shard_map/ppermute | solution.py:513
  14.4 5.2 %collective-permute-start.5 = (f32[32,256]{1,0:T(8,128)S(1)}, f32[32,256]{1,0:T(8,128)S(1)}, u32[]{:S(2)}, u32[]{:S(2)}) collective-permute-start(f32[32,256]{1,0:T(8,128)S(1)} %sum.3.refs_0_), channel_id=1, source_target_pairs={{3,0},{2,1},{1,2},{0,3},{7,4},{6,5},{5,6},{4,7},{11,8},{10,9},{9,1... | collective-permute-start | bytes 98312 | tf_op jit(solution)/shard_map/ppermute | solution.py:452
  17.8 10.4 %collective-permute-start.9 = (f32[512,128]{1,0:T(8,128)S(1)}, f32[512,128]{1,0:T(8,128)S(1)}, u32[]{:S(2)}, u32[]{:S(2)}) collective-permute-start(f32[512,128]{1,0:T(8,128)S(1)} %get-tuple-element.41.refs_1_), channel_id=1, source_target_pairs={{1,0},{0,1},{3,2},{2,3},{5,4},{4,5},{7,6},{6,7},{9,8},{8,9},{11,10... | collective-permute-start | bytes 786440 | tf_op jit(solution)/shard_map/ppermute | solution.py:459
  19.5 3.9 %collective-permute-start.6 = (f32[64,256]{1,0:T(8,128)S(1)}, f32[64,256]{1,0:T(8,128)S(1)}, u32[]{:S(2)}, u32[]{:S(2)}) collective-permute-start(f32[64,256]{1,0:T(8,128)S(1)} %gather.1.terms_ref), channel_id=1, source_target_pairs={{0,10},{2,8},{4,14},{6,12},{8,2},{10,0},{12,6},{14,4},{16,26},{18,... | collective-permute-start | bytes 196616 | tf_op jit(solution)/shard_map/ppermute | solution.py:443
  23.4 4.1 %collective-permute-start.7 = (f32[64,256]{1,0:T(8,128)S(1)}, f32[64,256]{1,0:T(8,128)S(1)}, u32[]{:S(2)}, u32[]{:S(2)}) collective-permute-start(f32[64,256]{1,0:T(8,128)S(1)} %sum.4.terms_ref), channel_id=1, source_target_pairs={{0,6},{2,4},{4,2},{6,0},{8,14},{10,12},{12,10},{14,8},{16,22},{18,... | collective-permute-start | bytes 196616 | tf_op jit(solution)/shard_map/ppermute | solution.py:443
  25.8 8.0 %collective-permute-start.11 = (f32[128,512]{1,0:T(8,128)S(1)}, f32[128,512]{1,0:T(8,128)S(1)}, u32[]{:S(2)}, u32[]{:S(2)}) collective-permute-start(f32[128,512]{1,0:T(8,128)S(1)} %complete.1.refs_0_), channel_id=1, source_target_pairs={{1,0},{0,1},{3,2},{2,3},{5,4},{4,5},{7,6},{6,7},{9,8},{8,9},{11,10... | collective-permute-start | bytes 786440 | tf_op jit(solution)/shard_map/ppermute | solution.py:459
  27.5 1.6 %copy-start = (f32[2,64,256]{2,1,0:T(8,128)S(1)}, f32[2,64,256]{2,1,0:T(8,128)}, u32[]{:S(2)}) copy-start(f32[2,64,256]{2,1,0:T(8,128)} %noise_ref.1) | copy-start | bytes 393220
  27.6 1.6 %collective-permute-start.8 = (f32[64,256]{1,0:T(8,128)S(1)}, f32[64,256]{1,0:T(8,128)S(1)}, u32[]{:S(2)}, u32[]{:S(2)}) collective-permute-start(f32[64,256]{1,0:T(8,128)S(1)} %sum.5.kept_ref), channel_id=1, source_target_pairs={{0,2},{2,0},{4,6},{6,4},{8,10},{10,8},{12,14},{14,12},{16,18},{18,... | collective-permute-start | bytes 196616 | tf_op jit(solution)/shard_map/ppermute | solution.py:443
  28.2 0.9 %copy-start.2 = (f32[2,256]{1,0:T(2,128)S(1)}, f32[2,256]{1,0:T(2,128)}, u32[]{:S(2)}) copy-start(f32[2,256]{1,0:T(2,128)} %error_ref.1) | copy-start | bytes 6148
  29.0 0.7 %copy-start.1 = (f32[2,256]{1,0:T(2,128)S(1)}, f32[2,256]{1,0:T(2,128)}, u32[]{:S(2)}) copy-start(f32[2,256]{1,0:T(2,128)} %value_ref.1) | copy-start | bytes 6148

commit v16 on v12

--- a/solution.py
+++ b/solution.py
@@ -120,7 +120,7 @@
     flat = lambda ref: jnp.concatenate([ref[b : b + 1, :] for b in range(batches)], axis=1)
     rows, cols, kinds = flat(row_ref), flat(col_ref), flat(field_ref)
     own_row = lax.axis_index("slab")
-    for k, row in enumerate((own_row, own_row - 1)):
+    for k, row in enumerate((own_row, own_row + 1)):
         kinds_ref[k : k + 1, :] = jnp.where(rows == row, kinds, -1)
     at = lax.broadcasted_iota(jnp.int32, shape, 0).astype(F32) * 0.25
     taps_ref[...] = jnp.maximum(0.5 - jnp.abs(at - cols.astype(F32) * 0.25), 0.0).astype(BF16)
@@ -168,7 +168,7 @@
     fields,
     chunks,
     packed_ref,
-    up_ref,
+    next_ref,
     part_ref,
     part_obs_ref,
     here_ref,
@@ -178,12 +178,15 @@
     send_ref,
     partial_ref,
 ):
-    above, _ = weights(packed_ref, chunks)
-    _, below_of_above = weights(up_ref, chunks)
-    taken = above * stacked_planes(up_ref, members, fields, chunks)
-    given = below_of_above * here_ref[...]
+    _, below = weights(packed_ref, chunks)
+    above_of_below, _ = weights(next_ref, chunks)
+    taken = below * stacked_planes(next_ref, members, fields, chunks)
+    given = above_of_below * here_ref[...]
     partial_ref[...] = part_ref[...] + taken
-    picked = picked_values(jnp.concatenate([taken, given], axis=0), taps_ref[...])
+    picked = sum(
+        jnp.dot(part, taps_ref[...], preferred_element_type=F32)
+        for part in reversed(split_two(jnp.concatenate([taken, given], axis=0)))
+    )
     observed = part_obs_ref[...]
     for side in range(2):
         kinds = kinds_ref[side : side + 1, :]
@@ -201,10 +204,10 @@
     refs[-1][...] = terms_ref[...] + other_ref[...]
 
 
-def complete_kernel(members, fields, chunks, partial_ref, down_ref, packed_ref, forecast_ref):
-    _, below = weights(packed_ref, chunks)
-    forecast_ref[...] = partial_ref[...] + below * stacked_planes(
-        down_ref, members, fields, chunks
+def complete_kernel(members, fields, chunks, partial_ref, previous_ref, packed_ref, forecast_ref):
+    above, _ = weights(packed_ref, chunks)
+    forecast_ref[...] = partial_ref[...] + above * stacked_planes(
+        previous_ref, members, fields, chunks
     )
 
 
@@ -439,11 +442,10 @@
         name="load",
     )(*sources)
     up = [(i, i + 1) for i in range(slabs - 1)]
-    from_above = lax.ppermute(packed, "slab", up)
+    from_below = lax.ppermute(packed, "slab", [(j, i) for i, j in up])
     others_delayed = from_partners(
         lax.optimization_barrier((delayed, packed))[0]
     )
-    from_below = lax.ppermute(packed, "slab", [(j, i) for i, j in up])
     taps, kinds = pl.pallas_call(
         selector_kernel,
         out_shape=(shape_of((width, total), BF16), shape_of((2, total), jnp.int32)),
@@ -458,6 +460,7 @@
         cost_estimate=estimate(OWN_FLOPS),
         name="own_row",
     )(packed, *held[:2], taps, kinds)
+    from_above = lax.ppermute(lax.optimization_barrier((packed, part))[0], "slab", up)
     keep, send, partial = pl.pallas_call(
         functools.partial(observe_kernel, parts, *sizes),
         out_shape=(
@@ -467,7 +470,7 @@
         ),
         compiler_params=PARAMS,
         name="observe",
-    )(packed, from_above, part, part_obs, here, taps, kinds)
+    )(packed, from_below, part, part_obs, here, taps, kinds)
     def summed(terms, other, flops, *arrived):
         return pl.pallas_call(
             sum_kernel,
@@ -493,7 +496,7 @@
         compiler_params=PARAMS,
         name="complete",
     )(
-        lax.optimization_barrier((partial, after_far))[0], from_below, packed
+        lax.optimization_barrier((partial, after_far))[0], from_above, packed
     )
 
     prior = pl.pallas_call(

time: 33.9 us -> 32.6 us (0.962)
  waiting for transfers between devices: 9.01 us -> 6.38 us
  starting transfers between devices: 17 us -> 18.6 us
    ppermute x5, waiting for transfers between devices: 6.63 us -> 4.48 us  [from_slab(): return lax.ppermute(array, 'slab', [(i, i ^ bit) for i in range(slabs)])]
    ppermute x2, starting transfers between devices: 3.59 us -> 4.57 us  [from_partners(): lax.ppermute(array, 'mem', [((i + d) % parts, i) for i in range(parts)])]
    ppermute x1, waiting for transfers between devices: 2.37 us -> 1.89 us  [from_other_mem(): lax.ppermute(array, ('slab', 'mem'), [(i ^ 3, i) for i in range(slabs * p...]
    ppermute x1, starting transfers between devices: 2.37 us -> 2.77 us  [shards(): lax.ppermute(lax.optimization_barrier((packed, part))[0], 'slab', up)]
where the time goes in v16:
time: 32.6 us; the launch traced here: 32.4 us
  starting transfers between devices  18.6 us (57%)
  Pallas kernels  7.34 us (23%)
  waiting for transfers between devices  6.38 us (20%)
    ppermute x5, starting transfers between devices, from_slab(): return lax.ppermute(array, 'slab', [(i, i ^ bit) for i in range(slabs)])  8.39 us
    ppermute x2, starting transfers between devices, from_partners(): lax.ppermute(array, 'mem', [((i + d) % parts, i) for i in range(parts)])  4.57 us
    ppermute x5, waiting for transfers between devices, from_slab(): return lax.ppermute(array, 'slab', [(i, i ^ bit) for i in range(slabs)])  4.48 us
    pallas_call x1, Pallas kernels, shards(): pl.pallas_call(functools.partial(solve_kernel, parts), out_shape=shape_of...  2.93 us
    ppermute x1, starting transfers between devices, shards(): lax.ppermute(lax.optimization_barrier((packed, part))[0], 'slab', up)  2.77 us
    ppermute x1, waiting for transfers between devices, from_other_mem(): lax.ppermute(array, ('slab', 'mem'), [(i ^ 3, i) for i in range(slabs * p...  1.89 us
    ppermute x1, starting transfers between devices, from_other_mem(): lax.ppermute(array, ('slab', 'mem'), [(i ^ 3, i) for i in range(slabs * p...  1.55 us
    pallas_call x1, Pallas kernels, shards(): pl.pallas_call(functools.partial(combine_kernel, parts, fields), out_shap...  1.36 us
  transfers between devices with their start and end apart: 10, of which 6 were waited for; matrix products, arithmetic and copies ran while one was open for 0% of the time, Pallas kernels for 15%

profile of v16, /device:TPU:0, one launch (start us, length us, event | category | flops | bytes accessed | tf_op | source)
XLA Modules:
  0.0 32.4 jit_solution(8831420360638050937)
XLA Ops:
  0.0 1.0 %load.1 = (f32[520,128]{1,0:T(8,128)S(1)}, f32[4,128]{1,0:T(4,128)S(1)}, f32[8,128]{1,0:T(8,128)S(1)}, s32[2,256]{1,0:T(2,128)S(1)}, s32[2,256]{1,0:T(2,128)S(1)}, /*index=5*/s32[2,256]{1,0:T(2,128)S(1)}) custom-call(f32[512,128]{1,0:T(8,128)} %bitcast.7, f32[4,128]{1,0:T(4,128)} %bitcast.9, f32[8,128]{1,0:T(8,128)} %bitcast.8, s32[2,256]{1,0:T(2,128)} %refs_3_.1, ...), custom_call_target="tpu_custom_call" | custom-call | tf_op jit(solution)/shard_map/load/pallas_call | solution.py:435
  1.0 1.3 %collective-permute-start = (f32[520,128]{1,0:T(8,128)S(1)}, f32[520,128]{1,0:T(8,128)S(1)}, u32[]{:S(2)}, u32[]{:S(2)}) collective-permute-start(f32[520,128]{1,0:T(8,128)S(1)} %get-tuple-element.40.packed_ref), channel_id=1, source_target_pairs={{2,0},{4,2},{6,4},{8,6},{10,8},{12,10},{14,12},{16,14},{18,16},{20... | collective-permute-start | bytes 798728 | tf_op jit(solution)/shard_map/ppermute | solution.py:445
  2.3 3.0 %collective-permute-start.5 = (f32[1024,128]{1,0:T(8,128)}, f32[1024,128]{1,0:T(8,128)S(1)}, u32[]{:S(2)}, u32[]{:S(2)}) collective-permute-start(f32[1024,128]{1,0:T(8,128)} %bitcast.5), channel_id=1, source_target_pairs={{1,0},{0,1},{3,2},{2,3},{5,4},{4,5},{7,6},{6,7},{9,8},{8,9},{11,10... | collective-permute-start | bytes 1572872 | tf_op jit(solution)/shard_map/ppermute | solution.py:428
  5.3 0.2 selector.1
  5.5 0.5 %own_row.1 = (f32[128,512]{1,0:T(8,128)S(1)}, f32[128,512]{1,0:T(8,128)S(1)}, f32[32,512]{1,0:T(8,128)S(1)}) custom-call(f32[520,128]{1,0:T(8,128)S(1)} %get-tuple-element.40.packed_ref, f32[4,128]{1,0:T(4,128)S(1)} %get-tuple-element.25.spread_ref, f32[8,128]{1,0:T(8,128)S(1)} %get-tuple-element.26.ratio_ref, ...), custom_call_target="tpu_custom_call" | custom-call | flops 1 | tf_op jit(solution)/shard_map/own_row/pallas_call | solution.py:456
  6.0 2.8 %collective-permute-start.8 = (f32[520,128]{1,0:T(8,128)S(1)}, f32[520,128]{1,0:T(8,128)S(1)}, u32[]{:S(2)}, u32[]{:S(2)}) collective-permute-start(f32[520,128]{1,0:T(8,128)S(1)} %get-tuple-element.40.packed_ref), channel_id=1, source_target_pairs={{0,2},{2,4},{4,6},{6,8},{8,10},{10,12},{12,14},{14,16},{16,18},{18... | collective-permute-start | bytes 798728 | tf_op jit(solution)/shard_map/ppermute | solution.py:463
  8.8 0.5 %observe.1 = (f32[32,256]{1,0:T(8,128)S(1)}, f32[32,256]{1,0:T(8,128)S(1)}, f32[128,512]{1,0:T(8,128)S(1)}) custom-call(f32[520,128]{1,0:T(8,128)S(1)} %get-tuple-element.40.packed_ref, f32[520,128]{1,0:T(8,128)S(1)} %collective-permute-done.next_ref, f32[128,512]{1,0:T(8,128)S(1)} %get-tuple-element.32.part_ref, ...), custom_call_target="tpu_custom_call" | custom-call | tf_op jit(solution)/shard_map/observe/pallas_call | solution.py:464
  9.3 1.6 %collective-permute-start.1 = (f32[32,256]{1,0:T(8,128)S(1)}, f32[32,256]{1,0:T(8,128)S(1)}, u32[]{:S(2)}, u32[]{:S(2)}) collective-permute-start(f32[32,256]{1,0:T(8,128)S(1)} %get-tuple-element.36), channel_id=1, source_target_pairs={{0,2},{2,0},{4,6},{6,4},{8,10},{10,8},{12,14},{14,12},{16,18},{18,... | collective-permute-start | bytes 98312 | tf_op jit(solution)/shard_map/ppermute | solution.py:412
  10.9 0.9 %collective-permute-done.1 = f32[32,256]{1,0:T(8,128)S(1)} collective-permute-done((f32[32,256]{1,0:T(8,128)S(1)}, f32[32,256]{1,0:T(8,128)S(1)}, u32[]{:S(2)}, u32[]{:S(2)}) %collective-permute-start.1) | collective-permute-done | bytes 32800 | tf_op jit(solution)/shard_map/ppermute | solution.py:412
  11.8 2.5 %collective-permute-start.2 = (f32[32,256]{1,0:T(8,128)S(1)}, f32[32,256]{1,0:T(8,128)S(1)}, u32[]{:S(2)}, u32[]{:S(2)}) collective-permute-start(f32[32,256]{1,0:T(8,128)S(1)} %add.3.terms_ref), channel_id=1, source_target_pairs={{0,18},{2,16},{4,22},{6,20},{8,26},{10,24},{12,30},{14,28},{16,2},... | collective-permute-start | bytes 98312 | tf_op jit(solution)/shard_map/ppermute | solution.py:412
  14.4 1.7 %collective-permute-done.2.other_ref = f32[32,256]{1,0:T(8,128)S(1)} collective-permute-done((f32[32,256]{1,0:T(8,128)S(1)}, f32[32,256]{1,0:T(8,128)S(1)}, u32[]{:S(2)}, u32[]{:S(2)}) %collective-permute-start.2) | collective-permute-done | bytes 32800 | tf_op jit(solution)/shard_map/ppermute | solution.py:412
  16.1 1.5 %collective-permute-start.3 = (f32[32,256]{1,0:T(8,128)S(1)}, f32[32,256]{1,0:T(8,128)S(1)}, u32[]{:S(2)}, u32[]{:S(2)}) collective-permute-start(f32[32,256]{1,0:T(8,128)S(1)} %sum.3.terms_ref), channel_id=1, source_target_pairs={{0,10},{2,8},{4,14},{6,12},{8,2},{10,0},{12,6},{14,4},{16,26},{18,... | collective-permute-start | bytes 98312 | tf_op jit(solution)/shard_map/ppermute | solution.py:412
  17.6 0.1 complete.1.refs_0_
  17.7 1.6 %collective-permute-start.9 = (f32[128,512]{1,0:T(8,128)S(1)}, f32[128,512]{1,0:T(8,128)S(1)}, u32[]{:S(2)}, u32[]{:S(2)}) collective-permute-start(f32[128,512]{1,0:T(8,128)S(1)} %complete.1.refs_0_), channel_id=1, source_target_pairs={{1,0},{0,1},{3,2},{2,3},{5,4},{4,5},{7,6},{6,7},{9,8},{8,9},{11,10... | collective-permute-start | bytes 786440 | tf_op jit(solution)/shard_map/ppermute | solution.py:428
  19.3 0.1 collective-permute-done.3.other_ref
  19.4 2.2 %collective-permute-start.4 = (f32[32,256]{1,0:T(8,128)S(1)}, f32[32,256]{1,0:T(8,128)S(1)}, u32[]{:S(2)}, u32[]{:S(2)}) collective-permute-start(f32[32,256]{1,0:T(8,128)S(1)} %sum.4.terms_ref), channel_id=1, source_target_pairs={{0,6},{2,4},{4,2},{6,0},{8,14},{10,12},{12,10},{14,8},{16,22},{18,... | collective-permute-start | bytes 98312 | tf_op jit(solution)/shard_map/ppermute | solution.py:412
  21.6 1.6 %collective-permute-done.4.other_ref = f32[32,256]{1,0:T(8,128)S(1)} collective-permute-done((f32[32,256]{1,0:T(8,128)S(1)}, f32[32,256]{1,0:T(8,128)S(1)}, u32[]{:S(2)}, u32[]{:S(2)}) %collective-permute-start.4) | collective-permute-done | bytes 32800 | tf_op jit(solution)/shard_map/ppermute | solution.py:412
  23.2 1.5 %collective-permute-start.6 = (f32[32,256]{1,0:T(8,128)S(1)}, f32[32,256]{1,0:T(8,128)S(1)}, u32[]{:S(2)}, u32[]{:S(2)}) collective-permute-start(f32[32,256]{1,0:T(8,128)S(1)} %sum.5.refs_0_), channel_id=1, source_target_pairs={{3,0},{2,1},{1,2},{0,3},{7,4},{6,5},{5,6},{4,7},{11,8},{10,9},{9,1... | collective-permute-start | bytes 98312 | tf_op jit(solution)/shard_map/ppermute | solution.py:421
  24.8 1.9 %collective-permute-done.6.refs_1_ = f32[32,256]{1,0:T(8,128)S(1)} collective-permute-done((f32[32,256]{1,0:T(8,128)S(1)}, f32[32,256]{1,0:T(8,128)S(1)}, u32[]{:S(2)}, u32[]{:S(2)}) %collective-permute-start.6) | collective-permute-done | bytes 32800 | tf_op jit(solution)/shard_map/ppermute | solution.py:421
  26.7 0.5 %collective-permute-start.7 = (f32[64,256]{1,0:T(8,128)S(1)}, f32[64,256]{1,0:T(8,128)S(1)}, u32[]{:S(2)}, u32[]{:S(2)}) collective-permute-start(f32[64,256]{1,0:T(8,128)S(1)} %gather.1.kept_ref), channel_id=1, source_target_pairs={{0,2},{2,0},{4,6},{6,4},{8,10},{10,8},{12,14},{14,12},{16,18},{18,... | collective-permute-start | bytes 196616 | tf_op jit(solution)/shard_map/ppermute | solution.py:412
  27.2 0.7 %prepare.1 = (bf16[64,4096]{1,0:T(8,128)(2,1)S(1)}, bf16[64,4096]{1,0:T(8,128)(2,1)S(1)}) custom-call(f32[1024,128]{1,0:T(8,128)S(1)} %bitcast.6, f32[1024,128]{1,0:T(8,128)S(1)} %collective-permute-done.5.refs_0_.refs_1_), custom_call_target="tpu_custom_call" | custom-call | tf_op jit(solution)/shard_map/prepare/pallas_call | solution.py:516
  27.9 0.2 collective-permute-done.7.received_ref
  28.1 2.9 %solve.1.mine_ref = f32[32,64]{1,0:T(8,128)S(1)} custom-call(f32[2,256]{1,0:T(2,128)S(1)} %copy-done.2, f32[2,256]{1,0:T(2,128)S(1)} %copy-done.3, f32[2,64,256]{2,1,0:T(8,128)S(1)} %copy-done.1, f32[64,256]{1,0:T(8,128)S(1)} %gather.1.kept_ref, f32[64,256]{1,0:T(8,128)S(1)} %collective-permute-done.7.received_ref), custom_call_target="tpu_custom_call" | custom-call | flops 500000000 | tf_op jit(solution)/shard_map/solve/pallas_call | solution.py:509
  31.1 1.4 %combine.1 = f32[32,48,128]{2,1,0:T(8,128)} custom-call(f32[32,64]{1,0:T(8,128)S(1)} %solve.1.mine_ref, f32[128,512]{1,0:T(8,128)S(1)} %complete.1.refs_0_, f32[128,512]{1,0:T(8,128)S(1)} %collective-permute-done.9.refs_1_, bf16[64,4096]{1,0:T(8,128)(2,1)S(1)} %get-tuple-element.41.refs_2_, bf16[64,4096]{1,0:T(8,128)(2,1)S(1)} %get-tuple-element.42.refs_3_), custom_call_target="tpu_custom_call" | custom-call | tf_op jit(solution)/shard_map/combine/pallas_call | solution.py:522
  (17 shorter events, 0.1 us)
Async XLA Ops:
  1.0 7.8 %collective-permute-start = (f32[520,128]{1,0:T(8,128)S(1)}, f32[520,128]{1,0:T(8,128)S(1)}, u32[]{:S(2)}, u32[]{:S(2)}) collective-permute-start(f32[520,128]{1,0:T(8,128)S(1)} %get-tuple-element.40.packed_ref), channel_id=1, source_target_pairs={{2,0},{4,2},{6,4},{8,6},{10,8},{12,10},{14,12},{16,14},{18,16},{20... | collective-permute-start | bytes 798728 | tf_op jit(solution)/shard_map/ppermute | solution.py:445
  2.3 20.9 %collective-permute-start.5 = (f32[1024,128]{1,0:T(8,128)}, f32[1024,128]{1,0:T(8,128)S(1)}, u32[]{:S(2)}, u32[]{:S(2)}) collective-permute-start(f32[1024,128]{1,0:T(8,128)} %bitcast.5), channel_id=1, source_target_pairs={{1,0},{0,1},{3,2},{2,3},{5,4},{4,5},{7,6},{6,7},{9,8},{8,9},{11,10... | collective-permute-start | bytes 1572872 | tf_op jit(solution)/shard_map/ppermute | solution.py:428
  6.0 11.6 %collective-permute-start.8 = (f32[520,128]{1,0:T(8,128)S(1)}, f32[520,128]{1,0:T(8,128)S(1)}, u32[]{:S(2)}, u32[]{:S(2)}) collective-permute-start(f32[520,128]{1,0:T(8,128)S(1)} %get-tuple-element.40.packed_ref), channel_id=1, source_target_pairs={{0,2},{2,4},{4,6},{6,8},{8,10},{10,12},{12,14},{14,16},{16,18},{18... | collective-permute-start | bytes 798728 | tf_op jit(solution)/shard_map/ppermute | solution.py:463
  9.3 2.5 %collective-permute-start.1 = (f32[32,256]{1,0:T(8,128)S(1)}, f32[32,256]{1,0:T(8,128)S(1)}, u32[]{:S(2)}, u32[]{:S(2)}) collective-permute-start(f32[32,256]{1,0:T(8,128)S(1)} %get-tuple-element.36), channel_id=1, source_target_pairs={{0,2},{2,0},{4,6},{6,4},{8,10},{10,8},{12,14},{14,12},{16,18},{18,... | collective-permute-start | bytes 98312 | tf_op jit(solution)/shard_map/ppermute | solution.py:412
  11.8 4.2 %collective-permute-start.2 = (f32[32,256]{1,0:T(8,128)S(1)}, f32[32,256]{1,0:T(8,128)S(1)}, u32[]{:S(2)}, u32[]{:S(2)}) collective-permute-start(f32[32,256]{1,0:T(8,128)S(1)} %add.3.terms_ref), channel_id=1, source_target_pairs={{0,18},{2,16},{4,22},{6,20},{8,26},{10,24},{12,30},{14,28},{16,2},... | collective-permute-start | bytes 98312 | tf_op jit(solution)/shard_map/ppermute | solution.py:412
  16.1 3.3 %collective-permute-start.3 = (f32[32,256]{1,0:T(8,128)S(1)}, f32[32,256]{1,0:T(8,128)S(1)}, u32[]{:S(2)}, u32[]{:S(2)}) collective-permute-start(f32[32,256]{1,0:T(8,128)S(1)} %sum.3.terms_ref), channel_id=1, source_target_pairs={{0,10},{2,8},{4,14},{6,12},{8,2},{10,0},{12,6},{14,4},{16,26},{18,... | collective-permute-start | bytes 98312 | tf_op jit(solution)/shard_map/ppermute | solution.py:412
  17.7 13.3 %collective-permute-start.9 = (f32[128,512]{1,0:T(8,128)S(1)}, f32[128,512]{1,0:T(8,128)S(1)}, u32[]{:S(2)}, u32[]{:S(2)}) collective-permute-start(f32[128,512]{1,0:T(8,128)S(1)} %complete.1.refs_0_), channel_id=1, source_target_pairs={{1,0},{0,1},{3,2},{2,3},{5,4},{4,5},{7,6},{6,7},{9,8},{8,9},{11,10... | collective-permute-start | bytes 786440 | tf_op jit(solution)/shard_map/ppermute | solution.py:428
  19.4 7.8 %copy-start = (f32[32,2,4,1,512]{4,3,2,1,0:T(1,128)S(1)}, f32[32,2,4,1,512]{4,3,2,1,0:T(1,128)}, u32[]{:S(2)}) copy-start(f32[32,2,4,1,512]{4,3,2,1,0:T(1,128)} %param.11) | copy-start | bytes 1572868
  19.4 3.8 %collective-permute-start.4 = (f32[32,256]{1,0:T(8,128)S(1)}, f32[32,256]{1,0:T(8,128)S(1)}, u32[]{:S(2)}, u32[]{:S(2)}) collective-permute-start(f32[32,256]{1,0:T(8,128)S(1)} %sum.4.terms_ref), channel_id=1, source_target_pairs={{0,6},{2,4},{4,2},{6,0},{8,14},{10,12},{12,10},{14,8},{16,22},{18,... | collective-permute-start | bytes 98312 | tf_op jit(solution)/shard_map/ppermute | solution.py:412
  23.2 3.4 %collective-permute-start.6 = (f32[32,256]{1,0:T(8,128)S(1)}, f32[32,256]{1,0:T(8,128)S(1)}, u32[]{:S(2)}, u32[]{:S(2)}) collective-permute-start(f32[32,256]{1,0:T(8,128)S(1)} %sum.5.refs_0_), channel_id=1, source_target_pairs={{3,0},{2,1},{1,2},{0,3},{7,4},{6,5},{5,6},{4,7},{11,8},{10,9},{9,1... | collective-permute-start | bytes 98312 | tf_op jit(solution)/shard_map/ppermute | solution.py:421
  26.7 1.4 %copy-start.1 = (f32[2,64,256]{2,1,0:T(8,128)S(1)}, f32[2,64,256]{2,1,0:T(8,128)}, u32[]{:S(2)}) copy-start(f32[2,64,256]{2,1,0:T(8,128)} %noise_ref.1) | copy-start | bytes 393220
  26.7 1.4 %copy-start.2 = (f32[2,256]{1,0:T(2,128)S(1)}, f32[2,256]{1,0:T(2,128)}, u32[]{:S(2)}) copy-start(f32[2,256]{1,0:T(2,128)} %value_ref.1) | copy-start | bytes 6148
  26.7 1.4 %copy-start.3 = (f32[2,256]{1,0:T(2,128)S(1)}, f32[2,256]{1,0:T(2,128)}, u32[]{:S(2)}) copy-start(f32[2,256]{1,0:T(2,128)} %error_ref.1) | copy-start | bytes 6148
  26.7 1.4 %collective-permute-start.7 = (f32[64,256]{1,0:T(8,128)S(1)}, f32[64,256]{1,0:T(8,128)S(1)}, u32[]{:S(2)}, u32[]{:S(2)}) collective-permute-start(f32[64,256]{1,0:T(8,128)S(1)} %gather.1.kept_ref), channel_id=1, source_target_pairs={{0,2},{2,0},{4,6},{6,4},{8,10},{10,8},{12,14},{14,12},{16,18},{18,... | collective-permute-start | bytes 196616 | tf_op jit(solution)/shard_map/ppermute | solution.py:412

commit v17 on v16

--- a/solution.py
+++ b/solution.py
@@ -443,9 +443,6 @@
     )(*sources)
     up = [(i, i + 1) for i in range(slabs - 1)]
     from_below = lax.ppermute(packed, "slab", [(j, i) for i, j in up])
-    others_delayed = from_partners(
-        lax.optimization_barrier((delayed, packed))[0]
-    )
     taps, kinds = pl.pallas_call(
         selector_kernel,
         out_shape=(shape_of((width, total), BF16), shape_of((2, total), jnp.int32)),
@@ -460,6 +457,7 @@
         cost_estimate=estimate(OWN_FLOPS),
         name="own_row",
     )(packed, *held[:2], taps, kinds)
+    others_delayed = from_partners(lax.optimization_barrier((delayed, part))[0])
     from_above = lax.ppermute(lax.optimization_barrier((packed, part))[0], "slab", up)
     keep, send, partial = pl.pallas_call(
         functools.partial(observe_kernel, parts, *sizes),

time: 32.6 us -> 32.6 us (level)
  no operation moved by 1% of the time
where the time goes in v17:
time: 32.6 us; the launch traced here: 32.4 us
  starting transfers between devices  18.4 us (56%)
  Pallas kernels  7.41 us (23%)
  waiting for transfers between devices  6.46 us (20%)
    ppermute x5, starting transfers between devices, from_slab(): return lax.ppermute(array, 'slab', [(i, i ^ bit) for i in range(slabs)])  8.27 us
    ppermute x2, starting transfers between devices, from_partners(): lax.ppermute(array, 'mem', [((i + d) % parts, i) for i in range(parts)])  4.56 us
    ppermute x5, waiting for transfers between devices, from_slab(): return lax.ppermute(array, 'slab', [(i, i ^ bit) for i in range(slabs)])  4.48 us
    pallas_call x1, Pallas kernels, shards(): pl.pallas_call(functools.partial(solve_kernel, parts), out_shape=shape_of...  2.94 us
    ppermute x1, starting transfers between devices, shards(): lax.ppermute(lax.optimization_barrier((packed, part))[0], 'slab', up)  2.76 us
    ppermute x1, waiting for transfers between devices, from_other_mem(): lax.ppermute(array, ('slab', 'mem'), [(i ^ 3, i) for i in range(slabs * p...  1.97 us
    ppermute x1, starting transfers between devices, from_other_mem(): lax.ppermute(array, ('slab', 'mem'), [(i ^ 3, i) for i in range(slabs * p...  1.54 us
    pallas_call x1, Pallas kernels, shards(): pl.pallas_call(functools.partial(combine_kernel, parts, fields), out_shap...  1.36 us
  transfers between devices with their start and end apart: 10, of which 6 were waited for; matrix products, arithmetic and copies ran while one was open for 0% of the time, Pallas kernels for 15%

profile of v17, /device:TPU:0, one launch (start us, length us, event | category | flops | bytes accessed | tf_op | source)
XLA Modules:
  0.0 32.4 jit_solution(9777002673640548667)
XLA Ops:
  0.0 1.1 %load.1 = (f32[520,128]{1,0:T(8,128)S(1)}, f32[4,128]{1,0:T(4,128)S(1)}, f32[8,128]{1,0:T(8,128)S(1)}, s32[2,256]{1,0:T(2,128)S(1)}, s32[2,256]{1,0:T(2,128)S(1)}, /*index=5*/s32[2,256]{1,0:T(2,128)S(1)}) custom-call(f32[512,128]{1,0:T(8,128)} %bitcast.7, f32[4,128]{1,0:T(4,128)} %bitcast.9, f32[8,128]{1,0:T(8,128)} %bitcast.8, s32[2,256]{1,0:T(2,128)} %refs_3_.1, ...), custom_call_target="tpu_custom_call" | custom-call | tf_op jit(solution)/shard_map/load/pallas_call | solution.py:435
  1.1 1.3 %collective-permute-start = (f32[520,128]{1,0:T(8,128)S(1)}, f32[520,128]{1,0:T(8,128)S(1)}, u32[]{:S(2)}, u32[]{:S(2)}) collective-permute-start(f32[520,128]{1,0:T(8,128)S(1)} %get-tuple-element.40.packed_ref), channel_id=1, source_target_pairs={{2,0},{4,2},{6,4},{8,6},{10,8},{12,10},{14,12},{16,14},{18,16},{20... | collective-permute-start | bytes 798728 | tf_op jit(solution)/shard_map/ppermute | solution.py:445
  2.4 0.2 selector.1
  2.6 0.5 %own_row.1 = (f32[128,512]{1,0:T(8,128)S(1)}, f32[128,512]{1,0:T(8,128)S(1)}, f32[32,512]{1,0:T(8,128)S(1)}) custom-call(f32[520,128]{1,0:T(8,128)S(1)} %get-tuple-element.40.packed_ref, f32[4,128]{1,0:T(4,128)S(1)} %get-tuple-element.25.spread_ref, f32[8,128]{1,0:T(8,128)S(1)} %get-tuple-element.26.ratio_ref, ...), custom_call_target="tpu_custom_call" | custom-call | flops 1 | tf_op jit(solution)/shard_map/own_row/pallas_call | solution.py:453
  3.1 3.0 %collective-permute-start.5 = (f32[1024,128]{1,0:T(8,128)S(1)}, f32[1024,128]{1,0:T(8,128)S(1)}, u32[]{:S(2)}, u32[]{:S(2)}) collective-permute-start(f32[1024,128]{1,0:T(8,128)S(1)} %bitcast.5), channel_id=1, source_target_pairs={{1,0},{0,1},{3,2},{2,3},{5,4},{4,5},{7,6},{6,7},{9,8},{8,9},{11,10... | collective-permute-start | bytes 1572872 | tf_op jit(solution)/shard_map/ppermute | solution.py:428
  6.1 2.8 %collective-permute-start.8 = (f32[520,128]{1,0:T(8,128)S(1)}, f32[520,128]{1,0:T(8,128)S(1)}, u32[]{:S(2)}, u32[]{:S(2)}) collective-permute-start(f32[520,128]{1,0:T(8,128)S(1)} %get-tuple-element.40.packed_ref), channel_id=1, source_target_pairs={{0,2},{2,4},{4,6},{6,8},{8,10},{10,12},{12,14},{14,16},{16,18},{18... | collective-permute-start | bytes 798728 | tf_op jit(solution)/shard_map/ppermute | solution.py:461
  8.9 0.5 %observe.1 = (f32[32,256]{1,0:T(8,128)S(1)}, f32[32,256]{1,0:T(8,128)S(1)}, f32[128,512]{1,0:T(8,128)S(1)}) custom-call(f32[520,128]{1,0:T(8,128)S(1)} %get-tuple-element.40.packed_ref, f32[520,128]{1,0:T(8,128)S(1)} %collective-permute-done.next_ref, f32[128,512]{1,0:T(8,128)S(1)} %get-tuple-element.32.part_ref, ...), custom_call_target="tpu_custom_call" | custom-call | tf_op jit(solution)/shard_map/observe/pallas_call | solution.py:462
  9.4 1.6 %collective-permute-start.1 = (f32[32,256]{1,0:T(8,128)S(1)}, f32[32,256]{1,0:T(8,128)S(1)}, u32[]{:S(2)}, u32[]{:S(2)}) collective-permute-start(f32[32,256]{1,0:T(8,128)S(1)} %get-tuple-element.36), channel_id=1, source_target_pairs={{0,2},{2,0},{4,6},{6,4},{8,10},{10,8},{12,14},{14,12},{16,18},{18,... | collective-permute-start | bytes 98312 | tf_op jit(solution)/shard_map/ppermute | solution.py:412
  11.0 0.9 %collective-permute-done.1 = f32[32,256]{1,0:T(8,128)S(1)} collective-permute-done((f32[32,256]{1,0:T(8,128)S(1)}, f32[32,256]{1,0:T(8,128)S(1)}, u32[]{:S(2)}, u32[]{:S(2)}) %collective-permute-start.1) | collective-permute-done | bytes 32800 | tf_op jit(solution)/shard_map/ppermute | solution.py:412
  11.9 2.5 %collective-permute-start.2 = (f32[32,256]{1,0:T(8,128)S(1)}, f32[32,256]{1,0:T(8,128)S(1)}, u32[]{:S(2)}, u32[]{:S(2)}) collective-permute-start(f32[32,256]{1,0:T(8,128)S(1)} %add.3.terms_ref), channel_id=1, source_target_pairs={{0,18},{2,16},{4,22},{6,20},{8,26},{10,24},{12,30},{14,28},{16,2},... | collective-permute-start | bytes 98312 | tf_op jit(solution)/shard_map/ppermute | solution.py:412
  14.4 1.7 %collective-permute-done.2.other_ref = f32[32,256]{1,0:T(8,128)S(1)} collective-permute-done((f32[32,256]{1,0:T(8,128)S(1)}, f32[32,256]{1,0:T(8,128)S(1)}, u32[]{:S(2)}, u32[]{:S(2)}) %collective-permute-start.2) | collective-permute-done | bytes 32800 | tf_op jit(solution)/shard_map/ppermute | solution.py:412
  16.1 1.5 %collective-permute-start.3 = (f32[32,256]{1,0:T(8,128)S(1)}, f32[32,256]{1,0:T(8,128)S(1)}, u32[]{:S(2)}, u32[]{:S(2)}) collective-permute-start(f32[32,256]{1,0:T(8,128)S(1)} %sum.3.terms_ref), channel_id=1, source_target_pairs={{0,10},{2,8},{4,14},{6,12},{8,2},{10,0},{12,6},{14,4},{16,26},{18,... | collective-permute-start | bytes 98312 | tf_op jit(solution)/shard_map/ppermute | solution.py:412
  17.7 0.1 complete.1.refs_0_
  17.8 1.6 %collective-permute-start.9 = (f32[128,512]{1,0:T(8,128)S(1)}, f32[128,512]{1,0:T(8,128)S(1)}, u32[]{:S(2)}, u32[]{:S(2)}) collective-permute-start(f32[128,512]{1,0:T(8,128)S(1)} %complete.1.refs_0_), channel_id=1, source_target_pairs={{1,0},{0,1},{3,2},{2,3},{5,4},{4,5},{7,6},{6,7},{9,8},{8,9},{11,10... | collective-permute-start | bytes 786440 | tf_op jit(solution)/shard_map/ppermute | solution.py:428
  19.3 0.1 collective-permute-done.3.other_ref
  19.5 2.1 %collective-permute-start.4 = (f32[32,256]{1,0:T(8,128)S(1)}, f32[32,256]{1,0:T(8,128)S(1)}, u32[]{:S(2)}, u32[]{:S(2)}) collective-permute-start(f32[32,256]{1,0:T(8,128)S(1)} %sum.4.terms_ref), channel_id=1, source_target_pairs={{0,6},{2,4},{4,2},{6,0},{8,14},{10,12},{12,10},{14,8},{16,22},{18,... | collective-permute-start | bytes 98312 | tf_op jit(solution)/shard_map/ppermute | solution.py:412
  21.6 1.6 %collective-permute-done.4.other_ref = f32[32,256]{1,0:T(8,128)S(1)} collective-permute-done((f32[32,256]{1,0:T(8,128)S(1)}, f32[32,256]{1,0:T(8,128)S(1)}, u32[]{:S(2)}, u32[]{:S(2)}) %collective-permute-start.4) | collective-permute-done | bytes 32800 | tf_op jit(solution)/shard_map/ppermute | solution.py:412
  23.2 1.5 %collective-permute-start.6 = (f32[32,256]{1,0:T(8,128)S(1)}, f32[32,256]{1,0:T(8,128)S(1)}, u32[]{:S(2)}, u32[]{:S(2)}) collective-permute-start(f32[32,256]{1,0:T(8,128)S(1)} %sum.5.refs_0_), channel_id=1, source_target_pairs={{3,0},{2,1},{1,2},{0,3},{7,4},{6,5},{5,6},{4,7},{11,8},{10,9},{9,1... | collective-permute-start | bytes 98312 | tf_op jit(solution)/shard_map/ppermute | solution.py:421
  24.8 2.0 %collective-permute-done.6.refs_1_ = f32[32,256]{1,0:T(8,128)S(1)} collective-permute-done((f32[32,256]{1,0:T(8,128)S(1)}, f32[32,256]{1,0:T(8,128)S(1)}, u32[]{:S(2)}, u32[]{:S(2)}) %collective-permute-start.6) | collective-permute-done | bytes 32800 | tf_op jit(solution)/shard_map/ppermute | solution.py:421
  26.8 0.4 %collective-permute-start.7 = (f32[64,256]{1,0:T(8,128)S(1)}, f32[64,256]{1,0:T(8,128)S(1)}, u32[]{:S(2)}, u32[]{:S(2)}) collective-permute-start(f32[64,256]{1,0:T(8,128)S(1)} %gather.1.kept_ref), channel_id=1, source_target_pairs={{0,2},{2,0},{4,6},{6,4},{8,10},{10,8},{12,14},{14,12},{16,18},{18,... | collective-permute-start | bytes 196616 | tf_op jit(solution)/shard_map/ppermute | solution.py:412
  27.2 0.7 %prepare.1 = (bf16[64,4096]{1,0:T(8,128)(2,1)S(1)}, bf16[64,4096]{1,0:T(8,128)(2,1)S(1)}) custom-call(f32[1024,128]{1,0:T(8,128)S(1)} %bitcast.6, f32[1024,128]{1,0:T(8,128)S(1)} %collective-permute-done.5.refs_0_.refs_1_), custom_call_target="tpu_custom_call" | custom-call | tf_op jit(solution)/shard_map/prepare/pallas_call | solution.py:514
  27.9 0.2 collective-permute-done.7.received_ref
  28.1 2.9 %solve.1.mine_ref = f32[32,64]{1,0:T(8,128)S(1)} custom-call(f32[2,256]{1,0:T(2,128)S(1)} %copy-done.2, f32[2,256]{1,0:T(2,128)S(1)} %copy-done.3, f32[2,64,256]{2,1,0:T(8,128)S(1)} %copy-done.1, f32[64,256]{1,0:T(8,128)S(1)} %gather.1.kept_ref, f32[64,256]{1,0:T(8,128)S(1)} %collective-permute-done.7.received_ref), custom_call_target="tpu_custom_call" | custom-call | flops 500000000 | tf_op jit(solution)/shard_map/solve/pallas_call | solution.py:507
  31.1 1.4 %combine.1 = f32[32,48,128]{2,1,0:T(8,128)} custom-call(f32[32,64]{1,0:T(8,128)S(1)} %solve.1.mine_ref, f32[128,512]{1,0:T(8,128)S(1)} %complete.1.refs_0_, f32[128,512]{1,0:T(8,128)S(1)} %collective-permute-done.9.refs_1_, bf16[64,4096]{1,0:T(8,128)(2,1)S(1)} %get-tuple-element.41.refs_2_, bf16[64,4096]{1,0:T(8,128)(2,1)S(1)} %get-tuple-element.42.refs_3_), custom_call_target="tpu_custom_call" | custom-call | tf_op jit(solution)/shard_map/combine/pallas_call | solution.py:520
  (17 shorter events, 0.1 us)
Async XLA Ops:
  0.0 3.1 %copy-start = (f32[32,2,4,1,512]{4,3,2,1,0:T(1,128)S(1)}, f32[32,2,4,1,512]{4,3,2,1,0:T(1,128)}, u32[]{:S(2)}) copy-start(f32[32,2,4,1,512]{4,3,2,1,0:T(1,128)} %param.11) | copy-start | bytes 1572868
  1.1 7.8 %collective-permute-start = (f32[520,128]{1,0:T(8,128)S(1)}, f32[520,128]{1,0:T(8,128)S(1)}, u32[]{:S(2)}, u32[]{:S(2)}) collective-permute-start(f32[520,128]{1,0:T(8,128)S(1)} %get-tuple-element.40.packed_ref), channel_id=1, source_target_pairs={{2,0},{4,2},{6,4},{8,6},{10,8},{12,10},{14,12},{16,14},{18,16},{20... | collective-permute-start | bytes 798728 | tf_op jit(solution)/shard_map/ppermute | solution.py:445
  3.1 20.1 %collective-permute-start.5 = (f32[1024,128]{1,0:T(8,128)S(1)}, f32[1024,128]{1,0:T(8,128)S(1)}, u32[]{:S(2)}, u32[]{:S(2)}) collective-permute-start(f32[1024,128]{1,0:T(8,128)S(1)} %bitcast.5), channel_id=1, source_target_pairs={{1,0},{0,1},{3,2},{2,3},{5,4},{4,5},{7,6},{6,7},{9,8},{8,9},{11,10... | collective-permute-start | bytes 1572872 | tf_op jit(solution)/shard_map/ppermute | solution.py:428
  6.1 11.5 %collective-permute-start.8 = (f32[520,128]{1,0:T(8,128)S(1)}, f32[520,128]{1,0:T(8,128)S(1)}, u32[]{:S(2)}, u32[]{:S(2)}) collective-permute-start(f32[520,128]{1,0:T(8,128)S(1)} %get-tuple-element.40.packed_ref), channel_id=1, source_target_pairs={{0,2},{2,4},{4,6},{6,8},{8,10},{10,12},{12,14},{14,16},{16,18},{18... | collective-permute-start | bytes 798728 | tf_op jit(solution)/shard_map/ppermute | solution.py:461
  9.4 2.5 %collective-permute-start.1 = (f32[32,256]{1,0:T(8,128)S(1)}, f32[32,256]{1,0:T(8,128)S(1)}, u32[]{:S(2)}, u32[]{:S(2)}) collective-permute-start(f32[32,256]{1,0:T(8,128)S(1)} %get-tuple-element.36), channel_id=1, source_target_pairs={{0,2},{2,0},{4,6},{6,4},{8,10},{10,8},{12,14},{14,12},{16,18},{18,... | collective-permute-start | bytes 98312 | tf_op jit(solution)/shard_map/ppermute | solution.py:412
  11.9 4.2 %collective-permute-start.2 = (f32[32,256]{1,0:T(8,128)S(1)}, f32[32,256]{1,0:T(8,128)S(1)}, u32[]{:S(2)}, u32[]{:S(2)}) collective-permute-start(f32[32,256]{1,0:T(8,128)S(1)} %add.3.terms_ref), channel_id=1, source_target_pairs={{0,18},{2,16},{4,22},{6,20},{8,26},{10,24},{12,30},{14,28},{16,2},... | collective-permute-start | bytes 98312 | tf_op jit(solution)/shard_map/ppermute | solution.py:412
  16.1 3.3 %collective-permute-start.3 = (f32[32,256]{1,0:T(8,128)S(1)}, f32[32,256]{1,0:T(8,128)S(1)}, u32[]{:S(2)}, u32[]{:S(2)}) collective-permute-start(f32[32,256]{1,0:T(8,128)S(1)} %sum.3.terms_ref), channel_id=1, source_target_pairs={{0,10},{2,8},{4,14},{6,12},{8,2},{10,0},{12,6},{14,4},{16,26},{18,... | collective-permute-start | bytes 98312 | tf_op jit(solution)/shard_map/ppermute | solution.py:412
  17.8 13.3 %collective-permute-start.9 = (f32[128,512]{1,0:T(8,128)S(1)}, f32[128,512]{1,0:T(8,128)S(1)}, u32[]{:S(2)}, u32[]{:S(2)}) collective-permute-start(f32[128,512]{1,0:T(8,128)S(1)} %complete.1.refs_0_), channel_id=1, source_target_pairs={{1,0},{0,1},{3,2},{2,3},{5,4},{4,5},{7,6},{6,7},{9,8},{8,9},{11,10... | collective-permute-start | bytes 786440 | tf_op jit(solution)/shard_map/ppermute | solution.py:428
  19.5 3.8 %collective-permute-start.4 = (f32[32,256]{1,0:T(8,128)S(1)}, f32[32,256]{1,0:T(8,128)S(1)}, u32[]{:S(2)}, u32[]{:S(2)}) collective-permute-start(f32[32,256]{1,0:T(8,128)S(1)} %sum.4.terms_ref), channel_id=1, source_target_pairs={{0,6},{2,4},{4,2},{6,0},{8,14},{10,12},{12,10},{14,8},{16,22},{18,... | collective-permute-start | bytes 98312 | tf_op jit(solution)/shard_map/ppermute | solution.py:412
  23.2 3.5 %collective-permute-start.6 = (f32[32,256]{1,0:T(8,128)S(1)}, f32[32,256]{1,0:T(8,128)S(1)}, u32[]{:S(2)}, u32[]{:S(2)}) collective-permute-start(f32[32,256]{1,0:T(8,128)S(1)} %sum.5.refs_0_), channel_id=1, source_target_pairs={{3,0},{2,1},{1,2},{0,3},{7,4},{6,5},{5,6},{4,7},{11,8},{10,9},{9,1... | collective-permute-start | bytes 98312 | tf_op jit(solution)/shard_map/ppermute | solution.py:421
  26.7 1.4 %copy-start.1 = (f32[2,64,256]{2,1,0:T(8,128)S(1)}, f32[2,64,256]{2,1,0:T(8,128)}, u32[]{:S(2)}) copy-start(f32[2,64,256]{2,1,0:T(8,128)} %noise_ref.1) | copy-start | bytes 393220
  26.7 1.4 %copy-start.2 = (f32[2,256]{1,0:T(2,128)S(1)}, f32[2,256]{1,0:T(2,128)}, u32[]{:S(2)}) copy-start(f32[2,256]{1,0:T(2,128)} %value_ref.1) | copy-start | bytes 6148
  26.8 1.4 %copy-start.3 = (f32[2,256]{1,0:T(2,128)S(1)}, f32[2,256]{1,0:T(2,128)}, u32[]{:S(2)}) copy-start(f32[2,256]{1,0:T(2,128)} %error_ref.1) | copy-start | bytes 6148
  26.8 1.3 %collective-permute-start.7 = (f32[64,256]{1,0:T(8,128)S(1)}, f32[64,256]{1,0:T(8,128)S(1)}, u32[]{:S(2)}, u32[]{:S(2)}) collective-permute-start(f32[64,256]{1,0:T(8,128)S(1)} %gather.1.kept_ref), channel_id=1, source_target_pairs={{0,2},{2,0},{4,6},{6,4},{8,10},{10,8},{12,14},{14,12},{16,18},{18,... | collective-permute-start | bytes 196616 | tf_op jit(solution)/shard_map/ppermute | solution.py:412

commit v18 on v16

--- a/solution.py
+++ b/solution.py
@@ -15,7 +15,7 @@
 
 
 SELECT_FLOPS = 1
-OWN_FLOPS, SUM_FLOPS, GATHER_FLOPS, SOLVE_FLOPS = 1, (7*10**8,7*10**8,1), 10**8, 5*10**8
+OWN_FLOPS, SUM_FLOPS, GATHER_FLOPS, SOLVE_FLOPS = 1, (7*10**8,7*10**8,1), 10**8, 8*10**8
 
 
 def estimate(flops):
@@ -211,12 +211,6 @@
     )
 
 
-def gather_kernel(*refs):
-    local = refs[0].shape[0]
-    for d, ref in enumerate(refs[:-1]):
-        refs[-1][d * local : (d + 1) * local, :] = ref[...]
-
-
 def identity(rows, columns):
     return (
         lax.broadcasted_iota(jnp.int32, (rows, columns), 0)
@@ -233,6 +227,33 @@
     y_high, y_low = split_two(y)
     dot = functools.partial(jnp.dot, preferred_element_type=F32)
     return dot(x_low, y_high) + dot(x_high, y_low) + dot(x_high, y_high)
+
+
+def precise_nt(x, y):
+    return lax.dot_general(
+        x, y, (((1,), (1,)), ((), ())), precision=HIGHEST, preferred_element_type=F32
+    )
+
+
+def gram_kernel(parts, value_ref, error_ref, noise_ref, *refs):
+    term_refs, grams_ref = refs[:parts], refs[parts]
+    members, count = noise_ref.shape[1:]
+    local = members // parts
+    own = lax.axis_index("mem")
+    batch = 1 - keeps_first(parts).astype(jnp.int32)
+    observed = jnp.concatenate([ref[...] for ref in term_refs], axis=0)
+    share = 1.0 / error_ref[pl.ds(batch, 1), :]
+    mean = jnp.mean(observed, axis=0, keepdims=True)
+    anomalies = (observed - mean) * share
+    noise = jnp.concatenate(
+        [
+            noise_ref[batch, pl.ds(pl.multiple_of(lax.rem(own + d, parts) * local, local), local), :]
+            for d in range(parts)
+        ],
+        axis=0,
+    )
+    innovation = (value_ref[pl.ds(batch, 1), :] - mean) * share + noise
+    grams_ref[...] = precise_nt(jnp.concatenate([anomalies, innovation], axis=0), anomalies)
 
 
 def solve_transposed(system, right_t, floor):
@@ -273,42 +294,20 @@
     )
 
 
-def precise_nt(x, y):
-    return lax.dot_general(
-        x, y, (((1,), (1,)), ((), ())), precision=HIGHEST, preferred_element_type=F32
-    )
-
-
-def solve_kernel(parts, value_ref, error_ref, noise_ref, kept_ref, received_ref, mine_ref):
-    batches, members, count = noise_ref.shape
+def solve_kernel(parts, batches, kept_ref, received_ref, mine_ref):
+    members = kept_ref.shape[1]
     local = members // parts
-    own = lax.axis_index("mem")
     first_here = keeps_first(parts)
-    halves = [
-        jnp.where(first_here, kept_ref[...], received_ref[...]),
-        jnp.where(first_here, received_ref[...], kept_ref[...]),
+    kept, received = kept_ref[...], received_ref[...]
+    grams = [
+        jnp.where(first_here, kept, received),
+        jnp.where(first_here, received, kept),
     ]
-    prior = jnp.concatenate(halves, axis=1)
-    grams = []
-    for b in range(batches):
-        wanted = local if b == batches - 1 else members
-        observed = prior[:, b * count : (b + 1) * count]
-        share = 1.0 / error_ref[b : b + 1, :]
-        mean = jnp.mean(observed, axis=0, keepdims=True)
-        anomalies = (observed - mean) * share
-        blocks = []
-        for d in range(wanted // local):
-            owner = lax.rem(own + d, parts)
-            blocks.append(
-                noise_ref[b, pl.ds(pl.multiple_of(owner * local, local), local), :]
-            )
-        innovation = (value_ref[b : b + 1, :] - mean) * share + jnp.concatenate(blocks, axis=0)
-        both = precise_nt(jnp.concatenate([anomalies, innovation], axis=0), anomalies)
-        grams.append((both[:members], both[members:]))
     diagonal = (members - 1.0) * identity(members, members)
     product_t = None
-    for b, (gram, cross) in enumerate(grams):
-        wanted = cross.shape[0]
+    for b, both in enumerate(grams):
+        wanted = local if b == batches - 1 else members
+        gram, cross = both[:members], both[members : members + wanted]
         if product_t is None:
             system, right_t = gram, cross - gram[:wanted]
         else:
@@ -499,20 +498,21 @@
         lax.optimization_barrier((partial, after_far))[0], from_above, packed
     )
 
-    prior = pl.pallas_call(
-        gather_kernel,
-        out_shape=shape_of((all_members, total // 2)),
+    assert batches == 2
+    grams = pl.pallas_call(
+        functools.partial(gram_kernel, parts),
+        out_shape=shape_of((2 * all_members, all_members)),
         cost_estimate=estimate(GATHER_FLOPS),
         compiler_params=PARAMS,
-        name="gather",
-    )(terms, *from_other_mem(terms))
+        name="gram",
+    )(obs_value, obs_error, obs_noise, terms, *from_other_mem(terms))
     mine = pl.pallas_call(
-        functools.partial(solve_kernel, parts),
+        functools.partial(solve_kernel, parts, batches),
         out_shape=shape_of((members, all_members)),
         compiler_params=PARAMS,
         cost_estimate=estimate(SOLVE_FLOPS),
         name="solve",
-    )(obs_value, obs_error, obs_noise, prior, from_slab(prior, 1))
+    )(grams, from_slab(grams, 1))
     lagged_parts = pl.pallas_call(
         functools.partial(prepare_kernel, parts),
         out_shape=[shape_of((all_members, delayed.size // members), BF16)] * 2,

time: 32.6 us -> 32.6 us (level)
  no operation moved by 1% of the time
where the time goes in v18:
time: 32.6 us; the launch traced here: 32.4 us
  starting transfers between devices  18.6 us (57%)
  Pallas kernels  7.29 us (22%)
  waiting for transfers between devices  6.35 us (19%)
    ppermute x5, starting transfers between devices, from_slab(): return lax.ppermute(array, 'slab', [(i, i ^ bit) for i in range(slabs)])  8.43 us
    ppermute x2, starting transfers between devices, from_partners(): lax.ppermute(array, 'mem', [((i + d) % parts, i) for i in range(parts)])  4.57 us
    ppermute x5, waiting for transfers between devices, from_slab(): return lax.ppermute(array, 'slab', [(i, i ^ bit) for i in range(slabs)])  4.48 us
    ppermute x1, starting transfers between devices, shards(): lax.ppermute(lax.optimization_barrier((packed, part))[0], 'slab', up)  2.77 us
    pallas_call x1, Pallas kernels, shards(): pl.pallas_call(functools.partial(solve_kernel, parts, batches), out_shape...  2.59 us
    ppermute x1, waiting for transfers between devices, from_other_mem(): lax.ppermute(array, ('slab', 'mem'), [(i ^ 3, i) for i in range(slabs * p...  1.86 us
    ppermute x1, starting transfers between devices, from_other_mem(): lax.ppermute(array, ('slab', 'mem'), [(i ^ 3, i) for i in range(slabs * p...  1.55 us
    pallas_call x1, Pallas kernels, shards(): pl.pallas_call(functools.partial(combine_kernel, parts, fields), out_shap...  1.36 us
  transfers between devices with their start and end apart: 10, of which 6 were waited for; matrix products, arithmetic and copies ran while one was open for 0% of the time, Pallas kernels for 15%

profile of v18, /device:TPU:0, one launch (start us, length us, event | category | flops | bytes accessed | tf_op | source)
XLA Modules:
  0.0 32.4 jit_solution(10308500082370616711)
XLA Ops:
  0.0 1.0 %load.1 = (f32[520,128]{1,0:T(8,128)S(1)}, f32[4,128]{1,0:T(4,128)S(1)}, f32[8,128]{1,0:T(8,128)S(1)}, s32[2,256]{1,0:T(2,128)S(1)}, s32[2,256]{1,0:T(2,128)S(1)}, /*index=5*/s32[2,256]{1,0:T(2,128)S(1)}) custom-call(f32[512,128]{1,0:T(8,128)} %bitcast.7, f32[4,128]{1,0:T(4,128)} %bitcast.9, f32[8,128]{1,0:T(8,128)} %bitcast.8, s32[2,256]{1,0:T(2,128)} %refs_3_.1, ...), custom_call_target="tpu_custom_call" | custom-call | tf_op jit(solution)/shard_map/load/pallas_call | solution.py:434
  1.0 1.3 %collective-permute-start = (f32[520,128]{1,0:T(8,128)S(1)}, f32[520,128]{1,0:T(8,128)S(1)}, u32[]{:S(2)}, u32[]{:S(2)}) collective-permute-start(f32[520,128]{1,0:T(8,128)S(1)} %get-tuple-element.40.packed_ref), channel_id=1, source_target_pairs={{2,0},{4,2},{6,4},{8,6},{10,8},{12,10},{14,12},{16,14},{18,16},{20... | collective-permute-start | bytes 798728 | tf_op jit(solution)/shard_map/ppermute | solution.py:444
  2.3 3.0 %collective-permute-start.5 = (f32[1024,128]{1,0:T(8,128)}, f32[1024,128]{1,0:T(8,128)S(1)}, u32[]{:S(2)}, u32[]{:S(2)}) collective-permute-start(f32[1024,128]{1,0:T(8,128)} %bitcast.5), channel_id=1, source_target_pairs={{1,0},{0,1},{3,2},{2,3},{5,4},{4,5},{7,6},{6,7},{9,8},{8,9},{11,10... | collective-permute-start | bytes 1572872 | tf_op jit(solution)/shard_map/ppermute | solution.py:427
  5.3 0.2 selector.1
  5.5 0.5 %own_row.1 = (f32[128,512]{1,0:T(8,128)S(1)}, f32[128,512]{1,0:T(8,128)S(1)}, f32[32,512]{1,0:T(8,128)S(1)}) custom-call(f32[520,128]{1,0:T(8,128)S(1)} %get-tuple-element.40.packed_ref, f32[4,128]{1,0:T(4,128)S(1)} %get-tuple-element.25.spread_ref, f32[8,128]{1,0:T(8,128)S(1)} %get-tuple-element.26.ratio_ref, ...), custom_call_target="tpu_custom_call" | custom-call | flops 1 | tf_op jit(solution)/shard_map/own_row/pallas_call | solution.py:455
  6.0 2.8 %collective-permute-start.8 = (f32[520,128]{1,0:T(8,128)S(1)}, f32[520,128]{1,0:T(8,128)S(1)}, u32[]{:S(2)}, u32[]{:S(2)}) collective-permute-start(f32[520,128]{1,0:T(8,128)S(1)} %get-tuple-element.40.packed_ref), channel_id=1, source_target_pairs={{0,2},{2,4},{4,6},{6,8},{8,10},{10,12},{12,14},{14,16},{16,18},{18... | collective-permute-start | bytes 798728 | tf_op jit(solution)/shard_map/ppermute | solution.py:462
  8.8 0.5 %observe.1 = (f32[32,256]{1,0:T(8,128)S(1)}, f32[32,256]{1,0:T(8,128)S(1)}, f32[128,512]{1,0:T(8,128)S(1)}) custom-call(f32[520,128]{1,0:T(8,128)S(1)} %get-tuple-element.40.packed_ref, f32[520,128]{1,0:T(8,128)S(1)} %collective-permute-done.next_ref, f32[128,512]{1,0:T(8,128)S(1)} %get-tuple-element.32.part_ref, ...), custom_call_target="tpu_custom_call" | custom-call | tf_op jit(solution)/shard_map/observe/pallas_call | solution.py:463
  9.3 1.6 %collective-permute-start.1 = (f32[32,256]{1,0:T(8,128)S(1)}, f32[32,256]{1,0:T(8,128)S(1)}, u32[]{:S(2)}, u32[]{:S(2)}) collective-permute-start(f32[32,256]{1,0:T(8,128)S(1)} %get-tuple-element.36), channel_id=1, source_target_pairs={{0,2},{2,0},{4,6},{6,4},{8,10},{10,8},{12,14},{14,12},{16,18},{18,... | collective-permute-start | bytes 98312 | tf_op jit(solution)/shard_map/ppermute | solution.py:411
  10.9 0.9 %collective-permute-done.1 = f32[32,256]{1,0:T(8,128)S(1)} collective-permute-done((f32[32,256]{1,0:T(8,128)S(1)}, f32[32,256]{1,0:T(8,128)S(1)}, u32[]{:S(2)}, u32[]{:S(2)}) %collective-permute-start.1) | collective-permute-done | bytes 32800 | tf_op jit(solution)/shard_map/ppermute | solution.py:411
  11.8 2.5 %collective-permute-start.2 = (f32[32,256]{1,0:T(8,128)S(1)}, f32[32,256]{1,0:T(8,128)S(1)}, u32[]{:S(2)}, u32[]{:S(2)}) collective-permute-start(f32[32,256]{1,0:T(8,128)S(1)} %add.3.terms_ref), channel_id=1, source_target_pairs={{0,18},{2,16},{4,22},{6,20},{8,26},{10,24},{12,30},{14,28},{16,2},... | collective-permute-start | bytes 98312 | tf_op jit(solution)/shard_map/ppermute | solution.py:411
  14.4 1.7 %collective-permute-done.2.other_ref = f32[32,256]{1,0:T(8,128)S(1)} collective-permute-done((f32[32,256]{1,0:T(8,128)S(1)}, f32[32,256]{1,0:T(8,128)S(1)}, u32[]{:S(2)}, u32[]{:S(2)}) %collective-permute-start.2) | collective-permute-done | bytes 32800 | tf_op jit(solution)/shard_map/ppermute | solution.py:411
  16.1 1.5 %collective-permute-start.3 = (f32[32,256]{1,0:T(8,128)S(1)}, f32[32,256]{1,0:T(8,128)S(1)}, u32[]{:S(2)}, u32[]{:S(2)}) collective-permute-start(f32[32,256]{1,0:T(8,128)S(1)} %sum.3.terms_ref), channel_id=1, source_target_pairs={{0,10},{2,8},{4,14},{6,12},{8,2},{10,0},{12,6},{14,4},{16,26},{18,... | collective-permute-start | bytes 98312 | tf_op jit(solution)/shard_map/ppermute | solution.py:411
  17.7 1.6 %collective-permute-start.9 = (f32[128,512]{1,0:T(8,128)S(1)}, f32[128,512]{1,0:T(8,128)S(1)}, u32[]{:S(2)}, u32[]{:S(2)}) collective-permute-start(f32[128,512]{1,0:T(8,128)S(1)} %complete.1.refs_0_), channel_id=1, source_target_pairs={{1,0},{0,1},{3,2},{2,3},{5,4},{4,5},{7,6},{6,7},{9,8},{8,9},{11,10... | collective-permute-start | bytes 786440 | tf_op jit(solution)/shard_map/ppermute | solution.py:427
  19.3 0.1 collective-permute-done.3.other_ref
  19.4 2.2 %collective-permute-start.4 = (f32[32,256]{1,0:T(8,128)S(1)}, f32[32,256]{1,0:T(8,128)S(1)}, u32[]{:S(2)}, u32[]{:S(2)}) collective-permute-start(f32[32,256]{1,0:T(8,128)S(1)} %sum.4.terms_ref), channel_id=1, source_target_pairs={{0,6},{2,4},{4,2},{6,0},{8,14},{10,12},{12,10},{14,8},{16,22},{18,... | collective-permute-start | bytes 98312 | tf_op jit(solution)/shard_map/ppermute | solution.py:411
  21.7 1.6 %collective-permute-done.4.other_ref = f32[32,256]{1,0:T(8,128)S(1)} collective-permute-done((f32[32,256]{1,0:T(8,128)S(1)}, f32[32,256]{1,0:T(8,128)S(1)}, u32[]{:S(2)}, u32[]{:S(2)}) %collective-permute-start.4) | collective-permute-done | bytes 32800 | tf_op jit(solution)/shard_map/ppermute | solution.py:411
  23.3 1.5 %collective-permute-start.6 = (f32[32,256]{1,0:T(8,128)S(1)}, f32[32,256]{1,0:T(8,128)S(1)}, u32[]{:S(2)}, u32[]{:S(2)}) collective-permute-start(f32[32,256]{1,0:T(8,128)S(1)} %sum.5.refs_0_), channel_id=1, source_target_pairs={{3,0},{2,1},{1,2},{0,3},{7,4},{6,5},{5,6},{4,7},{11,8},{10,9},{9,1... | collective-permute-start | bytes 98312 | tf_op jit(solution)/shard_map/ppermute | solution.py:420
  24.8 1.9 %collective-permute-done.6.refs_1_ = f32[32,256]{1,0:T(8,128)S(1)} collective-permute-done((f32[32,256]{1,0:T(8,128)S(1)}, f32[32,256]{1,0:T(8,128)S(1)}, u32[]{:S(2)}, u32[]{:S(2)}) %collective-permute-start.6) | collective-permute-done | bytes 32800 | tf_op jit(solution)/shard_map/ppermute | solution.py:420
  26.7 0.3 gram.1.kept_ref
  27.0 0.5 %collective-permute-start.7 = (f32[128,64]{1,0:T(8,128)S(1)}, f32[128,64]{1,0:T(8,128)S(1)}, u32[]{:S(2)}, u32[]{:S(2)}) collective-permute-start(f32[128,64]{1,0:T(8,128)S(1)} %gram.1.kept_ref), channel_id=1, source_target_pairs={{0,2},{2,0},{4,6},{6,4},{8,10},{10,8},{12,14},{14,12},{16,18},{18,... | collective-permute-start | bytes 98312 | tf_op jit(solution)/shard_map/ppermute | solution.py:411
  27.5 0.7 %prepare.1 = (bf16[64,4096]{1,0:T(8,128)(2,1)S(1)}, bf16[64,4096]{1,0:T(8,128)(2,1)S(1)}) custom-call(f32[1024,128]{1,0:T(8,128)S(1)} %bitcast.6, f32[1024,128]{1,0:T(8,128)S(1)} %collective-permute-done.5.refs_0_.refs_1_), custom_call_target="tpu_custom_call" | custom-call | tf_op jit(solution)/shard_map/prepare/pallas_call | solution.py:516
  28.2 0.2 collective-permute-done.7.received_ref
  28.4 2.6 %solve.1.mine_ref = f32[32,64]{1,0:T(8,128)S(1)} custom-call(f32[128,64]{1,0:T(8,128)S(1)} %gram.1.kept_ref, f32[128,64]{1,0:T(8,128)S(1)} %collective-permute-done.7.received_ref), custom_call_target="tpu_custom_call" | custom-call | flops 800000000 | tf_op jit(solution)/shard_map/solve/pallas_call | solution.py:509
  31.0 1.4 %combine.1 = f32[32,48,128]{2,1,0:T(8,128)} custom-call(f32[32,64]{1,0:T(8,128)S(1)} %solve.1.mine_ref, f32[128,512]{1,0:T(8,128)S(1)} %complete.1.refs_0_, f32[128,512]{1,0:T(8,128)S(1)} %collective-permute-done.9.refs_1_, bf16[64,4096]{1,0:T(8,128)(2,1)S(1)} %get-tuple-element.41.refs_2_, bf16[64,4096]{1,0:T(8,128)(2,1)S(1)} %get-tuple-element.42.refs_3_), custom_call_target="tpu_custom_call" | custom-call | tf_op jit(solution)/shard_map/combine/pallas_call | solution.py:522
  (17 shorter events, 0.2 us)
Async XLA Ops:
  1.0 7.8 %collective-permute-start = (f32[520,128]{1,0:T(8,128)S(1)}, f32[520,128]{1,0:T(8,128)S(1)}, u32[]{:S(2)}, u32[]{:S(2)}) collective-permute-start(f32[520,128]{1,0:T(8,128)S(1)} %get-tuple-element.40.packed_ref), channel_id=1, source_target_pairs={{2,0},{4,2},{6,4},{8,6},{10,8},{12,10},{14,12},{16,14},{18,16},{20... | collective-permute-start | bytes 798728 | tf_op jit(solution)/shard_map/ppermute | solution.py:444
  2.3 20.9 %collective-permute-start.5 = (f32[1024,128]{1,0:T(8,128)}, f32[1024,128]{1,0:T(8,128)S(1)}, u32[]{:S(2)}, u32[]{:S(2)}) collective-permute-start(f32[1024,128]{1,0:T(8,128)} %bitcast.5), channel_id=1, source_target_pairs={{1,0},{0,1},{3,2},{2,3},{5,4},{4,5},{7,6},{6,7},{9,8},{8,9},{11,10... | collective-permute-start | bytes 1572872 | tf_op jit(solution)/shard_map/ppermute | solution.py:427
  6.0 11.6 %collective-permute-start.8 = (f32[520,128]{1,0:T(8,128)S(1)}, f32[520,128]{1,0:T(8,128)S(1)}, u32[]{:S(2)}, u32[]{:S(2)}) collective-permute-start(f32[520,128]{1,0:T(8,128)S(1)} %get-tuple-element.40.packed_ref), channel_id=1, source_target_pairs={{0,2},{2,4},{4,6},{6,8},{8,10},{10,12},{12,14},{14,16},{16,18},{18... | collective-permute-start | bytes 798728 | tf_op jit(solution)/shard_map/ppermute | solution.py:462
  9.3 2.5 %collective-permute-start.1 = (f32[32,256]{1,0:T(8,128)S(1)}, f32[32,256]{1,0:T(8,128)S(1)}, u32[]{:S(2)}, u32[]{:S(2)}) collective-permute-start(f32[32,256]{1,0:T(8,128)S(1)} %get-tuple-element.36), channel_id=1, source_target_pairs={{0,2},{2,0},{4,6},{6,4},{8,10},{10,8},{12,14},{14,12},{16,18},{18,... | collective-permute-start | bytes 98312 | tf_op jit(solution)/shard_map/ppermute | solution.py:411
  11.8 4.2 %collective-permute-start.2 = (f32[32,256]{1,0:T(8,128)S(1)}, f32[32,256]{1,0:T(8,128)S(1)}, u32[]{:S(2)}, u32[]{:S(2)}) collective-permute-start(f32[32,256]{1,0:T(8,128)S(1)} %add.3.terms_ref), channel_id=1, source_target_pairs={{0,18},{2,16},{4,22},{6,20},{8,26},{10,24},{12,30},{14,28},{16,2},... | collective-permute-start | bytes 98312 | tf_op jit(solution)/shard_map/ppermute | solution.py:411
  16.1 3.3 %collective-permute-start.3 = (f32[32,256]{1,0:T(8,128)S(1)}, f32[32,256]{1,0:T(8,128)S(1)}, u32[]{:S(2)}, u32[]{:S(2)}) collective-permute-start(f32[32,256]{1,0:T(8,128)S(1)} %sum.3.terms_ref), channel_id=1, source_target_pairs={{0,10},{2,8},{4,14},{6,12},{8,2},{10,0},{12,6},{14,4},{16,26},{18,... | collective-permute-start | bytes 98312 | tf_op jit(solution)/shard_map/ppermute | solution.py:411
  17.7 13.3 %collective-permute-start.9 = (f32[128,512]{1,0:T(8,128)S(1)}, f32[128,512]{1,0:T(8,128)S(1)}, u32[]{:S(2)}, u32[]{:S(2)}) collective-permute-start(f32[128,512]{1,0:T(8,128)S(1)} %complete.1.refs_0_), channel_id=1, source_target_pairs={{1,0},{0,1},{3,2},{2,3},{5,4},{4,5},{7,6},{6,7},{9,8},{8,9},{11,10... | collective-permute-start | bytes 786440 | tf_op jit(solution)/shard_map/ppermute | solution.py:427
  19.4 7.3 %copy-start.1 = (f32[2,64,256]{2,1,0:T(8,128)S(1)}, f32[2,64,256]{2,1,0:T(8,128)}, u32[]{:S(2)}) copy-start(f32[2,64,256]{2,1,0:T(8,128)} %noise_ref.1) | copy-start | bytes 393220
  19.4 7.3 %copy-start.2 = (f32[2,256]{1,0:T(2,128)S(1)}, f32[2,256]{1,0:T(2,128)}, u32[]{:S(2)}) copy-start(f32[2,256]{1,0:T(2,128)} %value_ref.1) | copy-start | bytes 6148
  19.4 7.3 %copy-start.3 = (f32[2,256]{1,0:T(2,128)S(1)}, f32[2,256]{1,0:T(2,128)}, u32[]{:S(2)}) copy-start(f32[2,256]{1,0:T(2,128)} %error_ref.1) | copy-start | bytes 6148
  19.4 8.1 %copy-start = (f32[32,2,4,1,512]{4,3,2,1,0:T(1,128)S(1)}, f32[32,2,4,1,512]{4,3,2,1,0:T(1,128)}, u32[]{:S(2)}) copy-start(f32[32,2,4,1,512]{4,3,2,1,0:T(1,128)} %param.11) | copy-start | bytes 1572868
  19.4 3.8 %collective-permute-start.4 = (f32[32,256]{1,0:T(8,128)S(1)}, f32[32,256]{1,0:T(8,128)S(1)}, u32[]{:S(2)}, u32[]{:S(2)}) collective-permute-start(f32[32,256]{1,0:T(8,128)S(1)} %sum.4.terms_ref), channel_id=1, source_target_pairs={{0,6},{2,4},{4,2},{6,0},{8,14},{10,12},{12,10},{14,8},{16,22},{18,... | collective-permute-start | bytes 98312 | tf_op jit(solution)/shard_map/ppermute | solution.py:411
  23.3 3.4 %collective-permute-start.6 = (f32[32,256]{1,0:T(8,128)S(1)}, f32[32,256]{1,0:T(8,128)S(1)}, u32[]{:S(2)}, u32[]{:S(2)}) collective-permute-start(f32[32,256]{1,0:T(8,128)S(1)} %sum.5.refs_0_), channel_id=1, source_target_pairs={{3,0},{2,1},{1,2},{0,3},{7,4},{6,5},{5,6},{4,7},{11,8},{10,9},{9,1... | collective-permute-start | bytes 98312 | tf_op jit(solution)/shard_map/ppermute | solution.py:420
  27.0 1.4 %collective-permute-start.7 = (f32[128,64]{1,0:T(8,128)S(1)}, f32[128,64]{1,0:T(8,128)S(1)}, u32[]{:S(2)}, u32[]{:S(2)}) collective-permute-start(f32[128,64]{1,0:T(8,128)S(1)} %gram.1.kept_ref), channel_id=1, source_target_pairs={{0,2},{2,0},{4,6},{6,4},{8,10},{10,8},{12,14},{14,12},{16,18},{18,... | collective-permute-start | bytes 98312 | tf_op jit(solution)/shard_map/ppermute | solution.py:411

commit v19 on v16

--- a/solution.py
+++ b/solution.py
@@ -481,22 +481,24 @@
         )(terms, other, *arrived)
 
     terms = keep + from_slab(send, 1)
-    for bit in [1 << k for k in reversed(range(1, slabs.bit_length() - 1))]:
+    bits = [1 << k for k in reversed(range(1, slabs.bit_length() - 1))]
+    bits[:2] = bits[1::-1]
+    for k, bit in enumerate(bits):
         terms = summed(
             terms,
             from_other_pair(terms, bit),
-            SUM_FLOPS[min(slabs // 2 // bit, 4) // 2],
-            *([others_delayed[0]] if bit == 2 else []),
+            SUM_FLOPS[min(k, 2)],
+            *([others_delayed[0]] if bit == bits[-1] else []),
         )
-        if bit == slabs // 2:
-            after_far = terms
+        if k == 0:
+            after_first = terms
     forecast = pl.pallas_call(
         functools.partial(complete_kernel, *sizes),
         out_shape=shape_of(stacked),
         compiler_params=PARAMS,
         name="complete",
     )(
-        lax.optimization_barrier((partial, after_far))[0], from_above, packed
+        lax.optimization_barrier((partial, after_first))[0], from_above, packed
     )
 
     prior = pl.pallas_call(

time: 32.6 us -> 33.5 us (1.028)
  waiting for transfers between devices: 6.38 us -> 7.44 us
    ppermute x1, waiting for transfers between devices: 1.89 us -> 2.47 us  [from_other_mem(): lax.ppermute(array, ('slab', 'mem'), [(i ^ 3, i) for i in range(slabs * p...]
    ppermute x5, waiting for transfers between devices: 4.48 us -> 4.96 us  [from_slab(): return lax.ppermute(array, 'slab', [(i, i ^ bit) for i in range(slabs)])]
    ppermute x1, starting transfers between devices: 1.55 us -> 1.08 us  [from_other_mem(): lax.ppermute(array, ('slab', 'mem'), [(i ^ 3, i) for i in range(slabs * p...]
    ppermute x5, starting transfers between devices: 8.39 us -> 8.74 us  [from_slab(): return lax.ppermute(array, 'slab', [(i, i ^ bit) for i in range(slabs)])]
  transfers between devices with their start and end apart: 10 -> 10, of which waited for: 6 -> 5; matrix products, arithmetic and copies ran while one was open for 0% -> 0% of each run, Pallas kernels for 15% -> 15%
where the time goes in v19:
time: 33.5 us; the launch traced here: 33.4 us
  starting transfers between devices  18.4 us (55%)
  waiting for transfers between devices  7.44 us (22%)
  Pallas kernels  7.35 us (22%)
    ppermute x5, starting transfers between devices, from_slab(): return lax.ppermute(array, 'slab', [(i, i ^ bit) for i in range(slabs)])  8.74 us
    ppermute x5, waiting for transfers between devices, from_slab(): return lax.ppermute(array, 'slab', [(i, i ^ bit) for i in range(slabs)])  4.96 us
    ppermute x2, starting transfers between devices, from_partners(): lax.ppermute(array, 'mem', [((i + d) % parts, i) for i in range(parts)])  4.55 us
    pallas_call x1, Pallas kernels, shards(): pl.pallas_call(functools.partial(solve_kernel, parts), out_shape=shape_of...  2.94 us
    ppermute x1, starting transfers between devices, shards(): lax.ppermute(lax.optimization_barrier((packed, part))[0], 'slab', up)  2.77 us
    ppermute x1, waiting for transfers between devices, from_other_mem(): lax.ppermute(array, ('slab', 'mem'), [(i ^ 3, i) for i in range(slabs * p...  2.47 us
    pallas_call x1, Pallas kernels, shards(): pl.pallas_call(functools.partial(combine_kernel, parts, fields), out_shap...  1.36 us
    ppermute x1, starting transfers between devices, shards(): from_below = lax.ppermute(packed, 'slab', [(j, i) for i, j in up])  1.29 us
  transfers between devices with their start and end apart: 10, of which 5 were waited for; matrix products, arithmetic and copies ran while one was open for 0% of the time, Pallas kernels for 15%

profile of v19, /device:TPU:0, one launch (start us, length us, event | category | flops | bytes accessed | tf_op | source)
XLA Modules:
  0.0 33.4 jit_solution(7682304427797262064)
XLA Ops:
  0.0 1.0 %load.1 = (f32[520,128]{1,0:T(8,128)S(1)}, f32[4,128]{1,0:T(4,128)S(1)}, f32[8,128]{1,0:T(8,128)S(1)}, s32[2,256]{1,0:T(2,128)S(1)}, s32[2,256]{1,0:T(2,128)S(1)}, /*index=5*/s32[2,256]{1,0:T(2,128)S(1)}) custom-call(f32[512,128]{1,0:T(8,128)} %bitcast.7, f32[4,128]{1,0:T(4,128)} %bitcast.9, f32[8,128]{1,0:T(8,128)} %bitcast.8, s32[2,256]{1,0:T(2,128)} %refs_3_.1, ...), custom_call_target="tpu_custom_call" | custom-call | tf_op jit(solution)/shard_map/load/pallas_call | solution.py:435
  1.0 1.3 %collective-permute-start = (f32[520,128]{1,0:T(8,128)S(1)}, f32[520,128]{1,0:T(8,128)S(1)}, u32[]{:S(2)}, u32[]{:S(2)}) collective-permute-start(f32[520,128]{1,0:T(8,128)S(1)} %get-tuple-element.40.packed_ref), channel_id=1, source_target_pairs={{2,0},{4,2},{6,4},{8,6},{10,8},{12,10},{14,12},{16,14},{18,16},{20... | collective-permute-start | bytes 798728 | tf_op jit(solution)/shard_map/ppermute | solution.py:445
  2.3 3.0 %collective-permute-start.5 = (f32[1024,128]{1,0:T(8,128)}, f32[1024,128]{1,0:T(8,128)S(1)}, u32[]{:S(2)}, u32[]{:S(2)}) collective-permute-start(f32[1024,128]{1,0:T(8,128)} %bitcast.5), channel_id=1, source_target_pairs={{1,0},{0,1},{3,2},{2,3},{5,4},{4,5},{7,6},{6,7},{9,8},{8,9},{11,10... | collective-permute-start | bytes 1572872 | tf_op jit(solution)/shard_map/ppermute | solution.py:428
  5.3 0.2 selector.1
  5.5 0.5 %own_row.1 = (f32[128,512]{1,0:T(8,128)S(1)}, f32[128,512]{1,0:T(8,128)S(1)}, f32[32,512]{1,0:T(8,128)S(1)}) custom-call(f32[520,128]{1,0:T(8,128)S(1)} %get-tuple-element.40.packed_ref, f32[4,128]{1,0:T(4,128)S(1)} %get-tuple-element.25.spread_ref, f32[8,128]{1,0:T(8,128)S(1)} %get-tuple-element.26.ratio_ref, ...), custom_call_target="tpu_custom_call" | custom-call | flops 1 | tf_op jit(solution)/shard_map/own_row/pallas_call | solution.py:456
  6.0 2.8 %collective-permute-start.8 = (f32[520,128]{1,0:T(8,128)S(1)}, f32[520,128]{1,0:T(8,128)S(1)}, u32[]{:S(2)}, u32[]{:S(2)}) collective-permute-start(f32[520,128]{1,0:T(8,128)S(1)} %get-tuple-element.40.packed_ref), channel_id=1, source_target_pairs={{0,2},{2,4},{4,6},{6,8},{8,10},{10,12},{12,14},{14,16},{16,18},{18... | collective-permute-start | bytes 798728 | tf_op jit(solution)/shard_map/ppermute | solution.py:463
  8.8 0.5 %observe.1 = (f32[32,256]{1,0:T(8,128)S(1)}, f32[32,256]{1,0:T(8,128)S(1)}, f32[128,512]{1,0:T(8,128)S(1)}) custom-call(f32[520,128]{1,0:T(8,128)S(1)} %get-tuple-element.40.packed_ref, f32[520,128]{1,0:T(8,128)S(1)} %collective-permute-done.next_ref, f32[128,512]{1,0:T(8,128)S(1)} %get-tuple-element.32.part_ref, ...), custom_call_target="tpu_custom_call" | custom-call | tf_op jit(solution)/shard_map/observe/pallas_call | solution.py:464
  9.3 1.6 %collective-permute-start.1 = (f32[32,256]{1,0:T(8,128)S(1)}, f32[32,256]{1,0:T(8,128)S(1)}, u32[]{:S(2)}, u32[]{:S(2)}) collective-permute-start(f32[32,256]{1,0:T(8,128)S(1)} %get-tuple-element.36), channel_id=1, source_target_pairs={{0,2},{2,0},{4,6},{6,4},{8,10},{10,8},{12,14},{14,12},{16,18},{18,... | collective-permute-start | bytes 98312 | tf_op jit(solution)/shard_map/ppermute | solution.py:412
  10.9 0.9 %collective-permute-done.1 = f32[32,256]{1,0:T(8,128)S(1)} collective-permute-done((f32[32,256]{1,0:T(8,128)S(1)}, f32[32,256]{1,0:T(8,128)S(1)}, u32[]{:S(2)}, u32[]{:S(2)}) %collective-permute-start.1) | collective-permute-done | bytes 32800 | tf_op jit(solution)/shard_map/ppermute | solution.py:412
  11.8 1.5 %collective-permute-start.2 = (f32[32,256]{1,0:T(8,128)S(1)}, f32[32,256]{1,0:T(8,128)S(1)}, u32[]{:S(2)}, u32[]{:S(2)}) collective-permute-start(f32[32,256]{1,0:T(8,128)S(1)} %add.3.terms_ref), channel_id=1, source_target_pairs={{0,10},{2,8},{4,14},{6,12},{8,2},{10,0},{12,6},{14,4},{16,26},{18,... | collective-permute-start | bytes 98312 | tf_op jit(solution)/shard_map/ppermute | solution.py:412
  13.3 1.8 %collective-permute-done.2.other_ref = f32[32,256]{1,0:T(8,128)S(1)} collective-permute-done((f32[32,256]{1,0:T(8,128)S(1)}, f32[32,256]{1,0:T(8,128)S(1)}, u32[]{:S(2)}, u32[]{:S(2)}) %collective-permute-start.2) | collective-permute-done | bytes 32800 | tf_op jit(solution)/shard_map/ppermute | solution.py:412
  15.2 2.8 %collective-permute-start.3 = (f32[32,256]{1,0:T(8,128)S(1)}, f32[32,256]{1,0:T(8,128)S(1)}, u32[]{:S(2)}, u32[]{:S(2)}) collective-permute-start(f32[32,256]{1,0:T(8,128)S(1)} %sum.3.terms_ref), channel_id=1, source_target_pairs={{0,18},{2,16},{4,22},{6,20},{8,26},{10,24},{12,30},{14,28},{16,2},... | collective-permute-start | bytes 98312 | tf_op jit(solution)/shard_map/ppermute | solution.py:412
  18.0 0.1 complete.1.refs_0_
  18.1 1.6 %collective-permute-start.9 = (f32[128,512]{1,0:T(8,128)S(1)}, f32[128,512]{1,0:T(8,128)S(1)}, u32[]{:S(2)}, u32[]{:S(2)}) collective-permute-start(f32[128,512]{1,0:T(8,128)S(1)} %complete.1.refs_0_), channel_id=1, source_target_pairs={{1,0},{0,1},{3,2},{2,3},{5,4},{4,5},{7,6},{6,7},{9,8},{8,9},{11,10... | collective-permute-start | bytes 786440 | tf_op jit(solution)/shard_map/ppermute | solution.py:428
  19.7 0.0 copy-start
  19.7 2.6 %collective-permute-start.4 = (f32[32,256]{1,0:T(8,128)S(1)}, f32[32,256]{1,0:T(8,128)S(1)}, u32[]{:S(2)}, u32[]{:S(2)}) collective-permute-start(f32[32,256]{1,0:T(8,128)S(1)} %sum.4.terms_ref), channel_id=1, source_target_pairs={{0,6},{2,4},{4,2},{6,0},{8,14},{10,12},{12,10},{14,8},{16,22},{18,... | collective-permute-start | bytes 98312 | tf_op jit(solution)/shard_map/ppermute | solution.py:412
  22.3 1.9 %collective-permute-done.4.other_ref = f32[32,256]{1,0:T(8,128)S(1)} collective-permute-done((f32[32,256]{1,0:T(8,128)S(1)}, f32[32,256]{1,0:T(8,128)S(1)}, u32[]{:S(2)}, u32[]{:S(2)}) %collective-permute-start.4) | collective-permute-done | bytes 32800 | tf_op jit(solution)/shard_map/ppermute | solution.py:412
  24.1 1.1 %collective-permute-start.6 = (f32[32,256]{1,0:T(8,128)S(1)}, f32[32,256]{1,0:T(8,128)S(1)}, u32[]{:S(2)}, u32[]{:S(2)}) collective-permute-start(f32[32,256]{1,0:T(8,128)S(1)} %sum.5.refs_0_), channel_id=1, source_target_pairs={{3,0},{2,1},{1,2},{0,3},{7,4},{6,5},{5,6},{4,7},{11,8},{10,9},{9,1... | collective-permute-start | bytes 98312 | tf_op jit(solution)/shard_map/ppermute | solution.py:421
  25.2 2.5 %collective-permute-done.6.refs_1_ = f32[32,256]{1,0:T(8,128)S(1)} collective-permute-done((f32[32,256]{1,0:T(8,128)S(1)}, f32[32,256]{1,0:T(8,128)S(1)}, u32[]{:S(2)}, u32[]{:S(2)}) %collective-permute-start.6) | collective-permute-done | bytes 32800 | tf_op jit(solution)/shard_map/ppermute | solution.py:421
  27.7 0.2 collective-permute-start.7
  27.9 0.7 %prepare.1 = (bf16[64,4096]{1,0:T(8,128)(2,1)S(1)}, bf16[64,4096]{1,0:T(8,128)(2,1)S(1)}) custom-call(f32[1024,128]{1,0:T(8,128)S(1)} %bitcast.6, f32[1024,128]{1,0:T(8,128)S(1)} %collective-permute-done.5.refs_0_.refs_1_), custom_call_target="tpu_custom_call" | custom-call | tf_op jit(solution)/shard_map/prepare/pallas_call | solution.py:518
  28.6 0.4 %collective-permute-done.7.received_ref = f32[64,256]{1,0:T(8,128)S(1)} collective-permute-done((f32[64,256]{1,0:T(8,128)S(1)}, f32[64,256]{1,0:T(8,128)S(1)}, u32[]{:S(2)}, u32[]{:S(2)}) %collective-permute-start.7) | collective-permute-done | bytes 65568 | tf_op jit(solution)/shard_map/ppermute | solution.py:412
  29.1 2.9 %solve.1.mine_ref = f32[32,64]{1,0:T(8,128)S(1)} custom-call(f32[2,256]{1,0:T(2,128)S(1)} %copy-done.2, f32[2,256]{1,0:T(2,128)S(1)} %copy-done.3, f32[2,64,256]{2,1,0:T(8,128)S(1)} %copy-done.1, f32[64,256]{1,0:T(8,128)S(1)} %gather.1.kept_ref, f32[64,256]{1,0:T(8,128)S(1)} %collective-permute-done.7.received_ref), custom_call_target="tpu_custom_call" | custom-call | flops 500000000 | tf_op jit(solution)/shard_map/solve/pallas_call | solution.py:511
  32.0 1.4 %combine.1 = f32[32,48,128]{2,1,0:T(8,128)} custom-call(f32[32,64]{1,0:T(8,128)S(1)} %solve.1.mine_ref, f32[128,512]{1,0:T(8,128)S(1)} %complete.1.refs_0_, f32[128,512]{1,0:T(8,128)S(1)} %collective-permute-done.9.refs_1_, bf16[64,4096]{1,0:T(8,128)(2,1)S(1)} %get-tuple-element.41.refs_2_, bf16[64,4096]{1,0:T(8,128)(2,1)S(1)} %get-tuple-element.42.refs_3_), custom_call_target="tpu_custom_call" | custom-call | tf_op jit(solution)/shard_map/combine/pallas_call | solution.py:524
  (17 shorter events, 0.1 us)
Async XLA Ops:
  1.0 7.8 %collective-permute-start = (f32[520,128]{1,0:T(8,128)S(1)}, f32[520,128]{1,0:T(8,128)S(1)}, u32[]{:S(2)}, u32[]{:S(2)}) collective-permute-start(f32[520,128]{1,0:T(8,128)S(1)} %get-tuple-element.40.packed_ref), channel_id=1, source_target_pairs={{2,0},{4,2},{6,4},{8,6},{10,8},{12,10},{14,12},{16,14},{18,16},{20... | collective-permute-start | bytes 798728 | tf_op jit(solution)/shard_map/ppermute | solution.py:445
  2.3 21.8 %collective-permute-start.5 = (f32[1024,128]{1,0:T(8,128)}, f32[1024,128]{1,0:T(8,128)S(1)}, u32[]{:S(2)}, u32[]{:S(2)}) collective-permute-start(f32[1024,128]{1,0:T(8,128)} %bitcast.5), channel_id=1, source_target_pairs={{1,0},{0,1},{3,2},{2,3},{5,4},{4,5},{7,6},{6,7},{9,8},{8,9},{11,10... | collective-permute-start | bytes 1572872 | tf_op jit(solution)/shard_map/ppermute | solution.py:428
  6.0 12.0 %collective-permute-start.8 = (f32[520,128]{1,0:T(8,128)S(1)}, f32[520,128]{1,0:T(8,128)S(1)}, u32[]{:S(2)}, u32[]{:S(2)}) collective-permute-start(f32[520,128]{1,0:T(8,128)S(1)} %get-tuple-element.40.packed_ref), channel_id=1, source_target_pairs={{0,2},{2,4},{4,6},{6,8},{8,10},{10,12},{12,14},{14,16},{16,18},{18... | collective-permute-start | bytes 798728 | tf_op jit(solution)/shard_map/ppermute | solution.py:463
  9.3 2.5 %collective-permute-start.1 = (f32[32,256]{1,0:T(8,128)S(1)}, f32[32,256]{1,0:T(8,128)S(1)}, u32[]{:S(2)}, u32[]{:S(2)}) collective-permute-start(f32[32,256]{1,0:T(8,128)S(1)} %get-tuple-element.36), channel_id=1, source_target_pairs={{0,2},{2,0},{4,6},{6,4},{8,10},{10,8},{12,14},{14,12},{16,18},{18,... | collective-permute-start | bytes 98312 | tf_op jit(solution)/shard_map/ppermute | solution.py:412
  11.8 3.3 %collective-permute-start.2 = (f32[32,256]{1,0:T(8,128)S(1)}, f32[32,256]{1,0:T(8,128)S(1)}, u32[]{:S(2)}, u32[]{:S(2)}) collective-permute-start(f32[32,256]{1,0:T(8,128)S(1)} %add.3.terms_ref), channel_id=1, source_target_pairs={{0,10},{2,8},{4,14},{6,12},{8,2},{10,0},{12,6},{14,4},{16,26},{18,... | collective-permute-start | bytes 98312 | tf_op jit(solution)/shard_map/ppermute | solution.py:412
  15.2 4.5 %collective-permute-start.3 = (f32[32,256]{1,0:T(8,128)S(1)}, f32[32,256]{1,0:T(8,128)S(1)}, u32[]{:S(2)}, u32[]{:S(2)}) collective-permute-start(f32[32,256]{1,0:T(8,128)S(1)} %sum.3.terms_ref), channel_id=1, source_target_pairs={{0,18},{2,16},{4,22},{6,20},{8,26},{10,24},{12,30},{14,28},{16,2},... | collective-permute-start | bytes 98312 | tf_op jit(solution)/shard_map/ppermute | solution.py:412
  18.1 13.9 %collective-permute-start.9 = (f32[128,512]{1,0:T(8,128)S(1)}, f32[128,512]{1,0:T(8,128)S(1)}, u32[]{:S(2)}, u32[]{:S(2)}) collective-permute-start(f32[128,512]{1,0:T(8,128)S(1)} %complete.1.refs_0_), channel_id=1, source_target_pairs={{1,0},{0,1},{3,2},{2,3},{5,4},{4,5},{7,6},{6,7},{9,8},{8,9},{11,10... | collective-permute-start | bytes 786440 | tf_op jit(solution)/shard_map/ppermute | solution.py:428
  19.7 8.2 %copy-start = (f32[32,2,4,1,512]{4,3,2,1,0:T(1,128)S(1)}, f32[32,2,4,1,512]{4,3,2,1,0:T(1,128)}, u32[]{:S(2)}) copy-start(f32[32,2,4,1,512]{4,3,2,1,0:T(1,128)} %param.11) | copy-start | bytes 1572868
  19.7 4.4 %collective-permute-start.4 = (f32[32,256]{1,0:T(8,128)S(1)}, f32[32,256]{1,0:T(8,128)S(1)}, u32[]{:S(2)}, u32[]{:S(2)}) collective-permute-start(f32[32,256]{1,0:T(8,128)S(1)} %sum.4.terms_ref), channel_id=1, source_target_pairs={{0,6},{2,4},{4,2},{6,0},{8,14},{10,12},{12,10},{14,8},{16,22},{18,... | collective-permute-start | bytes 98312 | tf_op jit(solution)/shard_map/ppermute | solution.py:412
  24.1 3.6 %collective-permute-start.6 = (f32[32,256]{1,0:T(8,128)S(1)}, f32[32,256]{1,0:T(8,128)S(1)}, u32[]{:S(2)}, u32[]{:S(2)}) collective-permute-start(f32[32,256]{1,0:T(8,128)S(1)} %sum.5.refs_0_), channel_id=1, source_target_pairs={{3,0},{2,1},{1,2},{0,3},{7,4},{6,5},{5,6},{4,7},{11,8},{10,9},{9,1... | collective-permute-start | bytes 98312 | tf_op jit(solution)/shard_map/ppermute | solution.py:421
  27.7 1.4 %copy-start.1 = (f32[2,64,256]{2,1,0:T(8,128)S(1)}, f32[2,64,256]{2,1,0:T(8,128)}, u32[]{:S(2)}) copy-start(f32[2,64,256]{2,1,0:T(8,128)} %noise_ref.1) | copy-start | bytes 393220
  27.7 1.3 %copy-start.2 = (f32[2,256]{1,0:T(2,128)S(1)}, f32[2,256]{1,0:T(2,128)}, u32[]{:S(2)}) copy-start(f32[2,256]{1,0:T(2,128)} %value_ref.1) | copy-start | bytes 6148
  27.7 1.3 %copy-start.3 = (f32[2,256]{1,0:T(2,128)S(1)}, f32[2,256]{1,0:T(2,128)}, u32[]{:S(2)}) copy-start(f32[2,256]{1,0:T(2,128)} %error_ref.1) | copy-start | bytes 6148
  27.7 1.3 %collective-permute-start.7 = (f32[64,256]{1,0:T(8,128)S(1)}, f32[64,256]{1,0:T(8,128)S(1)}, u32[]{:S(2)}, u32[]{:S(2)}) collective-permute-start(f32[64,256]{1,0:T(8,128)S(1)} %gather.1.kept_ref), channel_id=1, source_target_pairs={{0,2},{2,0},{4,6},{6,4},{8,10},{10,8},{12,14},{14,12},{16,18},{18,... | collective-permute-start | bytes 196616 | tf_op jit(solution)/shard_map/ppermute | solution.py:412

commit v20 on v16

--- a/solution.py
+++ b/solution.py
@@ -212,8 +212,8 @@
 
 
 def gather_kernel(*refs):
-    local = refs[0].shape[0]
-    for d, ref in enumerate(refs[:-1]):
+    local = refs[2].shape[0]
+    for d, ref in enumerate(refs[2:-1]):
         refs[-1][d * local : (d + 1) * local, :] = ref[...]
 
 
@@ -431,7 +431,7 @@
 
     present, delayed = rows_of(present_ensemble), rows_of(delayed_ensemble)
     spread, ratios = rows_of(spreading_coefficient), rows_of(transport_ratios)
-    sources = in_hbm((present, spread, ratios, obs_row, obs_col, obs_field))
+    sources = in_hbm((present, spread, ratios))
     packed, *held = pl.pallas_call(
         functools.partial(load_kernel, chunks),
         out_shape=[shape_of((present.shape[0] + 2 * chunks, LANES))]
@@ -452,14 +452,14 @@
         compiler_params=PARAMS,
         cost_estimate=estimate(SELECT_FLOPS),
         name="selector",
-    )(*held[2:])
+    )(obs_row, obs_col, obs_field)
     part, here, part_obs = pl.pallas_call(
         functools.partial(own_row_kernel, *sizes),
         out_shape=(shape_of(stacked), shape_of(stacked), shape_of((members, total))),
         compiler_params=PARAMS,
         cost_estimate=estimate(OWN_FLOPS),
         name="own_row",
-    )(packed, *held[:2], taps, kinds)
+    )(packed, *held, taps, kinds)
     from_above = lax.ppermute(lax.optimization_barrier((packed, part))[0], "slab", up)
     keep, send, partial = pl.pallas_call(
         functools.partial(observe_kernel, parts, *sizes),
@@ -499,13 +499,19 @@
         lax.optimization_barrier((partial, after_far))[0], from_above, packed
     )
 
+    lagged_parts = pl.pallas_call(
+        functools.partial(prepare_kernel, parts),
+        out_shape=[shape_of((all_members, delayed.size // members), BF16)] * 2,
+        compiler_params=PARAMS,
+        name="prepare",
+    )(delayed, *others_delayed)
     prior = pl.pallas_call(
         gather_kernel,
         out_shape=shape_of((all_members, total // 2)),
         cost_estimate=estimate(GATHER_FLOPS),
         compiler_params=PARAMS,
         name="gather",
-    )(terms, *from_other_mem(terms))
+    )(*lagged_parts, terms, *from_other_mem(terms))
     mine = pl.pallas_call(
         functools.partial(solve_kernel, parts),
         out_shape=shape_of((members, all_members)),
@@ -513,12 +519,6 @@
         cost_estimate=estimate(SOLVE_FLOPS),
         name="solve",
     )(obs_value, obs_error, obs_noise, prior, from_slab(prior, 1))
-    lagged_parts = pl.pallas_call(
-        functools.partial(prepare_kernel, parts),
-        out_shape=[shape_of((all_members, delayed.size // members), BF16)] * 2,
-        compiler_params=PARAMS,
-        name="prepare",
-    )(delayed, *others_delayed)
     out = pl.pallas_call(
         functools.partial(combine_kernel, parts, fields),
         out_shape=shape_of((members, planes, LANES)),

time: 32.6 us -> 32.7 us (level)
    ppermute x5, waiting for transfers between devices: 4.48 us -> 5.21 us  [from_slab(): return lax.ppermute(array, 'slab', [(i, i ^ bit) for i in range(slabs)])]
    ppermute x1, waiting for transfers between devices: 1.89 us -> 1.18 us  [from_other_mem(): lax.ppermute(array, ('slab', 'mem'), [(i ^ 3, i) for i in range(slabs * p...]
where the time goes in v20:
time: 32.7 us; the launch traced here: 32.4 us
  starting transfers between devices  18.6 us (57%)
  Pallas kernels  7.34 us (22%)
  waiting for transfers between devices  6.4 us (20%)
    ppermute x5, starting transfers between devices, from_slab(): return lax.ppermute(array, 'slab', [(i, i ^ bit) for i in range(slabs)])  8.41 us
    ppermute x5, waiting for transfers between devices, from_slab(): return lax.ppermute(array, 'slab', [(i, i ^ bit) for i in range(slabs)])  5.21 us
    ppermute x2, starting transfers between devices, from_partners(): lax.ppermute(array, 'mem', [((i + d) % parts, i) for i in range(parts)])  4.56 us
    pallas_call x1, Pallas kernels, shards(): pl.pallas_call(functools.partial(solve_kernel, parts), out_shape=shape_of...  2.94 us
    ppermute x1, starting transfers between devices, shards(): lax.ppermute(lax.optimization_barrier((packed, part))[0], 'slab', up)  2.77 us
    ppermute x1, starting transfers between devices, from_other_mem(): lax.ppermute(array, ('slab', 'mem'), [(i ^ 3, i) for i in range(slabs * p...  1.53 us
    pallas_call x1, Pallas kernels, shards(): pl.pallas_call(functools.partial(combine_kernel, parts, fields), out_shap...  1.36 us
    ppermute x1, starting transfers between devices, shards(): from_below = lax.ppermute(packed, 'slab', [(j, i) for i, j in up])  1.29 us
  transfers between devices with their start and end apart: 10, of which 6 were waited for; matrix products, arithmetic and copies ran while one was open for 0% of the time, Pallas kernels for 15%

profile of v20, /device:TPU:0, one launch (start us, length us, event | category | flops | bytes accessed | tf_op | source)
XLA Modules:
  0.0 32.4 jit_solution(5534102681622950404)
XLA Ops:
  0.0 1.0 %load.1 = (f32[520,128]{1,0:T(8,128)S(1)}, f32[4,128]{1,0:T(4,128)S(1)}, f32[8,128]{1,0:T(8,128)S(1)}) custom-call(f32[512,128]{1,0:T(8,128)} %bitcast.7, f32[4,128]{1,0:T(4,128)} %bitcast.9, f32[8,128]{1,0:T(8,128)} %bitcast.8), custom_call_target="tpu_custom_call" | custom-call | tf_op jit(solution)/shard_map/load/pallas_call | solution.py:435
  1.0 1.3 %collective-permute-start.1 = (f32[520,128]{1,0:T(8,128)S(1)}, f32[520,128]{1,0:T(8,128)S(1)}, u32[]{:S(2)}, u32[]{:S(2)}) collective-permute-start(f32[520,128]{1,0:T(8,128)S(1)} %get-tuple-element.36.packed_ref), channel_id=1, source_target_pairs={{2,0},{4,2},{6,4},{8,6},{10,8},{12,10},{14,12},{16,14},{18,16},{20... | collective-permute-start | bytes 798728 | tf_op jit(solution)/shard_map/ppermute | solution.py:445
  2.3 3.0 %collective-permute-start = (f32[1024,128]{1,0:T(8,128)}, f32[1024,128]{1,0:T(8,128)S(1)}, u32[]{:S(2)}, u32[]{:S(2)}) collective-permute-start(f32[1024,128]{1,0:T(8,128)} %bitcast.5), channel_id=1, source_target_pairs={{1,0},{0,1},{3,2},{2,3},{5,4},{4,5},{7,6},{6,7},{9,8},{8,9},{11,10... | collective-permute-start | bytes 1572872 | tf_op jit(solution)/shard_map/ppermute | solution.py:428
  5.3 0.2 selector.1
  5.5 0.5 %own_row.1 = (f32[128,512]{1,0:T(8,128)S(1)}, f32[128,512]{1,0:T(8,128)S(1)}, f32[32,512]{1,0:T(8,128)S(1)}) custom-call(f32[520,128]{1,0:T(8,128)S(1)} %get-tuple-element.36.packed_ref, f32[4,128]{1,0:T(4,128)S(1)} %get-tuple-element.25.spread_ref, f32[8,128]{1,0:T(8,128)S(1)} %get-tuple-element.26.ratio_ref, ...), custom_call_target="tpu_custom_call" | custom-call | flops 1 | tf_op jit(solution)/shard_map/own_row/pallas_call | solution.py:456
  6.1 2.8 %collective-permute-start.8 = (f32[520,128]{1,0:T(8,128)S(1)}, f32[520,128]{1,0:T(8,128)S(1)}, u32[]{:S(2)}, u32[]{:S(2)}) collective-permute-start(f32[520,128]{1,0:T(8,128)S(1)} %get-tuple-element.36.packed_ref), channel_id=1, source_target_pairs={{0,2},{2,4},{4,6},{6,8},{8,10},{10,12},{12,14},{14,16},{16,18},{18... | collective-permute-start | bytes 798728 | tf_op jit(solution)/shard_map/ppermute | solution.py:463
  8.8 0.5 %observe.1 = (f32[32,256]{1,0:T(8,128)S(1)}, f32[32,256]{1,0:T(8,128)S(1)}, f32[128,512]{1,0:T(8,128)S(1)}) custom-call(f32[520,128]{1,0:T(8,128)S(1)} %get-tuple-element.36.packed_ref, f32[520,128]{1,0:T(8,128)S(1)} %collective-permute-done.1.next_ref, f32[128,512]{1,0:T(8,128)S(1)} %get-tuple-element.29.part_ref, ...), custom_call_target="tpu_custom_call" | custom-call | tf_op jit(solution)/shard_map/observe/pallas_call | solution.py:464
  9.3 1.6 %collective-permute-start.2 = (f32[32,256]{1,0:T(8,128)S(1)}, f32[32,256]{1,0:T(8,128)S(1)}, u32[]{:S(2)}, u32[]{:S(2)}) collective-permute-start(f32[32,256]{1,0:T(8,128)S(1)} %get-tuple-element.33), channel_id=1, source_target_pairs={{0,2},{2,0},{4,6},{6,4},{8,10},{10,8},{12,14},{14,12},{16,18},{18,... | collective-permute-start | bytes 98312 | tf_op jit(solution)/shard_map/ppermute | solution.py:412
  11.0 0.9 %collective-permute-done.2 = f32[32,256]{1,0:T(8,128)S(1)} collective-permute-done((f32[32,256]{1,0:T(8,128)S(1)}, f32[32,256]{1,0:T(8,128)S(1)}, u32[]{:S(2)}, u32[]{:S(2)}) %collective-permute-start.2) | collective-permute-done | bytes 32800 | tf_op jit(solution)/shard_map/ppermute | solution.py:412
  11.8 2.5 %collective-permute-start.3 = (f32[32,256]{1,0:T(8,128)S(1)}, f32[32,256]{1,0:T(8,128)S(1)}, u32[]{:S(2)}, u32[]{:S(2)}) collective-permute-start(f32[32,256]{1,0:T(8,128)S(1)} %add.3.terms_ref), channel_id=1, source_target_pairs={{0,18},{2,16},{4,22},{6,20},{8,26},{10,24},{12,30},{14,28},{16,2},... | collective-permute-start | bytes 98312 | tf_op jit(solution)/shard_map/ppermute | solution.py:412
  14.4 1.7 %collective-permute-done.3.other_ref = f32[32,256]{1,0:T(8,128)S(1)} collective-permute-done((f32[32,256]{1,0:T(8,128)S(1)}, f32[32,256]{1,0:T(8,128)S(1)}, u32[]{:S(2)}, u32[]{:S(2)}) %collective-permute-start.3) | collective-permute-done | bytes 32800 | tf_op jit(solution)/shard_map/ppermute | solution.py:412
  16.1 1.5 %collective-permute-start.4 = (f32[32,256]{1,0:T(8,128)S(1)}, f32[32,256]{1,0:T(8,128)S(1)}, u32[]{:S(2)}, u32[]{:S(2)}) collective-permute-start(f32[32,256]{1,0:T(8,128)S(1)} %sum.3.terms_ref), channel_id=1, source_target_pairs={{0,10},{2,8},{4,14},{6,12},{8,2},{10,0},{12,6},{14,4},{16,26},{18,... | collective-permute-start | bytes 98312 | tf_op jit(solution)/shard_map/ppermute | solution.py:412
  17.6 0.1 complete.1.refs_0_
  17.7 1.6 %collective-permute-start.9 = (f32[128,512]{1,0:T(8,128)S(1)}, f32[128,512]{1,0:T(8,128)S(1)}, u32[]{:S(2)}, u32[]{:S(2)}) collective-permute-start(f32[128,512]{1,0:T(8,128)S(1)} %complete.1.refs_0_), channel_id=1, source_target_pairs={{1,0},{0,1},{3,2},{2,3},{5,4},{4,5},{7,6},{6,7},{9,8},{8,9},{11,10... | collective-permute-start | bytes 786440 | tf_op jit(solution)/shard_map/ppermute | solution.py:428
  19.3 0.1 collective-permute-done.4.other_ref
  19.4 2.2 %collective-permute-start.5 = (f32[32,256]{1,0:T(8,128)S(1)}, f32[32,256]{1,0:T(8,128)S(1)}, u32[]{:S(2)}, u32[]{:S(2)}) collective-permute-start(f32[32,256]{1,0:T(8,128)S(1)} %sum.4.terms_ref), channel_id=1, source_target_pairs={{0,6},{2,4},{4,2},{6,0},{8,14},{10,12},{12,10},{14,8},{16,22},{18,... | collective-permute-start | bytes 98312 | tf_op jit(solution)/shard_map/ppermute | solution.py:412
  21.6 1.6 %collective-permute-done.5.other_ref = f32[32,256]{1,0:T(8,128)S(1)} collective-permute-done((f32[32,256]{1,0:T(8,128)S(1)}, f32[32,256]{1,0:T(8,128)S(1)}, u32[]{:S(2)}, u32[]{:S(2)}) %collective-permute-start.5) | collective-permute-done | bytes 32800 | tf_op jit(solution)/shard_map/ppermute | solution.py:412
  23.3 1.5 %collective-permute-start.6 = (f32[32,256]{1,0:T(8,128)S(1)}, f32[32,256]{1,0:T(8,128)S(1)}, u32[]{:S(2)}, u32[]{:S(2)}) collective-permute-start(f32[32,256]{1,0:T(8,128)S(1)} %sum.5.refs_2_), channel_id=1, source_target_pairs={{3,0},{2,1},{1,2},{0,3},{7,4},{6,5},{5,6},{4,7},{11,8},{10,9},{9,1... | collective-permute-start | bytes 98312 | tf_op jit(solution)/shard_map/ppermute | solution.py:421
  24.8 0.7 %prepare.1 = (bf16[64,4096]{1,0:T(8,128)(2,1)S(1)}, bf16[64,4096]{1,0:T(8,128)(2,1)S(1)}) custom-call(f32[1024,128]{1,0:T(8,128)S(1)} %bitcast.6, f32[1024,128]{1,0:T(8,128)S(1)} %collective-permute-done.refs_1_.refs_0_), custom_call_target="tpu_custom_call" | custom-call | tf_op jit(solution)/shard_map/prepare/pallas_call | solution.py:502
  25.5 1.2 %collective-permute-done.6.refs_3_ = f32[32,256]{1,0:T(8,128)S(1)} collective-permute-done((f32[32,256]{1,0:T(8,128)S(1)}, f32[32,256]{1,0:T(8,128)S(1)}, u32[]{:S(2)}, u32[]{:S(2)}) %collective-permute-start.6) | collective-permute-done | bytes 32800 | tf_op jit(solution)/shard_map/ppermute | solution.py:421
  26.7 0.5 %collective-permute-start.7 = (f32[64,256]{1,0:T(8,128)S(1)}, f32[64,256]{1,0:T(8,128)S(1)}, u32[]{:S(2)}, u32[]{:S(2)}) collective-permute-start(f32[64,256]{1,0:T(8,128)S(1)} %gather.1.kept_ref), channel_id=1, source_target_pairs={{0,2},{2,0},{4,6},{6,4},{8,10},{10,8},{12,14},{14,12},{16,18},{18,... | collective-permute-start | bytes 196616 | tf_op jit(solution)/shard_map/ppermute | solution.py:412
  27.2 0.9 %collective-permute-done.7.received_ref = f32[64,256]{1,0:T(8,128)S(1)} collective-permute-done((f32[64,256]{1,0:T(8,128)S(1)}, f32[64,256]{1,0:T(8,128)S(1)}, u32[]{:S(2)}, u32[]{:S(2)}) %collective-permute-start.7) | collective-permute-done | bytes 65568 | tf_op jit(solution)/shard_map/ppermute | solution.py:412
  28.1 2.9 %solve.1.mine_ref = f32[32,64]{1,0:T(8,128)S(1)} custom-call(f32[2,256]{1,0:T(2,128)S(1)} %copy-done.5, f32[2,256]{1,0:T(2,128)S(1)} %copy-done.6, f32[2,64,256]{2,1,0:T(8,128)S(1)} %copy-done.4, f32[64,256]{1,0:T(8,128)S(1)} %gather.1.kept_ref, f32[64,256]{1,0:T(8,128)S(1)} %collective-permute-done.7.received_ref), custom_call_target="tpu_custom_call" | custom-call | flops 500000000 | tf_op jit(solution)/shard_map/solve/pallas_call | solution.py:515
  31.1 1.4 %combine.1 = f32[32,48,128]{2,1,0:T(8,128)} custom-call(f32[32,64]{1,0:T(8,128)S(1)} %solve.1.mine_ref, f32[128,512]{1,0:T(8,128)S(1)} %complete.1.refs_0_, f32[128,512]{1,0:T(8,128)S(1)} %collective-permute-done.9.refs_1_, bf16[64,4096]{1,0:T(8,128)(2,1)S(1)} %get-tuple-element.23.refs_0_.refs_2_, bf16[64,4096]{1,0:T(8,128)(2,1)S(1)} %get-tuple-element.24.refs_1_.refs_3_), custom_call_target="tpu_custom_call" | custom-call | tf_op jit(solution)/shard_map/combine/pallas_call | solution.py:522
  (23 shorter events, 0.1 us)
Async XLA Ops:
  0.0 5.3 %copy-start.2 = (s32[2,256]{1,0:T(2,128)S(1)}, s32[2,256]{1,0:T(2,128)}, u32[]{:S(2)}) copy-start(s32[2,256]{1,0:T(2,128)} %col_ref.1) | copy-start | bytes 6148
  0.0 5.3 %copy-start.3 = (s32[2,256]{1,0:T(2,128)S(1)}, s32[2,256]{1,0:T(2,128)}, u32[]{:S(2)}) copy-start(s32[2,256]{1,0:T(2,128)} %field_ref.1) | copy-start | bytes 6148
  1.0 4.3 %copy-start.1 = (s32[2,256]{1,0:T(2,128)S(1)}, s32[2,256]{1,0:T(2,128)}, u32[]{:S(2)}) copy-start(s32[2,256]{1,0:T(2,128)} %row_ref.1) | copy-start | bytes 6148
  1.0 7.8 %collective-permute-start.1 = (f32[520,128]{1,0:T(8,128)S(1)}, f32[520,128]{1,0:T(8,128)S(1)}, u32[]{:S(2)}, u32[]{:S(2)}) collective-permute-start(f32[520,128]{1,0:T(8,128)S(1)} %get-tuple-element.36.packed_ref), channel_id=1, source_target_pairs={{2,0},{4,2},{6,4},{8,6},{10,8},{12,10},{14,12},{16,14},{18,16},{20... | collective-permute-start | bytes 798728 | tf_op jit(solution)/shard_map/ppermute | solution.py:445
  2.3 20.9 %collective-permute-start = (f32[1024,128]{1,0:T(8,128)}, f32[1024,128]{1,0:T(8,128)S(1)}, u32[]{:S(2)}, u32[]{:S(2)}) collective-permute-start(f32[1024,128]{1,0:T(8,128)} %bitcast.5), channel_id=1, source_target_pairs={{1,0},{0,1},{3,2},{2,3},{5,4},{4,5},{7,6},{6,7},{9,8},{8,9},{11,10... | collective-permute-start | bytes 1572872 | tf_op jit(solution)/shard_map/ppermute | solution.py:428
  6.1 11.5 %collective-permute-start.8 = (f32[520,128]{1,0:T(8,128)S(1)}, f32[520,128]{1,0:T(8,128)S(1)}, u32[]{:S(2)}, u32[]{:S(2)}) collective-permute-start(f32[520,128]{1,0:T(8,128)S(1)} %get-tuple-element.36.packed_ref), channel_id=1, source_target_pairs={{0,2},{2,4},{4,6},{6,8},{8,10},{10,12},{12,14},{14,16},{16,18},{18... | collective-permute-start | bytes 798728 | tf_op jit(solution)/shard_map/ppermute | solution.py:463
  9.3 2.5 %collective-permute-start.2 = (f32[32,256]{1,0:T(8,128)S(1)}, f32[32,256]{1,0:T(8,128)S(1)}, u32[]{:S(2)}, u32[]{:S(2)}) collective-permute-start(f32[32,256]{1,0:T(8,128)S(1)} %get-tuple-element.33), channel_id=1, source_target_pairs={{0,2},{2,0},{4,6},{6,4},{8,10},{10,8},{12,14},{14,12},{16,18},{18,... | collective-permute-start | bytes 98312 | tf_op jit(solution)/shard_map/ppermute | solution.py:412
  11.8 4.2 %collective-permute-start.3 = (f32[32,256]{1,0:T(8,128)S(1)}, f32[32,256]{1,0:T(8,128)S(1)}, u32[]{:S(2)}, u32[]{:S(2)}) collective-permute-start(f32[32,256]{1,0:T(8,128)S(1)} %add.3.terms_ref), channel_id=1, source_target_pairs={{0,18},{2,16},{4,22},{6,20},{8,26},{10,24},{12,30},{14,28},{16,2},... | collective-permute-start | bytes 98312 | tf_op jit(solution)/shard_map/ppermute | solution.py:412
  16.1 3.3 %collective-permute-start.4 = (f32[32,256]{1,0:T(8,128)S(1)}, f32[32,256]{1,0:T(8,128)S(1)}, u32[]{:S(2)}, u32[]{:S(2)}) collective-permute-start(f32[32,256]{1,0:T(8,128)S(1)} %sum.3.terms_ref), channel_id=1, source_target_pairs={{0,10},{2,8},{4,14},{6,12},{8,2},{10,0},{12,6},{14,4},{16,26},{18,... | collective-permute-start | bytes 98312 | tf_op jit(solution)/shard_map/ppermute | solution.py:412
  17.7 13.3 %collective-permute-start.9 = (f32[128,512]{1,0:T(8,128)S(1)}, f32[128,512]{1,0:T(8,128)S(1)}, u32[]{:S(2)}, u32[]{:S(2)}) collective-permute-start(f32[128,512]{1,0:T(8,128)S(1)} %complete.1.refs_0_), channel_id=1, source_target_pairs={{1,0},{0,1},{3,2},{2,3},{5,4},{4,5},{7,6},{6,7},{9,8},{8,9},{11,10... | collective-permute-start | bytes 786440 | tf_op jit(solution)/shard_map/ppermute | solution.py:428
  19.4 5.4 %copy-start = (f32[32,2,4,1,512]{4,3,2,1,0:T(1,128)S(1)}, f32[32,2,4,1,512]{4,3,2,1,0:T(1,128)}, u32[]{:S(2)}) copy-start(f32[32,2,4,1,512]{4,3,2,1,0:T(1,128)} %param.11) | copy-start | bytes 1572868
  19.4 3.8 %collective-permute-start.5 = (f32[32,256]{1,0:T(8,128)S(1)}, f32[32,256]{1,0:T(8,128)S(1)}, u32[]{:S(2)}, u32[]{:S(2)}) collective-permute-start(f32[32,256]{1,0:T(8,128)S(1)} %sum.4.terms_ref), channel_id=1, source_target_pairs={{0,6},{2,4},{4,2},{6,0},{8,14},{10,12},{12,10},{14,8},{16,22},{18,... | collective-permute-start | bytes 98312 | tf_op jit(solution)/shard_map/ppermute | solution.py:412
  23.3 3.4 %collective-permute-start.6 = (f32[32,256]{1,0:T(8,128)S(1)}, f32[32,256]{1,0:T(8,128)S(1)}, u32[]{:S(2)}, u32[]{:S(2)}) collective-permute-start(f32[32,256]{1,0:T(8,128)S(1)} %sum.5.refs_2_), channel_id=1, source_target_pairs={{3,0},{2,1},{1,2},{0,3},{7,4},{6,5},{5,6},{4,7},{11,8},{10,9},{9,1... | collective-permute-start | bytes 98312 | tf_op jit(solution)/shard_map/ppermute | solution.py:421
  26.7 1.4 %copy-start.4 = (f32[2,64,256]{2,1,0:T(8,128)S(1)}, f32[2,64,256]{2,1,0:T(8,128)}, u32[]{:S(2)}) copy-start(f32[2,64,256]{2,1,0:T(8,128)} %noise_ref.1) | copy-start | bytes 393220
  26.7 1.4 %copy-start.5 = (f32[2,256]{1,0:T(2,128)S(1)}, f32[2,256]{1,0:T(2,128)}, u32[]{:S(2)}) copy-start(f32[2,256]{1,0:T(2,128)} %value_ref.1) | copy-start | bytes 6148
  26.7 1.4 %copy-start.6 = (f32[2,256]{1,0:T(2,128)S(1)}, f32[2,256]{1,0:T(2,128)}, u32[]{:S(2)}) copy-start(f32[2,256]{1,0:T(2,128)} %error_ref.1) | copy-start | bytes 6148
  26.7 1.4 %collective-permute-start.7 = (f32[64,256]{1,0:T(8,128)S(1)}, f32[64,256]{1,0:T(8,128)S(1)}, u32[]{:S(2)}, u32[]{:S(2)}) collective-permute-start(f32[64,256]{1,0:T(8,128)S(1)} %gather.1.kept_ref), channel_id=1, source_target_pairs={{0,2},{2,0},{4,6},{6,4},{8,10},{10,8},{12,14},{14,12},{16,18},{18,... | collective-permute-start | bytes 196616 | tf_op jit(solution)/shard_map/ppermute | solution.py:412

commit v21 on v16

--- a/solution.py
+++ b/solution.py
@@ -15,7 +15,7 @@
 
 
 SELECT_FLOPS = 1
-OWN_FLOPS, SUM_FLOPS, GATHER_FLOPS, SOLVE_FLOPS = 1, (7*10**8,7*10**8,1), 10**8, 5*10**8
+OWN_FLOPS, SUM_FLOPS, GATHER_FLOPS, SOLVE_FLOPS = 1, (2*10**9,1,8*10**8), 10**8, 7*10**8
 
 
 def estimate(flops):
@@ -460,7 +460,6 @@
         cost_estimate=estimate(OWN_FLOPS),
         name="own_row",
     )(packed, *held[:2], taps, kinds)
-    from_above = lax.ppermute(lax.optimization_barrier((packed, part))[0], "slab", up)
     keep, send, partial = pl.pallas_call(
         functools.partial(observe_kernel, parts, *sizes),
         out_shape=(
@@ -481,6 +480,7 @@
         )(terms, other, *arrived)
 
     terms = keep + from_slab(send, 1)
+    from_above = lax.ppermute(lax.optimization_barrier((packed, terms))[0], "slab", up)
     for bit in [1 << k for k in reversed(range(1, slabs.bit_length() - 1))]:
         terms = summed(
             terms,
@@ -488,15 +488,15 @@
             SUM_FLOPS[min(slabs // 2 // bit, 4) // 2],
             *([others_delayed[0]] if bit == 2 else []),
         )
-        if bit == slabs // 2:
-            after_far = terms
+        if bit == 4:
+            before_last = terms
     forecast = pl.pallas_call(
         functools.partial(complete_kernel, *sizes),
         out_shape=shape_of(stacked),
         compiler_params=PARAMS,
         name="complete",
     )(
-        lax.optimization_barrier((partial, after_far))[0], from_above, packed
+        lax.optimization_barrier((partial, before_last))[0], from_above, packed
     )
 
     prior = pl.pallas_call(

time: 32.6 us -> 38.1 us (1.17)
  the two profiles are of different devices: /device:TPU:0 before, /device:TPU:11 now
where the time goes in v21:
time: 38.1 us; the launch traced here: 37.9 us
  waiting for transfers between devices  17.7 us (46%)
  starting transfers between devices  12.8 us (34%)
  Pallas kernels  7.31 us (19%)
    ppermute x5, starting transfers between devices, from_slab(): return lax.ppermute(array, 'slab', [(i, i ^ bit) for i in range(slabs)])  7.59 us
    ppermute x1, waiting for transfers between devices, from_other_mem(): lax.ppermute(array, ('slab', 'mem'), [(i ^ 3, i) for i in range(slabs * p...  7.36 us
    ppermute x5, waiting for transfers between devices, from_slab(): return lax.ppermute(array, 'slab', [(i, i ^ bit) for i in range(slabs)])  5.83 us
    ppermute x1, waiting for transfers between devices, shards(): from_below = lax.ppermute(packed, 'slab', [(j, i) for i, j in up])  4.48 us
    pallas_call x1, Pallas kernels, shards(): pl.pallas_call(functools.partial(solve_kernel, parts), out_shape=shape_of...  2.94 us
    ppermute x1, starting transfers between devices, shards(): from_below = lax.ppermute(packed, 'slab', [(j, i) for i, j in up])  2.58 us
    ppermute x1, starting transfers between devices, shards(): lax.ppermute(lax.optimization_barrier((packed, terms))[0], 'slab', up)  1.91 us
    pallas_call x1, Pallas kernels, shards(): pl.pallas_call(functools.partial(combine_kernel, parts, fields), out_shap...  1.36 us
  transfers between devices with their start and end apart: 10, of which 6 were waited for; matrix products, arithmetic and copies ran while one was open for 0% of the time, Pallas kernels for 13%

profile of v21, /device:TPU:11, one launch (start us, length us, event | category | flops | bytes accessed | tf_op | source)
XLA Modules:
  0.0 37.9 jit_solution(17274170418604644611)
XLA Ops:
  0.0 1.0 %load.1 = (f32[520,128]{1,0:T(8,128)S(1)}, f32[4,128]{1,0:T(4,128)S(1)}, f32[8,128]{1,0:T(8,128)S(1)}, s32[2,256]{1,0:T(2,128)S(1)}, s32[2,256]{1,0:T(2,128)S(1)}, /*index=5*/s32[2,256]{1,0:T(2,128)S(1)}) custom-call(f32[512,128]{1,0:T(8,128)} %bitcast.7, f32[4,128]{1,0:T(4,128)} %bitcast.9, f32[8,128]{1,0:T(8,128)} %bitcast.8, s32[2,256]{1,0:T(2,128)} %refs_3_.1, ...), custom_call_target="tpu_custom_call" | custom-call | tf_op jit(solution)/shard_map/load/pallas_call | solution.py:435
  1.0 2.6 %collective-permute-start = (f32[520,128]{1,0:T(8,128)S(1)}, f32[520,128]{1,0:T(8,128)S(1)}, u32[]{:S(2)}, u32[]{:S(2)}) collective-permute-start(f32[520,128]{1,0:T(8,128)S(1)} %get-tuple-element.40.packed_ref), channel_id=1, source_target_pairs={{2,0},{4,2},{6,4},{8,6},{10,8},{12,10},{14,12},{16,14},{18,16},{20... | collective-permute-start | bytes 798728 | tf_op jit(solution)/shard_map/ppermute | solution.py:445
  3.6 0.3 collective-permute-start.5
  3.9 0.2 selector.1
  4.1 0.5 %own_row.1 = (f32[128,512]{1,0:T(8,128)S(1)}, f32[128,512]{1,0:T(8,128)S(1)}, f32[32,512]{1,0:T(8,128)S(1)}) custom-call(f32[520,128]{1,0:T(8,128)S(1)} %get-tuple-element.40.packed_ref, f32[4,128]{1,0:T(4,128)S(1)} %get-tuple-element.25.spread_ref, f32[8,128]{1,0:T(8,128)S(1)} %get-tuple-element.26.ratio_ref, ...), custom_call_target="tpu_custom_call" | custom-call | flops 1 | tf_op jit(solution)/shard_map/own_row/pallas_call | solution.py:456
  4.6 4.5 %collective-permute-done.next_ref = f32[520,128]{1,0:T(8,128)S(1)} collective-permute-done((f32[520,128]{1,0:T(8,128)S(1)}, f32[520,128]{1,0:T(8,128)S(1)}, u32[]{:S(2)}, u32[]{:S(2)}) %collective-permute-start) | collective-permute-done | bytes 266272 | tf_op jit(solution)/shard_map/ppermute | solution.py:445
  9.1 0.5 %observe.1 = (f32[32,256]{1,0:T(8,128)S(1)}, f32[32,256]{1,0:T(8,128)S(1)}, f32[128,512]{1,0:T(8,128)S(1)}) custom-call(f32[520,128]{1,0:T(8,128)S(1)} %get-tuple-element.40.packed_ref, f32[520,128]{1,0:T(8,128)S(1)} %collective-permute-done.next_ref, f32[128,512]{1,0:T(8,128)S(1)} %get-tuple-element.32.part_ref, ...), custom_call_target="tpu_custom_call" | custom-call | tf_op jit(solution)/shard_map/observe/pallas_call | solution.py:463
  9.6 0.1 collective-permute-start.1
  9.7 1.2 %collective-permute-done.1 = f32[32,256]{1,0:T(8,128)S(1)} collective-permute-done((f32[32,256]{1,0:T(8,128)S(1)}, f32[32,256]{1,0:T(8,128)S(1)}, u32[]{:S(2)}, u32[]{:S(2)}) %collective-permute-start.1) | collective-permute-done | bytes 32800 | tf_op jit(solution)/shard_map/ppermute | solution.py:412
  10.9 2.4 %collective-permute-start.2 = (f32[32,256]{1,0:T(8,128)S(1)}, f32[32,256]{1,0:T(8,128)S(1)}, u32[]{:S(2)}, u32[]{:S(2)}) collective-permute-start(f32[32,256]{1,0:T(8,128)S(1)} %add.3.terms_ref), channel_id=1, source_target_pairs={{0,18},{2,16},{4,22},{6,20},{8,26},{10,24},{12,30},{14,28},{16,2},... | collective-permute-start | bytes 98312 | tf_op jit(solution)/shard_map/ppermute | solution.py:412
  13.2 1.9 %collective-permute-start.8 = (f32[520,128]{1,0:T(8,128)S(1)}, f32[520,128]{1,0:T(8,128)S(1)}, u32[]{:S(2)}, u32[]{:S(2)}) collective-permute-start(f32[520,128]{1,0:T(8,128)S(1)} %get-tuple-element.40.packed_ref), channel_id=1, source_target_pairs={{0,2},{2,4},{4,6},{6,8},{8,10},{10,12},{12,14},{14,16},{16,18},{18... | collective-permute-start | bytes 798728 | tf_op jit(solution)/shard_map/ppermute | solution.py:483
  15.2 0.6 %collective-permute-start.3 = (f32[32,256]{1,0:T(8,128)S(1)}, f32[32,256]{1,0:T(8,128)S(1)}, u32[]{:S(2)}, u32[]{:S(2)}) collective-permute-start(f32[32,256]{1,0:T(8,128)S(1)} %sum.3.terms_ref), channel_id=1, source_target_pairs={{0,10},{2,8},{4,14},{6,12},{8,2},{10,0},{12,6},{14,4},{16,26},{18,... | collective-permute-start | bytes 98312 | tf_op jit(solution)/shard_map/ppermute | solution.py:412
  15.8 3.3 %collective-permute-done.3.other_ref = f32[32,256]{1,0:T(8,128)S(1)} collective-permute-done((f32[32,256]{1,0:T(8,128)S(1)}, f32[32,256]{1,0:T(8,128)S(1)}, u32[]{:S(2)}, u32[]{:S(2)}) %collective-permute-start.3) | collective-permute-done | bytes 32800 | tf_op jit(solution)/shard_map/ppermute | solution.py:412
  19.1 4.0 %collective-permute-start.4 = (f32[32,256]{1,0:T(8,128)S(1)}, f32[32,256]{1,0:T(8,128)S(1)}, u32[]{:S(2)}, u32[]{:S(2)}) collective-permute-start(f32[32,256]{1,0:T(8,128)S(1)} %sum.4.terms_ref), channel_id=1, source_target_pairs={{0,6},{2,4},{4,2},{6,0},{8,14},{10,12},{12,10},{14,8},{16,22},{18,... | collective-permute-start | bytes 98312 | tf_op jit(solution)/shard_map/ppermute | solution.py:412
  23.1 0.1 complete.1.refs_0_
  23.2 0.3 collective-permute-start.9
  23.5 1.2 %collective-permute-done.4.other_ref = f32[32,256]{1,0:T(8,128)S(1)} collective-permute-done((f32[32,256]{1,0:T(8,128)S(1)}, f32[32,256]{1,0:T(8,128)S(1)}, u32[]{:S(2)}, u32[]{:S(2)}) %collective-permute-start.4) | collective-permute-done | bytes 32800 | tf_op jit(solution)/shard_map/ppermute | solution.py:412
  24.7 0.1 collective-permute-start.6
  24.8 7.4 %collective-permute-done.6.refs_1_ = f32[32,256]{1,0:T(8,128)S(1)} collective-permute-done((f32[32,256]{1,0:T(8,128)S(1)}, f32[32,256]{1,0:T(8,128)S(1)}, u32[]{:S(2)}, u32[]{:S(2)}) %collective-permute-start.6) | collective-permute-done | bytes 32800 | tf_op jit(solution)/shard_map/ppermute | solution.py:421
  32.2 0.5 %collective-permute-start.7 = (f32[64,256]{1,0:T(8,128)S(1)}, f32[64,256]{1,0:T(8,128)S(1)}, u32[]{:S(2)}, u32[]{:S(2)}) collective-permute-start(f32[64,256]{1,0:T(8,128)S(1)} %gather.1.kept_ref), channel_id=1, source_target_pairs={{0,2},{2,0},{4,6},{6,4},{8,10},{10,8},{12,14},{14,12},{16,18},{18,... | collective-permute-start | bytes 196616 | tf_op jit(solution)/shard_map/ppermute | solution.py:412
  32.7 0.7 %prepare.1 = (bf16[64,4096]{1,0:T(8,128)(2,1)S(1)}, bf16[64,4096]{1,0:T(8,128)(2,1)S(1)}) custom-call(f32[1024,128]{1,0:T(8,128)S(1)} %bitcast.6, f32[1024,128]{1,0:T(8,128)S(1)} %collective-permute-done.5.refs_0_.refs_1_), custom_call_target="tpu_custom_call" | custom-call | tf_op jit(solution)/shard_map/prepare/pallas_call | solution.py:516
  33.4 0.2 collective-permute-done.7.received_ref
  33.6 2.9 %solve.1.mine_ref = f32[32,64]{1,0:T(8,128)S(1)} custom-call(f32[2,256]{1,0:T(2,128)S(1)} %copy-done.2, f32[2,256]{1,0:T(2,128)S(1)} %copy-done.3, f32[2,64,256]{2,1,0:T(8,128)S(1)} %copy-done.1, f32[64,256]{1,0:T(8,128)S(1)} %gather.1.kept_ref, f32[64,256]{1,0:T(8,128)S(1)} %collective-permute-done.7.received_ref), custom_call_target="tpu_custom_call" | custom-call | flops 700000000 | tf_op jit(solution)/shard_map/solve/pallas_call | solution.py:509
  36.6 1.4 %combine.1 = f32[32,48,128]{2,1,0:T(8,128)} custom-call(f32[32,64]{1,0:T(8,128)S(1)} %solve.1.mine_ref, f32[128,512]{1,0:T(8,128)S(1)} %complete.1.refs_0_, f32[128,512]{1,0:T(8,128)S(1)} %collective-permute-done.9.refs_1_, bf16[64,4096]{1,0:T(8,128)(2,1)S(1)} %get-tuple-element.41.refs_2_, bf16[64,4096]{1,0:T(8,128)(2,1)S(1)} %get-tuple-element.42.refs_3_), custom_call_target="tpu_custom_call" | custom-call | tf_op jit(solution)/shard_map/combine/pallas_call | solution.py:522
  (17 shorter events, 0.1 us)
Async XLA Ops:
  1.0 8.1 %collective-permute-start = (f32[520,128]{1,0:T(8,128)S(1)}, f32[520,128]{1,0:T(8,128)S(1)}, u32[]{:S(2)}, u32[]{:S(2)}) collective-permute-start(f32[520,128]{1,0:T(8,128)S(1)} %get-tuple-element.40.packed_ref), channel_id=1, source_target_pairs={{2,0},{4,2},{6,4},{8,6},{10,8},{12,10},{14,12},{16,14},{18,16},{20... | collective-permute-start | bytes 798728 | tf_op jit(solution)/shard_map/ppermute | solution.py:445
  3.6 21.1 %collective-permute-start.5 = (f32[1024,128]{1,0:T(8,128)}, f32[1024,128]{1,0:T(8,128)S(1)}, u32[]{:S(2)}, u32[]{:S(2)}) collective-permute-start(f32[1024,128]{1,0:T(8,128)} %bitcast.5), channel_id=1, source_target_pairs={{1,0},{0,1},{3,2},{2,3},{5,4},{4,5},{7,6},{6,7},{9,8},{8,9},{11,10... | collective-permute-start | bytes 1572872 | tf_op jit(solution)/shard_map/ppermute | solution.py:428
  9.6 1.3 %collective-permute-start.1 = (f32[32,256]{1,0:T(8,128)S(1)}, f32[32,256]{1,0:T(8,128)S(1)}, u32[]{:S(2)}, u32[]{:S(2)}) collective-permute-start(f32[32,256]{1,0:T(8,128)S(1)} %get-tuple-element.36), channel_id=1, source_target_pairs={{0,2},{2,0},{4,6},{6,4},{8,10},{10,8},{12,14},{14,12},{16,18},{18,... | collective-permute-start | bytes 98312 | tf_op jit(solution)/shard_map/ppermute | solution.py:412
  10.9 4.3 %collective-permute-start.2 = (f32[32,256]{1,0:T(8,128)S(1)}, f32[32,256]{1,0:T(8,128)S(1)}, u32[]{:S(2)}, u32[]{:S(2)}) collective-permute-start(f32[32,256]{1,0:T(8,128)S(1)} %add.3.terms_ref), channel_id=1, source_target_pairs={{0,18},{2,16},{4,22},{6,20},{8,26},{10,24},{12,30},{14,28},{16,2},... | collective-permute-start | bytes 98312 | tf_op jit(solution)/shard_map/ppermute | solution.py:412
  13.2 9.8 %collective-permute-start.8 = (f32[520,128]{1,0:T(8,128)S(1)}, f32[520,128]{1,0:T(8,128)S(1)}, u32[]{:S(2)}, u32[]{:S(2)}) collective-permute-start(f32[520,128]{1,0:T(8,128)S(1)} %get-tuple-element.40.packed_ref), channel_id=1, source_target_pairs={{0,2},{2,4},{4,6},{6,8},{8,10},{10,12},{12,14},{14,16},{16,18},{18... | collective-permute-start | bytes 798728 | tf_op jit(solution)/shard_map/ppermute | solution.py:483
  15.2 3.9 %collective-permute-start.3 = (f32[32,256]{1,0:T(8,128)S(1)}, f32[32,256]{1,0:T(8,128)S(1)}, u32[]{:S(2)}, u32[]{:S(2)}) collective-permute-start(f32[32,256]{1,0:T(8,128)S(1)} %sum.3.terms_ref), channel_id=1, source_target_pairs={{0,10},{2,8},{4,14},{6,12},{8,2},{10,0},{12,6},{14,4},{16,26},{18,... | collective-permute-start | bytes 98312 | tf_op jit(solution)/shard_map/ppermute | solution.py:412
  19.1 5.6 %collective-permute-start.4 = (f32[32,256]{1,0:T(8,128)S(1)}, f32[32,256]{1,0:T(8,128)S(1)}, u32[]{:S(2)}, u32[]{:S(2)}) collective-permute-start(f32[32,256]{1,0:T(8,128)S(1)} %sum.4.terms_ref), channel_id=1, source_target_pairs={{0,6},{2,4},{4,2},{6,0},{8,14},{10,12},{12,10},{14,8},{16,22},{18,... | collective-permute-start | bytes 98312 | tf_op jit(solution)/shard_map/ppermute | solution.py:412
  23.2 13.4 %collective-permute-start.9 = (f32[128,512]{1,0:T(8,128)S(1)}, f32[128,512]{1,0:T(8,128)S(1)}, u32[]{:S(2)}, u32[]{:S(2)}) collective-permute-start(f32[128,512]{1,0:T(8,128)S(1)} %complete.1.refs_0_), channel_id=1, source_target_pairs={{1,0},{0,1},{3,2},{2,3},{5,4},{4,5},{7,6},{6,7},{9,8},{8,9},{11,10... | collective-permute-start | bytes 786440 | tf_op jit(solution)/shard_map/ppermute | solution.py:428
  24.7 8.0 %copy-start = (f32[32,2,4,1,512]{4,3,2,1,0:T(1,128)S(1)}, f32[32,2,4,1,512]{4,3,2,1,0:T(1,128)}, u32[]{:S(2)}) copy-start(f32[32,2,4,1,512]{4,3,2,1,0:T(1,128)} %param.11) | copy-start | bytes 1572868
  24.7 7.4 %collective-permute-start.6 = (f32[32,256]{1,0:T(8,128)S(1)}, f32[32,256]{1,0:T(8,128)S(1)}, u32[]{:S(2)}, u32[]{:S(2)}) collective-permute-start(f32[32,256]{1,0:T(8,128)S(1)} %sum.5.refs_0_), channel_id=1, source_target_pairs={{3,0},{2,1},{1,2},{0,3},{7,4},{6,5},{5,6},{4,7},{11,8},{10,9},{9,1... | collective-permute-start | bytes 98312 | tf_op jit(solution)/shard_map/ppermute | solution.py:421
  32.1 1.5 %copy-start.1 = (f32[2,64,256]{2,1,0:T(8,128)S(1)}, f32[2,64,256]{2,1,0:T(8,128)}, u32[]{:S(2)}) copy-start(f32[2,64,256]{2,1,0:T(8,128)} %noise_ref.1) | copy-start | bytes 393220
  32.1 1.5 %copy-start.2 = (f32[2,256]{1,0:T(2,128)S(1)}, f32[2,256]{1,0:T(2,128)}, u32[]{:S(2)}) copy-start(f32[2,256]{1,0:T(2,128)} %value_ref.1) | copy-start | bytes 6148
  32.1 1.5 %copy-start.3 = (f32[2,256]{1,0:T(2,128)S(1)}, f32[2,256]{1,0:T(2,128)}, u32[]{:S(2)}) copy-start(f32[2,256]{1,0:T(2,128)} %error_ref.1) | copy-start | bytes 6148
  32.2 1.4 %collective-permute-start.7 = (f32[64,256]{1,0:T(8,128)S(1)}, f32[64,256]{1,0:T(8,128)S(1)}, u32[]{:S(2)}, u32[]{:S(2)}) collective-permute-start(f32[64,256]{1,0:T(8,128)S(1)} %gather.1.kept_ref), channel_id=1, source_target_pairs={{0,2},{2,0},{4,6},{6,4},{8,10},{10,8},{12,14},{14,12},{16,18},{18,... | collective-permute-start | bytes 196616 | tf_op jit(solution)/shard_map/ppermute | solution.py:412

commit v22 on v16

--- a/solution.py
+++ b/solution.py
@@ -15,6 +15,7 @@
 
 
 SELECT_FLOPS = 1
+PIECES = 4
 OWN_FLOPS, SUM_FLOPS, GATHER_FLOPS, SOLVE_FLOPS = 1, (7*10**8,7*10**8,1), 10**8, 5*10**8
 
 
@@ -87,16 +88,27 @@
 
 def load_kernel(chunks, *refs):
     count = (len(refs) - 1) // 2
-    sources, packed_ref, held, sems = refs[:count], refs[count], refs[count + 1 : -1], refs[-1]
-    rows = sources[0].shape[0]
-    copies = at_once(sources, (packed_ref.at[:rows], *held), sems)
-    copies[1].wait()
-    copies[2].wait()
+    (present, *others), packed_ref, held, sems = (
+        refs[:count],
+        refs[count],
+        refs[count + 1 : -1],
+        refs[-1],
+    )
+    rows = present.shape[0]
+    piece = rows // PIECES
+    pieces = [pl.ds(k * piece, piece) for k in range(PIECES)]
+    copies = at_once(
+        [*(present.at[p] for p in pieces), *others],
+        [*(packed_ref.at[p] for p in pieces), *held],
+        sems,
+    )
+    copies[PIECES].wait()
+    copies[PIECES + 1].wait()
     spread = held[0][...]
     half = held[1][:chunks, :] * 0.5
     packed_ref[rows : rows + chunks, :] = spread + half
     packed_ref[rows + chunks : rows + 2 * chunks, :] = spread - half
-    for copy in (copies[0], *copies[3:]):
+    for copy in (*copies[:PIECES], *copies[PIECES + 2 :]):
         copy.wait()
 
 
@@ -371,14 +383,17 @@
                 done_ref[pl.ds(start + c, local, stride=planes), :] = result[
                     :, c * LANES : (c + 1) * LANES
                 ]
-        copies.append(
-            pltpu.make_async_copy(
-                done_ref.reshape(local, planes, LANES).at[:, first : first + level, :],
-                out_ref.at[:, first : first + level, :],
-                sems.at[len(copies)],
-            )
-        )
-        copies[-1].start()
+            if f == fields // 2 - 1 or f == fields - 1:
+                count = fields // 2 * chunks
+                out_planes = slice(start + chunks - count, start + chunks)
+                copies.append(
+                    pltpu.make_async_copy(
+                        done_ref.reshape(local, planes, LANES).at[:, out_planes, :],
+                        out_ref.at[:, out_planes, :],
+                        sems.at[len(copies)],
+                    )
+                )
+                copies[-1].start()
     for copy in copies:
         copy.wait()
 
@@ -437,7 +452,7 @@
         out_shape=[shape_of((present.shape[0] + 2 * chunks, LANES))]
         + [shape_of(x.shape, x.dtype) for x in sources[1:]],
         in_specs=[hbm] * len(sources),
-        scratch_shapes=[pltpu.SemaphoreType.DMA((len(sources),))],
+        scratch_shapes=[pltpu.SemaphoreType.DMA((len(sources) - 1 + PIECES,))],
         compiler_params=PARAMS,
         name="load",
     )(*sources)
@@ -525,7 +540,7 @@
         out_specs=hbm,
         scratch_shapes=[
             pltpu.VMEM((members * planes, LANES), F32),
-            pltpu.SemaphoreType.DMA((1 + lagged,)),
+            pltpu.SemaphoreType.DMA((2 * (1 + lagged),)),
         ],
         compiler_params=PARAMS,
         name="combine",

time: 32.6 us -> 32.7 us (level)
  no operation moved by 1% of the time
where the time goes in v22:
time: 32.7 us; the launch traced here: 32.4 us
  starting transfers between devices  18.5 us (57%)
  Pallas kernels  7.32 us (22%)
  waiting for transfers between devices  6.41 us (20%)
    ppermute x5, starting transfers between devices, from_slab(): return lax.ppermute(array, 'slab', [(i, i ^ bit) for i in range(slabs)])  8.39 us
    ppermute x2, starting transfers between devices, from_partners(): lax.ppermute(array, 'mem', [((i + d) % parts, i) for i in range(parts)])  4.56 us
    ppermute x5, waiting for transfers between devices, from_slab(): return lax.ppermute(array, 'slab', [(i, i ^ bit) for i in range(slabs)])  4.51 us
    pallas_call x1, Pallas kernels, shards(): pl.pallas_call(functools.partial(solve_kernel, parts), out_shape=shape_of...  2.93 us
    ppermute x1, starting transfers between devices, shards(): lax.ppermute(lax.optimization_barrier((packed, part))[0], 'slab', up)  2.77 us
    ppermute x1, waiting for transfers between devices, from_other_mem(): lax.ppermute(array, ('slab', 'mem'), [(i ^ 3, i) for i in range(slabs * p...  1.89 us
    ppermute x1, starting transfers between devices, from_other_mem(): lax.ppermute(array, ('slab', 'mem'), [(i ^ 3, i) for i in range(slabs * p...  1.54 us
    pallas_call x1, Pallas kernels, shards(): pl.pallas_call(functools.partial(combine_kernel, parts, fields), out_shap...  1.33 us
  transfers between devices with their start and end apart: 10, of which 6 were waited for; matrix products, arithmetic and copies ran while one was open for 0% of the time, Pallas kernels for 15%

profile of v22, /device:TPU:0, one launch (start us, length us, event | category | flops | bytes accessed | tf_op | source)
XLA Modules:
  0.0 32.4 jit_solution(11023558215042808808)
XLA Ops:
  0.0 1.0 %load.1 = (f32[520,128]{1,0:T(8,128)S(1)}, f32[4,128]{1,0:T(4,128)S(1)}, f32[8,128]{1,0:T(8,128)S(1)}, s32[2,256]{1,0:T(2,128)S(1)}, s32[2,256]{1,0:T(2,128)S(1)}, /*index=5*/s32[2,256]{1,0:T(2,128)S(1)}) custom-call(f32[512,128]{1,0:T(8,128)} %bitcast.7, f32[4,128]{1,0:T(4,128)} %bitcast.9, f32[8,128]{1,0:T(8,128)} %bitcast.8, s32[2,256]{1,0:T(2,128)} %refs_3_.1, ...), custom_call_target="tpu_custom_call" | custom-call | tf_op jit(solution)/shard_map/load/pallas_call | solution.py:450
  1.0 1.3 %collective-permute-start = (f32[520,128]{1,0:T(8,128)S(1)}, f32[520,128]{1,0:T(8,128)S(1)}, u32[]{:S(2)}, u32[]{:S(2)}) collective-permute-start(f32[520,128]{1,0:T(8,128)S(1)} %get-tuple-element.40.packed_ref), channel_id=1, source_target_pairs={{2,0},{4,2},{6,4},{8,6},{10,8},{12,10},{14,12},{16,14},{18,16},{20... | collective-permute-start | bytes 798728 | tf_op jit(solution)/shard_map/ppermute | solution.py:460
  2.3 3.0 %collective-permute-start.5 = (f32[1024,128]{1,0:T(8,128)}, f32[1024,128]{1,0:T(8,128)S(1)}, u32[]{:S(2)}, u32[]{:S(2)}) collective-permute-start(f32[1024,128]{1,0:T(8,128)} %bitcast.5), channel_id=1, source_target_pairs={{1,0},{0,1},{3,2},{2,3},{5,4},{4,5},{7,6},{6,7},{9,8},{8,9},{11,10... | collective-permute-start | bytes 1572872 | tf_op jit(solution)/shard_map/ppermute | solution.py:443
  5.3 0.2 selector.1
  5.5 0.5 %own_row.1 = (f32[128,512]{1,0:T(8,128)S(1)}, f32[128,512]{1,0:T(8,128)S(1)}, f32[32,512]{1,0:T(8,128)S(1)}) custom-call(f32[520,128]{1,0:T(8,128)S(1)} %get-tuple-element.40.packed_ref, f32[4,128]{1,0:T(4,128)S(1)} %get-tuple-element.25.spread_ref, f32[8,128]{1,0:T(8,128)S(1)} %get-tuple-element.26.ratio_ref, ...), custom_call_target="tpu_custom_call" | custom-call | flops 1 | tf_op jit(solution)/shard_map/own_row/pallas_call | solution.py:471
  6.0 2.8 %collective-permute-start.8 = (f32[520,128]{1,0:T(8,128)S(1)}, f32[520,128]{1,0:T(8,128)S(1)}, u32[]{:S(2)}, u32[]{:S(2)}) collective-permute-start(f32[520,128]{1,0:T(8,128)S(1)} %get-tuple-element.40.packed_ref), channel_id=1, source_target_pairs={{0,2},{2,4},{4,6},{6,8},{8,10},{10,12},{12,14},{14,16},{16,18},{18... | collective-permute-start | bytes 798728 | tf_op jit(solution)/shard_map/ppermute | solution.py:478
  8.8 0.5 %observe.1 = (f32[32,256]{1,0:T(8,128)S(1)}, f32[32,256]{1,0:T(8,128)S(1)}, f32[128,512]{1,0:T(8,128)S(1)}) custom-call(f32[520,128]{1,0:T(8,128)S(1)} %get-tuple-element.40.packed_ref, f32[520,128]{1,0:T(8,128)S(1)} %collective-permute-done.next_ref, f32[128,512]{1,0:T(8,128)S(1)} %get-tuple-element.32.part_ref, ...), custom_call_target="tpu_custom_call" | custom-call | tf_op jit(solution)/shard_map/observe/pallas_call | solution.py:479
  9.3 1.6 %collective-permute-start.1 = (f32[32,256]{1,0:T(8,128)S(1)}, f32[32,256]{1,0:T(8,128)S(1)}, u32[]{:S(2)}, u32[]{:S(2)}) collective-permute-start(f32[32,256]{1,0:T(8,128)S(1)} %get-tuple-element.36), channel_id=1, source_target_pairs={{0,2},{2,0},{4,6},{6,4},{8,10},{10,8},{12,14},{14,12},{16,18},{18,... | collective-permute-start | bytes 98312 | tf_op jit(solution)/shard_map/ppermute | solution.py:427
  11.0 0.9 %collective-permute-done.1 = f32[32,256]{1,0:T(8,128)S(1)} collective-permute-done((f32[32,256]{1,0:T(8,128)S(1)}, f32[32,256]{1,0:T(8,128)S(1)}, u32[]{:S(2)}, u32[]{:S(2)}) %collective-permute-start.1) | collective-permute-done | bytes 32800 | tf_op jit(solution)/shard_map/ppermute | solution.py:427
  11.8 2.5 %collective-permute-start.2 = (f32[32,256]{1,0:T(8,128)S(1)}, f32[32,256]{1,0:T(8,128)S(1)}, u32[]{:S(2)}, u32[]{:S(2)}) collective-permute-start(f32[32,256]{1,0:T(8,128)S(1)} %add.3.terms_ref), channel_id=1, source_target_pairs={{0,18},{2,16},{4,22},{6,20},{8,26},{10,24},{12,30},{14,28},{16,2},... | collective-permute-start | bytes 98312 | tf_op jit(solution)/shard_map/ppermute | solution.py:427
  14.4 1.7 %collective-permute-done.2.other_ref = f32[32,256]{1,0:T(8,128)S(1)} collective-permute-done((f32[32,256]{1,0:T(8,128)S(1)}, f32[32,256]{1,0:T(8,128)S(1)}, u32[]{:S(2)}, u32[]{:S(2)}) %collective-permute-start.2) | collective-permute-done | bytes 32800 | tf_op jit(solution)/shard_map/ppermute | solution.py:427
  16.1 1.5 %collective-permute-start.3 = (f32[32,256]{1,0:T(8,128)S(1)}, f32[32,256]{1,0:T(8,128)S(1)}, u32[]{:S(2)}, u32[]{:S(2)}) collective-permute-start(f32[32,256]{1,0:T(8,128)S(1)} %sum.3.terms_ref), channel_id=1, source_target_pairs={{0,10},{2,8},{4,14},{6,12},{8,2},{10,0},{12,6},{14,4},{16,26},{18,... | collective-permute-start | bytes 98312 | tf_op jit(solution)/shard_map/ppermute | solution.py:427
  17.6 0.1 complete.1.refs_0_
  17.7 1.6 %collective-permute-start.9 = (f32[128,512]{1,0:T(8,128)S(1)}, f32[128,512]{1,0:T(8,128)S(1)}, u32[]{:S(2)}, u32[]{:S(2)}) collective-permute-start(f32[128,512]{1,0:T(8,128)S(1)} %complete.1.refs_0_), channel_id=1, source_target_pairs={{1,0},{0,1},{3,2},{2,3},{5,4},{4,5},{7,6},{6,7},{9,8},{8,9},{11,10... | collective-permute-start | bytes 786440 | tf_op jit(solution)/shard_map/ppermute | solution.py:443
  19.3 0.1 collective-permute-done.3.other_ref
  19.4 2.2 %collective-permute-start.4 = (f32[32,256]{1,0:T(8,128)S(1)}, f32[32,256]{1,0:T(8,128)S(1)}, u32[]{:S(2)}, u32[]{:S(2)}) collective-permute-start(f32[32,256]{1,0:T(8,128)S(1)} %sum.4.terms_ref), channel_id=1, source_target_pairs={{0,6},{2,4},{4,2},{6,0},{8,14},{10,12},{12,10},{14,8},{16,22},{18,... | collective-permute-start | bytes 98312 | tf_op jit(solution)/shard_map/ppermute | solution.py:427
  21.6 1.6 %collective-permute-done.4.other_ref = f32[32,256]{1,0:T(8,128)S(1)} collective-permute-done((f32[32,256]{1,0:T(8,128)S(1)}, f32[32,256]{1,0:T(8,128)S(1)}, u32[]{:S(2)}, u32[]{:S(2)}) %collective-permute-start.4) | collective-permute-done | bytes 32800 | tf_op jit(solution)/shard_map/ppermute | solution.py:427
  23.2 1.5 %collective-permute-start.6 = (f32[32,256]{1,0:T(8,128)S(1)}, f32[32,256]{1,0:T(8,128)S(1)}, u32[]{:S(2)}, u32[]{:S(2)}) collective-permute-start(f32[32,256]{1,0:T(8,128)S(1)} %sum.5.refs_0_), channel_id=1, source_target_pairs={{3,0},{2,1},{1,2},{0,3},{7,4},{6,5},{5,6},{4,7},{11,8},{10,9},{9,1... | collective-permute-start | bytes 98312 | tf_op jit(solution)/shard_map/ppermute | solution.py:436
  24.8 1.9 %collective-permute-done.6.refs_1_ = f32[32,256]{1,0:T(8,128)S(1)} collective-permute-done((f32[32,256]{1,0:T(8,128)S(1)}, f32[32,256]{1,0:T(8,128)S(1)}, u32[]{:S(2)}, u32[]{:S(2)}) %collective-permute-start.6) | collective-permute-done | bytes 32800 | tf_op jit(solution)/shard_map/ppermute | solution.py:436
  26.7 0.5 %collective-permute-start.7 = (f32[64,256]{1,0:T(8,128)S(1)}, f32[64,256]{1,0:T(8,128)S(1)}, u32[]{:S(2)}, u32[]{:S(2)}) collective-permute-start(f32[64,256]{1,0:T(8,128)S(1)} %gather.1.kept_ref), channel_id=1, source_target_pairs={{0,2},{2,0},{4,6},{6,4},{8,10},{10,8},{12,14},{14,12},{16,18},{18,... | collective-permute-start | bytes 196616 | tf_op jit(solution)/shard_map/ppermute | solution.py:427
  27.2 0.7 %prepare.1 = (bf16[64,4096]{1,0:T(8,128)(2,1)S(1)}, bf16[64,4096]{1,0:T(8,128)(2,1)S(1)}) custom-call(f32[1024,128]{1,0:T(8,128)S(1)} %bitcast.6, f32[1024,128]{1,0:T(8,128)S(1)} %collective-permute-done.5.refs_0_.refs_1_), custom_call_target="tpu_custom_call" | custom-call | tf_op jit(solution)/shard_map/prepare/pallas_call | solution.py:531
  27.9 0.2 collective-permute-done.7.received_ref
  28.1 2.9 %solve.1.mine_ref = f32[32,64]{1,0:T(8,128)S(1)} custom-call(f32[2,256]{1,0:T(2,128)S(1)} %copy-done.2, f32[2,256]{1,0:T(2,128)S(1)} %copy-done.3, f32[2,64,256]{2,1,0:T(8,128)S(1)} %copy-done.1, f32[64,256]{1,0:T(8,128)S(1)} %gather.1.kept_ref, f32[64,256]{1,0:T(8,128)S(1)} %collective-permute-done.7.received_ref), custom_call_target="tpu_custom_call" | custom-call | flops 500000000 | tf_op jit(solution)/shard_map/solve/pallas_call | solution.py:524
  31.1 1.3 %combine.1 = f32[32,48,128]{2,1,0:T(8,128)} custom-call(f32[32,64]{1,0:T(8,128)S(1)} %solve.1.mine_ref, f32[128,512]{1,0:T(8,128)S(1)} %complete.1.refs_0_, f32[128,512]{1,0:T(8,128)S(1)} %collective-permute-done.9.refs_1_, bf16[64,4096]{1,0:T(8,128)(2,1)S(1)} %get-tuple-element.41.refs_2_, bf16[64,4096]{1,0:T(8,128)(2,1)S(1)} %get-tuple-element.42.refs_3_), custom_call_target="tpu_custom_call" | custom-call | tf_op jit(solution)/shard_map/combine/pallas_call | solution.py:537
  (17 shorter events, 0.1 us)
Async XLA Ops:
  1.0 7.8 %collective-permute-start = (f32[520,128]{1,0:T(8,128)S(1)}, f32[520,128]{1,0:T(8,128)S(1)}, u32[]{:S(2)}, u32[]{:S(2)}) collective-permute-start(f32[520,128]{1,0:T(8,128)S(1)} %get-tuple-element.40.packed_ref), channel_id=1, source_target_pairs={{2,0},{4,2},{6,4},{8,6},{10,8},{12,10},{14,12},{16,14},{18,16},{20... | collective-permute-start | bytes 798728 | tf_op jit(solution)/shard_map/ppermute | solution.py:460
  2.3 20.9 %collective-permute-start.5 = (f32[1024,128]{1,0:T(8,128)}, f32[1024,128]{1,0:T(8,128)S(1)}, u32[]{:S(2)}, u32[]{:S(2)}) collective-permute-start(f32[1024,128]{1,0:T(8,128)} %bitcast.5), channel_id=1, source_target_pairs={{1,0},{0,1},{3,2},{2,3},{5,4},{4,5},{7,6},{6,7},{9,8},{8,9},{11,10... | collective-permute-start | bytes 1572872 | tf_op jit(solution)/shard_map/ppermute | solution.py:443
  6.0 11.6 %collective-permute-start.8 = (f32[520,128]{1,0:T(8,128)S(1)}, f32[520,128]{1,0:T(8,128)S(1)}, u32[]{:S(2)}, u32[]{:S(2)}) collective-permute-start(f32[520,128]{1,0:T(8,128)S(1)} %get-tuple-element.40.packed_ref), channel_id=1, source_target_pairs={{0,2},{2,4},{4,6},{6,8},{8,10},{10,12},{12,14},{14,16},{16,18},{18... | collective-permute-start | bytes 798728 | tf_op jit(solution)/shard_map/ppermute | solution.py:478
  9.3 2.5 %collective-permute-start.1 = (f32[32,256]{1,0:T(8,128)S(1)}, f32[32,256]{1,0:T(8,128)S(1)}, u32[]{:S(2)}, u32[]{:S(2)}) collective-permute-start(f32[32,256]{1,0:T(8,128)S(1)} %get-tuple-element.36), channel_id=1, source_target_pairs={{0,2},{2,0},{4,6},{6,4},{8,10},{10,8},{12,14},{14,12},{16,18},{18,... | collective-permute-start | bytes 98312 | tf_op jit(solution)/shard_map/ppermute | solution.py:427
  11.8 4.2 %collective-permute-start.2 = (f32[32,256]{1,0:T(8,128)S(1)}, f32[32,256]{1,0:T(8,128)S(1)}, u32[]{:S(2)}, u32[]{:S(2)}) collective-permute-start(f32[32,256]{1,0:T(8,128)S(1)} %add.3.terms_ref), channel_id=1, source_target_pairs={{0,18},{2,16},{4,22},{6,20},{8,26},{10,24},{12,30},{14,28},{16,2},... | collective-permute-start | bytes 98312 | tf_op jit(solution)/shard_map/ppermute | solution.py:427
  16.1 3.3 %collective-permute-start.3 = (f32[32,256]{1,0:T(8,128)S(1)}, f32[32,256]{1,0:T(8,128)S(1)}, u32[]{:S(2)}, u32[]{:S(2)}) collective-permute-start(f32[32,256]{1,0:T(8,128)S(1)} %sum.3.terms_ref), channel_id=1, source_target_pairs={{0,10},{2,8},{4,14},{6,12},{8,2},{10,0},{12,6},{14,4},{16,26},{18,... | collective-permute-start | bytes 98312 | tf_op jit(solution)/shard_map/ppermute | solution.py:427
  17.7 13.3 %collective-permute-start.9 = (f32[128,512]{1,0:T(8,128)S(1)}, f32[128,512]{1,0:T(8,128)S(1)}, u32[]{:S(2)}, u32[]{:S(2)}) collective-permute-start(f32[128,512]{1,0:T(8,128)S(1)} %complete.1.refs_0_), channel_id=1, source_target_pairs={{1,0},{0,1},{3,2},{2,3},{5,4},{4,5},{7,6},{6,7},{9,8},{8,9},{11,10... | collective-permute-start | bytes 786440 | tf_op jit(solution)/shard_map/ppermute | solution.py:443
  19.4 7.8 %copy-start = (f32[32,2,4,1,512]{4,3,2,1,0:T(1,128)S(1)}, f32[32,2,4,1,512]{4,3,2,1,0:T(1,128)}, u32[]{:S(2)}) copy-start(f32[32,2,4,1,512]{4,3,2,1,0:T(1,128)} %param.11) | copy-start | bytes 1572868
  19.4 3.8 %collective-permute-start.4 = (f32[32,256]{1,0:T(8,128)S(1)}, f32[32,256]{1,0:T(8,128)S(1)}, u32[]{:S(2)}, u32[]{:S(2)}) collective-permute-start(f32[32,256]{1,0:T(8,128)S(1)} %sum.4.terms_ref), channel_id=1, source_target_pairs={{0,6},{2,4},{4,2},{6,0},{8,14},{10,12},{12,10},{14,8},{16,22},{18,... | collective-permute-start | bytes 98312 | tf_op jit(solution)/shard_map/ppermute | solution.py:427
  23.2 3.4 %collective-permute-start.6 = (f32[32,256]{1,0:T(8,128)S(1)}, f32[32,256]{1,0:T(8,128)S(1)}, u32[]{:S(2)}, u32[]{:S(2)}) collective-permute-start(f32[32,256]{1,0:T(8,128)S(1)} %sum.5.refs_0_), channel_id=1, source_target_pairs={{3,0},{2,1},{1,2},{0,3},{7,4},{6,5},{5,6},{4,7},{11,8},{10,9},{9,1... | collective-permute-start | bytes 98312 | tf_op jit(solution)/shard_map/ppermute | solution.py:436
  26.7 1.4 %copy-start.1 = (f32[2,64,256]{2,1,0:T(8,128)S(1)}, f32[2,64,256]{2,1,0:T(8,128)}, u32[]{:S(2)}) copy-start(f32[2,64,256]{2,1,0:T(8,128)} %noise_ref.1) | copy-start | bytes 393220
  26.7 1.4 %copy-start.2 = (f32[2,256]{1,0:T(2,128)S(1)}, f32[2,256]{1,0:T(2,128)}, u32[]{:S(2)}) copy-start(f32[2,256]{1,0:T(2,128)} %value_ref.1) | copy-start | bytes 6148
  26.7 1.4 %copy-start.3 = (f32[2,256]{1,0:T(2,128)S(1)}, f32[2,256]{1,0:T(2,128)}, u32[]{:S(2)}) copy-start(f32[2,256]{1,0:T(2,128)} %error_ref.1) | copy-start | bytes 6148
  26.7 1.4 %collective-permute-start.7 = (f32[64,256]{1,0:T(8,128)S(1)}, f32[64,256]{1,0:T(8,128)S(1)}, u32[]{:S(2)}, u32[]{:S(2)}) collective-permute-start(f32[64,256]{1,0:T(8,128)S(1)} %gather.1.kept_ref), channel_id=1, source_target_pairs={{0,2},{2,0},{4,6},{6,4},{8,10},{10,8},{12,14},{14,12},{16,18},{18,... | collective-permute-start | bytes 196616 | tf_op jit(solution)/shard_map/ppermute | solution.py:427

commit v23 on v16

--- a/solution.py
+++ b/solution.py
@@ -116,14 +116,17 @@
 
 def selector_kernel(row_ref, col_ref, field_ref, taps_ref, kinds_ref):
     batches, count = row_ref.shape
-    shape = taps_ref.shape
+    width, total = taps_ref.shape[0] // 2, taps_ref.shape[1]
     flat = lambda ref: jnp.concatenate([ref[b : b + 1, :] for b in range(batches)], axis=1)
-    rows, cols, kinds = flat(row_ref), flat(col_ref), flat(field_ref)
+    rows, cols = flat(row_ref), flat(col_ref)
+    kinds_ref[...] = flat(field_ref)
+    at = lax.broadcasted_iota(jnp.int32, (width, total), 0).astype(F32) * 0.25
+    taps = jnp.maximum(0.5 - jnp.abs(at - cols.astype(F32) * 0.25), 0.0)
     own_row = lax.axis_index("slab")
-    for k, row in enumerate((own_row, own_row + 1)):
-        kinds_ref[k : k + 1, :] = jnp.where(rows == row, kinds, -1)
-    at = lax.broadcasted_iota(jnp.int32, shape, 0).astype(F32) * 0.25
-    taps_ref[...] = jnp.maximum(0.5 - jnp.abs(at - cols.astype(F32) * 0.25), 0.0).astype(BF16)
+    for k in range(2):
+        taps_ref[k * width : (k + 1) * width, :] = jnp.where(
+            rows == own_row + k, taps, 0.0
+        ).astype(BF16)
 
 
 def own_row_kernel(
@@ -153,7 +156,7 @@
         - along_columns * (right - left) * 0.5
     )
     part_ref[...] = part
-    picked = picked_values(part, taps_ref[...])
+    picked = picked_values(part, taps_ref[:width, :])
     observed = jnp.zeros(obs_ref.shape, F32)
     for f in range(fields):
         observed += jnp.where(
@@ -185,14 +188,13 @@
     partial_ref[...] = part_ref[...] + taken
     picked = sum(
         jnp.dot(part, taps_ref[...], preferred_element_type=F32)
-        for part in reversed(split_two(jnp.concatenate([taken, given], axis=0)))
+        for part in reversed(split_two(jnp.concatenate([taken, given], axis=1)))
     )
     observed = part_obs_ref[...]
-    for side in range(2):
-        kinds = kinds_ref[side : side + 1, :]
-        for f in range(fields):
-            start = (side * fields + f) * members
-            observed += jnp.where(kinds == f, picked[start : start + members], 0.0)
+    for f in range(fields):
+        observed += jnp.where(
+            kinds_ref[...] == f, picked[f * members : (f + 1) * members], 0.0
+        )
     first_here = keeps_first(parts)
     half = observed.shape[1] // 2
     first, second = observed[:, :half], observed[:, half:]
@@ -448,7 +450,7 @@
     )
     taps, kinds = pl.pallas_call(
         selector_kernel,
-        out_shape=(shape_of((width, total), BF16), shape_of((2, total), jnp.int32)),
+        out_shape=(shape_of((2 * width, total), BF16), shape_of((1, total), jnp.int32)),
         compiler_params=PARAMS,
         cost_estimate=estimate(SELECT_FLOPS),
         name="selector",

time: 32.6 us -> 32.9 us (level)
  Pallas kernels: 7.34 us -> 7.72 us
  transfers between devices with their start and end apart: 10 -> 10, of which waited for: 6 -> 6; matrix products, arithmetic and copies ran while one was open for 0% -> 0% of each run, Pallas kernels for 15% -> 16%
where the time goes in v23:
time: 32.9 us; the launch traced here: 32.8 us
  starting transfers between devices  18.4 us (56%)
  Pallas kernels  7.72 us (23%)
  waiting for transfers between devices  6.53 us (20%)
    ppermute x5, starting transfers between devices, from_slab(): return lax.ppermute(array, 'slab', [(i, i ^ bit) for i in range(slabs)])  8.43 us
    ppermute x2, starting transfers between devices, from_partners(): lax.ppermute(array, 'mem', [((i + d) % parts, i) for i in range(parts)])  4.56 us
    ppermute x5, waiting for transfers between devices, from_slab(): return lax.ppermute(array, 'slab', [(i, i ^ bit) for i in range(slabs)])  4.5 us
    pallas_call x1, Pallas kernels, shards(): pl.pallas_call(functools.partial(solve_kernel, parts), out_shape=shape_of...  3.13 us
    ppermute x1, starting transfers between devices, shards(): lax.ppermute(lax.optimization_barrier((packed, part))[0], 'slab', up)  2.77 us
    ppermute x1, waiting for transfers between devices, from_other_mem(): lax.ppermute(array, ('slab', 'mem'), [(i ^ 3, i) for i in range(slabs * p...  2.01 us
    ppermute x1, starting transfers between devices, from_other_mem(): lax.ppermute(array, ('slab', 'mem'), [(i ^ 3, i) for i in range(slabs * p...  1.39 us
    pallas_call x1, Pallas kernels, shards(): pl.pallas_call(functools.partial(combine_kernel, parts, fields), out_shap...  1.36 us
  transfers between devices with their start and end apart: 10, of which 6 were waited for; matrix products, arithmetic and copies ran while one was open for 0% of the time, Pallas kernels for 16%

profile of v23, /device:TPU:0, one launch (start us, length us, event | category | flops | bytes accessed | tf_op | source)
XLA Modules:
  0.0 32.8 jit_solution(7989284806360557496)
XLA Ops:
  0.0 1.0 %load.1 = (f32[520,128]{1,0:T(8,128)S(1)}, f32[4,128]{1,0:T(4,128)S(1)}, f32[8,128]{1,0:T(8,128)S(1)}, s32[2,256]{1,0:T(2,128)S(1)}, s32[2,256]{1,0:T(2,128)S(1)}, /*index=5*/s32[2,256]{1,0:T(2,128)S(1)}) custom-call(f32[512,128]{1,0:T(8,128)} %bitcast.7, f32[4,128]{1,0:T(4,128)} %bitcast.9, f32[8,128]{1,0:T(8,128)} %bitcast.8, s32[2,256]{1,0:T(2,128)} %refs_3_.1, ...), custom_call_target="tpu_custom_call" | custom-call | tf_op jit(solution)/shard_map/load/pallas_call | solution.py:437
  1.0 1.3 %collective-permute-start = (f32[520,128]{1,0:T(8,128)S(1)}, f32[520,128]{1,0:T(8,128)S(1)}, u32[]{:S(2)}, u32[]{:S(2)}) collective-permute-start(f32[520,128]{1,0:T(8,128)S(1)} %get-tuple-element.40.packed_ref), channel_id=1, source_target_pairs={{2,0},{4,2},{6,4},{8,6},{10,8},{12,10},{14,12},{16,14},{18,16},{20... | collective-permute-start | bytes 798728 | tf_op jit(solution)/shard_map/ppermute | solution.py:447
  2.3 3.0 %collective-permute-start.5 = (f32[1024,128]{1,0:T(8,128)}, f32[1024,128]{1,0:T(8,128)S(1)}, u32[]{:S(2)}, u32[]{:S(2)}) collective-permute-start(f32[1024,128]{1,0:T(8,128)} %bitcast.5), channel_id=1, source_target_pairs={{1,0},{0,1},{3,2},{2,3},{5,4},{4,5},{7,6},{6,7},{9,8},{8,9},{11,10... | collective-permute-start | bytes 1572872 | tf_op jit(solution)/shard_map/ppermute | solution.py:430
  5.3 0.3 selector.1
  5.6 0.5 %own_row.1 = (f32[128,512]{1,0:T(8,128)S(1)}, f32[128,512]{1,0:T(8,128)S(1)}, f32[32,512]{1,0:T(8,128)S(1)}) custom-call(f32[520,128]{1,0:T(8,128)S(1)} %get-tuple-element.40.packed_ref, f32[4,128]{1,0:T(4,128)S(1)} %get-tuple-element.25.spread_ref, f32[8,128]{1,0:T(8,128)S(1)} %get-tuple-element.26.ratio_ref, ...), custom_call_target="tpu_custom_call" | custom-call | flops 1 | tf_op jit(solution)/shard_map/own_row/pallas_call | solution.py:458
  6.2 2.8 %collective-permute-start.8 = (f32[520,128]{1,0:T(8,128)S(1)}, f32[520,128]{1,0:T(8,128)S(1)}, u32[]{:S(2)}, u32[]{:S(2)}) collective-permute-start(f32[520,128]{1,0:T(8,128)S(1)} %get-tuple-element.40.packed_ref), channel_id=1, source_target_pairs={{0,2},{2,4},{4,6},{6,8},{8,10},{10,12},{12,14},{14,16},{16,18},{18... | collective-permute-start | bytes 798728 | tf_op jit(solution)/shard_map/ppermute | solution.py:465
  9.0 0.5 %observe.1 = (f32[32,256]{1,0:T(8,128)S(1)}, f32[32,256]{1,0:T(8,128)S(1)}, f32[128,512]{1,0:T(8,128)S(1)}) custom-call(f32[520,128]{1,0:T(8,128)S(1)} %get-tuple-element.40.packed_ref, f32[520,128]{1,0:T(8,128)S(1)} %collective-permute-done.next_ref, f32[128,512]{1,0:T(8,128)S(1)} %get-tuple-element.32.part_ref, ...), custom_call_target="tpu_custom_call" | custom-call | tf_op jit(solution)/shard_map/observe/pallas_call | solution.py:466
  9.5 1.5 %collective-permute-start.1 = (f32[32,256]{1,0:T(8,128)S(1)}, f32[32,256]{1,0:T(8,128)S(1)}, u32[]{:S(2)}, u32[]{:S(2)}) collective-permute-start(f32[32,256]{1,0:T(8,128)S(1)} %get-tuple-element.36), channel_id=1, source_target_pairs={{0,2},{2,0},{4,6},{6,4},{8,10},{10,8},{12,14},{14,12},{16,18},{18,... | collective-permute-start | bytes 98312 | tf_op jit(solution)/shard_map/ppermute | solution.py:414
  11.0 0.9 %collective-permute-done.1 = f32[32,256]{1,0:T(8,128)S(1)} collective-permute-done((f32[32,256]{1,0:T(8,128)S(1)}, f32[32,256]{1,0:T(8,128)S(1)}, u32[]{:S(2)}, u32[]{:S(2)}) %collective-permute-start.1) | collective-permute-done | bytes 32800 | tf_op jit(solution)/shard_map/ppermute | solution.py:414
  11.9 2.5 %collective-permute-start.2 = (f32[32,256]{1,0:T(8,128)S(1)}, f32[32,256]{1,0:T(8,128)S(1)}, u32[]{:S(2)}, u32[]{:S(2)}) collective-permute-start(f32[32,256]{1,0:T(8,128)S(1)} %add.3.terms_ref), channel_id=1, source_target_pairs={{0,18},{2,16},{4,22},{6,20},{8,26},{10,24},{12,30},{14,28},{16,2},... | collective-permute-start | bytes 98312 | tf_op jit(solution)/shard_map/ppermute | solution.py:414
  14.4 1.7 %collective-permute-done.2.other_ref = f32[32,256]{1,0:T(8,128)S(1)} collective-permute-done((f32[32,256]{1,0:T(8,128)S(1)}, f32[32,256]{1,0:T(8,128)S(1)}, u32[]{:S(2)}, u32[]{:S(2)}) %collective-permute-start.2) | collective-permute-done | bytes 32800 | tf_op jit(solution)/shard_map/ppermute | solution.py:414
  16.1 1.5 %collective-permute-start.3 = (f32[32,256]{1,0:T(8,128)S(1)}, f32[32,256]{1,0:T(8,128)S(1)}, u32[]{:S(2)}, u32[]{:S(2)}) collective-permute-start(f32[32,256]{1,0:T(8,128)S(1)} %sum.3.terms_ref), channel_id=1, source_target_pairs={{0,10},{2,8},{4,14},{6,12},{8,2},{10,0},{12,6},{14,4},{16,26},{18,... | collective-permute-start | bytes 98312 | tf_op jit(solution)/shard_map/ppermute | solution.py:414
  17.7 0.1 complete.1.refs_0_
  17.8 1.6 %collective-permute-start.9 = (f32[128,512]{1,0:T(8,128)S(1)}, f32[128,512]{1,0:T(8,128)S(1)}, u32[]{:S(2)}, u32[]{:S(2)}) collective-permute-start(f32[128,512]{1,0:T(8,128)S(1)} %complete.1.refs_0_), channel_id=1, source_target_pairs={{1,0},{0,1},{3,2},{2,3},{5,4},{4,5},{7,6},{6,7},{9,8},{8,9},{11,10... | collective-permute-start | bytes 786440 | tf_op jit(solution)/shard_map/ppermute | solution.py:430
  19.3 0.2 collective-permute-done.3.other_ref
  19.5 2.3 %collective-permute-start.4 = (f32[32,256]{1,0:T(8,128)S(1)}, f32[32,256]{1,0:T(8,128)S(1)}, u32[]{:S(2)}, u32[]{:S(2)}) collective-permute-start(f32[32,256]{1,0:T(8,128)S(1)} %sum.4.terms_ref), channel_id=1, source_target_pairs={{0,6},{2,4},{4,2},{6,0},{8,14},{10,12},{12,10},{14,8},{16,22},{18,... | collective-permute-start | bytes 98312 | tf_op jit(solution)/shard_map/ppermute | solution.py:414
  21.8 1.6 %collective-permute-done.4.other_ref = f32[32,256]{1,0:T(8,128)S(1)} collective-permute-done((f32[32,256]{1,0:T(8,128)S(1)}, f32[32,256]{1,0:T(8,128)S(1)}, u32[]{:S(2)}, u32[]{:S(2)}) %collective-permute-start.4) | collective-permute-done | bytes 32800 | tf_op jit(solution)/shard_map/ppermute | solution.py:414
  23.4 1.4 %collective-permute-start.6 = (f32[32,256]{1,0:T(8,128)S(1)}, f32[32,256]{1,0:T(8,128)S(1)}, u32[]{:S(2)}, u32[]{:S(2)}) collective-permute-start(f32[32,256]{1,0:T(8,128)S(1)} %sum.5.refs_0_), channel_id=1, source_target_pairs={{3,0},{2,1},{1,2},{0,3},{7,4},{6,5},{5,6},{4,7},{11,8},{10,9},{9,1... | collective-permute-start | bytes 98312 | tf_op jit(solution)/shard_map/ppermute | solution.py:423
  24.8 2.0 %collective-permute-done.6.refs_1_ = f32[32,256]{1,0:T(8,128)S(1)} collective-permute-done((f32[32,256]{1,0:T(8,128)S(1)}, f32[32,256]{1,0:T(8,128)S(1)}, u32[]{:S(2)}, u32[]{:S(2)}) %collective-permute-start.6) | collective-permute-done | bytes 32800 | tf_op jit(solution)/shard_map/ppermute | solution.py:423
  26.9 0.5 %collective-permute-start.7 = (f32[64,256]{1,0:T(8,128)S(1)}, f32[64,256]{1,0:T(8,128)S(1)}, u32[]{:S(2)}, u32[]{:S(2)}) collective-permute-start(f32[64,256]{1,0:T(8,128)S(1)} %gather.1.kept_ref), channel_id=1, source_target_pairs={{0,2},{2,0},{4,6},{6,4},{8,10},{10,8},{12,14},{14,12},{16,18},{18,... | collective-permute-start | bytes 196616 | tf_op jit(solution)/shard_map/ppermute | solution.py:414
  27.4 0.7 %prepare.1 = (bf16[64,4096]{1,0:T(8,128)(2,1)S(1)}, bf16[64,4096]{1,0:T(8,128)(2,1)S(1)}) custom-call(f32[1024,128]{1,0:T(8,128)S(1)} %bitcast.6, f32[1024,128]{1,0:T(8,128)S(1)} %collective-permute-done.5.refs_0_.refs_1_), custom_call_target="tpu_custom_call" | custom-call | tf_op jit(solution)/shard_map/prepare/pallas_call | solution.py:518
  28.1 0.2 collective-permute-done.7.received_ref
  28.3 3.1 %solve.1.mine_ref = f32[32,64]{1,0:T(8,128)S(1)} custom-call(f32[2,256]{1,0:T(2,128)S(1)} %copy-done.2, f32[2,256]{1,0:T(2,128)S(1)} %copy-done.3, f32[2,64,256]{2,1,0:T(8,128)S(1)} %copy-done.1, f32[64,256]{1,0:T(8,128)S(1)} %gather.1.kept_ref, f32[64,256]{1,0:T(8,128)S(1)} %collective-permute-done.7.received_ref), custom_call_target="tpu_custom_call" | custom-call | flops 500000000 | tf_op jit(solution)/shard_map/solve/pallas_call | solution.py:511
  31.5 1.4 %combine.1 = f32[32,48,128]{2,1,0:T(8,128)} custom-call(f32[32,64]{1,0:T(8,128)S(1)} %solve.1.mine_ref, f32[128,512]{1,0:T(8,128)S(1)} %complete.1.refs_0_, f32[128,512]{1,0:T(8,128)S(1)} %collective-permute-done.9.refs_1_, bf16[64,4096]{1,0:T(8,128)(2,1)S(1)} %get-tuple-element.41.refs_2_, bf16[64,4096]{1,0:T(8,128)(2,1)S(1)} %get-tuple-element.42.refs_3_), custom_call_target="tpu_custom_call" | custom-call | tf_op jit(solution)/shard_map/combine/pallas_call | solution.py:524
  (17 shorter events, 0.1 us)
Async XLA Ops:
  1.0 7.9 %collective-permute-start = (f32[520,128]{1,0:T(8,128)S(1)}, f32[520,128]{1,0:T(8,128)S(1)}, u32[]{:S(2)}, u32[]{:S(2)}) collective-permute-start(f32[520,128]{1,0:T(8,128)S(1)} %get-tuple-element.40.packed_ref), channel_id=1, source_target_pairs={{2,0},{4,2},{6,4},{8,6},{10,8},{12,10},{14,12},{16,14},{18,16},{20... | collective-permute-start | bytes 798728 | tf_op jit(solution)/shard_map/ppermute | solution.py:447
  2.3 21.1 %collective-permute-start.5 = (f32[1024,128]{1,0:T(8,128)}, f32[1024,128]{1,0:T(8,128)S(1)}, u32[]{:S(2)}, u32[]{:S(2)}) collective-permute-start(f32[1024,128]{1,0:T(8,128)} %bitcast.5), channel_id=1, source_target_pairs={{1,0},{0,1},{3,2},{2,3},{5,4},{4,5},{7,6},{6,7},{9,8},{8,9},{11,10... | collective-permute-start | bytes 1572872 | tf_op jit(solution)/shard_map/ppermute | solution.py:430
  6.2 11.5 %collective-permute-start.8 = (f32[520,128]{1,0:T(8,128)S(1)}, f32[520,128]{1,0:T(8,128)S(1)}, u32[]{:S(2)}, u32[]{:S(2)}) collective-permute-start(f32[520,128]{1,0:T(8,128)S(1)} %get-tuple-element.40.packed_ref), channel_id=1, source_target_pairs={{0,2},{2,4},{4,6},{6,8},{8,10},{10,12},{12,14},{14,16},{16,18},{18... | collective-permute-start | bytes 798728 | tf_op jit(solution)/shard_map/ppermute | solution.py:465
  9.5 2.4 %collective-permute-start.1 = (f32[32,256]{1,0:T(8,128)S(1)}, f32[32,256]{1,0:T(8,128)S(1)}, u32[]{:S(2)}, u32[]{:S(2)}) collective-permute-start(f32[32,256]{1,0:T(8,128)S(1)} %get-tuple-element.36), channel_id=1, source_target_pairs={{0,2},{2,0},{4,6},{6,4},{8,10},{10,8},{12,14},{14,12},{16,18},{18,... | collective-permute-start | bytes 98312 | tf_op jit(solution)/shard_map/ppermute | solution.py:414
  11.9 4.2 %collective-permute-start.2 = (f32[32,256]{1,0:T(8,128)S(1)}, f32[32,256]{1,0:T(8,128)S(1)}, u32[]{:S(2)}, u32[]{:S(2)}) collective-permute-start(f32[32,256]{1,0:T(8,128)S(1)} %add.3.terms_ref), channel_id=1, source_target_pairs={{0,18},{2,16},{4,22},{6,20},{8,26},{10,24},{12,30},{14,28},{16,2},... | collective-permute-start | bytes 98312 | tf_op jit(solution)/shard_map/ppermute | solution.py:414
  16.1 3.3 %collective-permute-start.3 = (f32[32,256]{1,0:T(8,128)S(1)}, f32[32,256]{1,0:T(8,128)S(1)}, u32[]{:S(2)}, u32[]{:S(2)}) collective-permute-start(f32[32,256]{1,0:T(8,128)S(1)} %sum.3.terms_ref), channel_id=1, source_target_pairs={{0,10},{2,8},{4,14},{6,12},{8,2},{10,0},{12,6},{14,4},{16,26},{18,... | collective-permute-start | bytes 98312 | tf_op jit(solution)/shard_map/ppermute | solution.py:414
  17.8 13.7 %collective-permute-start.9 = (f32[128,512]{1,0:T(8,128)S(1)}, f32[128,512]{1,0:T(8,128)S(1)}, u32[]{:S(2)}, u32[]{:S(2)}) collective-permute-start(f32[128,512]{1,0:T(8,128)S(1)} %complete.1.refs_0_), channel_id=1, source_target_pairs={{1,0},{0,1},{3,2},{2,3},{5,4},{4,5},{7,6},{6,7},{9,8},{8,9},{11,10... | collective-permute-start | bytes 786440 | tf_op jit(solution)/shard_map/ppermute | solution.py:430
  19.5 7.9 %copy-start = (f32[32,2,4,1,512]{4,3,2,1,0:T(1,128)S(1)}, f32[32,2,4,1,512]{4,3,2,1,0:T(1,128)}, u32[]{:S(2)}) copy-start(f32[32,2,4,1,512]{4,3,2,1,0:T(1,128)} %param.11) | copy-start | bytes 1572868
  19.5 3.9 %collective-permute-start.4 = (f32[32,256]{1,0:T(8,128)S(1)}, f32[32,256]{1,0:T(8,128)S(1)}, u32[]{:S(2)}, u32[]{:S(2)}) collective-permute-start(f32[32,256]{1,0:T(8,128)S(1)} %sum.4.terms_ref), channel_id=1, source_target_pairs={{0,6},{2,4},{4,2},{6,0},{8,14},{10,12},{12,10},{14,8},{16,22},{18,... | collective-permute-start | bytes 98312 | tf_op jit(solution)/shard_map/ppermute | solution.py:414
  23.4 3.4 %collective-permute-start.6 = (f32[32,256]{1,0:T(8,128)S(1)}, f32[32,256]{1,0:T(8,128)S(1)}, u32[]{:S(2)}, u32[]{:S(2)}) collective-permute-start(f32[32,256]{1,0:T(8,128)S(1)} %sum.5.refs_0_), channel_id=1, source_target_pairs={{3,0},{2,1},{1,2},{0,3},{7,4},{6,5},{5,6},{4,7},{11,8},{10,9},{9,1... | collective-permute-start | bytes 98312 | tf_op jit(solution)/shard_map/ppermute | solution.py:423
  26.8 1.5 %copy-start.1 = (f32[2,64,256]{2,1,0:T(8,128)S(1)}, f32[2,64,256]{2,1,0:T(8,128)}, u32[]{:S(2)}) copy-start(f32[2,64,256]{2,1,0:T(8,128)} %noise_ref.1) | copy-start | bytes 393220
  26.9 1.5 %copy-start.2 = (f32[2,256]{1,0:T(2,128)S(1)}, f32[2,256]{1,0:T(2,128)}, u32[]{:S(2)}) copy-start(f32[2,256]{1,0:T(2,128)} %value_ref.1) | copy-start | bytes 6148
  26.9 1.4 %copy-start.3 = (f32[2,256]{1,0:T(2,128)S(1)}, f32[2,256]{1,0:T(2,128)}, u32[]{:S(2)}) copy-start(f32[2,256]{1,0:T(2,128)} %error_ref.1) | copy-start | bytes 6148
  26.9 1.4 %collective-permute-start.7 = (f32[64,256]{1,0:T(8,128)S(1)}, f32[64,256]{1,0:T(8,128)S(1)}, u32[]{:S(2)}, u32[]{:S(2)}) collective-permute-start(f32[64,256]{1,0:T(8,128)S(1)} %gather.1.kept_ref), channel_id=1, source_target_pairs={{0,2},{2,0},{4,6},{6,4},{8,10},{10,8},{12,14},{14,12},{16,18},{18,... | collective-permute-start | bytes 196616 | tf_op jit(solution)/shard_map/ppermute | solution.py:414

commit v24 on v18

--- a/solution.py
+++ b/solution.py
@@ -15,6 +15,7 @@
 
 
 SELECT_FLOPS = 1
+PIECES = 4
 OWN_FLOPS, SUM_FLOPS, GATHER_FLOPS, SOLVE_FLOPS = 1, (7*10**8,7*10**8,1), 10**8, 8*10**8
 
 
@@ -87,16 +88,27 @@
 
 def load_kernel(chunks, *refs):
     count = (len(refs) - 1) // 2
-    sources, packed_ref, held, sems = refs[:count], refs[count], refs[count + 1 : -1], refs[-1]
-    rows = sources[0].shape[0]
-    copies = at_once(sources, (packed_ref.at[:rows], *held), sems)
-    copies[1].wait()
-    copies[2].wait()
+    (present, *others), packed_ref, held, sems = (
+        refs[:count],
+        refs[count],
+        refs[count + 1 : -1],
+        refs[-1],
+    )
+    rows = present.shape[0]
+    piece = rows // PIECES
+    pieces = [pl.ds(k * piece, piece) for k in range(PIECES)]
+    copies = at_once(
+        [*(present.at[p] for p in pieces), *others],
+        [*(packed_ref.at[p] for p in pieces), *held],
+        sems,
+    )
+    copies[PIECES].wait()
+    copies[PIECES + 1].wait()
     spread = held[0][...]
     half = held[1][:chunks, :] * 0.5
     packed_ref[rows : rows + chunks, :] = spread + half
     packed_ref[rows + chunks : rows + 2 * chunks, :] = spread - half
-    for copy in (copies[0], *copies[3:]):
+    for copy in (*copies[:PIECES], *copies[PIECES + 2 :]):
         copy.wait()
 
 
@@ -235,7 +247,7 @@
     )
 
 
-def gram_kernel(parts, value_ref, error_ref, noise_ref, *refs):
+def gram_kernel(parts, value_ref, error_ref, noise_ref, _high, _low, *refs):
     term_refs, grams_ref = refs[:parts], refs[parts]
     members, count = noise_ref.shape[1:]
     local = members // parts
@@ -370,14 +382,17 @@
                 done_ref[pl.ds(start + c, local, stride=planes), :] = result[
                     :, c * LANES : (c + 1) * LANES
                 ]
-        copies.append(
-            pltpu.make_async_copy(
-                done_ref.reshape(local, planes, LANES).at[:, first : first + level, :],
-                out_ref.at[:, first : first + level, :],
-                sems.at[len(copies)],
-            )
-        )
-        copies[-1].start()
+            if f == fields // 2 - 1 or f == fields - 1:
+                count = fields // 2 * chunks
+                out_planes = slice(start + chunks - count, start + chunks)
+                copies.append(
+                    pltpu.make_async_copy(
+                        done_ref.reshape(local, planes, LANES).at[:, out_planes, :],
+                        out_ref.at[:, out_planes, :],
+                        sems.at[len(copies)],
+                    )
+                )
+                copies[-1].start()
     for copy in copies:
         copy.wait()
 
@@ -436,7 +451,7 @@
         out_shape=[shape_of((present.shape[0] + 2 * chunks, LANES))]
         + [shape_of(x.shape, x.dtype) for x in sources[1:]],
         in_specs=[hbm] * len(sources),
-        scratch_shapes=[pltpu.SemaphoreType.DMA((len(sources),))],
+        scratch_shapes=[pltpu.SemaphoreType.DMA((len(sources) - 1 + PIECES,))],
         compiler_params=PARAMS,
         name="load",
     )(*sources)
@@ -499,13 +514,19 @@
     )
 
     assert batches == 2
+    lagged_parts = pl.pallas_call(
+        functools.partial(prepare_kernel, parts),
+        out_shape=[shape_of((all_members, delayed.size // members), BF16)] * 2,
+        compiler_params=PARAMS,
+        name="prepare",
+    )(delayed, *others_delayed)
     grams = pl.pallas_call(
         functools.partial(gram_kernel, parts),
         out_shape=shape_of((2 * all_members, all_members)),
         cost_estimate=estimate(GATHER_FLOPS),
         compiler_params=PARAMS,
         name="gram",
-    )(obs_value, obs_error, obs_noise, terms, *from_other_mem(terms))
+    )(obs_value, obs_error, obs_noise, *lagged_parts, terms, *from_other_mem(terms))
     mine = pl.pallas_call(
         functools.partial(solve_kernel, parts, batches),
         out_shape=shape_of((members, all_members)),
@@ -513,19 +534,13 @@
         cost_estimate=estimate(SOLVE_FLOPS),
         name="solve",
     )(grams, from_slab(grams, 1))
-    lagged_parts = pl.pallas_call(
-        functools.partial(prepare_kernel, parts),
-        out_shape=[shape_of((all_members, delayed.size // members), BF16)] * 2,
-        compiler_params=PARAMS,
-        name="prepare",
-    )(delayed, *others_delayed)
     out = pl.pallas_call(
         functools.partial(combine_kernel, parts, fields),
         out_shape=shape_of((members, planes, LANES)),
         out_specs=hbm,
         scratch_shapes=[
             pltpu.VMEM((members * planes, LANES), F32),
-            pltpu.SemaphoreType.DMA((1 + lagged,)),
+            pltpu.SemaphoreType.DMA((2 * (1 + lagged),)),
         ],
         compiler_params=PARAMS,
         name="combine",

time: 32.6 us -> 32.5 us (level)
    ppermute x5, waiting for transfers between devices: 4.48 us -> 5.22 us  [from_slab(): return lax.ppermute(array, 'slab', [(i, i ^ bit) for i in range(slabs)])]
    ppermute x1, waiting for transfers between devices: 1.86 us -> 1.16 us  [from_other_mem(): lax.ppermute(array, ('slab', 'mem'), [(i ^ 3, i) for i in range(slabs * p...]
where the time goes in v24:
time: 32.5 us; the launch traced here: 32.3 us
  starting transfers between devices  18.6 us (57%)
  Pallas kernels  7.27 us (22%)
  waiting for transfers between devices  6.38 us (20%)
    ppermute x5, starting transfers between devices, from_slab(): return lax.ppermute(array, 'slab', [(i, i ^ bit) for i in range(slabs)])  8.4 us
    ppermute x5, waiting for transfers between devices, from_slab(): return lax.ppermute(array, 'slab', [(i, i ^ bit) for i in range(slabs)])  5.22 us
    ppermute x2, starting transfers between devices, from_partners(): lax.ppermute(array, 'mem', [((i + d) % parts, i) for i in range(parts)])  4.56 us
    ppermute x1, starting transfers between devices, shards(): lax.ppermute(lax.optimization_barrier((packed, part))[0], 'slab', up)  2.77 us
    pallas_call x1, Pallas kernels, shards(): pl.pallas_call(functools.partial(solve_kernel, parts, batches), out_shape...  2.59 us
    ppermute x1, starting transfers between devices, from_other_mem(): lax.ppermute(array, ('slab', 'mem'), [(i ^ 3, i) for i in range(slabs * p...  1.54 us
    pallas_call x1, Pallas kernels, shards(): pl.pallas_call(functools.partial(combine_kernel, parts, fields), out_shap...  1.33 us
    ppermute x1, starting transfers between devices, shards(): from_below = lax.ppermute(packed, 'slab', [(j, i) for i, j in up])  1.29 us
  transfers between devices with their start and end apart: 10, of which 6 were waited for; matrix products, arithmetic and copies ran while one was open for 0% of the time, Pallas kernels for 15%

profile of v24, /device:TPU:0, one launch (start us, length us, event | category | flops | bytes accessed | tf_op | source)
XLA Modules:
  0.0 32.3 jit_solution(18312637082016697917)
XLA Ops:
  0.0 1.0 %load.1 = (f32[520,128]{1,0:T(8,128)S(1)}, f32[4,128]{1,0:T(4,128)S(1)}, f32[8,128]{1,0:T(8,128)S(1)}, s32[2,256]{1,0:T(2,128)S(1)}, s32[2,256]{1,0:T(2,128)S(1)}, /*index=5*/s32[2,256]{1,0:T(2,128)S(1)}) custom-call(f32[512,128]{1,0:T(8,128)} %bitcast.7, f32[4,128]{1,0:T(4,128)} %bitcast.9, f32[8,128]{1,0:T(8,128)} %bitcast.8, s32[2,256]{1,0:T(2,128)} %refs_3_.1, ...), custom_call_target="tpu_custom_call" | custom-call | tf_op jit(solution)/shard_map/load/pallas_call | solution.py:449
  1.0 1.3 %collective-permute-start.1 = (f32[520,128]{1,0:T(8,128)S(1)}, f32[520,128]{1,0:T(8,128)S(1)}, u32[]{:S(2)}, u32[]{:S(2)}) collective-permute-start(f32[520,128]{1,0:T(8,128)S(1)} %get-tuple-element.42.packed_ref), channel_id=1, source_target_pairs={{2,0},{4,2},{6,4},{8,6},{10,8},{12,10},{14,12},{16,14},{18,16},{20... | collective-permute-start | bytes 798728 | tf_op jit(solution)/shard_map/ppermute | solution.py:459
  2.3 3.0 %collective-permute-start = (f32[1024,128]{1,0:T(8,128)}, f32[1024,128]{1,0:T(8,128)S(1)}, u32[]{:S(2)}, u32[]{:S(2)}) collective-permute-start(f32[1024,128]{1,0:T(8,128)} %bitcast.5), channel_id=1, source_target_pairs={{1,0},{0,1},{3,2},{2,3},{5,4},{4,5},{7,6},{6,7},{9,8},{8,9},{11,10... | collective-permute-start | bytes 1572872 | tf_op jit(solution)/shard_map/ppermute | solution.py:442
  5.3 0.2 selector.1
  5.5 0.5 %own_row.1 = (f32[128,512]{1,0:T(8,128)S(1)}, f32[128,512]{1,0:T(8,128)S(1)}, f32[32,512]{1,0:T(8,128)S(1)}) custom-call(f32[520,128]{1,0:T(8,128)S(1)} %get-tuple-element.42.packed_ref, f32[4,128]{1,0:T(4,128)S(1)} %get-tuple-element.28.spread_ref, f32[8,128]{1,0:T(8,128)S(1)} %get-tuple-element.29.ratio_ref, ...), custom_call_target="tpu_custom_call" | custom-call | flops 1 | tf_op jit(solution)/shard_map/own_row/pallas_call | solution.py:470
  6.0 2.8 %collective-permute-start.8 = (f32[520,128]{1,0:T(8,128)S(1)}, f32[520,128]{1,0:T(8,128)S(1)}, u32[]{:S(2)}, u32[]{:S(2)}) collective-permute-start(f32[520,128]{1,0:T(8,128)S(1)} %get-tuple-element.42.packed_ref), channel_id=1, source_target_pairs={{0,2},{2,4},{4,6},{6,8},{8,10},{10,12},{12,14},{14,16},{16,18},{18... | collective-permute-start | bytes 798728 | tf_op jit(solution)/shard_map/ppermute | solution.py:477
  8.8 0.5 %observe.1 = (f32[32,256]{1,0:T(8,128)S(1)}, f32[32,256]{1,0:T(8,128)S(1)}, f32[128,512]{1,0:T(8,128)S(1)}) custom-call(f32[520,128]{1,0:T(8,128)S(1)} %get-tuple-element.42.packed_ref, f32[520,128]{1,0:T(8,128)S(1)} %collective-permute-done.1.next_ref, f32[128,512]{1,0:T(8,128)S(1)} %get-tuple-element.35.part_ref, ...), custom_call_target="tpu_custom_call" | custom-call | tf_op jit(solution)/shard_map/observe/pallas_call | solution.py:478
  9.3 1.6 %collective-permute-start.2 = (f32[32,256]{1,0:T(8,128)S(1)}, f32[32,256]{1,0:T(8,128)S(1)}, u32[]{:S(2)}, u32[]{:S(2)}) collective-permute-start(f32[32,256]{1,0:T(8,128)S(1)} %get-tuple-element.39), channel_id=1, source_target_pairs={{0,2},{2,0},{4,6},{6,4},{8,10},{10,8},{12,14},{14,12},{16,18},{18,... | collective-permute-start | bytes 98312 | tf_op jit(solution)/shard_map/ppermute | solution.py:426
  11.0 0.9 %collective-permute-done.2 = f32[32,256]{1,0:T(8,128)S(1)} collective-permute-done((f32[32,256]{1,0:T(8,128)S(1)}, f32[32,256]{1,0:T(8,128)S(1)}, u32[]{:S(2)}, u32[]{:S(2)}) %collective-permute-start.2) | collective-permute-done | bytes 32800 | tf_op jit(solution)/shard_map/ppermute | solution.py:426
  11.8 2.5 %collective-permute-start.3 = (f32[32,256]{1,0:T(8,128)S(1)}, f32[32,256]{1,0:T(8,128)S(1)}, u32[]{:S(2)}, u32[]{:S(2)}) collective-permute-start(f32[32,256]{1,0:T(8,128)S(1)} %add.3.terms_ref), channel_id=1, source_target_pairs={{0,18},{2,16},{4,22},{6,20},{8,26},{10,24},{12,30},{14,28},{16,2},... | collective-permute-start | bytes 98312 | tf_op jit(solution)/shard_map/ppermute | solution.py:426
  14.4 1.7 %collective-permute-done.3.other_ref = f32[32,256]{1,0:T(8,128)S(1)} collective-permute-done((f32[32,256]{1,0:T(8,128)S(1)}, f32[32,256]{1,0:T(8,128)S(1)}, u32[]{:S(2)}, u32[]{:S(2)}) %collective-permute-start.3) | collective-permute-done | bytes 32800 | tf_op jit(solution)/shard_map/ppermute | solution.py:426
  16.1 1.5 %collective-permute-start.4 = (f32[32,256]{1,0:T(8,128)S(1)}, f32[32,256]{1,0:T(8,128)S(1)}, u32[]{:S(2)}, u32[]{:S(2)}) collective-permute-start(f32[32,256]{1,0:T(8,128)S(1)} %sum.3.terms_ref), channel_id=1, source_target_pairs={{0,10},{2,8},{4,14},{6,12},{8,2},{10,0},{12,6},{14,4},{16,26},{18,... | collective-permute-start | bytes 98312 | tf_op jit(solution)/shard_map/ppermute | solution.py:426
  17.7 1.6 %collective-permute-start.9 = (f32[128,512]{1,0:T(8,128)S(1)}, f32[128,512]{1,0:T(8,128)S(1)}, u32[]{:S(2)}, u32[]{:S(2)}) collective-permute-start(f32[128,512]{1,0:T(8,128)S(1)} %complete.1.refs_0_), channel_id=1, source_target_pairs={{1,0},{0,1},{3,2},{2,3},{5,4},{4,5},{7,6},{6,7},{9,8},{8,9},{11,10... | collective-permute-start | bytes 786440 | tf_op jit(solution)/shard_map/ppermute | solution.py:442
  19.3 0.1 collective-permute-done.4.other_ref
  19.4 2.2 %collective-permute-start.5 = (f32[32,256]{1,0:T(8,128)S(1)}, f32[32,256]{1,0:T(8,128)S(1)}, u32[]{:S(2)}, u32[]{:S(2)}) collective-permute-start(f32[32,256]{1,0:T(8,128)S(1)} %sum.4.terms_ref), channel_id=1, source_target_pairs={{0,6},{2,4},{4,2},{6,0},{8,14},{10,12},{12,10},{14,8},{16,22},{18,... | collective-permute-start | bytes 98312 | tf_op jit(solution)/shard_map/ppermute | solution.py:426
  21.6 1.6 %collective-permute-done.5.other_ref = f32[32,256]{1,0:T(8,128)S(1)} collective-permute-done((f32[32,256]{1,0:T(8,128)S(1)}, f32[32,256]{1,0:T(8,128)S(1)}, u32[]{:S(2)}, u32[]{:S(2)}) %collective-permute-start.5) | collective-permute-done | bytes 32800 | tf_op jit(solution)/shard_map/ppermute | solution.py:426
  23.3 1.5 %collective-permute-start.6 = (f32[32,256]{1,0:T(8,128)S(1)}, f32[32,256]{1,0:T(8,128)S(1)}, u32[]{:S(2)}, u32[]{:S(2)}) collective-permute-start(f32[32,256]{1,0:T(8,128)S(1)} %sum.5.refs_0_), channel_id=1, source_target_pairs={{3,0},{2,1},{1,2},{0,3},{7,4},{6,5},{5,6},{4,7},{11,8},{10,9},{9,1... | collective-permute-start | bytes 98312 | tf_op jit(solution)/shard_map/ppermute | solution.py:435
  24.8 0.7 %prepare.1 = (bf16[64,4096]{1,0:T(8,128)(2,1)S(1)}, bf16[64,4096]{1,0:T(8,128)(2,1)S(1)}) custom-call(f32[1024,128]{1,0:T(8,128)S(1)} %bitcast.6, f32[1024,128]{1,0:T(8,128)S(1)} %collective-permute-done.refs_1_.refs_0_), custom_call_target="tpu_custom_call" | custom-call | tf_op jit(solution)/shard_map/prepare/pallas_call | solution.py:517
  25.5 1.2 %collective-permute-done.6.refs_1_ = f32[32,256]{1,0:T(8,128)S(1)} collective-permute-done((f32[32,256]{1,0:T(8,128)S(1)}, f32[32,256]{1,0:T(8,128)S(1)}, u32[]{:S(2)}, u32[]{:S(2)}) %collective-permute-start.6) | collective-permute-done | bytes 32800 | tf_op jit(solution)/shard_map/ppermute | solution.py:435
  26.7 0.3 gram.1.kept_ref
  27.0 0.5 %collective-permute-start.7 = (f32[128,64]{1,0:T(8,128)S(1)}, f32[128,64]{1,0:T(8,128)S(1)}, u32[]{:S(2)}, u32[]{:S(2)}) collective-permute-start(f32[128,64]{1,0:T(8,128)S(1)} %gram.1.kept_ref), channel_id=1, source_target_pairs={{0,2},{2,0},{4,6},{6,4},{8,10},{10,8},{12,14},{14,12},{16,18},{18,... | collective-permute-start | bytes 98312 | tf_op jit(solution)/shard_map/ppermute | solution.py:426
  27.5 0.9 %collective-permute-done.7.received_ref = f32[128,64]{1,0:T(8,128)S(1)} collective-permute-done((f32[128,64]{1,0:T(8,128)S(1)}, f32[128,64]{1,0:T(8,128)S(1)}, u32[]{:S(2)}, u32[]{:S(2)}) %collective-permute-start.7) | collective-permute-done | bytes 32800 | tf_op jit(solution)/shard_map/ppermute | solution.py:426
  28.4 2.6 %solve.1.mine_ref = f32[32,64]{1,0:T(8,128)S(1)} custom-call(f32[128,64]{1,0:T(8,128)S(1)} %gram.1.kept_ref, f32[128,64]{1,0:T(8,128)S(1)} %collective-permute-done.7.received_ref), custom_call_target="tpu_custom_call" | custom-call | flops 800000000 | tf_op jit(solution)/shard_map/solve/pallas_call | solution.py:530
  31.0 1.3 %combine.1 = f32[32,48,128]{2,1,0:T(8,128)} custom-call(f32[32,64]{1,0:T(8,128)S(1)} %solve.1.mine_ref, f32[128,512]{1,0:T(8,128)S(1)} %complete.1.refs_0_, f32[128,512]{1,0:T(8,128)S(1)} %collective-permute-done.9.refs_1_, bf16[64,4096]{1,0:T(8,128)(2,1)S(1)} %get-tuple-element.26._high.refs_2_, bf16[64,4096]{1,0:T(8,128)(2,1)S(1)} %get-tuple-element.27._low.refs_3_), custom_call_target="tpu_custom_call" | custom-call | tf_op jit(solution)/shard_map/combine/pallas_call | solution.py:537
  (17 shorter events, 0.2 us)
Async XLA Ops:
  1.0 7.8 %collective-permute-start.1 = (f32[520,128]{1,0:T(8,128)S(1)}, f32[520,128]{1,0:T(8,128)S(1)}, u32[]{:S(2)}, u32[]{:S(2)}) collective-permute-start(f32[520,128]{1,0:T(8,128)S(1)} %get-tuple-element.42.packed_ref), channel_id=1, source_target_pairs={{2,0},{4,2},{6,4},{8,6},{10,8},{12,10},{14,12},{16,14},{18,16},{20... | collective-permute-start | bytes 798728 | tf_op jit(solution)/shard_map/ppermute | solution.py:459
  2.3 20.9 %collective-permute-start = (f32[1024,128]{1,0:T(8,128)}, f32[1024,128]{1,0:T(8,128)S(1)}, u32[]{:S(2)}, u32[]{:S(2)}) collective-permute-start(f32[1024,128]{1,0:T(8,128)} %bitcast.5), channel_id=1, source_target_pairs={{1,0},{0,1},{3,2},{2,3},{5,4},{4,5},{7,6},{6,7},{9,8},{8,9},{11,10... | collective-permute-start | bytes 1572872 | tf_op jit(solution)/shard_map/ppermute | solution.py:442
  6.0 11.6 %collective-permute-start.8 = (f32[520,128]{1,0:T(8,128)S(1)}, f32[520,128]{1,0:T(8,128)S(1)}, u32[]{:S(2)}, u32[]{:S(2)}) collective-permute-start(f32[520,128]{1,0:T(8,128)S(1)} %get-tuple-element.42.packed_ref), channel_id=1, source_target_pairs={{0,2},{2,4},{4,6},{6,8},{8,10},{10,12},{12,14},{14,16},{16,18},{18... | collective-permute-start | bytes 798728 | tf_op jit(solution)/shard_map/ppermute | solution.py:477
  9.3 2.5 %collective-permute-start.2 = (f32[32,256]{1,0:T(8,128)S(1)}, f32[32,256]{1,0:T(8,128)S(1)}, u32[]{:S(2)}, u32[]{:S(2)}) collective-permute-start(f32[32,256]{1,0:T(8,128)S(1)} %get-tuple-element.39), channel_id=1, source_target_pairs={{0,2},{2,0},{4,6},{6,4},{8,10},{10,8},{12,14},{14,12},{16,18},{18,... | collective-permute-start | bytes 98312 | tf_op jit(solution)/shard_map/ppermute | solution.py:426
  11.8 4.2 %collective-permute-start.3 = (f32[32,256]{1,0:T(8,128)S(1)}, f32[32,256]{1,0:T(8,128)S(1)}, u32[]{:S(2)}, u32[]{:S(2)}) collective-permute-start(f32[32,256]{1,0:T(8,128)S(1)} %add.3.terms_ref), channel_id=1, source_target_pairs={{0,18},{2,16},{4,22},{6,20},{8,26},{10,24},{12,30},{14,28},{16,2},... | collective-permute-start | bytes 98312 | tf_op jit(solution)/shard_map/ppermute | solution.py:426
  16.1 3.3 %collective-permute-start.4 = (f32[32,256]{1,0:T(8,128)S(1)}, f32[32,256]{1,0:T(8,128)S(1)}, u32[]{:S(2)}, u32[]{:S(2)}) collective-permute-start(f32[32,256]{1,0:T(8,128)S(1)} %sum.3.terms_ref), channel_id=1, source_target_pairs={{0,10},{2,8},{4,14},{6,12},{8,2},{10,0},{12,6},{14,4},{16,26},{18,... | collective-permute-start | bytes 98312 | tf_op jit(solution)/shard_map/ppermute | solution.py:426
  17.7 13.3 %collective-permute-start.9 = (f32[128,512]{1,0:T(8,128)S(1)}, f32[128,512]{1,0:T(8,128)S(1)}, u32[]{:S(2)}, u32[]{:S(2)}) collective-permute-start(f32[128,512]{1,0:T(8,128)S(1)} %complete.1.refs_0_), channel_id=1, source_target_pairs={{1,0},{0,1},{3,2},{2,3},{5,4},{4,5},{7,6},{6,7},{9,8},{8,9},{11,10... | collective-permute-start | bytes 786440 | tf_op jit(solution)/shard_map/ppermute | solution.py:442
  19.4 5.4 %copy-start = (f32[32,2,4,1,512]{4,3,2,1,0:T(1,128)S(1)}, f32[32,2,4,1,512]{4,3,2,1,0:T(1,128)}, u32[]{:S(2)}) copy-start(f32[32,2,4,1,512]{4,3,2,1,0:T(1,128)} %param.11) | copy-start | bytes 1572868
  19.4 3.8 %collective-permute-start.5 = (f32[32,256]{1,0:T(8,128)S(1)}, f32[32,256]{1,0:T(8,128)S(1)}, u32[]{:S(2)}, u32[]{:S(2)}) collective-permute-start(f32[32,256]{1,0:T(8,128)S(1)} %sum.4.terms_ref), channel_id=1, source_target_pairs={{0,6},{2,4},{4,2},{6,0},{8,14},{10,12},{12,10},{14,8},{16,22},{18,... | collective-permute-start | bytes 98312 | tf_op jit(solution)/shard_map/ppermute | solution.py:426
  23.2 3.4 %copy-start.1 = (f32[2,64,256]{2,1,0:T(8,128)S(1)}, f32[2,64,256]{2,1,0:T(8,128)}, u32[]{:S(2)}) copy-start(f32[2,64,256]{2,1,0:T(8,128)} %noise_ref.1) | copy-start | bytes 393220
  23.3 3.4 %collective-permute-start.6 = (f32[32,256]{1,0:T(8,128)S(1)}, f32[32,256]{1,0:T(8,128)S(1)}, u32[]{:S(2)}, u32[]{:S(2)}) collective-permute-start(f32[32,256]{1,0:T(8,128)S(1)} %sum.5.refs_0_), channel_id=1, source_target_pairs={{3,0},{2,1},{1,2},{0,3},{7,4},{6,5},{5,6},{4,7},{11,8},{10,9},{9,1... | collective-permute-start | bytes 98312 | tf_op jit(solution)/shard_map/ppermute | solution.py:435
  24.8 1.9 %copy-start.3 = (f32[2,256]{1,0:T(2,128)S(1)}, f32[2,256]{1,0:T(2,128)}, u32[]{:S(2)}) copy-start(f32[2,256]{1,0:T(2,128)} %error_ref.1) | copy-start | bytes 6148
  25.5 1.2 %copy-start.2 = (f32[2,256]{1,0:T(2,128)S(1)}, f32[2,256]{1,0:T(2,128)}, u32[]{:S(2)}) copy-start(f32[2,256]{1,0:T(2,128)} %value_ref.1) | copy-start | bytes 6148
  27.0 1.4 %collective-permute-start.7 = (f32[128,64]{1,0:T(8,128)S(1)}, f32[128,64]{1,0:T(8,128)S(1)}, u32[]{:S(2)}, u32[]{:S(2)}) collective-permute-start(f32[128,64]{1,0:T(8,128)S(1)} %gram.1.kept_ref), channel_id=1, source_target_pairs={{0,2},{2,0},{4,6},{6,4},{8,10},{10,8},{12,14},{14,12},{16,18},{18,... | collective-permute-start | bytes 98312 | tf_op jit(solution)/shard_map/ppermute | solution.py:426

commit v25 on v16

--- a/solution.py
+++ b/solution.py
@@ -231,8 +231,11 @@
 def three_pass(x, y):
     x_high, x_low = split_two(x)
     y_high, y_low = split_two(y)
-    dot = functools.partial(jnp.dot, preferred_element_type=F32)
-    return dot(x_low, y_high) + dot(x_high, y_low) + dot(x_high, y_high)
+    return jnp.dot(
+        jnp.concatenate([x_high, x_high, x_low], axis=1),
+        jnp.concatenate([y_high, y_low, y_high], axis=0),
+        preferred_element_type=F32,
+    )
 
 
 def solve_transposed(system, right_t, floor):

time: 32.6 us -> 33 us (1.012)
  transfers between devices with their start and end apart: 10 -> 10, of which waited for: 6 -> 6; matrix products, arithmetic and copies ran while one was open for 0% -> 0% of each run, Pallas kernels for 15% -> 16%
where the time goes in v25:
time: 33 us; the launch traced here: 32.7 us
  starting transfers between devices  18.6 us (56%)
  Pallas kernels  7.64 us (23%)
  waiting for transfers between devices  6.38 us (19%)
    ppermute x5, starting transfers between devices, from_slab(): return lax.ppermute(array, 'slab', [(i, i ^ bit) for i in range(slabs)])  8.39 us
    ppermute x2, starting transfers between devices, from_partners(): lax.ppermute(array, 'mem', [((i + d) % parts, i) for i in range(parts)])  4.57 us
    ppermute x5, waiting for transfers between devices, from_slab(): return lax.ppermute(array, 'slab', [(i, i ^ bit) for i in range(slabs)])  4.48 us
    pallas_call x1, Pallas kernels, shards(): pl.pallas_call(functools.partial(solve_kernel, parts), out_shape=shape_of...  3.24 us
    ppermute x1, starting transfers between devices, shards(): lax.ppermute(lax.optimization_barrier((packed, part))[0], 'slab', up)  2.77 us
    ppermute x1, waiting for transfers between devices, from_other_mem(): lax.ppermute(array, ('slab', 'mem'), [(i ^ 3, i) for i in range(slabs * p...  1.89 us
    ppermute x1, starting transfers between devices, from_other_mem(): lax.ppermute(array, ('slab', 'mem'), [(i ^ 3, i) for i in range(slabs * p...  1.55 us
    pallas_call x1, Pallas kernels, shards(): pl.pallas_call(functools.partial(combine_kernel, parts, fields), out_shap...  1.36 us
  transfers between devices with their start and end apart: 10, of which 6 were waited for; matrix products, arithmetic and copies ran while one was open for 0% of the time, Pallas kernels for 16%

profile of v25, /device:TPU:0, one launch (start us, length us, event | category | flops | bytes accessed | tf_op | source)
XLA Modules:
  0.0 32.7 jit_solution(5278858009296929867)
XLA Ops:
  0.0 1.0 %load.1 = (f32[520,128]{1,0:T(8,128)S(1)}, f32[4,128]{1,0:T(4,128)S(1)}, f32[8,128]{1,0:T(8,128)S(1)}, s32[2,256]{1,0:T(2,128)S(1)}, s32[2,256]{1,0:T(2,128)S(1)}, /*index=5*/s32[2,256]{1,0:T(2,128)S(1)}) custom-call(f32[512,128]{1,0:T(8,128)} %bitcast.7, f32[4,128]{1,0:T(4,128)} %bitcast.9, f32[8,128]{1,0:T(8,128)} %bitcast.8, s32[2,256]{1,0:T(2,128)} %refs_3_.1, ...), custom_call_target="tpu_custom_call" | custom-call | tf_op jit(solution)/shard_map/load/pallas_call | solution.py:438
  1.0 1.3 %collective-permute-start = (f32[520,128]{1,0:T(8,128)S(1)}, f32[520,128]{1,0:T(8,128)S(1)}, u32[]{:S(2)}, u32[]{:S(2)}) collective-permute-start(f32[520,128]{1,0:T(8,128)S(1)} %get-tuple-element.40.packed_ref), channel_id=1, source_target_pairs={{2,0},{4,2},{6,4},{8,6},{10,8},{12,10},{14,12},{16,14},{18,16},{20... | collective-permute-start | bytes 798728 | tf_op jit(solution)/shard_map/ppermute | solution.py:448
  2.3 3.0 %collective-permute-start.5 = (f32[1024,128]{1,0:T(8,128)}, f32[1024,128]{1,0:T(8,128)S(1)}, u32[]{:S(2)}, u32[]{:S(2)}) collective-permute-start(f32[1024,128]{1,0:T(8,128)} %bitcast.5), channel_id=1, source_target_pairs={{1,0},{0,1},{3,2},{2,3},{5,4},{4,5},{7,6},{6,7},{9,8},{8,9},{11,10... | collective-permute-start | bytes 1572872 | tf_op jit(solution)/shard_map/ppermute | solution.py:431
  5.3 0.2 selector.1
  5.5 0.5 %own_row.1 = (f32[128,512]{1,0:T(8,128)S(1)}, f32[128,512]{1,0:T(8,128)S(1)}, f32[32,512]{1,0:T(8,128)S(1)}) custom-call(f32[520,128]{1,0:T(8,128)S(1)} %get-tuple-element.40.packed_ref, f32[4,128]{1,0:T(4,128)S(1)} %get-tuple-element.25.spread_ref, f32[8,128]{1,0:T(8,128)S(1)} %get-tuple-element.26.ratio_ref, ...), custom_call_target="tpu_custom_call" | custom-call | flops 1 | tf_op jit(solution)/shard_map/own_row/pallas_call | solution.py:459
  6.0 2.8 %collective-permute-start.8 = (f32[520,128]{1,0:T(8,128)S(1)}, f32[520,128]{1,0:T(8,128)S(1)}, u32[]{:S(2)}, u32[]{:S(2)}) collective-permute-start(f32[520,128]{1,0:T(8,128)S(1)} %get-tuple-element.40.packed_ref), channel_id=1, source_target_pairs={{0,2},{2,4},{4,6},{6,8},{8,10},{10,12},{12,14},{14,16},{16,18},{18... | collective-permute-start | bytes 798728 | tf_op jit(solution)/shard_map/ppermute | solution.py:466
  8.8 0.5 %observe.1 = (f32[32,256]{1,0:T(8,128)S(1)}, f32[32,256]{1,0:T(8,128)S(1)}, f32[128,512]{1,0:T(8,128)S(1)}) custom-call(f32[520,128]{1,0:T(8,128)S(1)} %get-tuple-element.40.packed_ref, f32[520,128]{1,0:T(8,128)S(1)} %collective-permute-done.next_ref, f32[128,512]{1,0:T(8,128)S(1)} %get-tuple-element.32.part_ref, ...), custom_call_target="tpu_custom_call" | custom-call | tf_op jit(solution)/shard_map/observe/pallas_call | solution.py:467
  9.3 1.6 %collective-permute-start.1 = (f32[32,256]{1,0:T(8,128)S(1)}, f32[32,256]{1,0:T(8,128)S(1)}, u32[]{:S(2)}, u32[]{:S(2)}) collective-permute-start(f32[32,256]{1,0:T(8,128)S(1)} %get-tuple-element.36), channel_id=1, source_target_pairs={{0,2},{2,0},{4,6},{6,4},{8,10},{10,8},{12,14},{14,12},{16,18},{18,... | collective-permute-start | bytes 98312 | tf_op jit(solution)/shard_map/ppermute | solution.py:415
  10.9 0.9 %collective-permute-done.1 = f32[32,256]{1,0:T(8,128)S(1)} collective-permute-done((f32[32,256]{1,0:T(8,128)S(1)}, f32[32,256]{1,0:T(8,128)S(1)}, u32[]{:S(2)}, u32[]{:S(2)}) %collective-permute-start.1) | collective-permute-done | bytes 32800 | tf_op jit(solution)/shard_map/ppermute | solution.py:415
  11.8 2.5 %collective-permute-start.2 = (f32[32,256]{1,0:T(8,128)S(1)}, f32[32,256]{1,0:T(8,128)S(1)}, u32[]{:S(2)}, u32[]{:S(2)}) collective-permute-start(f32[32,256]{1,0:T(8,128)S(1)} %add.3.terms_ref), channel_id=1, source_target_pairs={{0,18},{2,16},{4,22},{6,20},{8,26},{10,24},{12,30},{14,28},{16,2},... | collective-permute-start | bytes 98312 | tf_op jit(solution)/shard_map/ppermute | solution.py:415
  14.4 1.7 %collective-permute-done.2.other_ref = f32[32,256]{1,0:T(8,128)S(1)} collective-permute-done((f32[32,256]{1,0:T(8,128)S(1)}, f32[32,256]{1,0:T(8,128)S(1)}, u32[]{:S(2)}, u32[]{:S(2)}) %collective-permute-start.2) | collective-permute-done | bytes 32800 | tf_op jit(solution)/shard_map/ppermute | solution.py:415
  16.1 1.5 %collective-permute-start.3 = (f32[32,256]{1,0:T(8,128)S(1)}, f32[32,256]{1,0:T(8,128)S(1)}, u32[]{:S(2)}, u32[]{:S(2)}) collective-permute-start(f32[32,256]{1,0:T(8,128)S(1)} %sum.3.terms_ref), channel_id=1, source_target_pairs={{0,10},{2,8},{4,14},{6,12},{8,2},{10,0},{12,6},{14,4},{16,26},{18,... | collective-permute-start | bytes 98312 | tf_op jit(solution)/shard_map/ppermute | solution.py:415
  17.6 0.1 complete.1.refs_0_
  17.7 1.6 %collective-permute-start.9 = (f32[128,512]{1,0:T(8,128)S(1)}, f32[128,512]{1,0:T(8,128)S(1)}, u32[]{:S(2)}, u32[]{:S(2)}) collective-permute-start(f32[128,512]{1,0:T(8,128)S(1)} %complete.1.refs_0_), channel_id=1, source_target_pairs={{1,0},{0,1},{3,2},{2,3},{5,4},{4,5},{7,6},{6,7},{9,8},{8,9},{11,10... | collective-permute-start | bytes 786440 | tf_op jit(solution)/shard_map/ppermute | solution.py:431
  19.3 0.1 collective-permute-done.3.other_ref
  19.4 2.2 %collective-permute-start.4 = (f32[32,256]{1,0:T(8,128)S(1)}, f32[32,256]{1,0:T(8,128)S(1)}, u32[]{:S(2)}, u32[]{:S(2)}) collective-permute-start(f32[32,256]{1,0:T(8,128)S(1)} %sum.4.terms_ref), channel_id=1, source_target_pairs={{0,6},{2,4},{4,2},{6,0},{8,14},{10,12},{12,10},{14,8},{16,22},{18,... | collective-permute-start | bytes 98312 | tf_op jit(solution)/shard_map/ppermute | solution.py:415
  21.6 1.6 %collective-permute-done.4.other_ref = f32[32,256]{1,0:T(8,128)S(1)} collective-permute-done((f32[32,256]{1,0:T(8,128)S(1)}, f32[32,256]{1,0:T(8,128)S(1)}, u32[]{:S(2)}, u32[]{:S(2)}) %collective-permute-start.4) | collective-permute-done | bytes 32800 | tf_op jit(solution)/shard_map/ppermute | solution.py:415
  23.2 1.5 %collective-permute-start.6 = (f32[32,256]{1,0:T(8,128)S(1)}, f32[32,256]{1,0:T(8,128)S(1)}, u32[]{:S(2)}, u32[]{:S(2)}) collective-permute-start(f32[32,256]{1,0:T(8,128)S(1)} %sum.5.refs_0_), channel_id=1, source_target_pairs={{3,0},{2,1},{1,2},{0,3},{7,4},{6,5},{5,6},{4,7},{11,8},{10,9},{9,1... | collective-permute-start | bytes 98312 | tf_op jit(solution)/shard_map/ppermute | solution.py:424
  24.8 1.9 %collective-permute-done.6.refs_1_ = f32[32,256]{1,0:T(8,128)S(1)} collective-permute-done((f32[32,256]{1,0:T(8,128)S(1)}, f32[32,256]{1,0:T(8,128)S(1)}, u32[]{:S(2)}, u32[]{:S(2)}) %collective-permute-start.6) | collective-permute-done | bytes 32800 | tf_op jit(solution)/shard_map/ppermute | solution.py:424
  26.7 0.5 %collective-permute-start.7 = (f32[64,256]{1,0:T(8,128)S(1)}, f32[64,256]{1,0:T(8,128)S(1)}, u32[]{:S(2)}, u32[]{:S(2)}) collective-permute-start(f32[64,256]{1,0:T(8,128)S(1)} %gather.1.kept_ref), channel_id=1, source_target_pairs={{0,2},{2,0},{4,6},{6,4},{8,10},{10,8},{12,14},{14,12},{16,18},{18,... | collective-permute-start | bytes 196616 | tf_op jit(solution)/shard_map/ppermute | solution.py:415
  27.2 0.7 %prepare.1 = (bf16[64,4096]{1,0:T(8,128)(2,1)S(1)}, bf16[64,4096]{1,0:T(8,128)(2,1)S(1)}) custom-call(f32[1024,128]{1,0:T(8,128)S(1)} %bitcast.6, f32[1024,128]{1,0:T(8,128)S(1)} %collective-permute-done.5.refs_0_.refs_1_), custom_call_target="tpu_custom_call" | custom-call | tf_op jit(solution)/shard_map/prepare/pallas_call | solution.py:519
  27.9 0.2 collective-permute-done.7.received_ref
  28.1 3.2 %solve.1.mine_ref = f32[32,64]{1,0:T(8,128)S(1)} custom-call(f32[2,256]{1,0:T(2,128)S(1)} %copy-done.2, f32[2,256]{1,0:T(2,128)S(1)} %copy-done.3, f32[2,64,256]{2,1,0:T(8,128)S(1)} %copy-done.1, f32[64,256]{1,0:T(8,128)S(1)} %gather.1.kept_ref, f32[64,256]{1,0:T(8,128)S(1)} %collective-permute-done.7.received_ref), custom_call_target="tpu_custom_call" | custom-call | flops 500000000 | tf_op jit(solution)/shard_map/solve/pallas_call | solution.py:512
  31.4 1.4 %combine.1 = f32[32,48,128]{2,1,0:T(8,128)} custom-call(f32[32,64]{1,0:T(8,128)S(1)} %solve.1.mine_ref, f32[128,512]{1,0:T(8,128)S(1)} %complete.1.refs_0_, f32[128,512]{1,0:T(8,128)S(1)} %collective-permute-done.9.refs_1_, bf16[64,4096]{1,0:T(8,128)(2,1)S(1)} %get-tuple-element.41.refs_2_, bf16[64,4096]{1,0:T(8,128)(2,1)S(1)} %get-tuple-element.42.refs_3_), custom_call_target="tpu_custom_call" | custom-call | tf_op jit(solution)/shard_map/combine/pallas_call | solution.py:525
  (17 shorter events, 0.1 us)
Async XLA Ops:
  1.0 7.8 %collective-permute-start = (f32[520,128]{1,0:T(8,128)S(1)}, f32[520,128]{1,0:T(8,128)S(1)}, u32[]{:S(2)}, u32[]{:S(2)}) collective-permute-start(f32[520,128]{1,0:T(8,128)S(1)} %get-tuple-element.40.packed_ref), channel_id=1, source_target_pairs={{2,0},{4,2},{6,4},{8,6},{10,8},{12,10},{14,12},{16,14},{18,16},{20... | collective-permute-start | bytes 798728 | tf_op jit(solution)/shard_map/ppermute | solution.py:448
  2.3 20.9 %collective-permute-start.5 = (f32[1024,128]{1,0:T(8,128)}, f32[1024,128]{1,0:T(8,128)S(1)}, u32[]{:S(2)}, u32[]{:S(2)}) collective-permute-start(f32[1024,128]{1,0:T(8,128)} %bitcast.5), channel_id=1, source_target_pairs={{1,0},{0,1},{3,2},{2,3},{5,4},{4,5},{7,6},{6,7},{9,8},{8,9},{11,10... | collective-permute-start | bytes 1572872 | tf_op jit(solution)/shard_map/ppermute | solution.py:431
  6.0 11.6 %collective-permute-start.8 = (f32[520,128]{1,0:T(8,128)S(1)}, f32[520,128]{1,0:T(8,128)S(1)}, u32[]{:S(2)}, u32[]{:S(2)}) collective-permute-start(f32[520,128]{1,0:T(8,128)S(1)} %get-tuple-element.40.packed_ref), channel_id=1, source_target_pairs={{0,2},{2,4},{4,6},{6,8},{8,10},{10,12},{12,14},{14,16},{16,18},{18... | collective-permute-start | bytes 798728 | tf_op jit(solution)/shard_map/ppermute | solution.py:466
  9.3 2.5 %collective-permute-start.1 = (f32[32,256]{1,0:T(8,128)S(1)}, f32[32,256]{1,0:T(8,128)S(1)}, u32[]{:S(2)}, u32[]{:S(2)}) collective-permute-start(f32[32,256]{1,0:T(8,128)S(1)} %get-tuple-element.36), channel_id=1, source_target_pairs={{0,2},{2,0},{4,6},{6,4},{8,10},{10,8},{12,14},{14,12},{16,18},{18,... | collective-permute-start | bytes 98312 | tf_op jit(solution)/shard_map/ppermute | solution.py:415
  11.8 4.2 %collective-permute-start.2 = (f32[32,256]{1,0:T(8,128)S(1)}, f32[32,256]{1,0:T(8,128)S(1)}, u32[]{:S(2)}, u32[]{:S(2)}) collective-permute-start(f32[32,256]{1,0:T(8,128)S(1)} %add.3.terms_ref), channel_id=1, source_target_pairs={{0,18},{2,16},{4,22},{6,20},{8,26},{10,24},{12,30},{14,28},{16,2},... | collective-permute-start | bytes 98312 | tf_op jit(solution)/shard_map/ppermute | solution.py:415
  16.1 3.3 %collective-permute-start.3 = (f32[32,256]{1,0:T(8,128)S(1)}, f32[32,256]{1,0:T(8,128)S(1)}, u32[]{:S(2)}, u32[]{:S(2)}) collective-permute-start(f32[32,256]{1,0:T(8,128)S(1)} %sum.3.terms_ref), channel_id=1, source_target_pairs={{0,10},{2,8},{4,14},{6,12},{8,2},{10,0},{12,6},{14,4},{16,26},{18,... | collective-permute-start | bytes 98312 | tf_op jit(solution)/shard_map/ppermute | solution.py:415
  17.7 13.7 %collective-permute-start.9 = (f32[128,512]{1,0:T(8,128)S(1)}, f32[128,512]{1,0:T(8,128)S(1)}, u32[]{:S(2)}, u32[]{:S(2)}) collective-permute-start(f32[128,512]{1,0:T(8,128)S(1)} %complete.1.refs_0_), channel_id=1, source_target_pairs={{1,0},{0,1},{3,2},{2,3},{5,4},{4,5},{7,6},{6,7},{9,8},{8,9},{11,10... | collective-permute-start | bytes 786440 | tf_op jit(solution)/shard_map/ppermute | solution.py:431
  19.4 7.8 %copy-start = (f32[32,2,4,1,512]{4,3,2,1,0:T(1,128)S(1)}, f32[32,2,4,1,512]{4,3,2,1,0:T(1,128)}, u32[]{:S(2)}) copy-start(f32[32,2,4,1,512]{4,3,2,1,0:T(1,128)} %param.11) | copy-start | bytes 1572868
  19.4 3.8 %collective-permute-start.4 = (f32[32,256]{1,0:T(8,128)S(1)}, f32[32,256]{1,0:T(8,128)S(1)}, u32[]{:S(2)}, u32[]{:S(2)}) collective-permute-start(f32[32,256]{1,0:T(8,128)S(1)} %sum.4.terms_ref), channel_id=1, source_target_pairs={{0,6},{2,4},{4,2},{6,0},{8,14},{10,12},{12,10},{14,8},{16,22},{18,... | collective-permute-start | bytes 98312 | tf_op jit(solution)/shard_map/ppermute | solution.py:415
  23.2 3.4 %collective-permute-start.6 = (f32[32,256]{1,0:T(8,128)S(1)}, f32[32,256]{1,0:T(8,128)S(1)}, u32[]{:S(2)}, u32[]{:S(2)}) collective-permute-start(f32[32,256]{1,0:T(8,128)S(1)} %sum.5.refs_0_), channel_id=1, source_target_pairs={{3,0},{2,1},{1,2},{0,3},{7,4},{6,5},{5,6},{4,7},{11,8},{10,9},{9,1... | collective-permute-start | bytes 98312 | tf_op jit(solution)/shard_map/ppermute | solution.py:424
  26.7 1.4 %copy-start.1 = (f32[2,64,256]{2,1,0:T(8,128)S(1)}, f32[2,64,256]{2,1,0:T(8,128)}, u32[]{:S(2)}) copy-start(f32[2,64,256]{2,1,0:T(8,128)} %noise_ref.1) | copy-start | bytes 393220
  26.7 1.4 %copy-start.2 = (f32[2,256]{1,0:T(2,128)S(1)}, f32[2,256]{1,0:T(2,128)}, u32[]{:S(2)}) copy-start(f32[2,256]{1,0:T(2,128)} %value_ref.1) | copy-start | bytes 6148
  26.7 1.4 %copy-start.3 = (f32[2,256]{1,0:T(2,128)S(1)}, f32[2,256]{1,0:T(2,128)}, u32[]{:S(2)}) copy-start(f32[2,256]{1,0:T(2,128)} %error_ref.1) | copy-start | bytes 6148
  26.7 1.4 %collective-permute-start.7 = (f32[64,256]{1,0:T(8,128)S(1)}, f32[64,256]{1,0:T(8,128)S(1)}, u32[]{:S(2)}, u32[]{:S(2)}) collective-permute-start(f32[64,256]{1,0:T(8,128)S(1)} %gather.1.kept_ref), channel_id=1, source_target_pairs={{0,2},{2,0},{4,6},{6,4},{8,10},{10,8},{12,14},{14,12},{16,18},{18,... | collective-permute-start | bytes 196616 | tf_op jit(solution)/shard_map/ppermute | solution.py:415
